TPU v7x, 32 devices: a whole 2x2x4 slice. The times are simulated.
32 devices in a mesh: seq: 8 (over z, y), tp: 4 (over x, core).
Axes of the slice: x: 2, y: 2, z: 4, core: 2. Of those that a mesh axis runs over, the one named last changes fastest.
Arguments:
- normed: bfloat16 [4096, 2048], P('seq', 'tp'), may hold values from -24 to 24
- cluster: int32 [4096, 1], P('seq'), may hold values from 0 to 127; in each aligned block of 512 rows (0 to 511, 512 to 1023, ...) at most 8 rows name the same one
- w_query: bfloat16 [2048, 2048], P(None, 'tp'), may hold values from -1 to 1
- w_key: bfloat16 [2048, 2048], P(None, 'tp'), may hold values from -1 to 1
- w_value: bfloat16 [2048, 2048], P(None, 'tp'), may hold values from -0.125 to 0.125
- w_out: bfloat16 [2048, 2048], P('tp'), may hold values from -0.125 to 0.125
- grad_out: bfloat16 [4096, 2048], P('seq', 'tp'), may hold values from -6 to 6
Outputs:
- attended: bfloat16 [4096, 2048], P('seq', 'tp')
- grad_normed: float32 [4096, 2048], P('seq', 'tp')
Inputs may be any that keep to these rules, and one draw needn't show every extreme that they name: Among the tokens of one index of seq no cluster id appears more than 8 times, and some id appears exactly 8 times; every id appears somewhere.
All inputs are finite; a program needn't handle non-finite values.
Results may differ from a plain program's by a relative error of at most 0.011.
The roundings to bfloat16 on the way count: a program that leaves them out, or rounds other values in their place, can miss the bound.
Values may be sent and summed in bfloat16 or wider, within the bound.
No kernel may reach another device: no remote copies, remote signals or barrier semaphores. Data moves between devices by JAX's collectives and lax.ppermute only.
A program may use at most 128 MiB of HBM per device.

v0:
```python
import jax
import jax.numpy as jnp
from jax import lax
from jax.sharding import PartitionSpec as P

HEAD_DIM = 128
CLUSTERS = 128
CAP = 256
MOST = 8


def entering(x, axis, combine, identity):
    count, position = (lax.axis_size(axis), lax.axis_index(axis))
    everything = lax.all_gather(x, axis)
    start = jnp.broadcast_to(jnp.asarray(identity, x.dtype), x.shape)

    def lap(k, before):
        reached = k < position
        new = combine(before, everything[k])
        return jnp.where(reached, new, before)

    return lax.fori_loop(0, count, lap, start)


def cluster_probs(query, key_rows, usable):
    score_scale = query.shape[-1] ** (-0.5)
    scores = (
        jnp.einsum("qhd,khd->hqk", query, key_rows, preferred_element_type=jnp.float32)
        * score_scale
    )
    scores = jnp.where(usable[None, None, :], scores, -1e30)
    row_top = jnp.max(scores, axis=-1, keepdims=True)
    raised = jnp.exp(scores - row_top)
    return raised / jnp.sum(raised, axis=-1, keepdims=True)


def unpack(packed):
    width = packed.shape[1] // 3
    rows = packed.shape[0]
    query = packed[:, :width].reshape(rows, -1, HEAD_DIM)
    key_rows = packed[:, width : 2 * width].reshape(rows, -1, HEAD_DIM)
    value_rows = packed[:, 2 * width :].reshape(rows, -1, HEAD_DIM)
    return (query, key_rows, value_rows)


def forward_one(packed, usable):
    query, key_rows, value_rows = unpack(packed)
    probs = cluster_probs(query, key_rows, usable)
    mixed = jnp.einsum(
        "hqk,khd->qhd", probs.astype(jnp.bfloat16), value_rows, preferred_element_type=jnp.float32
    )
    return mixed.reshape(packed.shape[0], -1).astype(jnp.bfloat16)


def attention_core(packed, usable, grad_rows):
    query, key_rows, value_rows = unpack(packed)
    rows = packed.shape[0]
    score_scale = query.shape[-1] ** (-0.5)
    grad_heads = grad_rows.reshape(rows, -1, HEAD_DIM)
    probs = cluster_probs(query, key_rows, usable)
    rounded = probs.astype(jnp.bfloat16)
    mixed = jnp.einsum("hqk,khd->qhd", rounded, value_rows, preferred_element_type=jnp.float32)
    grad_value = jnp.einsum("hqk,qhd->khd", rounded, grad_heads, preferred_element_type=jnp.float32)
    grad_probs = jnp.einsum(
        "qhd,khd->hqk", grad_heads, value_rows, preferred_element_type=jnp.float32
    )
    inner = jnp.sum(grad_probs * probs, axis=-1, keepdims=True)
    grad_scores = (probs * (grad_probs - inner) * score_scale).astype(jnp.bfloat16)
    grad_query = jnp.einsum(
        "hqk,khd->qhd", grad_scores, key_rows, preferred_element_type=jnp.float32
    )
    grad_key = jnp.einsum("hqk,qhd->khd", grad_scores, query, preferred_element_type=jnp.float32)
    grads = jnp.concatenate(
        [
            grad_query.reshape(rows, -1).astype(jnp.bfloat16),
            grad_key.reshape(rows, -1).astype(jnp.bfloat16),
            grad_value.reshape(rows, -1).astype(jnp.bfloat16),
        ],
        axis=1,
    )
    return (mixed.reshape(rows, -1).astype(jnp.bfloat16), grads)


def body(normed, cluster, w_query, w_key, w_value, w_out, grad_out):
    seq_count = lax.axis_size("seq")
    local_cols = w_query.shape[1]
    cluster_here = CLUSTERS // seq_count
    cluster_ids = cluster[:, 0]
    columns = jnp.arange(CLUSTERS, dtype=jnp.int32)
    one_hot = (cluster_ids[:, None] == columns[None, :]).astype(jnp.int32)
    running = jnp.cumsum(one_hot, axis=0)
    local_rank = jnp.sum((running - one_hot) * one_hot, axis=1)
    counts = running[-1]
    offsets = entering(
        counts, "seq", lambda earlier, later: earlier + later, jnp.zeros_like(counts)
    )
    global_rank = local_rank + jnp.sum(one_hot * offsets[None, :], axis=1)
    kept_rows = (global_rank < CAP).astype(jnp.bfloat16)
    slot_index = cluster_ids * MOST + local_rank
    piece = lax.all_gather(normed, "tp", axis=1, tiled=True)
    query_sum = jnp.dot(piece, w_query, preferred_element_type=jnp.float32)
    key_sum = jnp.dot(piece, w_key, preferred_element_type=jnp.float32)
    value_sum = jnp.dot(piece, w_value, preferred_element_type=jnp.float32)
    packed_rows = jnp.concatenate(
        [
            query_sum.astype(jnp.bfloat16),
            key_sum.astype(jnp.bfloat16),
            value_sum.astype(jnp.bfloat16),
        ],
        axis=1,
    )
    head_grads = (
        lax.dot_general(
            lax.all_gather(grad_out, "tp", axis=1, tiled=True),
            w_out,
            (((1,), (1,)), ((), ())),
            preferred_element_type=jnp.float32,
        ).astype(jnp.bfloat16)
        * kept_rows[:, None]
    )

    def to_owners(rows):
        buffer = jnp.zeros((CLUSTERS * MOST, rows.shape[1]), rows.dtype).at[slot_index].set(rows)
        return buffer.reshape(seq_count, cluster_here, MOST, rows.shape[1])

    flags = (
        jnp.zeros((CLUSTERS * MOST,), jnp.bfloat16)
        .at[slot_index]
        .set(kept_rows)
        .reshape(seq_count, cluster_here, MOST)
    )

    def from_owners(slots):
        return slots.reshape(cluster_here, seq_count, MOST, slots.shape[-1])

    def to_tokens(returned):
        return (
            returned.reshape(CLUSTERS * MOST, returned.shape[-1])[slot_index] * kept_rows[:, None]
        )

    arrived, arrived_flags = (
        lax.all_to_all(to_owners(packed_rows), "seq", split_axis=0, concat_axis=2, tiled=True),
        lax.all_to_all(flags, "seq", split_axis=0, concat_axis=2, tiled=True),
    )
    usable = arrived_flags[0] > 0
    mixed_slots = lax.map(lambda pair: forward_one(pair[0], pair[1]), (arrived[0], usable))
    heads_tok = to_tokens(
        lax.all_to_all(from_owners(mixed_slots), "seq", split_axis=1, concat_axis=0, tiled=True)
    )
    grad_arrived = lax.all_to_all(
        to_owners(head_grads), "seq", split_axis=0, concat_axis=2, tiled=True
    )
    grad_slots = lax.map(
        lambda triple: attention_core(triple[0], triple[1], triple[2])[1],
        (arrived[0], usable, grad_arrived[0]),
    )
    grads_tok = to_tokens(
        lax.all_to_all(from_owners(grad_slots), "seq", split_axis=1, concat_axis=0, tiled=True)
    )
    partial_out = jnp.dot(heads_tok, w_out, preferred_element_type=jnp.float32)
    attended = lax.psum_scatter(partial_out, "tp", scatter_dimension=1, tiled=True).astype(
        jnp.bfloat16
    )
    contract = (((1,), (1,)), ((), ()))
    partial_grad = lax.dot_general(
        grads_tok[:, :local_cols], w_query, contract, preferred_element_type=jnp.float32
    )
    partial_grad = partial_grad + lax.dot_general(
        grads_tok[:, local_cols : 2 * local_cols],
        w_key,
        contract,
        preferred_element_type=jnp.float32,
    )
    partial_grad = partial_grad + lax.dot_general(
        grads_tok[:, 2 * local_cols :], w_value, contract, preferred_element_type=jnp.float32
    )
    grad_normed = lax.psum_scatter(partial_grad, "tp", scatter_dimension=1, tiled=True)
    return (attended, grad_normed)


def solution(mesh):
    in_specs = (
        P("seq", "tp"),
        P("seq", None),
        P(None, "tp"),
        P(None, "tp"),
        P(None, "tp"),
        P("tp", None),
        P("seq", "tp"),
    )
    out_specs = (P("seq", "tp"), P("seq", "tp"))
    return jax.shard_map(body, mesh=mesh, in_specs=in_specs, out_specs=out_specs, check_vma=False)
```

profile of v0, /device:TPU:0, one launch (start us, length us, event | category | flops | bytes accessed | tf_op | source)
XLA Modules:
  0.0 466.0 jit_solution(17904616771987971157)
XLA Ops:
  9.1 22.2 %all-gather = s32[8,1,128]{2,1,0:T(1,128)S(1)} all-gather(s32[1,1,128]{2,1,0:T(1,128)S(1)} %slice_bitcast_fusion.7), channel_id=1, replica_groups=mesh['seq'=8,'tp'=4] {'seq'}, dimensions={0}, use_global_device_ids=true | all-gather | bytes 4608 | tf_op jit(solution)/shard_map/all_gather | solution.py:14
  31.8 3.8 scatter_custom_fusion.1
  36.4 3.3 all-to-all-start.1
  39.8 3.7 convolution_convert_fusion.5
  43.5 1.3 convolution_convert_fusion.6
  45.1 1.3 convolution_convert_fusion.7
  46.4 1.2 pad_maximum_fusion
  47.6 2.6 copy.82
  50.2 6.0 %scatter_custom_fusion = bf16[1024,1536]{1,0:T(8,128)(2,1)} fusion(s32[512]{0:T(512)S(1)} %bitcast.214, bf16[512,1536]{1,0:T(8,128)(2,1)} %copy.82, bf16[]{:T(256)} %constant.82.clone.1), kind=kCustom, calls=%fused_computation.83 | custom fusion | bytes 3146240 | tf_op jit(solution)/shard_map/scatter | solution.py:123
  56.2 5.9 %all-to-all-start = ((bf16[8,16,8,1536]{3,2,1,0:T(8,128)(2,1)}), bf16[8,16,8,1536]{3,2,1,0:T(8,128)(2,1)}, u32[]{:S(2)}, u32[]{:S(2)}) async-start(bf16[8,16,8,1536]{3,2,1,0:T(8,128)(2,1)} %bitcast.200), calls=%async_computation | async-start | bytes 6291456 | tf_op jit(solution)/shard_map/all_to_all | solution.py:142
  63.0 25.6 %all-gather.6.cloned.1.call-done = bf16[512,2048]{1,0:T(8,128)(2,1)} async-done(((bf16[512,512]{1,0:T(8,128)(2,1)}), bf16[512,2048]{1,0:T(8,128)(2,1)}) %all-gather.6.cloned.1.call-update) | async-done | bytes 2097168 | tf_op jit(solution)/shard_map/all_gather | solution.py:114
  88.6 2.9 fusion.60
  91.4 3.5 scatter_custom_fusion.2
  94.9 34.2 %all-to-all-done = bf16[8,16,8,1536]{3,2,1,0:T(8,128)(2,1)} async-done(((bf16[8,16,8,1536]{3,2,1,0:T(8,128)(2,1)}), bf16[8,16,8,1536]{3,2,1,0:T(8,128)(2,1)}, u32[]{:S(2)}, u32[]{:S(2)}) %all-to-all-start) | async-done | bytes 3145760 | tf_op jit(solution)/shard_map/all_to_all | solution.py:142
  129.1 3.6 all-to-all-start.3
  132.7 3.9 copy_bitcast_fusion.3
  136.6 37.3 %while.34 = (s32[]{:T(128)}, bf16[16,64,512]{2,1,0:T(8,128)(2,1)}, bf16[16,64,1536]{2,1,0:T(8,128)(2,1)}, pred[16,64]{1,0:T(8,128)(4,1)S(1)}, s32[]{:T(128)}) while((s32[]{:T(128)}, bf16[16,64,512]{2,1,0:T(8,128)(2,1)}, bf16[16,64,1536]{2,1,0:T(8,128)(2,1)}, pred[16,64]{1,0:T(8,128)(4,1)S(1)}, s32[]{:T(128)}) %tuple.86), condition=%wide.region_11.12_spmd, body=%wide.region_8.11_spmd.sunk | while | flops 12763520 | bytes 1706321 | solution.py:146
  173.9 2.3 copy.86
  177.2 5.9 %all-to-all-start.2 = ((bf16[16,8,8,512]{3,2,0,1:T(8,128)(2,1)}), bf16[16,8,8,512]{3,2,0,1:T(8,128)(2,1)S(1)}, u32[]{:S(2)}, u32[]{:S(2)}) async-start(bf16[16,8,8,512]{3,2,0,1:T(8,128)(2,1)} %copy.86), calls=%async_computation.2 | async-start | bytes 2097152 | tf_op jit(solution)/shard_map/all_to_all | solution.py:148
  183.2 2.3 copy_bitcast_fusion.4
  185.5 23.1 %all-to-all-done.2 = bf16[16,8,8,512]{3,2,0,1:T(8,128)(2,1)S(1)} async-done(((bf16[16,8,8,512]{3,2,0,1:T(8,128)(2,1)}), bf16[16,8,8,512]{3,2,0,1:T(8,128)(2,1)S(1)}, u32[]{:S(2)}, u32[]{:S(2)}) %all-to-all-start.2) | async-done | bytes 1048608 | tf_op jit(solution)/shard_map/all_to_all | solution.py:148
  208.7 2.6 gather_fusion
  211.3 4.3 fusion.68
  215.6 1.8 copy-done.3
  217.4 112.4 %while.35 = (s32[]{:T(128)}, bf16[16,64,1536]{2,1,0:T(8,128)(2,1)S(1)}, bf16[16,64,1536]{2,1,0:T(8,128)(2,1)}, pred[16,64]{1,0:T(8,128)(4,1)S(1)}, bf16[16,64,512]{2,1,0:T(8,128)(2,1)}, /*index=5*/s32[]{:T(128)}) while((s32[]{:T(128)}, bf16[16,64,1536]{2,1,0:T(8,128)(2,1)S(1)}, bf16[16,64,1536]{2,1,0:T(8,128)(2,1)}, ...), condition=%wide.region_18.19_spmd, body=%wide.region_14.18_spmd.sunk | while | flops 21988032 | bytes 2953501 | solution.py:153
  219.4 1.4 fusion.146
  220.9 1.2 fusion.150
  222.1 1.3 fusion.149
  226.7 1.4 fusion.146
  228.1 1.2 fusion.150
  233.8 1.4 fusion.146
  235.2 1.2 fusion.150
  240.8 1.4 fusion.146
  242.2 1.2 fusion.150
  247.8 1.4 fusion.146
  249.2 1.2 fusion.150
  254.8 1.4 fusion.146
  256.2 1.2 fusion.150
  261.8 1.4 fusion.146
  263.3 1.2 fusion.150
  268.8 1.4 fusion.146
  270.3 1.2 fusion.150
  275.8 1.4 fusion.146
  277.3 1.2 fusion.150
  282.8 1.4 fusion.146
  284.3 1.2 fusion.150
  289.8 1.4 fusion.146
  291.3 1.2 fusion.150
  296.8 1.4 fusion.146
  298.3 1.2 fusion.150
  303.8 1.4 fusion.146
  305.3 1.2 fusion.150
  310.9 1.4 fusion.146
  312.3 1.2 fusion.150
  317.9 1.4 fusion.146
  324.9 1.4 fusion.146
  330.1 74.2 %all_to_all.69 = bf16[16,8,8,1536]{3,2,0,1:T(8,128)(2,1)S(1)} all-to-all(bf16[16,8,8,1536]{3,2,0,1:T(8,128)(2,1)S(1)} %copy.89), channel_id=1, replica_groups=mesh['seq'=8,'tp'=4] {'seq'}, dimensions={1} | all-to-all | bytes 6291456 | tf_op jit(solution)/shard_map/all_to_all | solution.py:158
  404.3 3.0 gather_fusion.1
  407.3 1.7 broadcast_multiply_fusion
  409.3 1.3 fusion.62
  410.9 1.3 fusion.64
  412.5 3.3 add_add_fusion
  415.8 2.2 convert_element_type.87
  418.0 41.4 %reduce-scatter.5.cloned.1.call-done = f32[512,512]{1,0:T(8,128)} async-done(((f32[512,2048]{1,0:T(8,128)}), f32[512,512]{1,0:T(8,128)}) %reduce-scatter.5.cloned.1.call-update) | async-done | bytes 1048592 | tf_op jit(solution)/shard_map/reduce_scatter | solution.py:177
  (384 shorter events, 113.2 us)
Async XLA Ops:
  7.2 81.4 %copy-start = (bf16[512,2048]{1,0:T(8,128)(2,1)S(1)}, bf16[512,2048]{1,0:T(8,128)(2,1)}, u32[]{:S(2)}) copy-start(bf16[512,2048]{1,0:T(8,128)(2,1)} %param.18) | copy-start | bytes 6291460
  7.2 24.3 %copy-start.9 = (s32[512,1]{0,1:T(1,128)S(1)}, s32[512,1]{0,1:T(1,128)}, u32[]{:S(2)}) copy-start(s32[512,1]{0,1:T(1,128)} %param.14) | copy-start | bytes 6148
  7.2 32.6 %all-gather.4.cloned.1.call-start = ((), (), s32[]{:S(2)}) async-start(), calls=%async_computation.7 | async-start | bytes 2621440 | tf_op jit(solution)/shard_map/all_gather | solution.py:100
  36.4 19.8 %all-to-all-start.1 = ((bf16[8,16,8]{1,2,0:T(8,128)(2,1)}), bf16[8,16,8]{1,2,0:T(8,128)(2,1)S(1)}, u32[]{:S(2)}, u32[]{:S(2)}) async-start(bf16[8,16,8]{1,2,0:T(8,128)(2,1)} %copy.84), calls=%async_computation.1 | async-start | bytes 32768 | tf_op jit(solution)/shard_map/all_to_all | solution.py:143
  39.8 3.7 copy-start.4
  39.8 3.7 copy-start.10
  43.5 1.6 copy-start.6
  56.2 72.9 %all-to-all-start = ((bf16[8,16,8,1536]{3,2,1,0:T(8,128)(2,1)}), bf16[8,16,8,1536]{3,2,1,0:T(8,128)(2,1)}, u32[]{:S(2)}, u32[]{:S(2)}) async-start(bf16[8,16,8,1536]{3,2,1,0:T(8,128)(2,1)} %bitcast.200), calls=%async_computation | async-start | bytes 6291456 | tf_op jit(solution)/shard_map/all_to_all | solution.py:142
  62.1 26.4 %all-gather.6.cloned.1.call-start = ((), (), s32[]{:S(2)}) async-start(), calls=%async_computation.9 | async-start | bytes 2621440 | tf_op jit(solution)/shard_map/all_gather | solution.py:114
  129.1 47.1 %all-to-all-start.3 = ((bf16[8,16,8,512]{3,2,1,0:T(8,128)(2,1)}), bf16[8,16,8,512]{3,2,1,0:T(8,128)(2,1)S(1)}, u32[]{:S(2)}, u32[]{:S(2)}) async-start(bf16[8,16,8,512]{3,2,1,0:T(8,128)(2,1)} %bitcast.202), calls=%async_computation.4 | async-start | bytes 2097152 | tf_op jit(solution)/shard_map/all_to_all | solution.py:150
  176.2 1.0 copy-start.2
  177.2 31.5 %all-to-all-start.2 = ((bf16[16,8,8,512]{3,2,0,1:T(8,128)(2,1)}), bf16[16,8,8,512]{3,2,0,1:T(8,128)(2,1)S(1)}, u32[]{:S(2)}, u32[]{:S(2)}) async-start(bf16[16,8,8,512]{3,2,0,1:T(8,128)(2,1)} %copy.86), calls=%async_computation.2 | async-start | bytes 2097152 | tf_op jit(solution)/shard_map/all_to_all | solution.py:148
  183.1 232.7 %reduce-scatter.3.cloned.1.call-start = ((), (), s32[]{:S(2)}) async-start(), calls=%async_computation.8 | async-start | bytes 5242880 | tf_op jit(solution)/shard_map/reduce_scatter | solution.py:161
  215.6 1.9 copy-start.3
  215.6 243.9 %reduce-scatter.5.cloned.1.call-start = ((), (), s32[]{:S(2)}) async-start(), calls=%async_computation.10 | async-start | bytes 5242880 | tf_op jit(solution)/shard_map/reduce_scatter | solution.py:177
  407.3 2.1 copy-start.5
  409.3 1.6 copy-start.7
  410.9 1.6 copy-start.8
  415.8 43.7 %copy-start.1 = (bf16[512,2048]{1,0:T(8,128)(2,1)S(1)}, bf16[512,2048]{1,0:T(8,128)(2,1)}, u32[]{:S(2)}) copy-start(bf16[512,2048]{1,0:T(8,128)(2,1)} %param.18) | copy-start | bytes 6291460
Sparse Core Ops, SparseCore 0:
  9.6 25.2 all-gather.3
  64.5 23.9 all-gather.5
  215.7 43.2 reduce-scatter.2
  415.9 43.5 reduce-scatter.4
where the time goes:
time: 469 us; the launch traced here: 466 us
  waiting for transfers between devices  126 us (27%)
  matrix products  109 us (23%)
  blocking collectives  96.3 us (21%)
  local copies, waits for them, and re-layouts  93.2 us (20%)
  starting transfers between devices  18.9 us (4%)
  between operations  14.1 us (3%)
  other arithmetic  6.26 us (1%)
    all_to_all x1, blocking collectives, body(): lax.all_to_all(from_owners(grad_slots), 'seq', split_axis=1, concat_axis=...  74.2 us
    reduce_scatter x1, waiting for transfers between devices, body(): lax.psum_scatter(partial_grad, 'tp', scatter_dimension=1, tiled=True)  41.4 us
    all_to_all x1, waiting for transfers between devices, body(): lax.all_to_all(to_owners(packed_rows), 'seq', split_axis=0, concat_axis=2...  34.2 us
    squeeze x32, local copies, waits for them, and re-layouts, body(): lax.map(lambda pair: forward_one(pair[0], pair[1]), (arrived[0], usable))  30.3 us
    sub x32, matrix products, cluster_probs(): raised = jnp.exp(scores - row_top)  26.4 us
    all_gather x1, waiting for transfers between devices, body(): lax.all_gather(grad_out, 'tp', axis=1, tiled=True)  25.6 us
    all_to_all x1, waiting for transfers between devices, body(): lax.all_to_all(from_owners(mixed_slots), 'seq', split_axis=1, concat_axis...  23.1 us
    all_gather x1, blocking collectives, entering(): everything = lax.all_gather(x, axis)  22.2 us
  transfers between devices with their start and end apart: 8, of which 4 were waited for; matrix products, arithmetic and copies ran while one was open for 43% of the time, Pallas kernels for 0%

commit v1 on v0

v1 whole, which is shorter than its diff:
```python
import functools
import jax
import jax.numpy as jnp
from jax import lax
from jax.experimental import pallas as pl
from jax.experimental.pallas import tpu as pltpu
from jax.sharding import PartitionSpec as P

HEAD_DIM = 128
CLUSTERS = 128
CAP = 256
MOST = 8
NT = (((1,), (1,)), ((), ()))
TN = (((0,), (0,)), ((), ()))
MB = 1024 * 1024
CHUNKS = 2


def dot(a, b, dims=(((1,), (0,)), ((), ()))):
    return lax.dot_general(a, b, dims, preferred_element_type=jnp.float32)


def swap(x, bit):
    count = lax.axis_size("tp")
    return lax.ppermute(x, "tp", [(i, i ^ bit) for i in range(count)])


def exchange(x):
    return lax.all_to_all(x, "seq", split_axis=0, concat_axis=0, tiled=True)


def place_kernel(base_col, base_row, x_ref, slot_col, slot_row, counts, out_ref):
    tokens = x_ref.shape[0]
    here = lax.broadcasted_iota(jnp.int32, (tokens, tokens), 0)
    there = lax.broadcasted_iota(jnp.int32, (tokens, tokens), 1)
    same = base_col[...] == base_row[...]
    earlier = jnp.where(same & (there < here), 1.0, 0.0)
    later = jnp.where(same & (here < there), 1.0, 0.0)
    slot_col[...] = base_col[...] + jnp.sum(earlier, axis=1, keepdims=True).astype(jnp.int32)
    slot_row[...] = base_row[...] + jnp.sum(later, axis=0, keepdims=True).astype(jnp.int32)
    lane = lax.broadcasted_iota(jnp.int32, (tokens, CLUSTERS), 1)
    named = jnp.where(base_col[...] == lane * MOST, 1.0, 0.0)
    counts[...] = jnp.sum(named, axis=0, keepdims=True).astype(jnp.int32)
    slots = out_ref.shape[0]
    place = lax.broadcasted_iota(jnp.int32, (slots, tokens), 0) == slot_row[...]
    out_ref[...] = dot(jnp.where(place, 1.0, 0.0).astype(jnp.bfloat16), x_ref[...]).astype(
        jnp.bfloat16
    )


def place(base, x):
    tokens = x.shape[0]
    return pl.pallas_call(
        place_kernel,
        out_shape=(
            jax.ShapeDtypeStruct((tokens, 1), jnp.int32),
            jax.ShapeDtypeStruct((1, tokens), jnp.int32),
            jax.ShapeDtypeStruct((1, CLUSTERS), jnp.int32),
            jax.ShapeDtypeStruct((CLUSTERS * MOST, x.shape[1]), jnp.bfloat16),
        ),
        compiler_params=pltpu.CompilerParams(vmem_limit_bytes=32 * MB),
        name="place",
    )(base[:, None], base[None, :], x)


def head_grads_kernel(blk, a0, a1, a2, a3, w_out, slot_row, out_ref):
    width = a0.shape[1]
    total = None
    for j, part in enumerate((a0, a1, a2, a3)):
        cols = pl.ds(pl.multiple_of(blk[j] * width, width), width)
        term = dot(part[...], w_out[:, cols], NT)
        total = term if total is None else total + term
    slots, tokens = (out_ref.shape[0], a0.shape[0])
    placed = lax.broadcasted_iota(jnp.int32, (slots, tokens), 0) == slot_row[...]
    out_ref[...] = dot(
        jnp.where(placed, 1.0, 0.0).astype(jnp.bfloat16), total.astype(jnp.bfloat16)
    ).astype(jnp.bfloat16)


VMEM = pl.BlockSpec(memory_space=pltpu.VMEM)
SMEM = pl.BlockSpec(memory_space=pltpu.SMEM)


def head_grads(blk, parts, w_out, slot_row):
    return pl.pallas_call(
        head_grads_kernel,
        out_shape=jax.ShapeDtypeStruct((CLUSTERS * MOST, w_out.shape[0]), jnp.bfloat16),
        in_specs=[SMEM] + [VMEM] * 6,
        out_specs=VMEM,
        compiler_params=pltpu.CompilerParams(vmem_limit_bytes=32 * MB),
        name="head_grads",
    )(blk, *parts, w_out, slot_row)


def core_kernel(
    blk, x0, x1, x2, x3, g_ref, vrow, vcol, wq, wk, wv, mixed, keep, give, dq, dk, dv
):
    sources, rows, width = x0.shape
    members = sources * rows
    heads = wq.shape[1] // HEAD_DIM
    scale = HEAD_DIM ** (-0.5)
    spans = [pl.ds(pl.multiple_of(blk[j] * width, width), width) for j in range(4)]
    xs = [r[...].reshape(members, width) for r in (x0, x1, x2, x3)]

    def project(w):
        total = dot(xs[0], w[spans[0], :])
        for j in range(1, 4):
            total = total + dot(xs[j], w[spans[j], :])
        return total.astype(jnp.bfloat16)

    queries, keys, values = (project(wq), project(wk), project(wv))
    here = lax.broadcasted_iota(jnp.int32, (members, members), 0) % rows // MOST
    there = lax.broadcasted_iota(jnp.int32, (members, members), 1) % rows // MOST
    usable = (here == there) & (vrow[0] > 0)
    row_kept = vcol[0]
    grads = (g_ref[...].reshape(members, -1).astype(jnp.float32) * row_kept).astype(jnp.bfloat16)
    for h in range(heads):
        cols = slice(h * HEAD_DIM, (h + 1) * HEAD_DIM)
        q, k, v, g = (queries[:, cols], keys[:, cols], values[:, cols], grads[:, cols])
        scores = jnp.where(usable, dot(q, k, NT) * scale, -1e30)
        raised = jnp.exp(scores - jnp.max(scores, axis=1, keepdims=True))
        probs = raised * (1.0 / jnp.sum(raised, axis=1, keepdims=True))
        rounded = probs.astype(jnp.bfloat16)
        out = (dot(rounded, v) * row_kept).astype(jnp.bfloat16)
        mixed[:, :, cols] = out.reshape(sources, rows, HEAD_DIM)
        dv[:, cols] = dot(rounded, g, TN).astype(jnp.bfloat16)
        grad_probs = dot(g, v, NT)
        inner = jnp.sum(grad_probs * probs, axis=1, keepdims=True)
        grad_scores = (probs * (grad_probs - inner) * scale).astype(jnp.bfloat16)
        dq[:, cols] = dot(grad_scores, k).astype(jnp.bfloat16)
        dk[:, cols] = dot(grad_scores, q, TN).astype(jnp.bfloat16)
    for j in range(4):
        total = dot(dq[...], wq[spans[j], :], NT)
        total = total + dot(dk[...], wk[spans[j], :], NT)
        total = total + dot(dv[...], wv[spans[j], :], NT)
        target = (keep, give, keep, give)[j]
        target[j // 2] = total.astype(jnp.bfloat16).reshape(sources, rows, width)


def core(blk, parts, grads, valid, wq, wk, wv):
    sources, rows, width = parts[0].shape
    heads_width = wq.shape[1]
    step = 16
    while step * 2 * sources <= 256 and rows % (step * 2) == 0:
        step *= 2
    members, steps = (sources * step, rows // step)
    by_step = valid.reshape(sources, steps, step).transpose(1, 0, 2).reshape(steps, members)
    block = pl.BlockSpec((sources, step, width), lambda p: (0, p, 0))
    hblock = pl.BlockSpec((sources, step, heads_width), lambda p: (0, p, 0))
    pair = pl.BlockSpec((2, sources, step, width), lambda p: (0, 0, p, 0))
    weight = pl.BlockSpec(wq.shape, lambda p: (0, 0), pipeline_mode=pl.Buffered(1))
    return pl.pallas_call(
        core_kernel,
        grid=(steps,),
        out_shape=(
            jax.ShapeDtypeStruct((sources, rows, heads_width), jnp.bfloat16),
            jax.ShapeDtypeStruct((2, sources, rows, width), jnp.bfloat16),
            jax.ShapeDtypeStruct((2, sources, rows, width), jnp.bfloat16),
        ),
        in_specs=[
            SMEM,
            block,
            block,
            block,
            block,
            hblock,
            pl.BlockSpec((1, 1, members), lambda p: (p, 0, 0)),
            pl.BlockSpec((1, members, 1), lambda p: (p, 0, 0)),
            weight,
            weight,
            weight,
        ],
        out_specs=(hblock, pair, pair),
        scratch_shapes=[pltpu.VMEM((members, heads_width), jnp.bfloat16)] * 3,
        compiler_params=pltpu.CompilerParams(vmem_limit_bytes=40 * MB),
        cost_estimate=pl.CostEstimate(
            flops=2 * sources * rows * width * 4 * heads_width * 6,
            bytes_accessed=16 * MB,
            transcendentals=sources * rows * members * 4,
        ),
        name="core",
    )(blk, *parts, grads, by_step[:, None, :], by_step[:, :, None], wq, wk, wv)


def core_many(blk, parts, grads, valid, wq, wk, wv):
    sources, rows, width = parts[0].shape
    heads = wq.shape[1] // HEAD_DIM
    clusters = rows // MOST
    scale = HEAD_DIM ** (-0.5)

    def slab(w, j):
        return lax.dynamic_slice_in_dim(w, blk[j] * width, width, 0)

    def by_cluster(x):
        x = x.reshape(sources, clusters, MOST, -1).transpose(1, 0, 2, 3)
        return x.reshape(clusters, sources * MOST, -1)

    def by_source(x):
        x = x.reshape(clusters, sources, MOST, -1).transpose(1, 0, 2, 3)
        return x.reshape(sources, rows, -1)

    def project(w):
        total = 0.0
        for j in range(4):
            total = total + jnp.einsum(
                "srd,dh->srh", parts[j], slab(w, j), preferred_element_type=jnp.float32
            )
        return by_cluster(total.astype(jnp.bfloat16))

    kept = by_cluster(valid[:, :, None])

    def one(args):
        q, k, v, g, live = args
        q, k, v, g = (a.reshape(a.shape[0], heads, HEAD_DIM) for a in (q, k, v, g))
        ein = functools.partial(jnp.einsum, preferred_element_type=jnp.float32)
        g = (g * live[:, :, None]).astype(jnp.bfloat16)
        scores = jnp.where(live[None, None, :, 0] > 0, ein("qhd,khd->hqk", q, k) * scale, -1e30)
        raised = jnp.exp(scores - jnp.max(scores, axis=-1, keepdims=True))
        probs = raised / jnp.sum(raised, axis=-1, keepdims=True)
        rounded = probs.astype(jnp.bfloat16)
        mixed = (ein("hqk,khd->qhd", rounded, v) * live[:, :, None]).astype(jnp.bfloat16)
        dv = ein("hqk,qhd->khd", rounded, g).astype(jnp.bfloat16)
        grad_probs = ein("qhd,khd->hqk", g, v)
        inner = jnp.sum(grad_probs * probs, axis=-1, keepdims=True)
        grad_scores = (probs * (grad_probs - inner) * scale).astype(jnp.bfloat16)
        dq = ein("hqk,khd->qhd", grad_scores, k).astype(jnp.bfloat16)
        dk = ein("hqk,qhd->khd", grad_scores, q).astype(jnp.bfloat16)
        return tuple(a.reshape(a.shape[0], -1) for a in (mixed, dq, dk, dv))

    mixed, dq, dk, dv = lax.map(
        one, (project(wq), project(wk), project(wv), by_cluster(grads), kept)
    )
    outs = []
    for j in range(4):
        total = 0.0
        for d, w in ((dq, wq), (dk, wk), (dv, wv)):
            total = total + jnp.einsum(
                "crh,wh->crw", d, slab(w, j), preferred_element_type=jnp.float32
            )
        outs.append(by_source(total.astype(jnp.bfloat16)))
    return (by_source(mixed), jnp.stack([outs[0], outs[2]]), jnp.stack([outs[1], outs[3]]))


def pick(slot_col, parts):
    tokens = slot_col.shape[0]
    total, first = (None, 0)
    for part in parts:
        rows = part.shape[0]
        slots = lax.broadcasted_iota(jnp.int32, (tokens, rows), 1) + first
        chosen = jnp.where(slots == slot_col[...], 1.0, 0.0).astype(jnp.bfloat16)
        term = dot(chosen, part[...])
        total = term if total is None else total + term
        first += rows
    return total


def out_kernel(blk, slot_col, w_out, *refs):
    parts, keep, give = (refs[:-2], refs[-2], refs[-1])
    heads = pick(slot_col, parts).astype(jnp.bfloat16)
    width = keep.shape[2]
    for j in range(4):
        cols = pl.ds(pl.multiple_of(blk[j] * width, width), width)
        target = (keep, give, keep, give)[j]
        target[j // 2] = dot(heads, w_out[:, cols]).astype(jnp.bfloat16)


def project_out(blk, slot_col, w_out, parts):
    tokens, width = (slot_col.shape[0], w_out.shape[1] // 4)
    shape = jax.ShapeDtypeStruct((2, tokens, width), jnp.bfloat16)
    return pl.pallas_call(
        out_kernel,
        out_shape=(shape, shape),
        in_specs=[SMEM] + [VMEM] * (2 + len(parts)),
        out_specs=(VMEM, VMEM),
        compiler_params=pltpu.CompilerParams(vmem_limit_bytes=32 * MB),
        name="project_out",
    )(blk, slot_col, w_out, *parts)


def final_kernel(slot_col, *refs):
    refs[-1][...] = pick(slot_col, refs[:-1])


def to_tokens(slot_col, parts):
    return pl.pallas_call(
        final_kernel,
        out_shape=jax.ShapeDtypeStruct((slot_col.shape[0], parts[0].shape[1]), jnp.float32),
        compiler_params=pltpu.CompilerParams(vmem_limit_bytes=32 * MB),
        name="to_tokens",
    )(slot_col, *parts)


def gather_parts(x):
    across = swap(x, 2)
    return (x, swap(x, 1), across, swap(across, 1))


def wide(x):
    return x.astype(jnp.float32)


def reduce_parts(keep, give):
    got = swap(give, 1)
    across = swap((wide(keep[1]) + wide(got[1])).astype(jnp.bfloat16), 2)
    return (wide(keep[0]) + wide(got[0]) + wide(across)).astype(jnp.bfloat16)


def body(normed, cluster, w_query, w_key, w_value, w_out, grad_out):
    seq_count = lax.axis_size("seq")
    cluster_here = CLUSTERS // seq_count
    chunks = CHUNKS if cluster_here * MOST // CHUNKS % 16 == 0 else 1
    per_chunk = cluster_here // chunks
    rows = per_chunk * MOST
    span = seq_count * rows
    ids = cluster[:, 0]
    owner, local = (ids // cluster_here, ids % cluster_here)
    base = (local // per_chunk) * span + owner * rows + (local % per_chunk) * MOST
    blk = lax.axis_index("tp") ^ jnp.arange(4, dtype=jnp.int32)

    slot_col, slot_row, counts, x_slots = place(base, normed)
    pieces = x_slots.reshape(chunks, seq_count, rows, -1)
    arrived = [exchange(pieces[c]) for c in range(chunks)]
    counts = counts.reshape(chunks, seq_count, per_chunk).transpose(1, 0, 2)
    counts = exchange(counts)
    before = jnp.cumsum(counts, axis=0) - counts
    kept = jnp.clip(CAP - before, 0, counts)
    valid = (jnp.arange(MOST) < kept[..., None]).astype(jnp.float32)
    valid = valid.reshape(seq_count, chunks, rows)

    g_slots = head_grads(blk, gather_parts(grad_out), w_out, slot_row)
    g_pieces = g_slots.reshape(chunks, seq_count, rows, -1)
    g_arrived = [exchange(g_pieces[c]) for c in range(chunks)]

    run = core if seq_count * 16 <= 256 else core_many
    mixed_back, grads_back = ([], [])
    for c in range(chunks):
        mixed, keep, give = run(
            blk, gather_parts(arrived[c]), g_arrived[c], valid[:, c], w_query, w_key, w_value
        )
        mixed_back.append(exchange(mixed).reshape(span, -1))
        grads_back.append(exchange(reduce_parts(keep, give)).reshape(span, -1))
    attended = reduce_parts(*project_out(blk, slot_col, w_out, mixed_back))
    return (attended, to_tokens(slot_col, grads_back))


def solution(mesh):
    in_specs = (
        P("seq", "tp"),
        P("seq", None),
        P(None, "tp"),
        P(None, "tp"),
        P(None, "tp"),
        P("tp", None),
        P("seq", "tp"),
    )
    out_specs = (P("seq", "tp"), P("seq", "tp"))
    return jax.shard_map(body, mesh=mesh, in_specs=in_specs, out_specs=out_specs, check_vma=False)
```

time: 469 us -> 208 us (0.44)
  matrix products: 109 us -> 0 us
  blocking collectives: 96.3 us -> 0 us
  local copies, waits for them, and re-layouts: 93.2 us -> 24.7 us
  waiting for transfers between devices: 126 us -> 73 us
  Pallas kernels: 0 us -> 37.6 us
  starting transfers between devices: 18.9 us -> 56.5 us
  between operations: 14.1 us -> 0.89 us
  other arithmetic: 6.26 us -> 13.6 us
    dot_general x104 -> x0, matrix products: 83 us -> none  [the longest x16 19.5 us: attention_core(): jnp.einsum('hqk,khd->qhd', grad_scores, key_rows, preferred_element_type=...]
    all_to_all x1 -> x0, blocking collectives: 74.2 us -> none  [body(): lax.all_to_all(from_owners(grad_slots), 'seq', split_axis=1, concat_axis=...]
    reduce_scatter x2 -> x0, waiting for transfers between devices: 41.5 us -> none  [the longest x1 41.4 us: body(): lax.psum_scatter(partial_grad, 'tp', scatter_dimension=1, tiled=True)]
    pallas_call x0 -> x6, Pallas kernels: none -> 37.6 us  [the longest x2 28.5 us: core(): pl.pallas_call(core_kernel, grid=(steps,), out_shape=(jax.ShapeDtypeStruc...]
    squeeze x34 -> x0, local copies, waits for them, and re-layouts: 36.5 us -> none  [the longest x32 30.3 us: body(): lax.map(lambda pair: forward_one(pair[0], pair[1]), (arrived[0], usable))]
    ppermute x0 -> x15, waiting for transfers between devices: none -> 28.7 us  [swap(): return lax.ppermute(x, 'tp', [(i, i ^ bit) for i in range(count)])]
    all_to_all x4 -> x9, starting transfers between devices: 18.7 us -> 46.9 us  [exchange(): return lax.all_to_all(x, 'seq', split_axis=0, concat_axis=0, tiled=True)]
    sub x32 -> x0, matrix products: 26.4 us -> none  [cluster_probs(): raised = jnp.exp(scores - row_top)]
  transfers between devices with their start and end apart: 8 -> 24, of which waited for: 4 -> 10; matrix products, arithmetic and copies ran while one was open for 43% -> 7% of each run, Pallas kernels for 0% -> 18%
where the time goes in v1:
time: 208 us; the launch traced here: 206 us
  waiting for transfers between devices  73 us (35%)
  starting transfers between devices  56.5 us (27%)
  Pallas kernels  37.6 us (18%)
  local copies, waits for them, and re-layouts  24.7 us (12%)
  other arithmetic  13.6 us (7%)
    all_to_all x9, starting transfers between devices, exchange(): return lax.all_to_all(x, 'seq', split_axis=0, concat_axis=0, tiled=True)  46.9 us
    all_to_all x9, waiting for transfers between devices, exchange(): return lax.all_to_all(x, 'seq', split_axis=0, concat_axis=0, tiled=True)  44.3 us
    ppermute x15, waiting for transfers between devices, swap(): return lax.ppermute(x, 'tp', [(i, i ^ bit) for i in range(count)])  28.7 us
    pallas_call x2, Pallas kernels, core(): pl.pallas_call(core_kernel, grid=(steps,), out_shape=(jax.ShapeDtypeStruc...  28.5 us
    unnamed x41, local copies, waits for them, and re-layouts  18.8 us
    ppermute x15, starting transfers between devices, swap(): return lax.ppermute(x, 'tp', [(i, i ^ bit) for i in range(count)])  9.52 us
    convert_element_type x3, other arithmetic, reduce_parts(): return (wide(keep[0]) + wide(got[0]) + wide(across)).astype(jnp.bfloat16)  6.38 us
    convert_element_type x3, other arithmetic, reduce_parts(): across = swap((wide(keep[1]) + wide(got[1])).astype(jnp.bfloat16), 2)  4.65 us
  transfers between devices with their start and end apart: 24, of which 10 were waited for; matrix products, arithmetic and copies ran while one was open for 7% of the time, Pallas kernels for 18%

profile of v1, /device:TPU:0, one launch (start us, length us, event | category | flops | bytes accessed | tf_op | source)
XLA Modules:
  0.0 206.4 jit_solution(2587539432550006482)
XLA Ops:
  0.6 0.8 copy.46
  1.5 0.7 broadcast_compare_fusion
  2.2 0.7 fusion.21.base_row
  3.1 0.5 fusion.11.base_col
  3.6 1.0 copy-done.8
  4.6 0.9 place.1
  5.5 0.5 broadcast.212
  6.1 0.7 reduce.3
  6.8 0.6 copy.53
  7.4 7.3 %all-to-all-start.2 = ((s32[8,2,8]{2,1,0:T(2,128)}), s32[8,2,8]{2,1,0:T(2,128)S(1)}, u32[]{:S(2)}, u32[]{:S(2)}) async-start(s32[8,2,8]{2,1,0:T(2,128)} %copy.53), calls=%async_computation.2 | async-start | bytes 16384 | tf_op jit(solution)/shard_map/all_to_all | solution.py:29
  14.7 1.0 fusion.23
  15.7 5.5 %all-to-all-done.2 = s32[8,2,8]{2,1,0:T(2,128)S(1)} async-done(((s32[8,2,8]{2,1,0:T(2,128)}), s32[8,2,8]{2,1,0:T(2,128)S(1)}, u32[]{:S(2)}, u32[]{:S(2)}) %all-to-all-start.2) | async-done | bytes 544 | tf_op jit(solution)/shard_map/all_to_all | solution.py:29
  21.2 4.1 %all-to-all-start.4 = ((bf16[8,64,512]{2,1,0:T(8,128)(2,1)}), bf16[8,64,512]{2,1,0:T(8,128)(2,1)}, u32[]{:S(2)}, u32[]{:S(2)}) async-start(bf16[8,64,512]{2,1,0:T(8,128)(2,1)} %bitcast.57), calls=%async_computation.4 | async-start | bytes 1048576 | tf_op jit(solution)/shard_map/all_to_all | solution.py:29
  25.4 1.6 collective-permute-start.4
  26.9 11.8 %all-to-all-done.4.x0 = bf16[8,64,512]{2,1,0:T(8,128)(2,1)} async-done(((bf16[8,64,512]{2,1,0:T(8,128)(2,1)}), bf16[8,64,512]{2,1,0:T(8,128)(2,1)}, u32[]{:S(2)}, u32[]{:S(2)}) %all-to-all-start.4) | async-done | bytes 524320 | tf_op jit(solution)/shard_map/all_to_all | solution.py:29
  38.7 4.2 %all-to-all-start = ((bf16[8,64,512]{2,1,0:T(8,128)(2,1)}), bf16[8,64,512]{2,1,0:T(8,128)(2,1)}, u32[]{:S(2)}, u32[]{:S(2)}) async-start(bf16[8,64,512]{2,1,0:T(8,128)(2,1)} %bitcast.56), calls=%async_computation | async-start | bytes 1048576 | tf_op jit(solution)/shard_map/all_to_all | solution.py:29
  43.5 1.5 collective-permute-done.3.a1
  45.0 0.7 collective-permute-done.5.a3
  45.7 3.1 %head_grads.1 = bf16[1024,512]{1,0:T(8,128)(2,1)S(1)} custom-call(s32[4]{0:T(128)S(1)} %iota_xor_fusion.blk, bf16[512,512]{1,0:T(8,128)(2,1)S(1)} %copy-done.7, bf16[512,512]{1,0:T(8,128)(2,1)} %collective-permute-done.3.a1, bf16[512,512]{1,0:T(8,128)(2,1)S(1)} %collective-permute-done.4.a2, bf16[512,512]{1,0:T(8,128)(2,1)} %collective-permute-done.5.a3, ...), custom_call_target="tpu_custom_call" | custom-call | tf_op jit(solution)/shard_map/head_grads/pallas_call | solution.py:85
  48.8 1.0 fusion.22
  49.9 6.4 %all-to-all-done.x0 = bf16[8,64,512]{2,1,0:T(8,128)(2,1)} async-done(((bf16[8,64,512]{2,1,0:T(8,128)(2,1)}), bf16[8,64,512]{2,1,0:T(8,128)(2,1)}, u32[]{:S(2)}, u32[]{:S(2)}) %all-to-all-start) | async-done | bytes 524320 | tf_op jit(solution)/shard_map/all_to_all | solution.py:29
  56.3 3.7 %all-to-all-start.5 = ((bf16[8,64,512]{2,1,0:T(8,128)(2,1)}), bf16[8,64,512]{2,1,0:T(8,128)(2,1)S(1)}, u32[]{:S(2)}, u32[]{:S(2)}) async-start(bf16[8,64,512]{2,1,0:T(8,128)(2,1)} %bitcast.7), calls=%async_computation.5 | async-start | bytes 1048576 | tf_op jit(solution)/shard_map/all_to_all | solution.py:29
  59.9 1.5 collective-permute-start.7
  61.5 0.6 collective-permute-start.1
  62.1 13.0 %collective-permute-done.7.x2 = bf16[8,64,512]{2,1,0:T(8,128)(2,1)} collective-permute-done((bf16[8,64,512]{2,1,0:T(8,128)(2,1)}, bf16[8,64,512]{2,1,0:T(8,128)(2,1)}, u32[]{:S(2)}, u32[]{:S(2)}) %collective-permute-start.7) | collective-permute-done | bytes 524320 | tf_op jit(solution)/shard_map/ppermute | solution.py:25
  75.3 6.0 %all-to-all-start.1 = ((bf16[8,64,512]{2,1,0:T(8,128)(2,1)}), bf16[8,64,512]{2,1,0:T(8,128)(2,1)S(1)}, u32[]{:S(2)}, u32[]{:S(2)}) async-start(bf16[8,64,512]{2,1,0:T(8,128)(2,1)} %bitcast.55), calls=%async_computation.1 | async-start | bytes 1048576 | tf_op jit(solution)/shard_map/all_to_all | solution.py:29
  81.4 1.0 broadcast_in_dim_reshape.17.vcol
  82.7 1.4 collective-permute-done.1.x2
  84.2 0.9 copy-done.11
  85.1 1.6 copy-done.13
  86.7 1.6 copy-done.15
  88.3 1.6 copy-done.17
  89.9 14.6 %core.3 = (bf16[8,64,512]{2,1,0:T(8,128)(2,1)S(1)}, bf16[2,8,64,512]{3,2,1,0:T(8,128)(2,1)S(1)}, bf16[2,8,64,512]{3,2,1,0:T(8,128)(2,1)}) custom-call(s32[4]{0:T(128)S(1)} %iota_xor_fusion.blk, bf16[8,64,512]{2,1,0:T(8,128)(2,1)} %all-to-all-done.4.x0, bf16[8,64,512]{2,1,0:T(8,128)(2,1)} %collective-permute-done.6.x1, ...), custom_call_target="tpu_custom_call" | custom-call | flops 6442450944 | bytes 16777216 | tf_op jit(solution)/shard_map/core/pallas_call | solution.py:152
  104.5 1.0 copy-done.1
  105.5 0.8 copy-done.9
  106.3 0.5 collective-permute-start.13
  106.8 5.7 %all-to-all-start.6 = ((bf16[8,64,512]{2,1,0:T(8,128)(2,1)}), bf16[8,64,512]{2,1,0:T(8,128)(2,1)S(1)}, u32[]{:S(2)}, u32[]{:S(2)}) async-start(bf16[8,64,512]{2,1,0:T(8,128)(2,1)} %copy-done.9), calls=%async_computation.6 | async-start | bytes 1048576 | tf_op jit(solution)/shard_map/all_to_all | solution.py:29
  112.6 1.0 broadcast_in_dim_reshape.16.vcol
  113.6 0.9 copy-done.12
  114.6 1.6 copy-done.14
  116.2 1.6 copy-done.16
  117.8 1.6 copy-done.18
  119.4 13.9 %core.2 = (bf16[8,64,512]{2,1,0:T(8,128)(2,1)S(1)}, bf16[2,8,64,512]{3,2,1,0:T(8,128)(2,1)S(1)}, bf16[2,8,64,512]{3,2,1,0:T(8,128)(2,1)S(1)}) custom-call(s32[4]{0:T(128)S(1)} %iota_xor_fusion.blk, bf16[8,64,512]{2,1,0:T(8,128)(2,1)} %all-to-all-done.x0, bf16[8,64,512]{2,1,0:T(8,128)(2,1)} %collective-permute-done.x1, ...), custom_call_target="tpu_custom_call" | custom-call | flops 6442450944 | bytes 16777216 | tf_op jit(solution)/shard_map/core/pallas_call | solution.py:152
  133.3 1.0 copy-done.3
  134.2 0.8 copy-done.10
  135.0 1.0 copy-done.19
  136.0 6.0 %all-to-all-start.3 = ((bf16[8,64,512]{2,1,0:T(8,128)(2,1)}), bf16[8,64,512]{2,1,0:T(8,128)(2,1)S(1)}, u32[]{:S(2)}, u32[]{:S(2)}) async-start(bf16[8,64,512]{2,1,0:T(8,128)(2,1)} %copy-done.10), calls=%async_computation.3 | async-start | bytes 1048576 | tf_op jit(solution)/shard_map/all_to_all | solution.py:29
  142.0 2.2 %fusion.8 = bf16[8,64,512]{2,1,0:T(8,128)(2,1)} fusion(bf16[2,8,64,512]{3,2,1,0:T(8,128)(2,1)} %collective-permute-done.13, bf16[2,8,64,512]{3,2,1,0:T(8,128)(2,1)} %copy-done.1), kind=kLoop, calls=%fused_computation.15 | loop fusion | flops 1048576 | bytes 1572864 | tf_op jit(solution)/shard_map/convert_element_type | solution.py:304
  144.2 1.5 collective-permute-start.14
  145.7 10.4 %all-to-all-done.3 = bf16[8,64,512]{2,1,0:T(8,128)(2,1)S(1)} async-done(((bf16[8,64,512]{2,1,0:T(8,128)(2,1)}), bf16[8,64,512]{2,1,0:T(8,128)(2,1)S(1)}, u32[]{:S(2)}, u32[]{:S(2)}) %all-to-all-start.3) | async-done | bytes 524320 | tf_op jit(solution)/shard_map/all_to_all | solution.py:29
  156.1 3.3 %project_out.1 = (bf16[2,512,512]{2,1,0:T(8,128)(2,1)S(1)}, bf16[2,512,512]{2,1,0:T(8,128)(2,1)}) custom-call(s32[4]{0:T(128)S(1)} %iota_xor_fusion.blk, s32[512,1]{1,0:T(8,128)S(1)} %get-tuple-element.14.slot_col, bf16[512,2048]{1,0:T(8,128)(2,1)S(1)} %copy-done, bf16[512,512]{1,0:T(8,128)(2,1)S(1)} %bitcast.53, bf16[512,512]{1,0:T(8,128)(2,1)S(1)} %bitcast.51), custom_call_target="tpu_custom_call" | custom-call | tf_op jit(solution)/shard_map/project_out/pallas_call | solution.py:270
  159.5 1.0 copy-done.5
  160.5 2.3 %fusion.3 = bf16[8,64,512]{2,1,0:T(8,128)(2,1)} fusion(bf16[8,64,512]{2,1,0:T(8,128)(2,1)} %collective-permute-done.14, bf16[2,8,64,512]{3,2,1,0:T(8,128)(2,1)} %collective-permute-done.13, bf16[2,8,64,512]{3,2,1,0:T(8,128)(2,1)S(1)} %copy-done.2), kind=kLoop, calls=%fused_computation.5 | loop fusion | flops 1572864 | bytes 2097152 | tf_op jit(solution)/shard_map/convert_element_type | solution.py:305
  162.8 4.3 %all-to-all-start.8 = ((bf16[8,64,512]{2,1,0:T(8,128)(2,1)}), bf16[8,64,512]{2,1,0:T(8,128)(2,1)S(1)}, u32[]{:S(2)}, u32[]{:S(2)}) async-start(bf16[8,64,512]{2,1,0:T(8,128)(2,1)} %fusion.3), calls=%async_computation.8 | async-start | bytes 1048576 | tf_op jit(solution)/shard_map/all_to_all | solution.py:29
  167.1 1.3 fusion.7
  168.4 1.5 collective-permute-start.12
  169.9 12.0 %collective-permute-done.12 = bf16[8,64,512]{2,1,0:T(8,128)(2,1)S(1)} collective-permute-done((bf16[8,64,512]{2,1,0:T(8,128)(2,1)S(1)}, bf16[8,64,512]{2,1,0:T(8,128)(2,1)S(1)}, u32[]{:S(2)}, u32[]{:S(2)}) %collective-permute-start.12) | collective-permute-done | bytes 524320 | tf_op jit(solution)/shard_map/ppermute | solution.py:25
  181.9 2.0 fusion.4
  183.9 5.6 %all-to-all-start.7 = ((bf16[8,64,512]{2,1,0:T(8,128)(2,1)}), bf16[8,64,512]{2,1,0:T(8,128)(2,1)S(1)}, u32[]{:S(2)}, u32[]{:S(2)}) async-start(bf16[8,64,512]{2,1,0:T(8,128)(2,1)} %fusion.4), calls=%async_computation.7 | async-start | bytes 1048576 | tf_op jit(solution)/shard_map/all_to_all | solution.py:29
  189.6 1.2 fusion.6
  190.8 1.5 collective-permute-start.10
  192.3 10.3 %all-to-all-done.7 = bf16[8,64,512]{2,1,0:T(8,128)(2,1)S(1)} async-done(((bf16[8,64,512]{2,1,0:T(8,128)(2,1)}), bf16[8,64,512]{2,1,0:T(8,128)(2,1)S(1)}, u32[]{:S(2)}, u32[]{:S(2)}) %all-to-all-start.7) | async-done | bytes 524320 | tf_op jit(solution)/shard_map/all_to_all | solution.py:29
  202.6 1.7 to_tokens.1
  204.3 2.0 fusion.5
  (64 shorter events, 1.8 us)
Async XLA Ops:
  3.6 1.0 copy-start.8
  7.4 13.8 %all-to-all-start.2 = ((s32[8,2,8]{2,1,0:T(2,128)}), s32[8,2,8]{2,1,0:T(2,128)S(1)}, u32[]{:S(2)}, u32[]{:S(2)}) async-start(s32[8,2,8]{2,1,0:T(2,128)} %copy.53), calls=%async_computation.2 | async-start | bytes 16384 | tf_op jit(solution)/shard_map/all_to_all | solution.py:29
  14.7 31.0 %copy-start = (bf16[512,2048]{1,0:T(8,128)(2,1)S(1)}, bf16[512,2048]{1,0:T(8,128)(2,1)}, u32[]{:S(2)}) copy-start(bf16[512,2048]{1,0:T(8,128)(2,1)} %w_out.3) | copy-start | bytes 6291460
  15.7 27.1 %copy-start.7 = (bf16[512,512]{1,0:T(8,128)(2,1)S(1)}, bf16[512,512]{1,0:T(8,128)(2,1)}, u32[]{:S(2)}) copy-start(bf16[512,512]{1,0:T(8,128)(2,1)} %a0.1) | copy-start | bytes 1572868
  21.2 17.5 %all-to-all-start.4 = ((bf16[8,64,512]{2,1,0:T(8,128)(2,1)}), bf16[8,64,512]{2,1,0:T(8,128)(2,1)}, u32[]{:S(2)}, u32[]{:S(2)}) async-start(bf16[8,64,512]{2,1,0:T(8,128)(2,1)} %bitcast.57), calls=%async_computation.4 | async-start | bytes 1048576 | tf_op jit(solution)/shard_map/all_to_all | solution.py:29
  25.4 17.6 %collective-permute-start.4 = (bf16[512,512]{1,0:T(8,128)(2,1)}, bf16[512,512]{1,0:T(8,128)(2,1)S(1)}, u32[]{:S(2)}, u32[]{:S(2)}) collective-permute-start(bf16[512,512]{1,0:T(8,128)(2,1)} %a0.1), channel_id=1, source_target_pairs={{0,2},{1,3},{2,0},{3,1},{4,6},{5,7},{6,4},{7,5},{8,10},{9,11},{10,... | collective-permute-start | bytes 1572872 | tf_op jit(solution)/shard_map/ppermute | solution.py:25
  38.7 17.6 %all-to-all-start = ((bf16[8,64,512]{2,1,0:T(8,128)(2,1)}), bf16[8,64,512]{2,1,0:T(8,128)(2,1)}, u32[]{:S(2)}, u32[]{:S(2)}) async-start(bf16[8,64,512]{2,1,0:T(8,128)(2,1)} %bitcast.56), calls=%async_computation | async-start | bytes 1048576 | tf_op jit(solution)/shard_map/all_to_all | solution.py:29
  42.9 2.1 %collective-permute-start.3 = (bf16[512,512]{1,0:T(8,128)(2,1)S(1)}, bf16[512,512]{1,0:T(8,128)(2,1)}, u32[]{:S(2)}, u32[]{:S(2)}) collective-permute-start(bf16[512,512]{1,0:T(8,128)(2,1)S(1)} %copy-done.7), channel_id=1, source_target_pairs={{0,1},{1,0},{2,3},{3,2},{4,5},{5,4},{6,7},{7,6},{8,9},{9,8},{10,11... | collective-permute-start | bytes 1572872 | tf_op jit(solution)/shard_map/ppermute | solution.py:25
  43.0 2.8 %collective-permute-start.5 = (bf16[512,512]{1,0:T(8,128)(2,1)S(1)}, bf16[512,512]{1,0:T(8,128)(2,1)}, u32[]{:S(2)}, u32[]{:S(2)}) collective-permute-start(bf16[512,512]{1,0:T(8,128)(2,1)S(1)} %collective-permute-done.4.a2), channel_id=1, source_target_pairs={{0,1},{1,0},{2,3},{3,2},{4,5},{5,4},{6,7},{7,6},{8,9},{9,8},{10,11... | collective-permute-start | bytes 1572872 | tf_op jit(solution)/shard_map/ppermute | solution.py:25
  56.3 19.1 %all-to-all-start.5 = ((bf16[8,64,512]{2,1,0:T(8,128)(2,1)}), bf16[8,64,512]{2,1,0:T(8,128)(2,1)S(1)}, u32[]{:S(2)}, u32[]{:S(2)}) async-start(bf16[8,64,512]{2,1,0:T(8,128)(2,1)} %bitcast.7), calls=%async_computation.5 | async-start | bytes 1048576 | tf_op jit(solution)/shard_map/all_to_all | solution.py:29
  59.9 15.2 %collective-permute-start.7 = (bf16[8,64,512]{2,1,0:T(8,128)(2,1)}, bf16[8,64,512]{2,1,0:T(8,128)(2,1)}, u32[]{:S(2)}, u32[]{:S(2)}) collective-permute-start(bf16[8,64,512]{2,1,0:T(8,128)(2,1)} %all-to-all-done.4.x0), channel_id=1, source_target_pairs={{0,2},{1,3},{2,0},{3,1},{4,6},{5,7},{6,4},{7,5},{8,10},{9,11},{10,... | collective-permute-start | bytes 1572872 | tf_op jit(solution)/shard_map/ppermute | solution.py:25
  61.5 22.6 %collective-permute-start.6 = (bf16[8,64,512]{2,1,0:T(8,128)(2,1)}, bf16[8,64,512]{2,1,0:T(8,128)(2,1)}, u32[]{:S(2)}, u32[]{:S(2)}) collective-permute-start(bf16[8,64,512]{2,1,0:T(8,128)(2,1)} %all-to-all-done.4.x0), channel_id=1, source_target_pairs={{0,1},{1,0},{2,3},{3,2},{4,5},{5,4},{6,7},{7,6},{8,9},{9,8},{10,11... | collective-permute-start | bytes 1572872 | tf_op jit(solution)/shard_map/ppermute | solution.py:25
  61.5 22.6 %collective-permute-start.1 = (bf16[8,64,512]{2,1,0:T(8,128)(2,1)}, bf16[8,64,512]{2,1,0:T(8,128)(2,1)}, u32[]{:S(2)}, u32[]{:S(2)}) collective-permute-start(bf16[8,64,512]{2,1,0:T(8,128)(2,1)} %all-to-all-done.x0), channel_id=1, source_target_pairs={{0,2},{1,3},{2,0},{3,1},{4,6},{5,7},{6,4},{7,5},{8,10},{9,11},{10,... | collective-permute-start | bytes 1572872 | tf_op jit(solution)/shard_map/ppermute | solution.py:25
  75.1 9.0 %collective-permute-start.8 = (bf16[8,64,512]{2,1,0:T(8,128)(2,1)}, bf16[8,64,512]{2,1,0:T(8,128)(2,1)}, u32[]{:S(2)}, u32[]{:S(2)}) collective-permute-start(bf16[8,64,512]{2,1,0:T(8,128)(2,1)} %collective-permute-done.7.x2), channel_id=1, source_target_pairs={{0,1},{1,0},{2,3},{3,2},{4,5},{5,4},{6,7},{7,6},{8,9},{9,8},{10,11... | collective-permute-start | bytes 1572872 | tf_op jit(solution)/shard_map/ppermute | solution.py:25
  75.3 31.4 %all-to-all-start.1 = ((bf16[8,64,512]{2,1,0:T(8,128)(2,1)}), bf16[8,64,512]{2,1,0:T(8,128)(2,1)S(1)}, u32[]{:S(2)}, u32[]{:S(2)}) async-start(bf16[8,64,512]{2,1,0:T(8,128)(2,1)} %bitcast.55), calls=%async_computation.1 | async-start | bytes 1048576 | tf_op jit(solution)/shard_map/all_to_all | solution.py:29
  82.5 31.1 %collective-permute-start = (bf16[8,64,512]{2,1,0:T(8,128)(2,1)}, bf16[8,64,512]{2,1,0:T(8,128)(2,1)}, u32[]{:S(2)}, u32[]{:S(2)}) collective-permute-start(bf16[8,64,512]{2,1,0:T(8,128)(2,1)} %all-to-all-done.x0), channel_id=1, source_target_pairs={{0,1},{1,0},{2,3},{3,2},{4,5},{5,4},{6,7},{7,6},{8,9},{9,8},{10,11... | collective-permute-start | bytes 1572872 | tf_op jit(solution)/shard_map/ppermute | solution.py:25
  84.1 29.5 %collective-permute-start.2 = (bf16[8,64,512]{2,1,0:T(8,128)(2,1)}, bf16[8,64,512]{2,1,0:T(8,128)(2,1)}, u32[]{:S(2)}, u32[]{:S(2)}) collective-permute-start(bf16[8,64,512]{2,1,0:T(8,128)(2,1)} %collective-permute-done.1.x2), channel_id=1, source_target_pairs={{0,1},{1,0},{2,3},{3,2},{4,5},{5,4},{6,7},{7,6},{8,9},{9,8},{10,11... | collective-permute-start | bytes 1572872 | tf_op jit(solution)/shard_map/ppermute | solution.py:25
  84.2 1.0 copy-start.11
  85.1 1.6 copy-start.13
  86.7 1.6 copy-start.15
  88.3 1.6 copy-start.17
  104.5 1.0 copy-start.1
  105.5 0.8 copy-start.9
  106.3 35.7 %collective-permute-start.13 = (bf16[2,8,64,512]{3,2,1,0:T(8,128)(2,1)}, bf16[2,8,64,512]{3,2,1,0:T(8,128)(2,1)}, u32[]{:S(2)}, u32[]{:S(2)}) collective-permute-start(bf16[2,8,64,512]{3,2,1,0:T(8,128)(2,1)} %get-tuple-element.25), channel_id=1, source_target_pairs={{0,1},{1,0},{2,3},{3,2},{4,5},{5,4},{6,7},{7,6},{8,9},{9,8},{10,11... | collective-permute-start | bytes 3145736 | tf_op jit(solution)/shard_map/ppermute | solution.py:25
  106.8 29.2 %all-to-all-start.6 = ((bf16[8,64,512]{2,1,0:T(8,128)(2,1)}), bf16[8,64,512]{2,1,0:T(8,128)(2,1)S(1)}, u32[]{:S(2)}, u32[]{:S(2)}) async-start(bf16[8,64,512]{2,1,0:T(8,128)(2,1)} %copy-done.9), calls=%async_computation.6 | async-start | bytes 1048576 | tf_op jit(solution)/shard_map/all_to_all | solution.py:29
  113.6 1.0 copy-start.12
  114.6 1.6 copy-start.14
  116.2 1.6 copy-start.16
  117.8 1.6 copy-start.18
  133.3 1.0 copy-start.3
  134.2 0.8 copy-start.10
  135.0 1.0 copy-start.19
  136.0 20.1 %all-to-all-start.3 = ((bf16[8,64,512]{2,1,0:T(8,128)(2,1)}), bf16[8,64,512]{2,1,0:T(8,128)(2,1)S(1)}, u32[]{:S(2)}, u32[]{:S(2)}) async-start(bf16[8,64,512]{2,1,0:T(8,128)(2,1)} %copy-done.10), calls=%async_computation.3 | async-start | bytes 1048576 | tf_op jit(solution)/shard_map/all_to_all | solution.py:29
  142.0 25.1 %collective-permute-start.11 = (bf16[2,8,64,512]{3,2,1,0:T(8,128)(2,1)}, bf16[2,8,64,512]{3,2,1,0:T(8,128)(2,1)}, u32[]{:S(2)}, u32[]{:S(2)}) collective-permute-start(bf16[2,8,64,512]{3,2,1,0:T(8,128)(2,1)} %copy-done.19), channel_id=1, source_target_pairs={{0,1},{1,0},{2,3},{3,2},{4,5},{5,4},{6,7},{7,6},{8,9},{9,8},{10,11... | collective-permute-start | bytes 3145736 | tf_op jit(solution)/shard_map/ppermute | solution.py:25
  144.2 16.2 %collective-permute-start.14 = (bf16[8,64,512]{2,1,0:T(8,128)(2,1)}, bf16[8,64,512]{2,1,0:T(8,128)(2,1)}, u32[]{:S(2)}, u32[]{:S(2)}) collective-permute-start(bf16[8,64,512]{2,1,0:T(8,128)(2,1)} %fusion.8), channel_id=1, source_target_pairs={{0,2},{1,3},{2,0},{3,1},{4,6},{5,7},{6,4},{7,5},{8,10},{9,11},{10,... | collective-permute-start | bytes 1572872 | tf_op jit(solution)/shard_map/ppermute | solution.py:25
  156.1 4.3 %copy-start.2 = (bf16[2,8,64,512]{3,2,1,0:T(8,128)(2,1)S(1)}, bf16[2,8,64,512]{3,2,1,0:T(8,128)(2,1)}, u32[]{:S(2)}) copy-start(bf16[2,8,64,512]{3,2,1,0:T(8,128)(2,1)} %copy-done.1) | copy-start | bytes 3145732
  159.5 1.0 copy-start.5
  160.5 6.6 %copy-start.4 = (bf16[2,8,64,512]{3,2,1,0:T(8,128)(2,1)S(1)}, bf16[2,8,64,512]{3,2,1,0:T(8,128)(2,1)}, u32[]{:S(2)}) copy-start(bf16[2,8,64,512]{3,2,1,0:T(8,128)(2,1)} %copy-done.3) | copy-start | bytes 3145732
  160.5 29.1 %collective-permute-start.9 = (bf16[2,512,512]{2,1,0:T(8,128)(2,1)}, bf16[2,512,512]{2,1,0:T(8,128)(2,1)}, u32[]{:S(2)}, u32[]{:S(2)}) collective-permute-start(bf16[2,512,512]{2,1,0:T(8,128)(2,1)} %get-tuple-element.21), channel_id=1, source_target_pairs={{0,1},{1,0},{2,3},{3,2},{4,5},{5,4},{6,7},{7,6},{8,9},{9,8},{10,11... | collective-permute-start | bytes 3145736 | tf_op jit(solution)/shard_map/ppermute | solution.py:25
  162.8 21.1 %all-to-all-start.8 = ((bf16[8,64,512]{2,1,0:T(8,128)(2,1)}), bf16[8,64,512]{2,1,0:T(8,128)(2,1)S(1)}, u32[]{:S(2)}, u32[]{:S(2)}) async-start(bf16[8,64,512]{2,1,0:T(8,128)(2,1)} %fusion.3), calls=%async_computation.8 | async-start | bytes 1048576 | tf_op jit(solution)/shard_map/all_to_all | solution.py:29
  167.1 22.5 %copy-start.6 = (bf16[2,512,512]{2,1,0:T(8,128)(2,1)S(1)}, bf16[2,512,512]{2,1,0:T(8,128)(2,1)}, u32[]{:S(2)}) copy-start(bf16[2,512,512]{2,1,0:T(8,128)(2,1)} %copy-done.5) | copy-start | bytes 3145732
  168.4 13.5 %collective-permute-start.12 = (bf16[8,64,512]{2,1,0:T(8,128)(2,1)S(1)}, bf16[8,64,512]{2,1,0:T(8,128)(2,1)S(1)}, u32[]{:S(2)}, u32[]{:S(2)}) collective-permute-start(bf16[8,64,512]{2,1,0:T(8,128)(2,1)S(1)} %fusion.7), channel_id=1, source_target_pairs={{0,2},{1,3},{2,0},{3,1},{4,6},{5,7},{6,4},{7,5},{8,10},{9,11},{10,... | collective-permute-start | bytes 1572872 | tf_op jit(solution)/shard_map/ppermute | solution.py:25
  183.9 18.6 %all-to-all-start.7 = ((bf16[8,64,512]{2,1,0:T(8,128)(2,1)}), bf16[8,64,512]{2,1,0:T(8,128)(2,1)S(1)}, u32[]{:S(2)}, u32[]{:S(2)}) async-start(bf16[8,64,512]{2,1,0:T(8,128)(2,1)} %fusion.4), calls=%async_computation.7 | async-start | bytes 1048576 | tf_op jit(solution)/shard_map/all_to_all | solution.py:29
  190.8 13.5 %collective-permute-start.10 = (bf16[512,512]{1,0:T(8,128)(2,1)S(1)}, bf16[512,512]{1,0:T(8,128)(2,1)S(1)}, u32[]{:S(2)}, u32[]{:S(2)}) collective-permute-start(bf16[512,512]{1,0:T(8,128)(2,1)S(1)} %fusion.6), channel_id=1, source_target_pairs={{0,2},{1,3},{2,0},{3,1},{4,6},{5,7},{6,4},{7,5},{8,10},{9,11},{10,... | collective-permute-start | bytes 1572872 | tf_op jit(solution)/shard_map/ppermute | solution.py:25

commit v2 on v1

v2 whole, which is shorter than its diff:
```python
import functools
import jax
import jax.numpy as jnp
from jax import lax
from jax.experimental import pallas as pl
from jax.experimental.pallas import tpu as pltpu
from jax.sharding import PartitionSpec as P

HEAD_DIM = 128
CLUSTERS = 128
CAP = 256
MOST = 8
LIMIT = 24.0
EMPTY = 32.0
NN = (((1,), (0,)), ((), ()))
NT = (((1,), (1,)), ((), ()))
TN = (((0,), (0,)), ((), ()))
MB = 1024 * 1024
CHUNKS = 2
VMEM = pl.BlockSpec(memory_space=pltpu.VMEM)
SMEM = pl.BlockSpec(memory_space=pltpu.SMEM)


def dot(a, b, dims=NN):
    return lax.dot_general(a, b, dims, preferred_element_type=jnp.float32)


def iota(shape, dim):
    return lax.broadcasted_iota(jnp.int32, shape, dim)


def swap(x, bit):
    count = lax.axis_size("tp")
    return lax.ppermute(x, "tp", [(i, i ^ bit) for i in range(count)])


def exchange(x):
    return lax.all_to_all(x, "seq", split_axis=0, concat_axis=0, tiled=True)


def after(x, *others):
    return lax.optimization_barrier((x,) + others)[0]


def place_kernel(ids_col, x_ref, slot_col, slot_row, *outs):
    tokens = x_ref.shape[0]
    here, there = (iota((tokens, tokens), 0), iota((tokens, tokens), 1))
    col = ids_col[...]
    row = jnp.sum(jnp.where(here == there, col, 0), axis=0, keepdims=True)
    same = col == row
    earlier = jnp.where(same & (there < here), 1.0, 0.0)
    later = jnp.where(same & (here < there), 1.0, 0.0)
    slot_col[...] = col * MOST + jnp.sum(earlier, axis=1, keepdims=True).astype(jnp.int32)
    slot_row[...] = row * MOST + jnp.sum(later, axis=0, keepdims=True).astype(jnp.int32)
    for c, out in enumerate(outs):
        owners, rows, width = out.shape
        shape = (owners, rows, tokens)
        slot = iota(shape, 0) * (rows * len(outs)) + iota(shape, 1) + c * rows
        chosen = jnp.where(slot.reshape(owners * rows, tokens) == slot_row[...], 1.0, 0.0)
        taken = jnp.sum(chosen, axis=1, keepdims=True)
        first = iota((owners * rows, width), 1) == 0
        value = dot(chosen.astype(jnp.bfloat16), x_ref[...])
        value = value + jnp.where(first & (taken == 0.0), EMPTY, 0.0)
        out[...] = value.astype(jnp.bfloat16).reshape(out.shape)


def place(cluster, x, owners, rows, chunks):
    tokens = x.shape[0]
    piece = jax.ShapeDtypeStruct((owners, rows, x.shape[1]), jnp.bfloat16)
    return pl.pallas_call(
        place_kernel,
        out_shape=(
            jax.ShapeDtypeStruct((tokens, 1), jnp.int32),
            jax.ShapeDtypeStruct((1, tokens), jnp.int32),
        )
        + (piece,) * chunks,
        compiler_params=pltpu.CompilerParams(vmem_limit_bytes=32 * MB),
        name="place",
    )(cluster, x)


def head_grads_kernel(blk, a0, a1, a2, a3, w_out, slot_row, out_ref):
    width = a0.shape[1]
    total = None
    for j, part in enumerate((a0, a1, a2, a3)):
        cols = pl.ds(pl.multiple_of(blk[j] * width, width), width)
        term = dot(part[...], w_out[:, cols], NT)
        total = term if total is None else total + term
    slots, tokens = (out_ref.shape[0], a0.shape[0])
    chosen = jnp.where(iota((slots, tokens), 0) == slot_row[...], 1.0, 0.0).astype(jnp.bfloat16)
    out_ref[...] = dot(chosen, total.astype(jnp.bfloat16)).astype(jnp.bfloat16)


def head_grads(blk, parts, w_out, slot_row):
    return pl.pallas_call(
        head_grads_kernel,
        out_shape=jax.ShapeDtypeStruct((CLUSTERS * MOST, w_out.shape[0]), jnp.bfloat16),
        in_specs=[SMEM] + [VMEM] * 6,
        out_specs=VMEM,
        compiler_params=pltpu.CompilerParams(vmem_limit_bytes=32 * MB),
        name="head_grads",
    )(blk, *parts, w_out, slot_row)


GROUP = 16


def spans(blk, width):
    return [pl.ds(pl.multiple_of(blk[j] * width, width), width) for j in range(4)]


def forward_kernel(blk, x0, x1, x2, x3, wq, wk, wv, *refs):
    mixed, saved, probs_ref = refs[-3:]
    sources, rows, width = x0.shape
    heads_width = wq.shape[1]
    heads = heads_width // HEAD_DIM
    scale = HEAD_DIM ** (-0.5)
    span = spans(blk, width)
    xs = [r[...].reshape(sources * rows, width) for r in (x0, x1, x2, x3)]
    for i, w in enumerate((wq, wk, wv)):
        total = dot(xs[0], w[span[0], :])
        for j in range(1, 4):
            total = total + dot(xs[j], w[span[j], :])
        saved[:, :, i * heads_width : (i + 1) * heads_width] = total.astype(jnp.bfloat16).reshape(
            sources, rows, heads_width
        )
    members = sources * GROUP
    shape = (sources, GROUP, members)
    here = (iota(shape, 1) // MOST).reshape(members, members)
    source_here = iota(shape, 0).reshape(members, members)
    place_here = iota(shape, 1).reshape(members, members)
    lane = iota((members, members), 1)
    there = lane % GROUP // MOST
    same = here == there
    earlier = same & (lane // GROUP < source_here)
    later = same & (lane // GROUP > source_here)
    diagonal = source_here * GROUP + place_here == lane
    rank_col = (place_here % MOST).astype(jnp.float32)[:, :1]
    rank_row = (lane % MOST).astype(jnp.float32)[:1, :]
    for n in range(rows // GROUP):
        group = slice(n * GROUP, (n + 1) * GROUP)
        mark = x0[:, group, :HEAD_DIM].reshape(members, HEAD_DIM)[:, :1].astype(jnp.float32)
        held_col = jnp.where(mark <= LIMIT, 1.0, 0.0)
        held_row = jnp.sum(jnp.where(diagonal, held_col, 0.0), axis=0, keepdims=True)
        place_col = rank_col + jnp.sum(jnp.where(earlier, held_row, 0.0), axis=1, keepdims=True)
        place_row = rank_row + jnp.sum(jnp.where(later, held_col, 0.0), axis=0, keepdims=True)
        kept_col = jnp.where(place_col < CAP, held_col, 0.0)
        usable = same & (jnp.where(place_row < CAP, held_row, 0.0) > 0)
        for h in range(heads):
            def part(i):
                first = i * heads_width + h * HEAD_DIM
                return saved[:, group, first : first + HEAD_DIM].reshape(members, HEAD_DIM)

            scores = jnp.where(usable, dot(part(0), part(1), NT) * scale, -1e30)
            raised = jnp.exp(scores - jnp.max(scores, axis=1, keepdims=True))
            probs = raised * (kept_col / jnp.sum(raised, axis=1, keepdims=True))
            probs_ref[0, n, h] = probs
            out = dot(probs.astype(jnp.bfloat16), part(2)).astype(jnp.bfloat16)
            mixed[:, group, h * HEAD_DIM : (h + 1) * HEAD_DIM] = out.reshape(
                sources, GROUP, HEAD_DIM
            )


def backward_kernel(blk, saved, probs_ref, g_ref, wq, wk, wv, keep, give, dq, dk, dv):
    sources, rows, _ = saved.shape
    width = keep.shape[3]
    heads_width = wq.shape[1]
    heads = heads_width // HEAD_DIM
    scale = HEAD_DIM ** (-0.5)
    span = spans(blk, width)
    members = sources * GROUP
    for n in range(rows // GROUP):
        group = slice(n * GROUP, (n + 1) * GROUP)
        for h in range(heads):
            cols = slice(h * HEAD_DIM, (h + 1) * HEAD_DIM)

            def part(i):
                first = i * heads_width + h * HEAD_DIM
                return saved[:, group, first : first + HEAD_DIM].reshape(members, HEAD_DIM)

            def put(ref, value):
                ref[:, group, cols] = value.astype(jnp.bfloat16).reshape(sources, GROUP, HEAD_DIM)

            g = g_ref[:, group, cols].reshape(members, HEAD_DIM)
            probs = probs_ref[0, n, h]
            put(dv, dot(probs.astype(jnp.bfloat16), g, TN))
            grad_probs = dot(g, part(2), NT)
            inner = jnp.sum(grad_probs * probs, axis=1, keepdims=True)
            grad_scores = (probs * (grad_probs - inner) * scale).astype(jnp.bfloat16)
            put(dq, dot(grad_scores, part(1)))
            put(dk, dot(grad_scores, part(0), TN))
    grads = [d[...].reshape(sources * rows, heads_width) for d in (dq, dk, dv)]
    for j in (1, 3, 0, 2):
        total = None
        for d, w in zip(grads, (wq, wk, wv)):
            term = dot(d, w[span[j], :], NT)
            total = term if total is None else total + term
        target = (keep, give)[j % 2]
        target[j // 2] = total.astype(jnp.bfloat16).reshape(sources, rows, width)


def step_of(sources, rows):
    step = GROUP
    while step * 2 * sources <= 256 and rows % (step * 2) == 0:
        step *= 2
    return step


def forward(blk, parts, wq, wk, wv, chunk, chunks, mixed):
    sources, rows, width = parts[0].shape
    heads_width = wq.shape[1]
    heads = heads_width // HEAD_DIM
    step = step_of(sources, rows)
    steps, groups, members = (rows // step, step // GROUP, sources * GROUP)
    block = pl.BlockSpec((sources, step, width), lambda p: (0, p, 0))
    weight = pl.BlockSpec(wq.shape, lambda p: (0, 0), pipeline_mode=pl.Buffered(1))
    in_specs = [SMEM] + [block] * 4 + [weight] * 3
    operands = [blk, *parts, wq, wk, wv]
    if mixed is not None:
        in_specs.append(pl.BlockSpec(memory_space=pl.ANY))
        operands.append(mixed)
    return pl.pallas_call(
        forward_kernel,
        grid=(steps,),
        out_shape=(
            jax.ShapeDtypeStruct((sources, rows * chunks, heads_width), jnp.bfloat16),
            jax.ShapeDtypeStruct((sources, rows, 3 * heads_width), jnp.bfloat16),
            jax.ShapeDtypeStruct((steps, groups, heads, members, members), jnp.float32),
        ),
        in_specs=in_specs,
        out_specs=(
            pl.BlockSpec((sources, step, heads_width), lambda p: (0, p + chunk * steps, 0)),
            pl.BlockSpec((sources, step, 3 * heads_width), lambda p: (0, p, 0)),
            pl.BlockSpec((1, groups, heads, members, members), lambda p: (p, 0, 0, 0, 0)),
        ),
        input_output_aliases={} if mixed is None else {len(operands) - 1: 0},
        compiler_params=pltpu.CompilerParams(vmem_limit_bytes=40 * MB),
        cost_estimate=pl.CostEstimate(
            flops=2 * sources * rows * width * 4 * heads_width * 3,
            bytes_accessed=10 * MB,
            transcendentals=sources * rows * members * heads,
        ),
        name="forward",
    )(*operands)


def backward(blk, saved, probs, grads, wq, wk, wv, chunk):
    sources, rows, _ = saved.shape
    heads_width = wq.shape[1]
    width = wq.shape[0] // 4
    heads = heads_width // HEAD_DIM
    step = step_of(sources, rows)
    steps, groups, members = (rows // step, step // GROUP, sources * GROUP)
    pair = pl.BlockSpec((2, sources, step, width), lambda p: (0, 0, p, 0))
    weight = pl.BlockSpec(wq.shape, lambda p: (0, 0), pipeline_mode=pl.Buffered(1))
    shape = jax.ShapeDtypeStruct((2, sources, rows, width), jnp.bfloat16)
    return pl.pallas_call(
        backward_kernel,
        grid=(steps,),
        out_shape=(shape, shape),
        in_specs=[
            SMEM,
            pl.BlockSpec((sources, step, 3 * heads_width), lambda p: (0, p, 0)),
            pl.BlockSpec((1, groups, heads, members, members), lambda p: (p, 0, 0, 0, 0)),
            pl.BlockSpec((sources, step, heads_width), lambda p: (0, p + chunk * steps, 0)),
            weight,
            weight,
            weight,
        ],
        out_specs=(pair, pair),
        scratch_shapes=[pltpu.VMEM((sources, step, heads_width), jnp.bfloat16)] * 3,
        compiler_params=pltpu.CompilerParams(vmem_limit_bytes=40 * MB),
        cost_estimate=pl.CostEstimate(
            flops=2 * sources * rows * width * 4 * heads_width * 3,
            bytes_accessed=12 * MB,
            transcendentals=0,
        ),
        name="backward",
    )(blk, saved, probs, grads, wq, wk, wv)


def slab(w, blk, j):
    width = w.shape[0] // 4
    return lax.dynamic_slice_in_dim(w, blk[j] * width, width, 0)


def by_cluster(x):
    sources, rows = x.shape[:2]
    x = x.reshape(sources, rows // MOST, MOST, -1).transpose(1, 0, 2, 3)
    return x.reshape(rows // MOST, sources * MOST, -1)


def by_source(x, sources):
    clusters = x.shape[0]
    x = x.reshape(clusters, sources, MOST, -1).transpose(1, 0, 2, 3)
    return x.reshape(sources, clusters * MOST, -1)


def split_heads(x):
    return x.reshape(x.shape[0], -1, HEAD_DIM)


ein = functools.partial(jnp.einsum, preferred_element_type=jnp.float32)


def forward_many(blk, parts, wq, wk, wv):
    sources, rows, _ = parts[0].shape

    def project(w):
        total = 0.0
        for j in range(4):
            total = total + ein("srd,dh->srh", parts[j], slab(w, blk, j))
        return by_cluster(total.astype(jnp.bfloat16))

    held = (parts[0][:, :, 0].astype(jnp.float32) <= LIMIT).reshape(sources, -1, MOST)
    counts = jnp.sum(held.astype(jnp.int32), axis=2, keepdims=True)
    rank = jnp.cumsum(counts, axis=0) - counts + jnp.arange(MOST)
    kept = by_cluster((held & (rank < CAP)).astype(jnp.float32).reshape(sources, rows, 1))
    scale = HEAD_DIM ** (-0.5)

    def one(args):
        q, k, v, live = args
        q, k, v = (split_heads(a) for a in (q, k, v))
        scores = jnp.where(live[None, None, :, 0] > 0, ein("qhd,khd->hqk", q, k) * scale, -1e30)
        raised = jnp.exp(scores - jnp.max(scores, axis=-1, keepdims=True))
        probs = raised * (live / jnp.sum(raised, axis=-1, keepdims=True))
        mixed = ein("hqk,khd->qhd", probs.astype(jnp.bfloat16), v).astype(jnp.bfloat16)
        return (mixed.reshape(mixed.shape[0], -1), probs)

    saved = tuple(project(w) for w in (wq, wk, wv))
    mixed, probs = lax.map(one, saved + (kept,))
    return (by_source(mixed, sources), saved, probs)


def backward_many(blk, saved, probs, grads, wq, wk, wv):
    sources = grads.shape[0]
    scale = HEAD_DIM ** (-0.5)

    def one(args):
        q, k, v, probs, g = args
        q, k, v, g = (split_heads(a) for a in (q, k, v, g))
        dv = ein("hqk,qhd->khd", probs.astype(jnp.bfloat16), g)
        grad_probs = ein("qhd,khd->hqk", g, v)
        inner = jnp.sum(grad_probs * probs, axis=-1, keepdims=True)
        grad_scores = (probs * (grad_probs - inner) * scale).astype(jnp.bfloat16)
        dq = ein("hqk,khd->qhd", grad_scores, k)
        dk = ein("hqk,qhd->khd", grad_scores, q)
        return tuple(a.astype(jnp.bfloat16).reshape(a.shape[0], -1) for a in (dq, dk, dv))

    dq, dk, dv = lax.map(one, saved + (probs, by_cluster(grads)))
    outs = []
    for j in range(4):
        total = 0.0
        for d, w in ((dq, wq), (dk, wk), (dv, wv)):
            total = total + ein("crh,wh->crw", d, slab(w, blk, j))
        outs.append(by_source(total.astype(jnp.bfloat16), sources))
    return (jnp.stack([outs[0], outs[2]]), jnp.stack([outs[1], outs[3]]))


def pick(slot_col, part, first, count, stride):
    owners = part.shape[0]
    i = iota((1, owners * count), 1)
    slots = i // count * stride + i % count + first
    chosen = jnp.where(slots == slot_col[...], 1.0, 0.0).astype(jnp.bfloat16)
    return dot(chosen, part[...].reshape(owners * count, -1))


def out_kernel(blk, slot_col, w_out, mixed, keep, give):
    per = mixed.shape[1]
    heads = pick(slot_col, mixed, 0, per, per).astype(jnp.bfloat16)
    width = keep.shape[2]
    span = spans(blk, width)
    for j in (1, 3, 0, 2):
        (keep, give)[j % 2][j // 2] = dot(heads, w_out[:, span[j]]).astype(jnp.bfloat16)


def project_out(blk, slot_col, w_out, mixed):
    tokens, width = (slot_col.shape[0], w_out.shape[1] // 4)
    shape = jax.ShapeDtypeStruct((2, tokens, width), jnp.bfloat16)
    return pl.pallas_call(
        out_kernel,
        out_shape=(shape, shape),
        in_specs=[SMEM] + [VMEM] * 3,
        out_specs=(VMEM, VMEM),
        compiler_params=pltpu.CompilerParams(vmem_limit_bytes=32 * MB),
        name="project_out",
    )(blk, slot_col, w_out, mixed)


def final_kernel(slot_col, *refs):
    parts, out = (refs[:-1], refs[-1])
    rows = parts[0].shape[1]
    total = None
    for c, part in enumerate(parts):
        term = pick(slot_col, part, c * rows, rows, rows * len(parts))
        total = term if total is None else total + term
    out[...] = total


def to_tokens(slot_col, parts):
    return pl.pallas_call(
        final_kernel,
        out_shape=jax.ShapeDtypeStruct((slot_col.shape[0], parts[0].shape[2]), jnp.float32),
        compiler_params=pltpu.CompilerParams(vmem_limit_bytes=32 * MB),
        name="to_tokens",
    )(slot_col, *parts)


def gather_parts(x):
    across = swap(x, 2)
    return (x, swap(x, 1), across, swap(across, 1))


def wide(x):
    return x.astype(jnp.float32)


def reduce_pairs(keep, give):
    got = swap(give, 1)
    return (got, (wide(keep[1]) + wide(got[1])).astype(jnp.bfloat16))


def reduce_across(keep, got, partial):
    return (wide(keep[0]) + wide(got[0]) + wide(swap(partial, 2))).astype(jnp.bfloat16)


def body(normed, cluster, w_query, w_key, w_value, w_out, grad_out):
    seq_count = lax.axis_size("seq")
    per = CLUSTERS // seq_count * MOST
    chunks = CHUNKS if per // CHUNKS % GROUP == 0 else 1
    rows = per // chunks
    blk = lax.axis_index("tp") ^ jnp.arange(4, dtype=jnp.int32)
    weights = (w_query, w_key, w_value)
    small = seq_count * GROUP <= 256

    slot_col, slot_row, *pieces = place(cluster, normed, seq_count, rows, chunks)
    arrived = [exchange(pieces[0])]
    for piece in pieces[1:]:
        arrived.append(exchange(after(piece, arrived[-1])))
    g_slots = head_grads(blk, gather_parts(grad_out), w_out, slot_row)
    g_slots = after(g_slots.reshape(seq_count, per, -1), arrived[-1])
    g_arrived = exchange(g_slots)

    if small:
        mixed, kept = (None, [])
        for c in range(chunks):
            parts = gather_parts(arrived[c])
            mixed, saved, probs = forward(blk, parts, *weights, c, chunks, mixed)
            kept.append((saved, probs))
    else:
        mixed, saved, probs = forward_many(blk, gather_parts(arrived[0]), *weights)
    mixed_back = exchange(after(mixed, g_arrived))

    partials = []
    for c in range(chunks):
        if small:
            keep, give = backward(blk, *kept[c], g_arrived, *weights, c)
        else:
            keep, give = backward_many(blk, saved, probs, g_arrived, *weights)
        got, partial = reduce_pairs(keep, give)
        partials.append((keep, got, partial))
        g_arrived = after(g_arrived, partial)
    back, last = ([], mixed_back)
    for keep, got, partial in partials:
        last = exchange(after(reduce_across(keep, got, partial), last))
        back.append(last)
    keep, give = project_out(blk, slot_col, w_out, mixed_back)
    got, partial = reduce_pairs(keep, give)
    attended = reduce_across(keep, got, partial)
    return (attended, to_tokens(slot_col, back))


def solution(mesh):
    in_specs = (
        P("seq", "tp"),
        P("seq", None),
        P(None, "tp"),
        P(None, "tp"),
        P(None, "tp"),
        P("tp", None),
        P("seq", "tp"),
    )
    out_specs = (P("seq", "tp"), P("seq", "tp"))
    return jax.shard_map(body, mesh=mesh, in_specs=in_specs, out_specs=out_specs, check_vma=False)
```

time: 208 us -> 215 us (1.034)
  Pallas kernels: 37.6 us -> 51.3 us
  starting transfers between devices: 56.5 us -> 43.1 us
  local copies, waits for them, and re-layouts: 24.7 us -> 34 us
  other arithmetic: 13.6 us -> 7.84 us
  waiting for transfers between devices: 73 us -> 76.2 us
    ppermute x15, waiting for transfers between devices: 28.7 us -> 56.2 us  [swap(): return lax.ppermute(x, 'tp', [(i, i ^ bit) for i in range(count)])]
    all_to_all x9 -> x6, waiting for transfers between devices: 44.3 us -> 20 us  [exchange(): return lax.all_to_all(x, 'seq', split_axis=0, concat_axis=0, tiled=True)]
    unnamed x41 -> x67, local copies, waits for them, and re-layouts: 18.8 us -> 34 us
    all_to_all x9 -> x6, starting transfers between devices: 46.9 us -> 32.7 us  [exchange(): return lax.all_to_all(x, 'seq', split_axis=0, concat_axis=0, tiled=True)]
    pallas_call x2 -> x4, Pallas kernels: 28.5 us -> 40.1 us  [the longest x2 20.7 us: forward(): pl.pallas_call(forward_kernel, grid=(steps,), out_shape=(jax.ShapeDtypeSt...]
    convert_element_type x7 -> x6, other arithmetic: 11 us -> 7.84 us  [the longest x3 5.09 us: reduce_across(): (wide(keep[0]) + wide(got[0]) + wide(swap(partial, 2))).astype(jnp.bfloat16)]
    another operation x6 -> x0, local copies, waits for them, and re-layouts: 2.25 us -> none  [the longest x2 1.93 us: core(): by_step[:, :, None]]
  transfers between devices with their start and end apart: 24 -> 21, of which waited for: 10 -> 11; matrix products, arithmetic and copies ran while one was open for 7% -> 4% of each run, Pallas kernels for 18% -> 22%
where the time goes in v2:
time: 215 us; the launch traced here: 213 us
  waiting for transfers between devices  76.2 us (35%)
  Pallas kernels  51.3 us (24%)
  starting transfers between devices  43.1 us (20%)
  local copies, waits for them, and re-layouts  34 us (16%)
  other arithmetic  7.84 us (4%)
    ppermute x15, waiting for transfers between devices, swap(): return lax.ppermute(x, 'tp', [(i, i ^ bit) for i in range(count)])  56.2 us
    unnamed x67, local copies, waits for them, and re-layouts  34 us
    all_to_all x6, starting transfers between devices, exchange(): return lax.all_to_all(x, 'seq', split_axis=0, concat_axis=0, tiled=True)  32.7 us
    pallas_call x2, Pallas kernels, forward(): pl.pallas_call(forward_kernel, grid=(steps,), out_shape=(jax.ShapeDtypeSt...  20.7 us
    all_to_all x6, waiting for transfers between devices, exchange(): return lax.all_to_all(x, 'seq', split_axis=0, concat_axis=0, tiled=True)  20 us
    pallas_call x2, Pallas kernels, backward(): pl.pallas_call(backward_kernel, grid=(steps,), out_shape=(shape, shape),...  19.4 us
    ppermute x15, starting transfers between devices, swap(): return lax.ppermute(x, 'tp', [(i, i ^ bit) for i in range(count)])  10.4 us
    convert_element_type x3, other arithmetic, reduce_across(): (wide(keep[0]) + wide(got[0]) + wide(swap(partial, 2))).astype(jnp.bfloat16)  5.09 us
  transfers between devices with their start and end apart: 21, of which 11 were waited for; matrix products, arithmetic and copies ran while one was open for 4% of the time, Pallas kernels for 22%

profile of v2, /device:TPU:0, one launch (start us, length us, event | category | flops | bytes accessed | tf_op | source)
XLA Modules:
  0.0 213.2 jit_solution(9940107659905406264)
XLA Ops:
  0.7 1.0 copy.10.ids_col
  1.6 1.0 copy-done.13
  2.7 1.1 place.1
  3.8 0.8 copy-done.14
  4.6 0.8 copy-done.15
  5.4 7.3 %all-to-all-start = ((bf16[8,64,512]{2,1,0:T(8,128)(2,1)}), bf16[8,64,512]{2,1,0:T(8,128)(2,1)}, u32[]{:S(2)}, u32[]{:S(2)}) async-start(bf16[8,64,512]{2,1,0:T(8,128)(2,1)} %copy-done.15), calls=%async_computation | async-start | bytes 1048576 | tf_op jit(solution)/shard_map/all_to_all | solution.py:38
  12.7 1.6 collective-permute-start.7
  14.3 13.0 %all-to-all-done.x0 = bf16[8,64,512]{2,1,0:T(8,128)(2,1)} async-done(((bf16[8,64,512]{2,1,0:T(8,128)(2,1)}), bf16[8,64,512]{2,1,0:T(8,128)(2,1)}, u32[]{:S(2)}, u32[]{:S(2)}) %all-to-all-start) | async-done | bytes 524320 | tf_op jit(solution)/shard_map/all_to_all | solution.py:38
  27.3 4.2 %all-to-all-start.1 = ((bf16[8,64,512]{2,1,0:T(8,128)(2,1)}), bf16[8,64,512]{2,1,0:T(8,128)(2,1)}, u32[]{:S(2)}, u32[]{:S(2)}) async-start(bf16[8,64,512]{2,1,0:T(8,128)(2,1)} %copy-done.14), calls=%async_computation.1 | async-start | bytes 1048576 | tf_op jit(solution)/shard_map/all_to_all | solution.py:38
  31.5 0.5 collective-permute-start.8
  32.0 1.5 collective-permute-done.6.a1
  33.5 1.0 collective-permute-done.8.a3
  34.5 4.2 %head_grads.1 = bf16[1024,512]{1,0:T(8,128)(2,1)} custom-call(s32[4]{0:T(128)S(1)} %iota_xor_fusion.blk, bf16[512,512]{1,0:T(8,128)(2,1)S(1)} %copy-done.12, bf16[512,512]{1,0:T(8,128)(2,1)} %collective-permute-done.6.a1, bf16[512,512]{1,0:T(8,128)(2,1)} %collective-permute-done.7.a2, bf16[512,512]{1,0:T(8,128)(2,1)} %collective-permute-done.8.a3, ...), custom_call_target="tpu_custom_call" | custom-call | tf_op jit(solution)/shard_map/head_grads/pallas_call | solution.py:95
  38.8 7.0 %all-to-all-done.1.x0 = bf16[8,64,512]{2,1,0:T(8,128)(2,1)} async-done(((bf16[8,64,512]{2,1,0:T(8,128)(2,1)}), bf16[8,64,512]{2,1,0:T(8,128)(2,1)}, u32[]{:S(2)}, u32[]{:S(2)}) %all-to-all-start.1) | async-done | bytes 524320 | tf_op jit(solution)/shard_map/all_to_all | solution.py:38
  45.7 3.6 %all-to-all-start.2 = ((bf16[8,128,512]{2,1,0:T(8,128)(2,1)}), bf16[8,128,512]{2,1,0:T(8,128)(2,1)S(1)}, u32[]{:S(2)}, u32[]{:S(2)}) async-start(bf16[8,128,512]{2,1,0:T(8,128)(2,1)} %bitcast), calls=%async_computation.2 | async-start | bytes 2097152 | tf_op jit(solution)/shard_map/all_to_all | solution.py:38
  49.3 1.5 collective-permute-start.4
  50.9 12.1 %collective-permute-done.4.x2 = bf16[8,64,512]{2,1,0:T(8,128)(2,1)S(1)} collective-permute-done((bf16[8,64,512]{2,1,0:T(8,128)(2,1)}, bf16[8,64,512]{2,1,0:T(8,128)(2,1)S(1)}, u32[]{:S(2)}, u32[]{:S(2)}) %collective-permute-start.4) | collective-permute-done | bytes 524320 | tf_op jit(solution)/shard_map/ppermute | solution.py:34
  63.0 1.5 collective-permute-start.1
  64.5 0.4 collective-permute-done.5.x3
  64.9 1.6 copy-done.16
  66.5 1.6 copy-done.19
  68.1 1.6 copy-done.22
  69.6 10.3 %forward.2 = (bf16[8,128,512]{2,1,0:T(8,128)(2,1)S(1)}, bf16[8,64,1536]{2,1,0:T(8,128)(2,1)S(1)}, f32[2,2,4,128,128]{4,3,2,1,0:T(8,128)S(1)}) custom-call(s32[4]{0:T(128)S(1)} %iota_xor_fusion.blk, bf16[8,64,512]{2,1,0:T(8,128)(2,1)} %all-to-all-done.x0, bf16[8,64,512]{2,1,0:T(8,128)(2,1)S(1)} %collective-permute-done.3.x1, ...), custom_call_target="tpu_custom_call" | custom-call | flops 3221225472 | bytes 10485760 | tf_op jit(solution)/shard_map/forward/pallas_call | solution.py:222
  80.0 1.0 copy-done.9
  80.9 1.2 copy-done.27
  82.1 1.0 copy-done.31
  83.1 2.0 copy-done.17
  85.1 1.6 copy-done.20
  86.7 1.6 copy-done.23
  88.3 1.4 copy-done.28
  89.7 1.2 copy-done.32
  90.9 9.7 %backward.2 = (bf16[2,8,64,512]{3,2,1,0:T(8,128)(2,1)S(1)}, bf16[2,8,64,512]{3,2,1,0:T(8,128)(2,1)}) custom-call(s32[4]{0:T(128)S(1)} %iota_xor_fusion.blk, bf16[8,64,1536]{2,1,0:T(8,128)(2,1)S(1)} %copy-done.28, f32[2,2,4,128,128]{4,3,2,1,0:T(8,128)S(1)} %copy-done.32, bf16[8,128,512]{2,1,0:T(8,128)(2,1)S(1)} %all-to-all-done.2.g_ref, ...), custom_call_target="tpu_custom_call" | custom-call | flops 3221225472 | bytes 12582912 | tf_op jit(solution)/shard_map/backward/pallas_call | solution.py:257
  100.6 1.0 copy-done.3
  102.2 3.0 %collective-permute-done.x1 = bf16[8,64,512]{2,1,0:T(8,128)(2,1)S(1)} collective-permute-done((bf16[8,64,512]{2,1,0:T(8,128)(2,1)}, bf16[8,64,512]{2,1,0:T(8,128)(2,1)S(1)}, u32[]{:S(2)}, u32[]{:S(2)}) %collective-permute-start) | collective-permute-done | bytes 524320 | tf_op jit(solution)/shard_map/ppermute | solution.py:34
  105.2 0.7 collective-permute-done.2.x3
  105.9 10.4 %forward.3 = (bf16[8,128,512]{2,1,0:T(8,128)(2,1)S(1)}, bf16[8,64,1536]{2,1,0:T(8,128)(2,1)S(1)}, f32[2,2,4,128,128]{4,3,2,1,0:T(8,128)S(1)}) custom-call(s32[4]{0:T(128)S(1)} %iota_xor_fusion.blk, bf16[8,64,512]{2,1,0:T(8,128)(2,1)} %all-to-all-done.1.x0, bf16[8,64,512]{2,1,0:T(8,128)(2,1)S(1)} %collective-permute-done.x1, ...), custom_call_target="tpu_custom_call", output_to_operand_aliasing={{0}: (8, {})} | custom-call | flops 3221225472 | bytes 10485760 | tf_op jit(solution)/shard_map/forward/pallas_call | solution.py:222
  116.4 1.0 copy-done.11
  117.3 1.2 copy-done.25
  118.5 1.0 copy-done.29
  119.5 5.7 %all-to-all-start.3 = ((bf16[8,128,512]{2,1,0:T(8,128)(2,1)}), bf16[8,128,512]{2,1,0:T(8,128)(2,1)S(1)}, u32[]{:S(2)}, u32[]{:S(2)}) async-start(bf16[8,128,512]{2,1,0:T(8,128)(2,1)} %copy-done.11), calls=%async_computation.3 | async-start | bytes 2097152 | tf_op jit(solution)/shard_map/all_to_all | solution.py:38
  125.2 1.3 fusion.4
  126.6 1.2 copy-done.2
  127.8 1.6 copy-done.18
  129.4 1.6 copy-done.21
  131.0 1.6 copy-done.24
  132.6 1.4 copy-done.26
  134.0 1.2 copy-done.30
  135.2 9.7 %backward.3 = (bf16[2,8,64,512]{3,2,1,0:T(8,128)(2,1)S(1)}, bf16[2,8,64,512]{3,2,1,0:T(8,128)(2,1)}) custom-call(s32[4]{0:T(128)S(1)} %iota_xor_fusion.blk, bf16[8,64,1536]{2,1,0:T(8,128)(2,1)S(1)} %copy-done.26, f32[2,2,4,128,128]{4,3,2,1,0:T(8,128)S(1)} %copy-done.30, bf16[8,128,512]{2,1,0:T(8,128)(2,1)S(1)} %copy-done.2, ...), custom_call_target="tpu_custom_call" | custom-call | flops 3221225472 | bytes 12582912 | tf_op jit(solution)/shard_map/backward/pallas_call | solution.py:257
  144.9 1.0 copy-done.5
  145.9 1.5 collective-permute-start.12
  147.4 12.8 %collective-permute-done.12 = bf16[8,64,512]{2,1,0:T(8,128)(2,1)S(1)} collective-permute-done((bf16[8,64,512]{2,1,0:T(8,128)(2,1)S(1)}, bf16[8,64,512]{2,1,0:T(8,128)(2,1)S(1)}, u32[]{:S(2)}, u32[]{:S(2)}) %collective-permute-start.12) | collective-permute-done | bytes 524320 | tf_op jit(solution)/shard_map/ppermute | solution.py:34
  160.2 2.0 fusion.1
  162.3 6.0 %all-to-all-start.4 = ((bf16[8,64,512]{2,1,0:T(8,128)(2,1)}), bf16[8,64,512]{2,1,0:T(8,128)(2,1)}, u32[]{:S(2)}, u32[]{:S(2)}) async-start(bf16[8,64,512]{2,1,0:T(8,128)(2,1)} %fusion.1), calls=%async_computation.4 | async-start | bytes 1048576 | tf_op jit(solution)/shard_map/all_to_all | solution.py:38
  168.3 3.0 %project_out.1 = (bf16[2,512,512]{2,1,0:T(8,128)(2,1)S(1)}, bf16[2,512,512]{2,1,0:T(8,128)(2,1)}) custom-call(s32[4]{0:T(128)S(1)} %iota_xor_fusion.blk, s32[512,1]{1,0:T(8,128)S(1)} %get-tuple-element.24.slot_col, bf16[512,2048]{1,0:T(8,128)(2,1)S(1)} %copy-done, bf16[8,128,512]{2,1,0:T(8,128)(2,1)S(1)} %all-to-all-done.3.mixed), custom_call_target="tpu_custom_call" | custom-call | tf_op jit(solution)/shard_map/project_out/pallas_call | solution.py:380
  171.3 1.0 copy-done.7
  172.3 1.3 fusion.5
  173.6 1.5 collective-permute-start.14
  175.1 12.8 %collective-permute-done.14 = bf16[8,64,512]{2,1,0:T(8,128)(2,1)S(1)} collective-permute-done((bf16[8,64,512]{2,1,0:T(8,128)(2,1)S(1)}, bf16[8,64,512]{2,1,0:T(8,128)(2,1)S(1)}, u32[]{:S(2)}, u32[]{:S(2)}) %collective-permute-start.14) | collective-permute-done | bytes 524320 | tf_op jit(solution)/shard_map/ppermute | solution.py:34
  188.0 2.0 fusion
  190.0 6.0 %all-to-all-start.5 = ((bf16[8,64,512]{2,1,0:T(8,128)(2,1)}), bf16[8,64,512]{2,1,0:T(8,128)(2,1)S(1)}, u32[]{:S(2)}, u32[]{:S(2)}) async-start(bf16[8,64,512]{2,1,0:T(8,128)(2,1)} %fusion), calls=%async_computation.5 | async-start | bytes 1048576 | tf_op jit(solution)/shard_map/all_to_all | solution.py:38
  196.2 1.6 collective-permute-start.10
  197.7 11.8 %collective-permute-done.10 = bf16[512,512]{1,0:T(8,128)(2,1)S(1)} collective-permute-done((bf16[512,512]{1,0:T(8,128)(2,1)S(1)}, bf16[512,512]{1,0:T(8,128)(2,1)S(1)}, u32[]{:S(2)}, u32[]{:S(2)}) %collective-permute-start.10) | collective-permute-done | bytes 524320 | tf_op jit(solution)/shard_map/ppermute | solution.py:34
  209.5 1.0 fusion.2
  210.5 2.8 %to_tokens.1 = f32[512,512]{1,0:T(8,128)} custom-call(s32[512,1]{1,0:T(8,128)S(1)} %get-tuple-element.24.slot_col, bf16[8,64,512]{2,1,0:T(8,128)(2,1)} %all-to-all-done.4.refs_0_, bf16[8,64,512]{2,1,0:T(8,128)(2,1)S(1)} %all-to-all-done.5.refs_1_), custom_call_target="tpu_custom_call" | custom-call | tf_op jit(solution)/shard_map/to_tokens/pallas_call | solution.py:401
  (60 shorter events, 1.0 us)
Async XLA Ops:
  0.6 12.1 %copy-start.12 = (bf16[512,512]{1,0:T(8,128)(2,1)S(1)}, bf16[512,512]{1,0:T(8,128)(2,1)}, u32[]{:S(2)}) copy-start(bf16[512,512]{1,0:T(8,128)(2,1)} %a0.1) | copy-start | bytes 1572868
  0.6 33.9 %copy-start = (bf16[512,2048]{1,0:T(8,128)(2,1)S(1)}, bf16[512,2048]{1,0:T(8,128)(2,1)}, u32[]{:S(2)}) copy-start(bf16[512,2048]{1,0:T(8,128)(2,1)} %w_out.3) | copy-start | bytes 6291460
  1.6 1.0 copy-start.13
  3.8 0.8 copy-start.14
  4.6 0.8 copy-start.15
  5.4 21.9 %all-to-all-start = ((bf16[8,64,512]{2,1,0:T(8,128)(2,1)}), bf16[8,64,512]{2,1,0:T(8,128)(2,1)}, u32[]{:S(2)}, u32[]{:S(2)}) async-start(bf16[8,64,512]{2,1,0:T(8,128)(2,1)} %copy-done.15), calls=%async_computation | async-start | bytes 1048576 | tf_op jit(solution)/shard_map/all_to_all | solution.py:38
  12.7 18.8 %collective-permute-start.7 = (bf16[512,512]{1,0:T(8,128)(2,1)S(1)}, bf16[512,512]{1,0:T(8,128)(2,1)}, u32[]{:S(2)}, u32[]{:S(2)}) collective-permute-start(bf16[512,512]{1,0:T(8,128)(2,1)S(1)} %copy-done.12), channel_id=1, source_target_pairs={{0,2},{1,3},{2,0},{3,1},{4,6},{5,7},{6,4},{7,5},{8,10},{9,11},{10,... | collective-permute-start | bytes 1572872 | tf_op jit(solution)/shard_map/ppermute | solution.py:34
  27.3 18.5 %all-to-all-start.1 = ((bf16[8,64,512]{2,1,0:T(8,128)(2,1)}), bf16[8,64,512]{2,1,0:T(8,128)(2,1)}, u32[]{:S(2)}, u32[]{:S(2)}) async-start(bf16[8,64,512]{2,1,0:T(8,128)(2,1)} %copy-done.14), calls=%async_computation.1 | async-start | bytes 1048576 | tf_op jit(solution)/shard_map/all_to_all | solution.py:38
  31.4 2.1 collective-permute-start.6
  31.5 3.0 %collective-permute-start.8 = (bf16[512,512]{1,0:T(8,128)(2,1)}, bf16[512,512]{1,0:T(8,128)(2,1)}, u32[]{:S(2)}, u32[]{:S(2)}) collective-permute-start(bf16[512,512]{1,0:T(8,128)(2,1)} %collective-permute-done.7.a2), channel_id=1, source_target_pairs={{0,1},{1,0},{2,3},{3,2},{4,5},{5,4},{6,7},{7,6},{8,9},{9,8},{10,11... | collective-permute-start | bytes 1572872 | tf_op jit(solution)/shard_map/ppermute | solution.py:34
  45.7 37.4 %all-to-all-start.2 = ((bf16[8,128,512]{2,1,0:T(8,128)(2,1)}), bf16[8,128,512]{2,1,0:T(8,128)(2,1)S(1)}, u32[]{:S(2)}, u32[]{:S(2)}) async-start(bf16[8,128,512]{2,1,0:T(8,128)(2,1)} %bitcast), calls=%async_computation.2 | async-start | bytes 2097152 | tf_op jit(solution)/shard_map/all_to_all | solution.py:38
  49.3 13.6 %collective-permute-start.4 = (bf16[8,64,512]{2,1,0:T(8,128)(2,1)}, bf16[8,64,512]{2,1,0:T(8,128)(2,1)S(1)}, u32[]{:S(2)}, u32[]{:S(2)}) collective-permute-start(bf16[8,64,512]{2,1,0:T(8,128)(2,1)} %all-to-all-done.x0), channel_id=1, source_target_pairs={{0,2},{1,3},{2,0},{3,1},{4,6},{5,7},{6,4},{7,5},{8,10},{9,11},{10,... | collective-permute-start | bytes 1572872 | tf_op jit(solution)/shard_map/ppermute | solution.py:34
  50.9 13.6 %collective-permute-start.3 = (bf16[8,64,512]{2,1,0:T(8,128)(2,1)}, bf16[8,64,512]{2,1,0:T(8,128)(2,1)S(1)}, u32[]{:S(2)}, u32[]{:S(2)}) collective-permute-start(bf16[8,64,512]{2,1,0:T(8,128)(2,1)} %all-to-all-done.x0), channel_id=1, source_target_pairs={{0,1},{1,0},{2,3},{3,2},{4,5},{5,4},{6,7},{7,6},{8,9},{9,8},{10,11... | collective-permute-start | bytes 1572872 | tf_op jit(solution)/shard_map/ppermute | solution.py:34
  63.0 1.9 collective-permute-start.5
  63.0 39.1 %collective-permute-start.1 = (bf16[8,64,512]{2,1,0:T(8,128)(2,1)}, bf16[8,64,512]{2,1,0:T(8,128)(2,1)}, u32[]{:S(2)}, u32[]{:S(2)}) collective-permute-start(bf16[8,64,512]{2,1,0:T(8,128)(2,1)} %all-to-all-done.1.x0), channel_id=1, source_target_pairs={{0,2},{1,3},{2,0},{3,1},{4,6},{5,7},{6,4},{7,5},{8,10},{9,11},{10,... | collective-permute-start | bytes 1572872 | tf_op jit(solution)/shard_map/ppermute | solution.py:34
  64.9 1.6 copy-start.16
  66.5 1.6 copy-start.19
  68.1 1.6 copy-start.22
  80.0 1.0 copy-start.9
  80.9 1.2 copy-start.27
  82.1 1.0 copy-start.31
  83.1 17.5 %copy-start.1 = (bf16[8,128,512]{2,1,0:T(8,128)(2,1)}, bf16[8,128,512]{2,1,0:T(8,128)(2,1)S(1)}, u32[]{:S(2)}) copy-start(bf16[8,128,512]{2,1,0:T(8,128)(2,1)S(1)} %all-to-all-done.2.g_ref) | copy-start | bytes 3145732
  83.1 2.0 copy-start.17
  85.1 1.6 copy-start.20
  86.7 1.6 copy-start.23
  88.2 1.4 copy-start.28
  89.7 1.2 copy-start.32
  90.9 15.1 %copy-start.10 = (bf16[8,128,512]{2,1,0:T(8,128)(2,1)S(1)}, bf16[8,128,512]{2,1,0:T(8,128)(2,1)}, u32[]{:S(2)}) copy-start(bf16[8,128,512]{2,1,0:T(8,128)(2,1)} %copy-done.9) | copy-start | bytes 3145732
  100.6 1.0 copy-start.3
  101.6 23.6 %collective-permute-start.11 = (bf16[2,8,64,512]{3,2,1,0:T(8,128)(2,1)}, bf16[2,8,64,512]{3,2,1,0:T(8,128)(2,1)}, u32[]{:S(2)}, u32[]{:S(2)}) collective-permute-start(bf16[2,8,64,512]{3,2,1,0:T(8,128)(2,1)} %get-tuple-element.38), channel_id=1, source_target_pairs={{0,1},{1,0},{2,3},{3,2},{4,5},{5,4},{6,7},{7,6},{8,9},{9,8},{10,11... | collective-permute-start | bytes 3145736 | tf_op jit(solution)/shard_map/ppermute | solution.py:34
  101.7 3.5 %collective-permute-start = (bf16[8,64,512]{2,1,0:T(8,128)(2,1)}, bf16[8,64,512]{2,1,0:T(8,128)(2,1)S(1)}, u32[]{:S(2)}, u32[]{:S(2)}) collective-permute-start(bf16[8,64,512]{2,1,0:T(8,128)(2,1)} %all-to-all-done.1.x0), channel_id=1, source_target_pairs={{0,1},{1,0},{2,3},{3,2},{4,5},{5,4},{6,7},{7,6},{8,9},{9,8},{10,11... | collective-permute-start | bytes 1572872 | tf_op jit(solution)/shard_map/ppermute | solution.py:34
  102.1 3.9 %collective-permute-start.2 = (bf16[8,64,512]{2,1,0:T(8,128)(2,1)}, bf16[8,64,512]{2,1,0:T(8,128)(2,1)S(1)}, u32[]{:S(2)}, u32[]{:S(2)}) collective-permute-start(bf16[8,64,512]{2,1,0:T(8,128)(2,1)} %collective-permute-done.1.x2), channel_id=1, source_target_pairs={{0,1},{1,0},{2,3},{3,2},{4,5},{5,4},{6,7},{7,6},{8,9},{9,8},{10,11... | collective-permute-start | bytes 1572872 | tf_op jit(solution)/shard_map/ppermute | solution.py:34
  116.4 1.0 copy-start.11
  117.3 1.2 copy-start.25
  118.5 1.0 copy-start.29
  119.5 42.8 %all-to-all-start.3 = ((bf16[8,128,512]{2,1,0:T(8,128)(2,1)}), bf16[8,128,512]{2,1,0:T(8,128)(2,1)S(1)}, u32[]{:S(2)}, u32[]{:S(2)}) async-start(bf16[8,128,512]{2,1,0:T(8,128)(2,1)} %copy-done.11), calls=%async_computation.3 | async-start | bytes 2097152 | tf_op jit(solution)/shard_map/all_to_all | solution.py:38
  126.5 1.2 copy-start.2
  127.8 1.6 copy-start.18
  129.4 1.6 copy-start.21
  131.0 1.6 copy-start.24
  132.5 1.4 copy-start.26
  134.0 1.2 copy-start.30
  135.2 25.0 %copy-start.4 = (bf16[2,8,64,512]{3,2,1,0:T(8,128)(2,1)S(1)}, bf16[2,8,64,512]{3,2,1,0:T(8,128)(2,1)}, u32[]{:S(2)}) copy-start(bf16[2,8,64,512]{3,2,1,0:T(8,128)(2,1)} %copy-done.3) | copy-start | bytes 3145732
  144.9 1.0 copy-start.5
  145.9 26.4 %collective-permute-start.13 = (bf16[2,8,64,512]{3,2,1,0:T(8,128)(2,1)}, bf16[2,8,64,512]{3,2,1,0:T(8,128)(2,1)}, u32[]{:S(2)}, u32[]{:S(2)}) collective-permute-start(bf16[2,8,64,512]{3,2,1,0:T(8,128)(2,1)} %get-tuple-element.44), channel_id=1, source_target_pairs={{0,1},{1,0},{2,3},{3,2},{4,5},{5,4},{6,7},{7,6},{8,9},{9,8},{10,11... | collective-permute-start | bytes 3145736 | tf_op jit(solution)/shard_map/ppermute | solution.py:34
  145.9 14.3 %collective-permute-start.12 = (bf16[8,64,512]{2,1,0:T(8,128)(2,1)S(1)}, bf16[8,64,512]{2,1,0:T(8,128)(2,1)S(1)}, u32[]{:S(2)}, u32[]{:S(2)}) collective-permute-start(bf16[8,64,512]{2,1,0:T(8,128)(2,1)S(1)} %fusion.4), channel_id=1, source_target_pairs={{0,2},{1,3},{2,0},{3,1},{4,6},{5,7},{6,4},{7,5},{8,10},{9,11},{10,... | collective-permute-start | bytes 1572872 | tf_op jit(solution)/shard_map/ppermute | solution.py:34
  162.3 27.8 %all-to-all-start.4 = ((bf16[8,64,512]{2,1,0:T(8,128)(2,1)}), bf16[8,64,512]{2,1,0:T(8,128)(2,1)}, u32[]{:S(2)}, u32[]{:S(2)}) async-start(bf16[8,64,512]{2,1,0:T(8,128)(2,1)} %fusion.1), calls=%async_computation.4 | async-start | bytes 1048576 | tf_op jit(solution)/shard_map/all_to_all | solution.py:38
  168.2 4.0 %copy-start.6 = (bf16[2,8,64,512]{3,2,1,0:T(8,128)(2,1)S(1)}, bf16[2,8,64,512]{3,2,1,0:T(8,128)(2,1)}, u32[]{:S(2)}) copy-start(bf16[2,8,64,512]{3,2,1,0:T(8,128)(2,1)} %copy-done.5) | copy-start | bytes 3145732
  171.3 1.0 copy-start.7
  172.3 23.7 %collective-permute-start.9 = (bf16[2,512,512]{2,1,0:T(8,128)(2,1)}, bf16[2,512,512]{2,1,0:T(8,128)(2,1)S(1)}, u32[]{:S(2)}, u32[]{:S(2)}) collective-permute-start(bf16[2,512,512]{2,1,0:T(8,128)(2,1)} %get-tuple-element.34), channel_id=1, source_target_pairs={{0,1},{1,0},{2,3},{3,2},{4,5},{5,4},{6,7},{7,6},{8,9},{9,8},{10,11... | collective-permute-start | bytes 3145736 | tf_op jit(solution)/shard_map/ppermute | solution.py:34
  172.3 23.7 %copy-start.8 = (bf16[2,512,512]{2,1,0:T(8,128)(2,1)S(1)}, bf16[2,512,512]{2,1,0:T(8,128)(2,1)}, u32[]{:S(2)}) copy-start(bf16[2,512,512]{2,1,0:T(8,128)(2,1)} %copy-done.7) | copy-start | bytes 3145732
  173.6 14.4 %collective-permute-start.14 = (bf16[8,64,512]{2,1,0:T(8,128)(2,1)S(1)}, bf16[8,64,512]{2,1,0:T(8,128)(2,1)S(1)}, u32[]{:S(2)}, u32[]{:S(2)}) collective-permute-start(bf16[8,64,512]{2,1,0:T(8,128)(2,1)S(1)} %fusion.5), channel_id=1, source_target_pairs={{0,2},{1,3},{2,0},{3,1},{4,6},{5,7},{6,4},{7,5},{8,10},{9,11},{10,... | collective-permute-start | bytes 1572872 | tf_op jit(solution)/shard_map/ppermute | solution.py:34
  190.0 20.5 %all-to-all-start.5 = ((bf16[8,64,512]{2,1,0:T(8,128)(2,1)}), bf16[8,64,512]{2,1,0:T(8,128)(2,1)S(1)}, u32[]{:S(2)}, u32[]{:S(2)}) async-start(bf16[8,64,512]{2,1,0:T(8,128)(2,1)} %fusion), calls=%async_computation.5 | async-start | bytes 1048576 | tf_op jit(solution)/shard_map/all_to_all | solution.py:38
  196.2 13.3 %collective-permute-start.10 = (bf16[512,512]{1,0:T(8,128)(2,1)S(1)}, bf16[512,512]{1,0:T(8,128)(2,1)S(1)}, u32[]{:S(2)}, u32[]{:S(2)}) collective-permute-start(bf16[512,512]{1,0:T(8,128)(2,1)S(1)} %fusion.3), channel_id=1, source_target_pairs={{0,2},{1,3},{2,0},{3,1},{4,6},{5,7},{6,4},{7,5},{8,10},{9,11},{10,... | collective-permute-start | bytes 1572872 | tf_op jit(solution)/shard_map/ppermute | solution.py:34

commit v3 on v2

v3 whole, which is shorter than its diff:
```python
import functools
import jax
import jax.numpy as jnp
from jax import lax
from jax.experimental import pallas as pl
from jax.experimental.pallas import tpu as pltpu
from jax.sharding import PartitionSpec as P

HEAD_DIM = 128
CLUSTERS = 128
CAP = 256
MOST = 8
LIMIT = 24.0
EMPTY = 32.0
NN = (((1,), (0,)), ((), ()))
NT = (((1,), (1,)), ((), ()))
TN = (((0,), (0,)), ((), ()))
MB = 1024 * 1024
CHUNKS = 2
GRANT = 60 * MB


def cost(giga):
    return pl.CostEstimate(flops=int(giga * 1e9), bytes_accessed=MB, transcendentals=0)


VMEM = pl.BlockSpec(memory_space=pltpu.VMEM)
SMEM = pl.BlockSpec(memory_space=pltpu.SMEM)


def dot(a, b, dims=NN):
    return lax.dot_general(a, b, dims, preferred_element_type=jnp.float32)


def iota(shape, dim):
    return lax.broadcasted_iota(jnp.int32, shape, dim)


def swap(x, bit):
    count = lax.axis_size("tp")
    return lax.ppermute(x, "tp", [(i, i ^ bit) for i in range(count)])


def exchange(x):
    return lax.all_to_all(x, "seq", split_axis=0, concat_axis=0, tiled=True)


def after(x, *others):
    return lax.optimization_barrier((x,) + others)[0]


def place_kernel(ids_col, x_ref, slot_col, slot_row, out):
    tokens = x_ref.shape[0]
    here, there = (iota((tokens, tokens), 0), iota((tokens, tokens), 1))
    col = ids_col[...]
    row = jnp.sum(jnp.where(here == there, col, 0), axis=0, keepdims=True)
    same = col == row
    earlier = jnp.where(same & (there < here), 1.0, 0.0)
    later = jnp.where(same & (here < there), 1.0, 0.0)
    slot_col[...] = col * MOST + jnp.sum(earlier, axis=1, keepdims=True).astype(jnp.int32)
    slot_row[...] = row * MOST + jnp.sum(later, axis=0, keepdims=True).astype(jnp.int32)
    slots, width = out.shape
    chosen = jnp.where(iota((slots, tokens), 0) == slot_row[...], 1.0, 0.0)
    taken = jnp.sum(chosen, axis=1, keepdims=True)
    value = dot(chosen.astype(jnp.bfloat16), x_ref[...])
    first = iota((slots, width), 1) == 0
    out[...] = (value + jnp.where(first & (taken == 0.0), EMPTY, 0.0)).astype(jnp.bfloat16)


def place(cluster, x):
    tokens = x.shape[0]
    return pl.pallas_call(
        place_kernel,
        out_shape=(
            jax.ShapeDtypeStruct((tokens, 1), jnp.int32),
            jax.ShapeDtypeStruct((1, tokens), jnp.int32),
            jax.ShapeDtypeStruct((CLUSTERS * MOST, x.shape[1]), jnp.bfloat16),
        ),
        compiler_params=pltpu.CompilerParams(vmem_limit_bytes=GRANT),
        cost_estimate=cost(1),
        name="place",
    )(cluster, x)


def head_grads_kernel(blk, a0, a1, a2, a3, w_out, slot_row, out_ref):
    width = a0.shape[1]
    total = None
    for j, part in enumerate((a0, a1, a2, a3)):
        cols = pl.ds(pl.multiple_of(blk[j] * width, width), width)
        term = dot(part[...], w_out[:, cols], NT)
        total = term if total is None else total + term
    slots, tokens = (out_ref.shape[0], a0.shape[0])
    chosen = jnp.where(iota((slots, tokens), 0) == slot_row[...], 1.0, 0.0).astype(jnp.bfloat16)
    out_ref[...] = dot(chosen, total.astype(jnp.bfloat16)).astype(jnp.bfloat16)


def head_grads(blk, parts, w_out, slot_row):
    return pl.pallas_call(
        head_grads_kernel,
        out_shape=jax.ShapeDtypeStruct((CLUSTERS * MOST, w_out.shape[0]), jnp.bfloat16),
        in_specs=[SMEM] + [VMEM] * 6,
        out_specs=VMEM,
        compiler_params=pltpu.CompilerParams(vmem_limit_bytes=GRANT),
        cost_estimate=cost(1),
        name="head_grads",
    )(blk, *parts, w_out, slot_row)


GROUP = 16


def spans(blk, width):
    return [pl.ds(pl.multiple_of(blk[j] * width, width), width) for j in range(4)]


def load_all(first, sources, targets, sems):
    @pl.when(first)
    def _():
        for source, target, i in zip(sources, targets, range(3)):
            pltpu.make_async_copy(source, target, sems.at[i]).start()


def wait_for(first, source, target, sem):
    @pl.when(first)
    def _():
        pltpu.make_async_copy(source, target, sem).wait()


def forward_kernel(blk, x0, x1, x2, x3, wq, wk, wv, *refs):
    mixed, saved, probs_ref, *loaded, sems = refs[-7:]
    sources, rows, width = x0.shape
    heads_width = wq.shape[1]
    heads = heads_width // HEAD_DIM
    scale = HEAD_DIM ** (-0.5)
    span = spans(blk, width)
    first = pl.program_id(0) == 0
    load_all(first, (wq, wk, wv), loaded, sems)
    members = sources * GROUP
    shape = (sources, GROUP, members)
    here = (iota(shape, 1) // MOST).reshape(members, members)
    source_here = iota(shape, 0).reshape(members, members)
    place_here = iota(shape, 1).reshape(members, members)
    lane = iota((members, members), 1)
    there = lane % GROUP // MOST
    same = here == there
    earlier = same & (lane // GROUP < source_here)
    later = same & (lane // GROUP > source_here)
    diagonal = source_here * GROUP + place_here == lane
    rank_col = (place_here % MOST).astype(jnp.float32)[:, :1]
    rank_row = (lane % MOST).astype(jnp.float32)[:1, :]
    groups = [slice(n * GROUP, (n + 1) * GROUP) for n in range(rows // GROUP)]
    kept, usable = ([], [])
    for group in groups:
        mark = x0[:, group, :HEAD_DIM].reshape(members, HEAD_DIM)[:, :1].astype(jnp.float32)
        held_col = jnp.where(mark <= LIMIT, 1.0, 0.0)
        held_row = jnp.sum(jnp.where(diagonal, held_col, 0.0), axis=0, keepdims=True)
        place_col = rank_col + jnp.sum(jnp.where(earlier, held_row, 0.0), axis=1, keepdims=True)
        place_row = rank_row + jnp.sum(jnp.where(later, held_col, 0.0), axis=0, keepdims=True)
        kept.append(jnp.where(place_col < CAP, held_col, 0.0))
        usable.append(same & (jnp.where(place_row < CAP, held_row, 0.0) > 0))

    xs = [r[...].reshape(sources * rows, width) for r in (x0, x1, x2, x3)]
    for i, (w, source) in enumerate(zip(loaded, (wq, wk, wv))):
        wait_for(first, source, w, sems.at[i])
        total = dot(xs[0], w[span[0], :])
        for j in range(1, 4):
            total = total + dot(xs[j], w[span[j], :])
        saved[:, :, i * heads_width : (i + 1) * heads_width] = total.astype(jnp.bfloat16).reshape(
            sources, rows, heads_width
        )

    def part(i, n, h):
        start = i * heads_width + h * HEAD_DIM
        return saved[:, groups[n], start : start + HEAD_DIM].reshape(members, HEAD_DIM)

    every = [(n, h) for n in range(len(groups)) for h in range(heads)]
    scores = [
        jnp.where(usable[n], dot(part(0, n, h), part(1, n, h), NT) * scale, -1e30)
        for n, h in every
    ]
    raised = [jnp.exp(s - jnp.max(s, axis=1, keepdims=True)) for s in scores]
    probs = [
        r * (kept[n] / jnp.sum(r, axis=1, keepdims=True)) for (n, h), r in zip(every, raised)
    ]
    for (n, h), p in zip(every, probs):
        probs_ref[0, n, h] = p
        out = dot(p.astype(jnp.bfloat16), part(2, n, h)).astype(jnp.bfloat16)
        mixed[:, groups[n], h * HEAD_DIM : (h + 1) * HEAD_DIM] = out.reshape(
            sources, GROUP, HEAD_DIM
        )


def backward_kernel(blk, saved, probs_ref, g_ref, wq, wk, wv, *refs):
    keep, give, (dq, dk, dv, *loaded, sems) = (refs[:2], refs[2:6], refs[6:])
    sources, rows, _ = saved.shape
    width = keep[0].shape[2]
    heads_width = wq.shape[1]
    heads = heads_width // HEAD_DIM
    scale = HEAD_DIM ** (-0.5)
    span = spans(blk, width)
    first = pl.program_id(0) == 0
    load_all(first, (wq, wk, wv), loaded, sems)
    members = sources * GROUP
    groups = [slice(n * GROUP, (n + 1) * GROUP) for n in range(rows // GROUP)]
    every = [(n, h) for n in range(len(groups)) for h in range(heads)]

    def part(i, n, h):
        start = i * heads_width + h * HEAD_DIM
        return saved[:, groups[n], start : start + HEAD_DIM].reshape(members, HEAD_DIM)

    def grad(n, h):
        return g_ref[:, groups[n], h * HEAD_DIM : (h + 1) * HEAD_DIM].reshape(members, HEAD_DIM)

    def put(ref, n, h, value):
        cols = slice(h * HEAD_DIM, (h + 1) * HEAD_DIM)
        ref[:, groups[n], cols] = value.astype(jnp.bfloat16).reshape(sources, GROUP, HEAD_DIM)

    grad_probs = [dot(grad(n, h), part(2, n, h), NT) for n, h in every]
    for n, h in every:
        put(dv, n, h, dot(probs_ref[0, n, h].astype(jnp.bfloat16), grad(n, h), TN))
    inner = [
        jnp.sum(gp * probs_ref[0, n, h], axis=1, keepdims=True)
        for (n, h), gp in zip(every, grad_probs)
    ]
    grad_scores = [
        (probs_ref[0, n, h] * (gp - i) * scale).astype(jnp.bfloat16)
        for (n, h), gp, i in zip(every, grad_probs, inner)
    ]
    for (n, h), gs in zip(every, grad_scores):
        put(dq, n, h, dot(gs, part(1, n, h)))
    for (n, h), gs in zip(every, grad_scores):
        put(dk, n, h, dot(gs, part(0, n, h), TN))
    for i, (w, source) in enumerate(zip(loaded, (wq, wk, wv))):
        wait_for(first, source, w, sems.at[i])
    grads = [d[...].reshape(sources * rows, heads_width) for d in (dq, dk, dv)]
    for j in (1, 3, 0, 2):
        total = None
        for d, w in zip(grads, loaded):
            term = dot(d, w[span[j], :], NT)
            total = term if total is None else total + term
        total = total.astype(jnp.bfloat16).reshape(sources, rows, width)
        if j % 2 == 0:
            keep[j // 2][...] = total
        else:
            give[j - 1][...] = total[: sources // 2]
            give[j][...] = total[sources // 2 :]


def step_of(sources, rows):
    step = GROUP
    while step * 2 * sources <= 256 and rows % (step * 2) == 0:
        step *= 2
    return step


def forward(blk, parts, wq, wk, wv, chunk, chunks, mixed):
    sources, rows, width = parts[2].shape
    heads_width = wq.shape[1]
    heads = heads_width // HEAD_DIM
    step = step_of(sources, rows)
    steps, groups, members = (rows // step, step // GROUP, sources * GROUP)
    block = pl.BlockSpec((sources, step, width), lambda p: (0, p, 0))
    whole = pl.BlockSpec((sources, step, width), lambda p: (0, p + chunk * steps, 0))
    weight = pl.BlockSpec(memory_space=pl.ANY)
    loaded = [pltpu.VMEM(wq.shape, wq.dtype)] * 3 + [pltpu.SemaphoreType.DMA((3,))]
    in_specs = [SMEM] + [whole] * 2 + [block] * 2 + [weight] * 3
    operands = [blk, *parts, wq, wk, wv]
    if mixed is not None:
        in_specs.append(pl.BlockSpec(memory_space=pl.ANY))
        operands.append(mixed)
    return pl.pallas_call(
        forward_kernel,
        grid=(steps,),
        out_shape=(
            jax.ShapeDtypeStruct((sources, rows * chunks, heads_width), jnp.bfloat16),
            jax.ShapeDtypeStruct((sources, rows, 3 * heads_width), jnp.bfloat16),
            jax.ShapeDtypeStruct((steps, groups, heads, members, members), jnp.float32),
        ),
        in_specs=in_specs,
        out_specs=(
            pl.BlockSpec((sources, step, heads_width), lambda p: (0, p + chunk * steps, 0)),
            pl.BlockSpec((sources, step, 3 * heads_width), lambda p: (0, p, 0)),
            pl.BlockSpec((1, groups, heads, members, members), lambda p: (p, 0, 0, 0, 0)),
        ),
        scratch_shapes=loaded,
        input_output_aliases={} if mixed is None else {len(operands) - 1: 0},
        compiler_params=pltpu.CompilerParams(vmem_limit_bytes=GRANT),
        cost_estimate=cost(6),
        name="forward",
    )(*operands)


def backward(blk, saved, probs, grads, wq, wk, wv, chunk):
    sources, rows, _ = saved.shape
    heads_width = wq.shape[1]
    width = wq.shape[0] // 4
    heads = heads_width // HEAD_DIM
    step = step_of(sources, rows)
    steps, groups, members = (rows // step, step // GROUP, sources * GROUP)
    block = pl.BlockSpec((sources, step, width), lambda p: (0, p, 0))
    half = pl.BlockSpec((sources // 2, step, width), lambda p: (0, p, 0))
    weight = pl.BlockSpec(memory_space=pl.ANY)
    loaded = [pltpu.VMEM(wq.shape, wq.dtype)] * 3 + [pltpu.SemaphoreType.DMA((3,))]
    shape = jax.ShapeDtypeStruct((sources, rows, width), jnp.bfloat16)
    half_shape = jax.ShapeDtypeStruct((sources // 2, rows, width), jnp.bfloat16)
    outs = pl.pallas_call(
        backward_kernel,
        grid=(steps,),
        out_shape=(shape,) * 2 + (half_shape,) * 4,
        in_specs=[
            SMEM,
            pl.BlockSpec((sources, step, 3 * heads_width), lambda p: (0, p, 0)),
            pl.BlockSpec((1, groups, heads, members, members), lambda p: (p, 0, 0, 0, 0)),
            pl.BlockSpec((sources, step, heads_width), lambda p: (0, p + chunk * steps, 0)),
            weight,
            weight,
            weight,
        ],
        out_specs=(block,) * 2 + (half,) * 4,
        scratch_shapes=[pltpu.VMEM((sources, step, heads_width), jnp.bfloat16)] * 3 + loaded,
        compiler_params=pltpu.CompilerParams(vmem_limit_bytes=GRANT),
        cost_estimate=cost(6),
        name="backward",
    )(blk, saved, probs, grads, wq, wk, wv)
    return (outs[:2], outs[2:])


def slab(w, blk, j):
    width = w.shape[0] // 4
    return lax.dynamic_slice_in_dim(w, blk[j] * width, width, 0)


def by_cluster(x):
    sources, rows = x.shape[:2]
    x = x.reshape(sources, rows // MOST, MOST, -1).transpose(1, 0, 2, 3)
    return x.reshape(rows // MOST, sources * MOST, -1)


def by_source(x, sources):
    clusters = x.shape[0]
    x = x.reshape(clusters, sources, MOST, -1).transpose(1, 0, 2, 3)
    return x.reshape(sources, clusters * MOST, -1)


def split_heads(x):
    return x.reshape(x.shape[0], -1, HEAD_DIM)


ein = functools.partial(jnp.einsum, preferred_element_type=jnp.float32)


def forward_many(blk, parts, wq, wk, wv):
    sources, rows, _ = parts[0].shape

    def project(w):
        total = 0.0
        for j in range(4):
            total = total + ein("srd,dh->srh", parts[j], slab(w, blk, j))
        return by_cluster(total.astype(jnp.bfloat16))

    held = (parts[0][:, :, 0].astype(jnp.float32) <= LIMIT).reshape(sources, -1, MOST)
    counts = jnp.sum(held.astype(jnp.int32), axis=2, keepdims=True)
    rank = jnp.cumsum(counts, axis=0) - counts + jnp.arange(MOST)
    kept = by_cluster((held & (rank < CAP)).astype(jnp.float32).reshape(sources, rows, 1))
    scale = HEAD_DIM ** (-0.5)

    def one(args):
        q, k, v, live = args
        q, k, v = (split_heads(a) for a in (q, k, v))
        scores = jnp.where(live[None, None, :, 0] > 0, ein("qhd,khd->hqk", q, k) * scale, -1e30)
        raised = jnp.exp(scores - jnp.max(scores, axis=-1, keepdims=True))
        probs = raised * (live / jnp.sum(raised, axis=-1, keepdims=True))
        mixed = ein("hqk,khd->qhd", probs.astype(jnp.bfloat16), v).astype(jnp.bfloat16)
        return (mixed.reshape(mixed.shape[0], -1), probs)

    saved = tuple(project(w) for w in (wq, wk, wv))
    mixed, probs = lax.map(one, saved + (kept,))
    return (by_source(mixed, sources), saved, probs)


def backward_many(blk, saved, probs, grads, wq, wk, wv):
    sources = grads.shape[0]
    scale = HEAD_DIM ** (-0.5)

    def one(args):
        q, k, v, probs, g = args
        q, k, v, g = (split_heads(a) for a in (q, k, v, g))
        dv = ein("hqk,qhd->khd", probs.astype(jnp.bfloat16), g)
        grad_probs = ein("qhd,khd->hqk", g, v)
        inner = jnp.sum(grad_probs * probs, axis=-1, keepdims=True)
        grad_scores = (probs * (grad_probs - inner) * scale).astype(jnp.bfloat16)
        dq = ein("hqk,khd->qhd", grad_scores, k)
        dk = ein("hqk,qhd->khd", grad_scores, q)
        return tuple(a.astype(jnp.bfloat16).reshape(a.shape[0], -1) for a in (dq, dk, dv))

    dq, dk, dv = lax.map(one, saved + (probs, by_cluster(grads)))
    outs = []
    for j in range(4):
        total = 0.0
        for d, w in ((dq, wq), (dk, wk), (dv, wv)):
            total = total + ein("crh,wh->crw", d, slab(w, blk, j))
        outs.append(by_source(total.astype(jnp.bfloat16), sources))
    half = sources // 2
    return ((outs[0], outs[2]), (outs[1][:half], outs[1][half:], outs[3][:half], outs[3][half:]))


def pick(slot_col, slots):
    held = iota((1, slots.shape[0]), 1) == slot_col[...]
    return dot(jnp.where(held, 1.0, 0.0).astype(jnp.bfloat16), slots[...])


def out_kernel(blk, slot_col, w_out, mixed, *outs):
    keep, give = (outs[:2], outs[2:])
    heads = pick(slot_col, mixed).astype(jnp.bfloat16)
    tokens, width = keep[0].shape
    span = spans(blk, width)
    for j in (1, 3, 0, 2):
        total = dot(heads, w_out[:, span[j]]).astype(jnp.bfloat16)
        if j % 2 == 0:
            keep[j // 2][...] = total
        else:
            give[j - 1][...] = total[: tokens // 2]
            give[j][...] = total[tokens // 2 :]


def project_out(blk, slot_col, w_out, mixed):
    tokens, width = (slot_col.shape[0], w_out.shape[1] // 4)
    shape = jax.ShapeDtypeStruct((tokens, width), jnp.bfloat16)
    half = jax.ShapeDtypeStruct((tokens // 2, width), jnp.bfloat16)
    outs = pl.pallas_call(
        out_kernel,
        out_shape=(shape,) * 2 + (half,) * 4,
        in_specs=[SMEM] + [VMEM] * 3,
        out_specs=(VMEM,) * 6,
        compiler_params=pltpu.CompilerParams(vmem_limit_bytes=GRANT),
        cost_estimate=cost(6),
        name="project_out",
    )(blk, slot_col, w_out, mixed)
    return (outs[:2], outs[2:])


def final_kernel(slot_col, slots, out):
    out[...] = pick(slot_col, slots)


def to_tokens(slot_col, slots):
    return pl.pallas_call(
        final_kernel,
        out_shape=jax.ShapeDtypeStruct((slot_col.shape[0], slots.shape[1]), jnp.float32),
        compiler_params=pltpu.CompilerParams(vmem_limit_bytes=GRANT),
        cost_estimate=cost(1),
        name="to_tokens",
    )(slot_col, slots)


def wide(x):
    return x.astype(jnp.float32)


def add_kernel(*refs):
    whole, halves, more, out = (refs[0], refs[1:3], refs[3:-1], refs[-1])
    size = whole.shape[0] // 2
    for i, half in enumerate(halves):
        rows = slice(i * size, (i + 1) * size)
        total = wide(whole[rows]) + wide(half[...])
        if more:
            total = total + wide(more[0][rows])
        out[rows] = total.astype(jnp.bfloat16)


def add(whole, first, second, *more, into=None, chunk=0, chunks=1):
    shape = whole.shape
    block = pl.BlockSpec(shape, lambda p: (0,) * len(shape))
    half = pl.BlockSpec(first.shape, lambda p: (0,) * len(shape))
    place = (0, chunk, 0)[: len(shape)]
    full = (shape[0], shape[1] * chunks) + shape[2:] if chunks > 1 else shape
    operands = [whole, first, second, *more]
    in_specs = [block, half, half] + [block] * len(more)
    kernel, aliases = (add_kernel, {})
    if into is not None:
        aliases = {len(operands): 0}
        operands.append(into)
        in_specs.append(pl.BlockSpec(memory_space=pl.ANY))

        def kernel(*refs):
            add_kernel(*refs[:-2], refs[-1])

    return pl.pallas_call(
        kernel,
        grid=(1,),
        out_shape=jax.ShapeDtypeStruct(full, jnp.bfloat16),
        in_specs=in_specs,
        out_specs=pl.BlockSpec(shape, lambda p: place if chunks > 1 else (0,) * len(shape)),
        input_output_aliases=aliases,
        compiler_params=pltpu.CompilerParams(vmem_limit_bytes=GRANT),
        cost_estimate=cost(0.001),
        name="add",
    )(*operands)


def reduce_pairs(keep, give):
    got = [swap(x, 1) for x in give]
    return (keep[0], got[:2], add(keep[1], *got[2:]))


def body(normed, cluster, w_query, w_key, w_value, w_out, grad_out):
    seq_count = lax.axis_size("seq")
    per = CLUSTERS // seq_count * MOST
    chunks = CHUNKS if per // CHUNKS % GROUP == 0 else 1
    rows = per // chunks
    blk = lax.axis_index("tp") ^ jnp.arange(4, dtype=jnp.int32)
    weights = (w_query, w_key, w_value)
    small = seq_count * GROUP <= 256

    g_across = swap(grad_out, 2)
    g_parts = (grad_out, swap(grad_out, 1), g_across, swap(g_across, 1))
    slot_col, slot_row, x_slots = place(cluster, normed)
    x = exchange(x_slots.reshape(seq_count, per, -1))
    g_slots = head_grads(blk, g_parts, w_out, slot_row).reshape(seq_count, per, -1)
    x = after(x, g_slots)
    g = exchange(after(g_slots, x))

    x_core, x_across = (swap(x, 1), [])
    for c in range(chunks):
        piece = x[:, c * rows : (c + 1) * rows]
        x_across.append(swap(piece, 2))
    mixed, saved = (None, [])
    for c in range(chunks):
        if c > 0:
            x_across[c] = after(x_across[c], mixed)
        parts = (x, x_core, x_across[c], swap(x_across[c], 1))
        if c > 0:
            parts = (after(x, g),) + parts[1:]
        if small:
            mixed, *kept = forward(blk, parts, *weights, c, chunks, mixed)
        else:
            mixed, *kept = forward_many(blk, parts, *weights)
        saved.append(kept)
    mixed_back = exchange(after(mixed, g))

    g = after(g, mixed)
    for c in range(chunks):
        if small:
            keep, give = backward(blk, *saved[c], g, *weights, c)
        else:
            keep, give = backward_many(blk, *saved[c], g, *weights)
        keep, got, partial = reduce_pairs(keep, give)
        g = after(g, partial)
        if c > 0:
            partial = after(partial, saved[c - 1][3])
        saved[c] = (keep, *got, swap(partial, 2))
    summed = None
    for c in range(chunks):
        summed = add(*saved[c], into=summed, chunk=c, chunks=chunks)
    back = exchange(after(summed, mixed_back))
    keep, give = project_out(blk, slot_col, w_out, mixed_back.reshape(CLUSTERS * MOST, -1))
    keep, got, partial = reduce_pairs(keep, give)
    attended = add(keep, *got, swap(partial, 2))
    return (attended, to_tokens(slot_col, back.reshape(CLUSTERS * MOST, -1)))


def solution(mesh):
    in_specs = (
        P("seq", "tp"),
        P("seq", None),
        P(None, "tp"),
        P(None, "tp"),
        P(None, "tp"),
        P("tp", None),
        P("seq", "tp"),
    )
    out_specs = (P("seq", "tp"), P("seq", "tp"))
    return jax.shard_map(body, mesh=mesh, in_specs=in_specs, out_specs=out_specs, check_vma=False)
```

time: 215 us -> 170 us (0.79)
  local copies, waits for them, and re-layouts: 34 us -> 9.52 us
  waiting for transfers between devices: 76.2 us -> 57.6 us
  Pallas kernels: 51.3 us -> 68.8 us
  starting transfers between devices: 43.1 us -> 31.8 us
  other arithmetic: 7.84 us -> 0.57 us
    unnamed x67 -> x57, local copies, waits for them, and re-layouts: 34 us -> 9.44 us
    pallas_call x3 -> x9, Pallas kernels: 22.4 us -> 37.5 us  [the longest x2 19.4 us: backward(): pl.pallas_call(backward_kernel, grid=(steps,), out_shape=(shape,) * 2 + (...]
    all_to_all x6 -> x4, starting transfers between devices: 32.7 us -> 20.5 us  [exchange(): return lax.all_to_all(x, 'seq', split_axis=0, concat_axis=0, tiled=True)]
    all_to_all x6 -> x4, waiting for transfers between devices: 20 us -> 9.49 us  [exchange(): return lax.all_to_all(x, 'seq', split_axis=0, concat_axis=0, tiled=True)]
    ppermute x15 -> x23, waiting for transfers between devices: 56.2 us -> 48.1 us  [swap(): return lax.ppermute(x, 'tp', [(i, i ^ bit) for i in range(count)])]
    convert_element_type x6 -> x0, other arithmetic: 7.84 us -> none  [the longest x3 5.09 us: reduce_across(): (wide(keep[0]) + wide(got[0]) + wide(swap(partial, 2))).astype(jnp.bfloat16)]
    pallas_call x1, Pallas kernels: 1.14 us -> 3.32 us  [place(): pl.pallas_call(place_kernel, out_shape=(jax.ShapeDtypeStruct((tokens, 1),...]
    ppermute x15 -> x23, starting transfers between devices: 10.4 us -> 11.3 us  [swap(): return lax.ppermute(x, 'tp', [(i, i ^ bit) for i in range(count)])]
  transfers between devices with their start and end apart: 21 -> 27, of which waited for: 11 -> 19; matrix products, arithmetic and copies ran while one was open for 4% -> 0% of each run, Pallas kernels for 22% -> 31%
where the time goes in v3:
time: 170 us; the launch traced here: 169 us
  Pallas kernels  68.8 us (40%)
  waiting for transfers between devices  57.6 us (34%)
  starting transfers between devices  31.8 us (19%)
  local copies, waits for them, and re-layouts  9.52 us (6%)
    ppermute x23, waiting for transfers between devices, swap(): return lax.ppermute(x, 'tp', [(i, i ^ bit) for i in range(count)])  48.1 us
    all_to_all x4, starting transfers between devices, exchange(): return lax.all_to_all(x, 'seq', split_axis=0, concat_axis=0, tiled=True)  20.5 us
    pallas_call x2, Pallas kernels, forward(): pl.pallas_call(forward_kernel, grid=(steps,), out_shape=(jax.ShapeDtypeSt...  19.8 us
    pallas_call x2, Pallas kernels, backward(): pl.pallas_call(backward_kernel, grid=(steps,), out_shape=(shape,) * 2 + (...  19.4 us
    pallas_call x6, Pallas kernels, add(): pl.pallas_call(kernel, grid=(1,), out_shape=jax.ShapeDtypeStruct(full, jn...  13.4 us
    ppermute x23, starting transfers between devices, swap(): return lax.ppermute(x, 'tp', [(i, i ^ bit) for i in range(count)])  11.3 us
    all_to_all x4, waiting for transfers between devices, exchange(): return lax.all_to_all(x, 'seq', split_axis=0, concat_axis=0, tiled=True)  9.49 us
    unnamed x57, local copies, waits for them, and re-layouts  9.44 us
  transfers between devices with their start and end apart: 27, of which 19 were waited for; matrix products, arithmetic and copies ran while one was open for 0% of the time, Pallas kernels for 31%

profile of v3, /device:TPU:0, one launch (start us, length us, event | category | flops | bytes accessed | tf_op | source)
XLA Modules:
  0.0 169.1 jit_solution(5735947720140985768)
XLA Ops:
  0.6 1.5 copy.11.ids_col
  2.2 3.3 %place.1 = (s32[512,1]{1,0:T(8,128)}, s32[1,512]{1,0:T(1,128)}, bf16[1024,512]{1,0:T(8,128)(2,1)}) custom-call(s32[512,1]{1,0:T(8,128)} %copy.11.ids_col, bf16[512,512]{1,0:T(8,128)(2,1)} %x_ref.1), custom_call_target="tpu_custom_call" | custom-call | flops 1000000000 | bytes 1048576 | tf_op jit(solution)/shard_map/place/pallas_call | solution.py:72
  5.5 7.3 %all-to-all-start = ((bf16[8,128,512]{2,1,0:T(8,128)(2,1)}), bf16[8,128,512]{2,1,0:T(8,128)(2,1)S(1)}, u32[]{:S(2)}, u32[]{:S(2)}) async-start(bf16[8,128,512]{2,1,0:T(8,128)(2,1)} %bitcast.6), calls=%async_computation | async-start | bytes 2097152 | tf_op jit(solution)/shard_map/all_to_all | solution.py:45
  12.8 1.6 collective-permute-start.1
  14.3 11.9 %collective-permute-done.1.a2 = bf16[512,512]{1,0:T(8,128)(2,1)S(1)} collective-permute-done((bf16[512,512]{1,0:T(8,128)(2,1)S(1)}, bf16[512,512]{1,0:T(8,128)(2,1)S(1)}, u32[]{:S(2)}, u32[]{:S(2)}) %collective-permute-start.1) | collective-permute-done | bytes 524320 | tf_op jit(solution)/shard_map/ppermute | solution.py:41
  26.2 0.6 iota_xor_fusion.blk
  26.8 1.3 collective-permute-done.2.a3
  28.1 0.8 copy-done.9
  28.9 5.2 %head_grads.1 = bf16[1024,512]{1,0:T(8,128)(2,1)} custom-call(s32[4]{0:T(128)} %iota_xor_fusion.blk, bf16[512,512]{1,0:T(8,128)(2,1)} %a0.1, bf16[512,512]{1,0:T(8,128)(2,1)} %copy-done.8, bf16[512,512]{1,0:T(8,128)(2,1)} %copy-done.7, bf16[512,512]{1,0:T(8,128)(2,1)} %copy-done.9, bf16[512,2048]{1,0:T(8,128)(2,1)} %w_out.3, s32[1,512]{1,0:T(1,128)} %get-tuple-element.40.slot_row), custom_call_target="tpu_custom_call" | custom-call | flops 1000000000 | bytes 1048576 | tf_op jit(solution)/shard_map/head_grads/pallas_call | solution.py:98
  34.1 4.4 %all-to-all-done.x0 = bf16[8,128,512]{2,1,0:T(8,128)(2,1)S(1)} async-done(((bf16[8,128,512]{2,1,0:T(8,128)(2,1)}), bf16[8,128,512]{2,1,0:T(8,128)(2,1)S(1)}, u32[]{:S(2)}, u32[]{:S(2)}) %all-to-all-start) | async-done | bytes 1048608 | tf_op jit(solution)/shard_map/all_to_all | solution.py:45
  38.6 1.6 collective-permute-start.5
  40.2 3.6 %all-to-all-start.1 = ((bf16[8,128,512]{2,1,0:T(8,128)(2,1)}), bf16[8,128,512]{2,1,0:T(8,128)(2,1)S(1)}, u32[]{:S(2)}, u32[]{:S(2)}) async-start(bf16[8,128,512]{2,1,0:T(8,128)(2,1)} %bitcast.1), calls=%async_computation.1 | async-start | bytes 2097152 | tf_op jit(solution)/shard_map/all_to_all | solution.py:45
  43.8 7.2 %collective-permute-done.5.x2 = bf16[8,64,512]{2,1,0:T(8,128)(2,1)} collective-permute-done((bf16[8,64,512]{2,1,0:T(8,128)(2,1)S(1)}, bf16[8,64,512]{2,1,0:T(8,128)(2,1)}, u32[]{:S(2)}, u32[]{:S(2)}) %collective-permute-start.5) | collective-permute-done | bytes 524320 | tf_op jit(solution)/shard_map/ppermute | solution.py:41
  51.0 1.5 collective-permute-start.4
  52.5 0.6 collective-permute-done.6.x3
  53.1 0.8 copy-done.24
  53.9 9.9 %forward.2 = (bf16[8,128,512]{2,1,0:T(8,128)(2,1)}, bf16[8,64,1536]{2,1,0:T(8,128)(2,1)}, f32[2,2,4,128,128]{4,3,2,1,0:T(8,128)}) custom-call(s32[4]{0:T(128)} %iota_xor_fusion.blk, bf16[8,128,512]{2,1,0:T(8,128)(2,1)} %copy-done, bf16[8,128,512]{2,1,0:T(8,128)(2,1)} %collective-permute-done.3.x1, bf16[8,64,512]{2,1,0:T(8,128)(2,1)} %collective-permute-done.5.x2, ...), custom_call_target="tpu_custom_call" | custom-call | flops 6000000000 | bytes 1048576 | tf_op jit(solution)/shard_map/forward/pallas_call | solution.py:271
  63.9 1.5 collective-permute-done.4.x2
  65.4 5.1 %all-to-all-done.1.g_ref = bf16[8,128,512]{2,1,0:T(8,128)(2,1)S(1)} async-done(((bf16[8,128,512]{2,1,0:T(8,128)(2,1)}), bf16[8,128,512]{2,1,0:T(8,128)(2,1)S(1)}, u32[]{:S(2)}, u32[]{:S(2)}) %all-to-all-start.1) | async-done | bytes 1048608 | tf_op jit(solution)/shard_map/all_to_all | solution.py:45
  70.5 0.8 copy-done.25
  71.3 9.9 %forward.3 = (bf16[8,128,512]{2,1,0:T(8,128)(2,1)}, bf16[8,64,1536]{2,1,0:T(8,128)(2,1)}, f32[2,2,4,128,128]{4,3,2,1,0:T(8,128)}) custom-call(s32[4]{0:T(128)} %iota_xor_fusion.blk, bf16[8,128,512]{2,1,0:T(8,128)(2,1)} %copy-done, bf16[8,128,512]{2,1,0:T(8,128)(2,1)} %collective-permute-done.3.x1, ...), custom_call_target="tpu_custom_call", output_to_operand_aliasing={{0}: (8, {})} | custom-call | flops 6000000000 | bytes 1048576 | tf_op jit(solution)/shard_map/forward/pallas_call | solution.py:271
  81.2 3.7 %all-to-all-start.2 = ((bf16[8,128,512]{2,1,0:T(8,128)(2,1)}), bf16[8,128,512]{2,1,0:T(8,128)(2,1)S(1)}, u32[]{:S(2)}, u32[]{:S(2)}) async-start(bf16[8,128,512]{2,1,0:T(8,128)(2,1)} %get-tuple-element.47), calls=%async_computation.2 | async-start | bytes 2097152 | tf_op jit(solution)/shard_map/all_to_all | solution.py:45
  85.0 9.6 %backward.2 = (bf16[8,64,512]{2,1,0:T(8,128)(2,1)}, bf16[8,64,512]{2,1,0:T(8,128)(2,1)}, bf16[4,64,512]{2,1,0:T(8,128)(2,1)}, bf16[4,64,512]{2,1,0:T(8,128)(2,1)...) custom-call(s32[4]{0:T(128)} %iota_xor_fusion.blk, bf16[8,64,1536]{2,1,0:T(8,128)(2,1)} %get-tuple-element.57.saved, ...), custom_call_target="tpu_custom_call" | custom-call | flops 6000000000 | bytes 1048576 | tf_op jit(solution)/shard_map/backward/pallas_call | solution.py:306
  94.7 0.5 collective-permute-start.14
  95.2 1.2 collective-permute-done.13.refs_1_
  96.4 0.4 collective-permute-done.14.refs_2_
  96.8 0.3 copy-done.15
  97.1 0.4 copy-done.18
  97.5 2.1 %add.8 = bf16[8,64,512]{2,1,0:T(8,128)(2,1)} custom-call(bf16[8,64,512]{2,1,0:T(8,128)(2,1)} %get-tuple-element.59.refs_0_, bf16[4,64,512]{2,1,0:T(8,128)(2,1)} %copy-done.15, bf16[4,64,512]{2,1,0:T(8,128)(2,1)} %copy-done.18), custom_call_target="tpu_custom_call" | custom-call | flops 1000000 | bytes 1048576 | tf_op jit(solution)/shard_map/add/pallas_call | solution.py:488
  99.6 0.5 collective-permute-start.19
  100.1 9.7 %backward.3 = (bf16[8,64,512]{2,1,0:T(8,128)(2,1)}, bf16[8,64,512]{2,1,0:T(8,128)(2,1)}, bf16[4,64,512]{2,1,0:T(8,128)(2,1)}, bf16[4,64,512]{2,1,0:T(8,128)(2,1)...) custom-call(s32[4]{0:T(128)} %iota_xor_fusion.blk, bf16[8,64,1536]{2,1,0:T(8,128)(2,1)} %get-tuple-element.54.saved, ...), custom_call_target="tpu_custom_call" | custom-call | flops 6000000000 | bytes 1048576 | tf_op jit(solution)/shard_map/backward/pallas_call | solution.py:306
  110.0 0.5 collective-permute-start.18
  110.4 1.2 collective-permute-done.17.refs_1_
  111.7 0.4 collective-permute-done.18.refs_2_
  112.1 0.3 copy-done.16
  112.4 0.4 copy-done.19
  112.8 2.1 %add.9 = bf16[8,64,512]{2,1,0:T(8,128)(2,1)} custom-call(bf16[8,64,512]{2,1,0:T(8,128)(2,1)} %get-tuple-element.66.refs_0_, bf16[4,64,512]{2,1,0:T(8,128)(2,1)} %copy-done.16, bf16[4,64,512]{2,1,0:T(8,128)(2,1)} %copy-done.19), custom_call_target="tpu_custom_call" | custom-call | flops 1000000 | bytes 1048576 | tf_op jit(solution)/shard_map/add/pallas_call | solution.py:488
  114.9 1.5 collective-permute-start.20
  116.5 0.5 collective-permute-start.22
  117.0 0.4 collective-permute-start.16
  117.5 0.5 collective-permute-done.21.refs_1_
  118.0 0.4 collective-permute-done.22.refs_2_
  118.7 0.4 copy-done.14
  119.1 2.4 %add.10.refs_4_ = bf16[8,128,512]{2,1,0:T(8,128)(2,1)} custom-call(bf16[8,64,512]{2,1,0:T(8,128)(2,1)} %get-tuple-element.70.refs_0_, bf16[4,64,512]{2,1,0:T(8,128)(2,1)} %copy-done.13, bf16[4,64,512]{2,1,0:T(8,128)(2,1)} %copy-done.14, bf16[8,64,512]{2,1,0:T(8,128)(2,1)} %copy-done.5), custom_call_target="tpu_custom_call" | custom-call | flops 1000000 | bytes 1048576 | tf_op jit(solution)/shard_map/add/pallas_call | solution.py:488
  121.4 7.6 %collective-permute-done.20.refs_3_ = bf16[8,64,512]{2,1,0:T(8,128)(2,1)S(1)} collective-permute-done((bf16[8,64,512]{2,1,0:T(8,128)(2,1)}, bf16[8,64,512]{2,1,0:T(8,128)(2,1)S(1)}, u32[]{:S(2)}, u32[]{:S(2)}) %collective-permute-start.20) | collective-permute-done | bytes 524320 | tf_op jit(solution)/shard_map/ppermute | solution.py:41
  129.1 0.8 copy-done.6
  129.9 2.3 %add.11 = bf16[8,128,512]{2,1,0:T(8,128)(2,1)} custom-call(bf16[8,64,512]{2,1,0:T(8,128)(2,1)} %get-tuple-element.63.refs_0_, bf16[4,64,512]{2,1,0:T(8,128)(2,1)} %copy-done.11, bf16[4,64,512]{2,1,0:T(8,128)(2,1)} %copy-done.12, bf16[8,64,512]{2,1,0:T(8,128)(2,1)} %copy-done.6, bf16[8,128,512]{2,1,0:T(8,128)(2,1)} %add.10.refs_4_), custom_call_target="tpu_custom_call", output_to_operand_aliasing={{}: (4, {})} | custom-call | flops 1000000 | bytes 1048576 | tf_op jit(solution)/shard_map/add/pallas_call | solution.py:488
  132.2 5.9 %all-to-all-start.3 = ((bf16[8,128,512]{2,1,0:T(8,128)(2,1)}), bf16[8,128,512]{2,1,0:T(8,128)(2,1)S(1)}, u32[]{:S(2)}, u32[]{:S(2)}) async-start(bf16[8,128,512]{2,1,0:T(8,128)(2,1)} %add.11), calls=%async_computation.3 | async-start | bytes 2097152 | tf_op jit(solution)/shard_map/all_to_all | solution.py:45
  138.1 4.7 %project_out.1 = (bf16[512,512]{1,0:T(8,128)(2,1)}, bf16[512,512]{1,0:T(8,128)(2,1)}, bf16[256,512]{1,0:T(8,128)(2,1)}, bf16[256,512]{1,0:T(8,128)(2,1)}, bf16[2...) custom-call(s32[4]{0:T(128)} %iota_xor_fusion.blk, s32[512,1]{1,0:T(8,128)} %get-tuple-element.38.slot_col, ...), custom_call_target="tpu_custom_call" | custom-call | flops 6000000000 | bytes 1048576 | tf_op jit(solution)/shard_map/project_out/pallas_call | solution.py:430
  142.8 0.5 collective-permute-start.11
  143.3 1.2 collective-permute-done.10.refs_1_
  144.5 0.4 collective-permute-done.11.refs_2_
  144.9 0.3 copy-done.17
  145.2 0.4 copy-done.20
  145.6 2.1 %add.6 = bf16[512,512]{1,0:T(8,128)(2,1)} custom-call(bf16[512,512]{1,0:T(8,128)(2,1)} %get-tuple-element.51.refs_0_, bf16[256,512]{1,0:T(8,128)(2,1)} %copy-done.17, bf16[256,512]{1,0:T(8,128)(2,1)} %copy-done.20), custom_call_target="tpu_custom_call" | custom-call | flops 1000000 | bytes 1048576 | tf_op jit(solution)/shard_map/add/pallas_call | solution.py:488
  147.7 1.5 collective-permute-start.12
  149.2 0.5 collective-permute-start.9
  149.7 1.2 collective-permute-done.8.refs_1_
  151.0 0.4 collective-permute-done.9.refs_2_
  151.3 10.6 %collective-permute-done.12.refs_3_ = bf16[512,512]{1,0:T(8,128)(2,1)S(1)} collective-permute-done((bf16[512,512]{1,0:T(8,128)(2,1)}, bf16[512,512]{1,0:T(8,128)(2,1)S(1)}, u32[]{:S(2)}, u32[]{:S(2)}) %collective-permute-start.12) | collective-permute-done | bytes 524320 | tf_op jit(solution)/shard_map/ppermute | solution.py:41
  161.9 0.8 copy-done.10
  162.7 2.3 %add.7 = bf16[512,512]{1,0:T(8,128)(2,1)} custom-call(bf16[512,512]{1,0:T(8,128)(2,1)} %get-tuple-element.48.refs_0_, bf16[256,512]{1,0:T(8,128)(2,1)} %copy-done.21, bf16[256,512]{1,0:T(8,128)(2,1)} %copy-done.22, bf16[512,512]{1,0:T(8,128)(2,1)} %copy-done.10), custom_call_target="tpu_custom_call" | custom-call | flops 1000000 | bytes 1048576 | tf_op jit(solution)/shard_map/add/pallas_call | solution.py:488
  165.0 1.0 copy-done.3
  166.1 3.0 %to_tokens.1 = f32[512,512]{1,0:T(8,128)} custom-call(s32[512,1]{1,0:T(8,128)} %get-tuple-element.38.slot_col, bf16[1024,512]{1,0:T(8,128)(2,1)} %bitcast.5), custom_call_target="tpu_custom_call" | custom-call | flops 1000000000 | bytes 1048576 | tf_op jit(solution)/shard_map/to_tokens/pallas_call | solution.py:447
  (63 shorter events, 0.7 us)
Async XLA Ops:
  2.2 10.6 %copy-start.4 = (bf16[512,512]{1,0:T(8,128)(2,1)S(1)}, bf16[512,512]{1,0:T(8,128)(2,1)}, u32[]{:S(2)}) copy-start(bf16[512,512]{1,0:T(8,128)(2,1)} %a0.1) | copy-start | bytes 1572868
  5.5 33.0 %all-to-all-start = ((bf16[8,128,512]{2,1,0:T(8,128)(2,1)}), bf16[8,128,512]{2,1,0:T(8,128)(2,1)S(1)}, u32[]{:S(2)}, u32[]{:S(2)}) async-start(bf16[8,128,512]{2,1,0:T(8,128)(2,1)} %bitcast.6), calls=%async_computation | async-start | bytes 2097152 | tf_op jit(solution)/shard_map/all_to_all | solution.py:45
  12.8 13.4 %collective-permute-start.1 = (bf16[512,512]{1,0:T(8,128)(2,1)S(1)}, bf16[512,512]{1,0:T(8,128)(2,1)S(1)}, u32[]{:S(2)}, u32[]{:S(2)}) collective-permute-start(bf16[512,512]{1,0:T(8,128)(2,1)S(1)} %copy-done.4), channel_id=1, source_target_pairs={{0,2},{1,3},{2,0},{3,1},{4,6},{5,7},{6,4},{7,5},{8,10},{9,11},{10,... | collective-permute-start | bytes 1572872 | tf_op jit(solution)/shard_map/ppermute | solution.py:41
  14.3 12.5 %collective-permute-start = (bf16[512,512]{1,0:T(8,128)(2,1)S(1)}, bf16[512,512]{1,0:T(8,128)(2,1)S(1)}, u32[]{:S(2)}, u32[]{:S(2)}) collective-permute-start(bf16[512,512]{1,0:T(8,128)(2,1)S(1)} %copy-done.4), channel_id=1, source_target_pairs={{0,1},{1,0},{2,3},{3,2},{4,5},{5,4},{6,7},{7,6},{8,9},{9,8},{10,11... | collective-permute-start | bytes 1572872 | tf_op jit(solution)/shard_map/ppermute | solution.py:41
  26.2 1.9 %copy-start.7 = (bf16[512,512]{1,0:T(8,128)(2,1)}, bf16[512,512]{1,0:T(8,128)(2,1)S(1)}, u32[]{:S(2)}) copy-start(bf16[512,512]{1,0:T(8,128)(2,1)S(1)} %collective-permute-done.1.a2) | copy-start | bytes 1572868
  26.2 1.9 %collective-permute-start.2 = (bf16[512,512]{1,0:T(8,128)(2,1)S(1)}, bf16[512,512]{1,0:T(8,128)(2,1)S(1)}, u32[]{:S(2)}, u32[]{:S(2)}) collective-permute-start(bf16[512,512]{1,0:T(8,128)(2,1)S(1)} %collective-permute-done.1.a2), channel_id=1, source_target_pairs={{0,1},{1,0},{2,3},{3,2},{4,5},{5,4},{6,7},{7,6},{8,9},{9,8},{10,11... | collective-permute-start | bytes 1572872 | tf_op jit(solution)/shard_map/ppermute | solution.py:41
  26.8 1.3 copy-start.8
  28.1 0.8 copy-start.9
  38.5 1.7 copy-start
  38.6 12.4 %collective-permute-start.5 = (bf16[8,64,512]{2,1,0:T(8,128)(2,1)S(1)}, bf16[8,64,512]{2,1,0:T(8,128)(2,1)}, u32[]{:S(2)}, u32[]{:S(2)}) collective-permute-start(bf16[8,64,512]{2,1,0:T(8,128)(2,1)S(1)} %get-tuple-element.74), channel_id=1, source_target_pairs={{0,2},{1,3},{2,0},{3,1},{4,6},{5,7},{6,4},{7,5},{8,10},{9,11},{10,... | collective-permute-start | bytes 1572872 | tf_op jit(solution)/shard_map/ppermute | solution.py:41
  40.2 13.0 %collective-permute-start.3 = (bf16[8,128,512]{2,1,0:T(8,128)(2,1)S(1)}, bf16[8,128,512]{2,1,0:T(8,128)(2,1)}, u32[]{:S(2)}, u32[]{:S(2)}) collective-permute-start(bf16[8,128,512]{2,1,0:T(8,128)(2,1)S(1)} %all-to-all-done.x0), channel_id=1, source_target_pairs={{0,1},{1,0},{2,3},{3,2},{4,5},{5,4},{6,7},{7,6},{8,9},{9,8},{10,11... | collective-permute-start | bytes 3145736 | tf_op jit(solution)/shard_map/ppermute | solution.py:41
  40.2 30.2 %all-to-all-start.1 = ((bf16[8,128,512]{2,1,0:T(8,128)(2,1)}), bf16[8,128,512]{2,1,0:T(8,128)(2,1)S(1)}, u32[]{:S(2)}, u32[]{:S(2)}) async-start(bf16[8,128,512]{2,1,0:T(8,128)(2,1)} %bitcast.1), calls=%async_computation.1 | async-start | bytes 2097152 | tf_op jit(solution)/shard_map/all_to_all | solution.py:45
  51.0 2.1 %collective-permute-start.6 = (bf16[8,64,512]{2,1,0:T(8,128)(2,1)}, bf16[8,64,512]{2,1,0:T(8,128)(2,1)S(1)}, u32[]{:S(2)}, u32[]{:S(2)}) collective-permute-start(bf16[8,64,512]{2,1,0:T(8,128)(2,1)} %collective-permute-done.5.x2), channel_id=1, source_target_pairs={{0,1},{1,0},{2,3},{3,2},{4,5},{5,4},{6,7},{7,6},{8,9},{9,8},{10,11... | collective-permute-start | bytes 1572872 | tf_op jit(solution)/shard_map/ppermute | solution.py:41
  51.0 14.3 %collective-permute-start.4 = (bf16[8,64,512]{2,1,0:T(8,128)(2,1)S(1)}, bf16[8,64,512]{2,1,0:T(8,128)(2,1)S(1)}, u32[]{:S(2)}, u32[]{:S(2)}) collective-permute-start(bf16[8,64,512]{2,1,0:T(8,128)(2,1)S(1)} %get-tuple-element.75), channel_id=1, source_target_pairs={{0,2},{1,3},{2,0},{3,1},{4,6},{5,7},{6,4},{7,5},{8,10},{9,11},{10,... | collective-permute-start | bytes 1572872 | tf_op jit(solution)/shard_map/ppermute | solution.py:41
  53.1 0.8 copy-start.24
  65.4 5.1 %copy-start.23 = (bf16[8,64,512]{2,1,0:T(8,128)(2,1)}, bf16[8,64,512]{2,1,0:T(8,128)(2,1)S(1)}, u32[]{:S(2)}) copy-start(bf16[8,64,512]{2,1,0:T(8,128)(2,1)S(1)} %collective-permute-done.4.x2) | copy-start | bytes 1572868
  65.4 5.1 %collective-permute-start.7 = (bf16[8,64,512]{2,1,0:T(8,128)(2,1)S(1)}, bf16[8,64,512]{2,1,0:T(8,128)(2,1)S(1)}, u32[]{:S(2)}, u32[]{:S(2)}) collective-permute-start(bf16[8,64,512]{2,1,0:T(8,128)(2,1)S(1)} %collective-permute-done.4.x2), channel_id=1, source_target_pairs={{0,1},{1,0},{2,3},{3,2},{4,5},{5,4},{6,7},{7,6},{8,9},{9,8},{10,11... | collective-permute-start | bytes 1572872 | tf_op jit(solution)/shard_map/ppermute | solution.py:41
  70.4 10.8 %copy-start.2 = (bf16[8,128,512]{2,1,0:T(8,128)(2,1)}, bf16[8,128,512]{2,1,0:T(8,128)(2,1)S(1)}, u32[]{:S(2)}) copy-start(bf16[8,128,512]{2,1,0:T(8,128)(2,1)S(1)} %all-to-all-done.1.g_ref) | copy-start | bytes 3145732
  70.4 0.8 copy-start.25
  81.2 51.0 %all-to-all-start.2 = ((bf16[8,128,512]{2,1,0:T(8,128)(2,1)}), bf16[8,128,512]{2,1,0:T(8,128)(2,1)S(1)}, u32[]{:S(2)}, u32[]{:S(2)}) async-start(bf16[8,128,512]{2,1,0:T(8,128)(2,1)} %get-tuple-element.47), calls=%async_computation.2 | async-start | bytes 2097152 | tf_op jit(solution)/shard_map/all_to_all | solution.py:45
  94.6 1.8 %collective-permute-start.13 = (bf16[4,64,512]{2,1,0:T(8,128)(2,1)}, bf16[4,64,512]{2,1,0:T(8,128)(2,1)S(1)}, u32[]{:S(2)}, u32[]{:S(2)}) collective-permute-start(bf16[4,64,512]{2,1,0:T(8,128)(2,1)} %get-tuple-element.60), channel_id=1, source_target_pairs={{0,1},{1,0},{2,3},{3,2},{4,5},{5,4},{6,7},{7,6},{8,9},{9,8},{10,11... | collective-permute-start | bytes 786440 | tf_op jit(solution)/shard_map/ppermute | solution.py:41
  94.7 2.1 %collective-permute-start.14 = (bf16[4,64,512]{2,1,0:T(8,128)(2,1)}, bf16[4,64,512]{2,1,0:T(8,128)(2,1)S(1)}, u32[]{:S(2)}, u32[]{:S(2)}) collective-permute-start(bf16[4,64,512]{2,1,0:T(8,128)(2,1)} %get-tuple-element.61), channel_id=1, source_target_pairs={{0,1},{1,0},{2,3},{3,2},{4,5},{5,4},{6,7},{7,6},{8,9},{9,8},{10,11... | collective-permute-start | bytes 786440 | tf_op jit(solution)/shard_map/ppermute | solution.py:41
  96.4 0.7 copy-start.15
  96.8 0.7 copy-start.18
  99.6 15.3 %collective-permute-start.19 = (bf16[8,64,512]{2,1,0:T(8,128)(2,1)}, bf16[8,64,512]{2,1,0:T(8,128)(2,1)S(1)}, u32[]{:S(2)}, u32[]{:S(2)}) collective-permute-start(bf16[8,64,512]{2,1,0:T(8,128)(2,1)} %add.8), channel_id=1, source_target_pairs={{0,2},{1,3},{2,0},{3,1},{4,6},{5,7},{6,4},{7,5},{8,10},{9,11},{10,... | collective-permute-start | bytes 1572872 | tf_op jit(solution)/shard_map/ppermute | solution.py:41
  100.1 16.3 %copy-start.27 = (bf16[4,64,512]{2,1,0:T(8,128)(2,1)S(1)}, bf16[4,64,512]{2,1,0:T(8,128)(2,1)}, u32[]{:S(2)}) copy-start(bf16[4,64,512]{2,1,0:T(8,128)(2,1)} %get-tuple-element.71) | copy-start | bytes 786436
  100.1 16.3 %copy-start.26 = (bf16[4,64,512]{2,1,0:T(8,128)(2,1)S(1)}, bf16[4,64,512]{2,1,0:T(8,128)(2,1)}, u32[]{:S(2)}) copy-start(bf16[4,64,512]{2,1,0:T(8,128)(2,1)} %get-tuple-element.72) | copy-start | bytes 786436
  109.9 1.8 %collective-permute-start.17 = (bf16[4,64,512]{2,1,0:T(8,128)(2,1)}, bf16[4,64,512]{2,1,0:T(8,128)(2,1)S(1)}, u32[]{:S(2)}, u32[]{:S(2)}) collective-permute-start(bf16[4,64,512]{2,1,0:T(8,128)(2,1)} %get-tuple-element.67), channel_id=1, source_target_pairs={{0,1},{1,0},{2,3},{3,2},{4,5},{5,4},{6,7},{7,6},{8,9},{9,8},{10,11... | collective-permute-start | bytes 786440 | tf_op jit(solution)/shard_map/ppermute | solution.py:41
  110.0 2.1 %collective-permute-start.18 = (bf16[4,64,512]{2,1,0:T(8,128)(2,1)}, bf16[4,64,512]{2,1,0:T(8,128)(2,1)S(1)}, u32[]{:S(2)}, u32[]{:S(2)}) collective-permute-start(bf16[4,64,512]{2,1,0:T(8,128)(2,1)} %get-tuple-element.68), channel_id=1, source_target_pairs={{0,1},{1,0},{2,3},{3,2},{4,5},{5,4},{6,7},{7,6},{8,9},{9,8},{10,11... | collective-permute-start | bytes 786440 | tf_op jit(solution)/shard_map/ppermute | solution.py:41
  111.7 0.7 copy-start.16
  112.1 0.7 copy-start.19
  114.9 3.5 %copy-start.5 = (bf16[8,64,512]{2,1,0:T(8,128)(2,1)}, bf16[8,64,512]{2,1,0:T(8,128)(2,1)S(1)}, u32[]{:S(2)}) copy-start(bf16[8,64,512]{2,1,0:T(8,128)(2,1)S(1)} %collective-permute-done.19.refs_3_) | copy-start | bytes 1572868
  114.9 14.2 %collective-permute-start.20 = (bf16[8,64,512]{2,1,0:T(8,128)(2,1)}, bf16[8,64,512]{2,1,0:T(8,128)(2,1)S(1)}, u32[]{:S(2)}, u32[]{:S(2)}) collective-permute-start(bf16[8,64,512]{2,1,0:T(8,128)(2,1)} %add.9), channel_id=1, source_target_pairs={{0,2},{1,3},{2,0},{3,1},{4,6},{5,7},{6,4},{7,5},{8,10},{9,11},{10,... | collective-permute-start | bytes 1572872 | tf_op jit(solution)/shard_map/ppermute | solution.py:41
  116.4 1.5 collective-permute-start.21
  116.5 1.9 %collective-permute-start.22 = (bf16[4,64,512]{2,1,0:T(8,128)(2,1)S(1)}, bf16[4,64,512]{2,1,0:T(8,128)(2,1)S(1)}, u32[]{:S(2)}, u32[]{:S(2)}) collective-permute-start(bf16[4,64,512]{2,1,0:T(8,128)(2,1)S(1)} %copy-done.26), channel_id=1, source_target_pairs={{0,1},{1,0},{2,3},{3,2},{4,5},{5,4},{6,7},{7,6},{8,9},{9,8},{10,11... | collective-permute-start | bytes 786440 | tf_op jit(solution)/shard_map/ppermute | solution.py:41
  117.0 4.5 %collective-permute-start.15 = (bf16[4,64,512]{2,1,0:T(8,128)(2,1)}, bf16[4,64,512]{2,1,0:T(8,128)(2,1)S(1)}, u32[]{:S(2)}, u32[]{:S(2)}) collective-permute-start(bf16[4,64,512]{2,1,0:T(8,128)(2,1)} %get-tuple-element.64), channel_id=1, source_target_pairs={{0,1},{1,0},{2,3},{3,2},{4,5},{5,4},{6,7},{7,6},{8,9},{9,8},{10,11... | collective-permute-start | bytes 786440 | tf_op jit(solution)/shard_map/ppermute | solution.py:41
  117.0 4.4 %collective-permute-start.16 = (bf16[4,64,512]{2,1,0:T(8,128)(2,1)}, bf16[4,64,512]{2,1,0:T(8,128)(2,1)S(1)}, u32[]{:S(2)}, u32[]{:S(2)}) collective-permute-start(bf16[4,64,512]{2,1,0:T(8,128)(2,1)} %get-tuple-element.65), channel_id=1, source_target_pairs={{0,1},{1,0},{2,3},{3,2},{4,5},{5,4},{6,7},{7,6},{8,9},{9,8},{10,11... | collective-permute-start | bytes 786440 | tf_op jit(solution)/shard_map/ppermute | solution.py:41
  118.0 0.7 copy-start.13
  118.4 0.7 copy-start.14
  121.4 7.7 %copy-start.11 = (bf16[4,64,512]{2,1,0:T(8,128)(2,1)}, bf16[4,64,512]{2,1,0:T(8,128)(2,1)S(1)}, u32[]{:S(2)}) copy-start(bf16[4,64,512]{2,1,0:T(8,128)(2,1)S(1)} %collective-permute-done.15.refs_1_) | copy-start | bytes 786436
  121.4 7.7 %copy-start.12 = (bf16[4,64,512]{2,1,0:T(8,128)(2,1)}, bf16[4,64,512]{2,1,0:T(8,128)(2,1)S(1)}, u32[]{:S(2)}) copy-start(bf16[4,64,512]{2,1,0:T(8,128)(2,1)S(1)} %collective-permute-done.16.refs_2_) | copy-start | bytes 786436
  129.1 0.8 copy-start.6
  132.2 5.9 %copy-start.1 = (bf16[8,128,512]{2,1,0:T(8,128)(2,1)}, bf16[8,128,512]{2,1,0:T(8,128)(2,1)S(1)}, u32[]{:S(2)}) copy-start(bf16[8,128,512]{2,1,0:T(8,128)(2,1)S(1)} %all-to-all-done.2) | copy-start | bytes 3145732
  132.2 32.8 %all-to-all-start.3 = ((bf16[8,128,512]{2,1,0:T(8,128)(2,1)}), bf16[8,128,512]{2,1,0:T(8,128)(2,1)S(1)}, u32[]{:S(2)}, u32[]{:S(2)}) async-start(bf16[8,128,512]{2,1,0:T(8,128)(2,1)} %add.11), calls=%async_computation.3 | async-start | bytes 2097152 | tf_op jit(solution)/shard_map/all_to_all | solution.py:45
  142.8 1.7 %collective-permute-start.10 = (bf16[256,512]{1,0:T(8,128)(2,1)}, bf16[256,512]{1,0:T(8,128)(2,1)S(1)}, u32[]{:S(2)}, u32[]{:S(2)}) collective-permute-start(bf16[256,512]{1,0:T(8,128)(2,1)} %get-tuple-element.52), channel_id=1, source_target_pairs={{0,1},{1,0},{2,3},{3,2},{4,5},{5,4},{6,7},{7,6},{8,9},{9,8},{10,11... | collective-permute-start | bytes 786440 | tf_op jit(solution)/shard_map/ppermute | solution.py:41
  142.8 2.1 %collective-permute-start.11 = (bf16[256,512]{1,0:T(8,128)(2,1)}, bf16[256,512]{1,0:T(8,128)(2,1)S(1)}, u32[]{:S(2)}, u32[]{:S(2)}) collective-permute-start(bf16[256,512]{1,0:T(8,128)(2,1)} %get-tuple-element.53), channel_id=1, source_target_pairs={{0,1},{1,0},{2,3},{3,2},{4,5},{5,4},{6,7},{7,6},{8,9},{9,8},{10,11... | collective-permute-start | bytes 786440 | tf_op jit(solution)/shard_map/ppermute | solution.py:41
  144.5 0.7 copy-start.17
  144.9 0.7 copy-start.20
  147.7 14.2 %collective-permute-start.12 = (bf16[512,512]{1,0:T(8,128)(2,1)}, bf16[512,512]{1,0:T(8,128)(2,1)S(1)}, u32[]{:S(2)}, u32[]{:S(2)}) collective-permute-start(bf16[512,512]{1,0:T(8,128)(2,1)} %add.6), channel_id=1, source_target_pairs={{0,2},{1,3},{2,0},{3,1},{4,6},{5,7},{6,4},{7,5},{8,10},{9,11},{10,... | collective-permute-start | bytes 1572872 | tf_op jit(solution)/shard_map/ppermute | solution.py:41
  149.2 1.7 %collective-permute-start.8 = (bf16[256,512]{1,0:T(8,128)(2,1)}, bf16[256,512]{1,0:T(8,128)(2,1)S(1)}, u32[]{:S(2)}, u32[]{:S(2)}) collective-permute-start(bf16[256,512]{1,0:T(8,128)(2,1)} %get-tuple-element.49), channel_id=1, source_target_pairs={{0,1},{1,0},{2,3},{3,2},{4,5},{5,4},{6,7},{7,6},{8,9},{9,8},{10,11... | collective-permute-start | bytes 786440 | tf_op jit(solution)/shard_map/ppermute | solution.py:41
  149.2 2.1 %collective-permute-start.9 = (bf16[256,512]{1,0:T(8,128)(2,1)}, bf16[256,512]{1,0:T(8,128)(2,1)S(1)}, u32[]{:S(2)}, u32[]{:S(2)}) collective-permute-start(bf16[256,512]{1,0:T(8,128)(2,1)} %get-tuple-element.50), channel_id=1, source_target_pairs={{0,1},{1,0},{2,3},{3,2},{4,5},{5,4},{6,7},{7,6},{8,9},{9,8},{10,11... | collective-permute-start | bytes 786440 | tf_op jit(solution)/shard_map/ppermute | solution.py:41
  151.0 10.9 %copy-start.21 = (bf16[256,512]{1,0:T(8,128)(2,1)}, bf16[256,512]{1,0:T(8,128)(2,1)S(1)}, u32[]{:S(2)}) copy-start(bf16[256,512]{1,0:T(8,128)(2,1)S(1)} %collective-permute-done.8.refs_1_) | copy-start | bytes 786436
  151.3 10.6 %copy-start.22 = (bf16[256,512]{1,0:T(8,128)(2,1)}, bf16[256,512]{1,0:T(8,128)(2,1)S(1)}, u32[]{:S(2)}) copy-start(bf16[256,512]{1,0:T(8,128)(2,1)S(1)} %collective-permute-done.9.refs_2_) | copy-start | bytes 786436
  161.9 0.8 copy-start.10
  165.0 1.0 copy-start.3

commit v4 on v3

--- a/solution.py
+++ b/solution.py
@@ -17,7 +17,7 @@
 TN = (((0,), (0,)), ((), ()))
 MB = 1024 * 1024
 CHUNKS = 2
-GRANT = 60 * MB
+GRANT = 24 * MB
 
 
 def cost(giga):
@@ -127,14 +127,12 @@
 
 
 def forward_kernel(blk, x0, x1, x2, x3, wq, wk, wv, *refs):
-    mixed, saved, probs_ref, *loaded, sems = refs[-7:]
+    mixed, saved, probs_ref = refs[-3:]
     sources, rows, width = x0.shape
     heads_width = wq.shape[1]
     heads = heads_width // HEAD_DIM
     scale = HEAD_DIM ** (-0.5)
     span = spans(blk, width)
-    first = pl.program_id(0) == 0
-    load_all(first, (wq, wk, wv), loaded, sems)
     members = sources * GROUP
     shape = (sources, GROUP, members)
     here = (iota(shape, 1) // MOST).reshape(members, members)
@@ -160,8 +158,7 @@
         usable.append(same & (jnp.where(place_row < CAP, held_row, 0.0) > 0))
 
     xs = [r[...].reshape(sources * rows, width) for r in (x0, x1, x2, x3)]
-    for i, (w, source) in enumerate(zip(loaded, (wq, wk, wv))):
-        wait_for(first, source, w, sems.at[i])
+    for i, w in enumerate((wq, wk, wv)):
         total = dot(xs[0], w[span[0], :])
         for j in range(1, 4):
             total = total + dot(xs[j], w[span[j], :])
@@ -191,15 +188,13 @@
 
 
 def backward_kernel(blk, saved, probs_ref, g_ref, wq, wk, wv, *refs):
-    keep, give, (dq, dk, dv, *loaded, sems) = (refs[:2], refs[2:6], refs[6:])
+    keep, give, (dq, dk, dv) = (refs[:2], refs[2:6], refs[6:])
     sources, rows, _ = saved.shape
     width = keep[0].shape[2]
     heads_width = wq.shape[1]
     heads = heads_width // HEAD_DIM
     scale = HEAD_DIM ** (-0.5)
     span = spans(blk, width)
-    first = pl.program_id(0) == 0
-    load_all(first, (wq, wk, wv), loaded, sems)
     members = sources * GROUP
     groups = [slice(n * GROUP, (n + 1) * GROUP) for n in range(rows // GROUP)]
     every = [(n, h) for n in range(len(groups)) for h in range(heads)]
@@ -230,12 +225,10 @@
         put(dq, n, h, dot(gs, part(1, n, h)))
     for (n, h), gs in zip(every, grad_scores):
         put(dk, n, h, dot(gs, part(0, n, h), TN))
-    for i, (w, source) in enumerate(zip(loaded, (wq, wk, wv))):
-        wait_for(first, source, w, sems.at[i])
     grads = [d[...].reshape(sources * rows, heads_width) for d in (dq, dk, dv)]
     for j in (1, 3, 0, 2):
         total = None
-        for d, w in zip(grads, loaded):
+        for d, w in zip(grads, (wq, wk, wv)):
             term = dot(d, w[span[j], :], NT)
             total = term if total is None else total + term
         total = total.astype(jnp.bfloat16).reshape(sources, rows, width)
@@ -261,8 +254,7 @@
     steps, groups, members = (rows // step, step // GROUP, sources * GROUP)
     block = pl.BlockSpec((sources, step, width), lambda p: (0, p, 0))
     whole = pl.BlockSpec((sources, step, width), lambda p: (0, p + chunk * steps, 0))
-    weight = pl.BlockSpec(memory_space=pl.ANY)
-    loaded = [pltpu.VMEM(wq.shape, wq.dtype)] * 3 + [pltpu.SemaphoreType.DMA((3,))]
+    weight = VMEM
     in_specs = [SMEM] + [whole] * 2 + [block] * 2 + [weight] * 3
     operands = [blk, *parts, wq, wk, wv]
     if mixed is not None:
@@ -282,10 +274,9 @@
             pl.BlockSpec((sources, step, 3 * heads_width), lambda p: (0, p, 0)),
             pl.BlockSpec((1, groups, heads, members, members), lambda p: (p, 0, 0, 0, 0)),
         ),
-        scratch_shapes=loaded,
         input_output_aliases={} if mixed is None else {len(operands) - 1: 0},
         compiler_params=pltpu.CompilerParams(vmem_limit_bytes=GRANT),
-        cost_estimate=cost(6),
+        cost_estimate=cost(1),
         name="forward",
     )(*operands)
 
@@ -299,8 +290,7 @@
     steps, groups, members = (rows // step, step // GROUP, sources * GROUP)
     block = pl.BlockSpec((sources, step, width), lambda p: (0, p, 0))
     half = pl.BlockSpec((sources // 2, step, width), lambda p: (0, p, 0))
-    weight = pl.BlockSpec(memory_space=pl.ANY)
-    loaded = [pltpu.VMEM(wq.shape, wq.dtype)] * 3 + [pltpu.SemaphoreType.DMA((3,))]
+    weight = VMEM
     shape = jax.ShapeDtypeStruct((sources, rows, width), jnp.bfloat16)
     half_shape = jax.ShapeDtypeStruct((sources // 2, rows, width), jnp.bfloat16)
     outs = pl.pallas_call(
@@ -317,9 +307,9 @@
             weight,
         ],
         out_specs=(block,) * 2 + (half,) * 4,
-        scratch_shapes=[pltpu.VMEM((sources, step, heads_width), jnp.bfloat16)] * 3 + loaded,
-        compiler_params=pltpu.CompilerParams(vmem_limit_bytes=GRANT),
-        cost_estimate=cost(6),
+        scratch_shapes=[pltpu.VMEM((sources, step, heads_width), jnp.bfloat16)] * 3,
+        compiler_params=pltpu.CompilerParams(vmem_limit_bytes=GRANT),
+        cost_estimate=cost(1),
         name="backward",
     )(blk, saved, probs, grads, wq, wk, wv)
     return (outs[:2], outs[2:])
@@ -433,7 +423,7 @@
         in_specs=[SMEM] + [VMEM] * 3,
         out_specs=(VMEM,) * 6,
         compiler_params=pltpu.CompilerParams(vmem_limit_bytes=GRANT),
-        cost_estimate=cost(6),
+        cost_estimate=cost(1),
         name="project_out",
     )(blk, slot_col, w_out, mixed)
     return (outs[:2], outs[2:])
@@ -529,8 +519,6 @@
         if c > 0:
             x_across[c] = after(x_across[c], mixed)
         parts = (x, x_core, x_across[c], swap(x_across[c], 1))
-        if c > 0:
-            parts = (after(x, g),) + parts[1:]
         if small:
             mixed, *kept = forward(blk, parts, *weights, c, chunks, mixed)
         else:

time: 170 us -> 160 us (0.941)
  Pallas kernels: 68.8 us -> 36.1 us
  waiting for transfers between devices: 57.6 us -> 70.2 us
  local copies, waits for them, and re-layouts: 9.52 us -> 16.4 us
  starting transfers between devices: 31.8 us -> 35.8 us
    ppermute x23, waiting for transfers between devices: 48.1 us -> 61.4 us  [swap(): return lax.ppermute(x, 'tp', [(i, i ^ bit) for i in range(count)])]
    pallas_call x6, Pallas kernels: 13.4 us -> 3.38 us  [add(): pl.pallas_call(kernel, grid=(1,), out_shape=jax.ShapeDtypeStruct(full, jn...]
    pallas_call x2, Pallas kernels: 19.8 us -> 11.6 us  [forward(): pl.pallas_call(forward_kernel, grid=(steps,), out_shape=(jax.ShapeDtypeSt...]
    pallas_call x2, Pallas kernels: 19.4 us -> 11.9 us  [backward(): pl.pallas_call(backward_kernel, grid=(steps,), out_shape=(shape,) * 2 + (...]
    unnamed x57 -> x43, local copies, waits for them, and re-layouts: 9.44 us -> 16.3 us
    all_to_all x4, starting transfers between devices: 20.5 us -> 23.4 us  [exchange(): return lax.all_to_all(x, 'seq', split_axis=0, concat_axis=0, tiled=True)]
    pallas_call x1, Pallas kernels: 3.32 us -> 1.16 us  [place(): pl.pallas_call(place_kernel, out_shape=(jax.ShapeDtypeStruct((tokens, 1),...]
    pallas_call x1, Pallas kernels: 5.18 us -> 3.26 us  [head_grads(): pl.pallas_call(head_grads_kernel, out_shape=jax.ShapeDtypeStruct((CLUSTER...]
  transfers between devices with their start and end apart: 27 -> 27, of which waited for: 19 -> 21; matrix products, arithmetic and copies ran while one was open for 0% -> 0% of each run, Pallas kernels for 31% -> 21%
where the time goes in v4:
time: 160 us; the launch traced here: 159 us
  waiting for transfers between devices  70.2 us (44%)
  Pallas kernels  36.1 us (23%)
  starting transfers between devices  35.8 us (22%)
  local copies, waits for them, and re-layouts  16.4 us (10%)
    ppermute x23, waiting for transfers between devices, swap(): return lax.ppermute(x, 'tp', [(i, i ^ bit) for i in range(count)])  61.4 us
    all_to_all x4, starting transfers between devices, exchange(): return lax.all_to_all(x, 'seq', split_axis=0, concat_axis=0, tiled=True)  23.4 us
    unnamed x43, local copies, waits for them, and re-layouts  16.3 us
    ppermute x23, starting transfers between devices, swap(): return lax.ppermute(x, 'tp', [(i, i ^ bit) for i in range(count)])  12.4 us
    pallas_call x2, Pallas kernels, backward(): pl.pallas_call(backward_kernel, grid=(steps,), out_shape=(shape,) * 2 + (...  11.9 us
    pallas_call x2, Pallas kernels, forward(): pl.pallas_call(forward_kernel, grid=(steps,), out_shape=(jax.ShapeDtypeSt...  11.6 us
    all_to_all x4, waiting for transfers between devices, exchange(): return lax.all_to_all(x, 'seq', split_axis=0, concat_axis=0, tiled=True)  8.85 us
    pallas_call x6, Pallas kernels, add(): pl.pallas_call(kernel, grid=(1,), out_shape=jax.ShapeDtypeStruct(full, jn...  3.38 us
  transfers between devices with their start and end apart: 27, of which 21 were waited for; matrix products, arithmetic and copies ran while one was open for 0% of the time, Pallas kernels for 21%

profile of v4, /device:TPU:0, one launch (start us, length us, event | category | flops | bytes accessed | tf_op | source)
XLA Modules:
  0.0 159.3 jit_solution(16407010448679230728)
XLA Ops:
  0.6 0.8 copy.11.ids_col
  1.5 1.0 copy-done.20
  2.5 1.2 place.1
  3.7 1.0 copy-done.18
  4.6 7.3 %all-to-all-start = ((bf16[8,128,512]{2,1,0:T(8,128)(2,1)}), bf16[8,128,512]{2,1,0:T(8,128)(2,1)S(1)}, u32[]{:S(2)}, u32[]{:S(2)}) async-start(bf16[8,128,512]{2,1,0:T(8,128)(2,1)} %bitcast.6), calls=%async_computation | async-start | bytes 2097152 | tf_op jit(solution)/shard_map/all_to_all | solution.py:45
  11.9 1.5 collective-permute-start.1
  13.4 12.2 %collective-permute-done.1.a2 = bf16[512,512]{1,0:T(8,128)(2,1)} collective-permute-done((bf16[512,512]{1,0:T(8,128)(2,1)}, bf16[512,512]{1,0:T(8,128)(2,1)}, u32[]{:S(2)}, u32[]{:S(2)}) %collective-permute-start.1) | collective-permute-done | bytes 524320 | tf_op jit(solution)/shard_map/ppermute | solution.py:41
  25.6 2.2 %collective-permute-done.2.a3 = bf16[512,512]{1,0:T(8,128)(2,1)} collective-permute-done((bf16[512,512]{1,0:T(8,128)(2,1)}, bf16[512,512]{1,0:T(8,128)(2,1)}, u32[]{:S(2)}, u32[]{:S(2)}) %collective-permute-start.2) | collective-permute-done | bytes 524320 | tf_op jit(solution)/shard_map/ppermute | solution.py:41
  27.9 1.0 copy-done.19
  28.9 3.3 %head_grads.1 = bf16[1024,512]{1,0:T(8,128)(2,1)S(1)} custom-call(s32[4]{0:T(128)S(1)} %iota_xor_fusion.blk, bf16[512,512]{1,0:T(8,128)(2,1)S(1)} %copy-done.19, bf16[512,512]{1,0:T(8,128)(2,1)} %collective-permute-done.a1, bf16[512,512]{1,0:T(8,128)(2,1)} %collective-permute-done.1.a2, bf16[512,512]{1,0:T(8,128)(2,1)} %collective-permute-done.2.a3, ...), custom_call_target="tpu_custom_call" | custom-call | flops 1000000000 | bytes 1048576 | tf_op jit(solution)/shard_map/head_grads/pallas_call | solution.py:98
  32.2 1.0 copy-done.6
  33.2 4.5 %all-to-all-done.x0 = bf16[8,128,512]{2,1,0:T(8,128)(2,1)S(1)} async-done(((bf16[8,128,512]{2,1,0:T(8,128)(2,1)}), bf16[8,128,512]{2,1,0:T(8,128)(2,1)S(1)}, u32[]{:S(2)}, u32[]{:S(2)}) %all-to-all-start) | async-done | bytes 1048608 | tf_op jit(solution)/shard_map/all_to_all | solution.py:45
  37.7 4.4 %all-to-all-start.1 = ((bf16[8,128,512]{2,1,0:T(8,128)(2,1)}), bf16[8,128,512]{2,1,0:T(8,128)(2,1)}, u32[]{:S(2)}, u32[]{:S(2)}) async-start(bf16[8,128,512]{2,1,0:T(8,128)(2,1)} %bitcast.4), calls=%async_computation.1 | async-start | bytes 2097152 | tf_op jit(solution)/shard_map/all_to_all | solution.py:45
  42.2 1.6 collective-permute-start.5
  43.8 11.4 %collective-permute-done.5.x2 = bf16[8,64,512]{2,1,0:T(8,128)(2,1)S(1)} collective-permute-done((bf16[8,64,512]{2,1,0:T(8,128)(2,1)S(1)}, bf16[8,64,512]{2,1,0:T(8,128)(2,1)S(1)}, u32[]{:S(2)}, u32[]{:S(2)}) %collective-permute-start.5) | collective-permute-done | bytes 524320 | tf_op jit(solution)/shard_map/ppermute | solution.py:41
  55.2 1.5 collective-permute-start.4
  56.7 0.4 collective-permute-done.6.x3
  57.1 1.6 copy-done.4
  58.7 5.8 %forward.2 = (bf16[8,128,512]{2,1,0:T(8,128)(2,1)S(1)}, bf16[8,64,1536]{2,1,0:T(8,128)(2,1)S(1)}, f32[2,2,4,128,128]{4,3,2,1,0:T(8,128)S(1)}) custom-call(s32[4]{0:T(128)S(1)} %iota_xor_fusion.blk, bf16[8,128,512]{2,1,0:T(8,128)(2,1)S(1)} %all-to-all-done.x0, bf16[8,128,512]{2,1,0:T(8,128)(2,1)S(1)} %collective-permute-done.3.x1, ...), custom_call_target="tpu_custom_call" | custom-call | flops 1000000000 | bytes 1048576 | tf_op jit(solution)/shard_map/forward/pallas_call | solution.py:263
  64.5 1.1 copy-done.12
  65.6 1.0 copy-done.16
  66.6 2.9 %collective-permute-done.4.x2 = bf16[8,64,512]{2,1,0:T(8,128)(2,1)S(1)} collective-permute-done((bf16[8,64,512]{2,1,0:T(8,128)(2,1)S(1)}, bf16[8,64,512]{2,1,0:T(8,128)(2,1)S(1)}, u32[]{:S(2)}, u32[]{:S(2)}) %collective-permute-start.4) | collective-permute-done | bytes 524320 | tf_op jit(solution)/shard_map/ppermute | solution.py:41
  69.5 1.9 %collective-permute-done.7.x3 = bf16[8,64,512]{2,1,0:T(8,128)(2,1)S(1)} collective-permute-done((bf16[8,64,512]{2,1,0:T(8,128)(2,1)S(1)}, bf16[8,64,512]{2,1,0:T(8,128)(2,1)S(1)}, u32[]{:S(2)}, u32[]{:S(2)}) %collective-permute-start.7) | collective-permute-done | bytes 524320 | tf_op jit(solution)/shard_map/ppermute | solution.py:41
  71.4 5.8 %forward.3 = (bf16[8,128,512]{2,1,0:T(8,128)(2,1)S(1)}, bf16[8,64,1536]{2,1,0:T(8,128)(2,1)S(1)}, f32[2,2,4,128,128]{4,3,2,1,0:T(8,128)S(1)}) custom-call(s32[4]{0:T(128)S(1)} %iota_xor_fusion.blk, bf16[8,128,512]{2,1,0:T(8,128)(2,1)S(1)} %all-to-all-done.x0, bf16[8,128,512]{2,1,0:T(8,128)(2,1)S(1)} %collective-permute-done.3.x1, ...), custom_call_target="tpu_custom_call", output_to_operand_aliasing={{0}: (8, {})} | custom-call | flops 1000000000 | bytes 1048576 | tf_op jit(solution)/shard_map/forward/pallas_call | solution.py:263
  77.2 1.0 copy-done.7
  78.2 1.2 copy-done.10
  79.4 1.0 copy-done.14
  80.3 5.8 %all-to-all-start.2 = ((bf16[8,128,512]{2,1,0:T(8,128)(2,1)}), bf16[8,128,512]{2,1,0:T(8,128)(2,1)}, u32[]{:S(2)}, u32[]{:S(2)}) async-start(bf16[8,128,512]{2,1,0:T(8,128)(2,1)} %copy-done.7), calls=%async_computation.2 | async-start | bytes 2097152 | tf_op jit(solution)/shard_map/all_to_all | solution.py:45
  86.2 1.6 copy-done.2
  87.8 1.6 copy-done.5
  89.4 1.4 copy-done.13
  90.8 6.0 %backward.2 = (bf16[8,64,512]{2,1,0:T(8,128)(2,1)S(1)}, bf16[8,64,512]{2,1,0:T(8,128)(2,1)S(1)}, bf16[4,64,512]{2,1,0:T(8,128)(2,1)S(1)}, bf16[4,64,512]{2,1,0:T...) custom-call(s32[4]{0:T(128)S(1)} %iota_xor_fusion.blk, ...), custom_call_target="tpu_custom_call" | custom-call | flops 1000000000 | bytes 1048576 | tf_op jit(solution)/shard_map/backward/pallas_call | solution.py:296
  96.9 0.5 collective-permute-start.14
  97.4 1.0 collective-permute-done.13.refs_1_
  98.4 0.4 collective-permute-done.14.refs_2_
  98.8 0.1 add.8
  98.9 1.6 collective-permute-start.19
  100.5 5.9 %backward.3 = (bf16[8,64,512]{2,1,0:T(8,128)(2,1)S(1)}, bf16[8,64,512]{2,1,0:T(8,128)(2,1)S(1)}, bf16[4,64,512]{2,1,0:T(8,128)(2,1)S(1)}, bf16[4,64,512]{2,1,0:T...) custom-call(s32[4]{0:T(128)S(1)} %iota_xor_fusion.blk, ...), custom_call_target="tpu_custom_call" | custom-call | flops 1000000000 | bytes 1048576 | tf_op jit(solution)/shard_map/backward/pallas_call | solution.py:296
  106.5 0.5 collective-permute-start.18
  107.0 1.0 collective-permute-done.17.refs_1_
  108.0 0.4 collective-permute-done.18.refs_2_
  108.4 0.1 add.9
  108.5 4.5 %collective-permute-done.19.refs_3_ = bf16[8,64,512]{2,1,0:T(8,128)(2,1)S(1)} collective-permute-done((bf16[8,64,512]{2,1,0:T(8,128)(2,1)S(1)}, bf16[8,64,512]{2,1,0:T(8,128)(2,1)S(1)}, u32[]{:S(2)}, u32[]{:S(2)}) %collective-permute-start.19) | collective-permute-done | bytes 524320 | tf_op jit(solution)/shard_map/ppermute | solution.py:41
  113.0 1.5 collective-permute-start.20
  114.4 0.5 collective-permute-start.22
  115.0 0.5 collective-permute-start.16
  115.5 0.5 collective-permute-done.21.refs_1_
  116.0 0.4 collective-permute-done.22.refs_2_
  116.4 1.0 add.10.refs_4_
  117.4 8.8 %collective-permute-done.20.refs_3_ = bf16[8,64,512]{2,1,0:T(8,128)(2,1)S(1)} collective-permute-done((bf16[8,64,512]{2,1,0:T(8,128)(2,1)S(1)}, bf16[8,64,512]{2,1,0:T(8,128)(2,1)S(1)}, u32[]{:S(2)}, u32[]{:S(2)}) %collective-permute-start.20) | collective-permute-done | bytes 524320 | tf_op jit(solution)/shard_map/ppermute | solution.py:41
  126.2 1.0 add.11
  127.2 5.9 %all-to-all-start.3 = ((bf16[8,128,512]{2,1,0:T(8,128)(2,1)}), bf16[8,128,512]{2,1,0:T(8,128)(2,1)S(1)}, u32[]{:S(2)}, u32[]{:S(2)}) async-start(bf16[8,128,512]{2,1,0:T(8,128)(2,1)} %add.11), calls=%async_computation.3 | async-start | bytes 2097152 | tf_op jit(solution)/shard_map/all_to_all | solution.py:45
  133.1 3.1 %project_out.1 = (bf16[512,512]{1,0:T(8,128)(2,1)S(1)}, bf16[512,512]{1,0:T(8,128)(2,1)S(1)}, bf16[256,512]{1,0:T(8,128)(2,1)S(1)}, bf16[256,512]{1,0:T(8,128)(2...) custom-call(s32[4]{0:T(128)S(1)} %iota_xor_fusion.blk, s32[512,1]{1,0:T(8,128)S(1)} %get-tuple-element.37.slot_col, ...), custom_call_target="tpu_custom_call" | custom-call | flops 1000000000 | bytes 1048576 | tf_op jit(solution)/shard_map/project_out/pallas_call | solution.py:420
  136.2 0.5 collective-permute-start.11
  136.7 1.0 collective-permute-done.10.refs_1_
  137.8 0.4 collective-permute-done.11.refs_2_
  138.3 1.6 collective-permute-start.12
  139.8 0.5 collective-permute-start.9
  140.3 1.0 collective-permute-done.8.refs_1_
  141.4 0.4 collective-permute-done.9.refs_2_
  141.7 10.6 %collective-permute-done.12.refs_3_ = bf16[512,512]{1,0:T(8,128)(2,1)S(1)} collective-permute-done((bf16[512,512]{1,0:T(8,128)(2,1)S(1)}, bf16[512,512]{1,0:T(8,128)(2,1)S(1)}, u32[]{:S(2)}, u32[]{:S(2)}) %collective-permute-start.12) | collective-permute-done | bytes 524320 | tf_op jit(solution)/shard_map/ppermute | solution.py:41
  152.3 1.0 add.7
  153.3 4.3 %all-to-all-done.3 = bf16[8,128,512]{2,1,0:T(8,128)(2,1)S(1)} async-done(((bf16[8,128,512]{2,1,0:T(8,128)(2,1)}), bf16[8,128,512]{2,1,0:T(8,128)(2,1)S(1)}, u32[]{:S(2)}, u32[]{:S(2)}) %all-to-all-start.3) | async-done | bytes 1048608 | tf_op jit(solution)/shard_map/all_to_all | solution.py:45
  157.6 1.7 %to_tokens.1 = f32[512,512]{1,0:T(8,128)} custom-call(s32[512,1]{1,0:T(8,128)S(1)} %get-tuple-element.37.slot_col, bf16[1024,512]{1,0:T(8,128)(2,1)S(1)} %bitcast.5), custom_call_target="tpu_custom_call" | custom-call | flops 1000000000 | bytes 1048576 | tf_op jit(solution)/shard_map/to_tokens/pallas_call | solution.py:437
  (49 shorter events, 0.5 us)
Async XLA Ops:
  1.5 1.0 copy-start.20
  2.5 25.4 %copy-start.8 = (bf16[512,2048]{1,0:T(8,128)(2,1)S(1)}, bf16[512,2048]{1,0:T(8,128)(2,1)}, u32[]{:S(2)}) copy-start(bf16[512,2048]{1,0:T(8,128)(2,1)} %w_out.3) | copy-start | bytes 6291460
  3.7 1.0 copy-start.18
  4.6 33.1 %all-to-all-start = ((bf16[8,128,512]{2,1,0:T(8,128)(2,1)}), bf16[8,128,512]{2,1,0:T(8,128)(2,1)S(1)}, u32[]{:S(2)}, u32[]{:S(2)}) async-start(bf16[8,128,512]{2,1,0:T(8,128)(2,1)} %bitcast.6), calls=%async_computation | async-start | bytes 2097152 | tf_op jit(solution)/shard_map/all_to_all | solution.py:45
  11.9 13.7 %collective-permute-start.1 = (bf16[512,512]{1,0:T(8,128)(2,1)}, bf16[512,512]{1,0:T(8,128)(2,1)}, u32[]{:S(2)}, u32[]{:S(2)}) collective-permute-start(bf16[512,512]{1,0:T(8,128)(2,1)} %a0.1), channel_id=1, source_target_pairs={{0,2},{1,3},{2,0},{3,1},{4,6},{5,7},{6,4},{7,5},{8,10},{9,11},{10,... | collective-permute-start | bytes 1572872 | tf_op jit(solution)/shard_map/ppermute | solution.py:41
  13.4 12.2 %collective-permute-start = (bf16[512,512]{1,0:T(8,128)(2,1)}, bf16[512,512]{1,0:T(8,128)(2,1)}, u32[]{:S(2)}, u32[]{:S(2)}) collective-permute-start(bf16[512,512]{1,0:T(8,128)(2,1)} %a0.1), channel_id=1, source_target_pairs={{0,1},{1,0},{2,3},{3,2},{4,5},{5,4},{6,7},{7,6},{8,9},{9,8},{10,11... | collective-permute-start | bytes 1572872 | tf_op jit(solution)/shard_map/ppermute | solution.py:41
  25.6 2.3 %collective-permute-start.2 = (bf16[512,512]{1,0:T(8,128)(2,1)}, bf16[512,512]{1,0:T(8,128)(2,1)}, u32[]{:S(2)}, u32[]{:S(2)}) collective-permute-start(bf16[512,512]{1,0:T(8,128)(2,1)} %collective-permute-done.1.a2), channel_id=1, source_target_pairs={{0,1},{1,0},{2,3},{3,2},{4,5},{5,4},{6,7},{7,6},{8,9},{9,8},{10,11... | collective-permute-start | bytes 1572872 | tf_op jit(solution)/shard_map/ppermute | solution.py:41
  27.9 1.0 copy-start.19
  32.2 1.0 copy-start.6
  37.7 19.4 %copy-start = (bf16[2048,512]{1,0:T(8,128)(2,1)S(1)}, bf16[2048,512]{1,0:T(8,128)(2,1)}, u32[]{:S(2)}) copy-start(bf16[2048,512]{1,0:T(8,128)(2,1)} %wq.7) | copy-start | bytes 6291460
  37.7 42.6 %all-to-all-start.1 = ((bf16[8,128,512]{2,1,0:T(8,128)(2,1)}), bf16[8,128,512]{2,1,0:T(8,128)(2,1)}, u32[]{:S(2)}, u32[]{:S(2)}) async-start(bf16[8,128,512]{2,1,0:T(8,128)(2,1)} %bitcast.4), calls=%async_computation.1 | async-start | bytes 2097152 | tf_op jit(solution)/shard_map/all_to_all | solution.py:45
  42.1 15.0 %copy-start.1 = (bf16[2048,512]{1,0:T(8,128)(2,1)S(1)}, bf16[2048,512]{1,0:T(8,128)(2,1)}, u32[]{:S(2)}) copy-start(bf16[2048,512]{1,0:T(8,128)(2,1)} %wk.7) | copy-start | bytes 6291460
  42.2 13.0 %collective-permute-start.5 = (bf16[8,64,512]{2,1,0:T(8,128)(2,1)S(1)}, bf16[8,64,512]{2,1,0:T(8,128)(2,1)S(1)}, u32[]{:S(2)}, u32[]{:S(2)}) collective-permute-start(bf16[8,64,512]{2,1,0:T(8,128)(2,1)S(1)} %get-tuple-element.72), channel_id=1, source_target_pairs={{0,2},{1,3},{2,0},{3,1},{4,6},{5,7},{6,4},{7,5},{8,10},{9,11},{10,... | collective-permute-start | bytes 1572872 | tf_op jit(solution)/shard_map/ppermute | solution.py:41
  43.8 13.3 %collective-permute-start.3 = (bf16[8,128,512]{2,1,0:T(8,128)(2,1)S(1)}, bf16[8,128,512]{2,1,0:T(8,128)(2,1)S(1)}, u32[]{:S(2)}, u32[]{:S(2)}) collective-permute-start(bf16[8,128,512]{2,1,0:T(8,128)(2,1)S(1)} %all-to-all-done.x0), channel_id=1, source_target_pairs={{0,1},{1,0},{2,3},{3,2},{4,5},{5,4},{6,7},{7,6},{8,9},{9,8},{10,11... | collective-permute-start | bytes 3145736 | tf_op jit(solution)/shard_map/ppermute | solution.py:41
  55.2 1.9 %collective-permute-start.6 = (bf16[8,64,512]{2,1,0:T(8,128)(2,1)S(1)}, bf16[8,64,512]{2,1,0:T(8,128)(2,1)S(1)}, u32[]{:S(2)}, u32[]{:S(2)}) collective-permute-start(bf16[8,64,512]{2,1,0:T(8,128)(2,1)S(1)} %collective-permute-done.5.x2), channel_id=1, source_target_pairs={{0,1},{1,0},{2,3},{3,2},{4,5},{5,4},{6,7},{7,6},{8,9},{9,8},{10,11... | collective-permute-start | bytes 1572872 | tf_op jit(solution)/shard_map/ppermute | solution.py:41
  55.2 14.3 %collective-permute-start.4 = (bf16[8,64,512]{2,1,0:T(8,128)(2,1)S(1)}, bf16[8,64,512]{2,1,0:T(8,128)(2,1)S(1)}, u32[]{:S(2)}, u32[]{:S(2)}) collective-permute-start(bf16[8,64,512]{2,1,0:T(8,128)(2,1)S(1)} %get-tuple-element.73), channel_id=1, source_target_pairs={{0,2},{1,3},{2,0},{3,1},{4,6},{5,7},{6,4},{7,5},{8,10},{9,11},{10,... | collective-permute-start | bytes 1572872 | tf_op jit(solution)/shard_map/ppermute | solution.py:41
  57.1 1.6 %copy-start.4 = (bf16[2048,512]{1,0:T(8,128)(2,1)S(1)}, bf16[2048,512]{1,0:T(8,128)(2,1)}, u32[]{:S(2)}) copy-start(bf16[2048,512]{1,0:T(8,128)(2,1)} %wv.7) | copy-start | bytes 6291460
  64.5 1.1 copy-start.12
  65.6 1.0 copy-start.16
  69.5 1.9 %collective-permute-start.7 = (bf16[8,64,512]{2,1,0:T(8,128)(2,1)S(1)}, bf16[8,64,512]{2,1,0:T(8,128)(2,1)S(1)}, u32[]{:S(2)}, u32[]{:S(2)}) collective-permute-start(bf16[8,64,512]{2,1,0:T(8,128)(2,1)S(1)} %collective-permute-done.4.x2), channel_id=1, source_target_pairs={{0,1},{1,0},{2,3},{3,2},{4,5},{5,4},{6,7},{7,6},{8,9},{9,8},{10,11... | collective-permute-start | bytes 1572872 | tf_op jit(solution)/shard_map/ppermute | solution.py:41
  77.2 1.0 copy-start.7
  78.2 1.2 copy-start.10
  79.3 1.0 copy-start.14
  80.3 5.9 %copy-start.17 = (f32[2,2,4,128,128]{4,3,2,1,0:T(8,128)S(1)}, f32[2,2,4,128,128]{4,3,2,1,0:T(8,128)}, u32[]{:S(2)}) copy-start(f32[2,2,4,128,128]{4,3,2,1,0:T(8,128)} %copy-done.16) | copy-start | bytes 3145732
  80.3 46.9 %all-to-all-start.2 = ((bf16[8,128,512]{2,1,0:T(8,128)(2,1)}), bf16[8,128,512]{2,1,0:T(8,128)(2,1)}, u32[]{:S(2)}, u32[]{:S(2)}) async-start(bf16[8,128,512]{2,1,0:T(8,128)(2,1)} %copy-done.7), calls=%async_computation.2 | async-start | bytes 2097152 | tf_op jit(solution)/shard_map/all_to_all | solution.py:45
  86.2 1.6 %copy-start.2 = (bf16[2048,512]{1,0:T(8,128)(2,1)S(1)}, bf16[2048,512]{1,0:T(8,128)(2,1)}, u32[]{:S(2)}) copy-start(bf16[2048,512]{1,0:T(8,128)(2,1)} %wk.7) | copy-start | bytes 6291460
  87.8 1.6 copy-start.5
  89.4 1.4 copy-start.13
  90.8 9.7 %copy-start.3 = (bf16[2048,512]{1,0:T(8,128)(2,1)S(1)}, bf16[2048,512]{1,0:T(8,128)(2,1)}, u32[]{:S(2)}) copy-start(bf16[2048,512]{1,0:T(8,128)(2,1)} %wk.7) | copy-start | bytes 6291460
  90.8 9.7 %copy-start.15 = (f32[2,2,4,128,128]{4,3,2,1,0:T(8,128)S(1)}, f32[2,2,4,128,128]{4,3,2,1,0:T(8,128)}, u32[]{:S(2)}) copy-start(f32[2,2,4,128,128]{4,3,2,1,0:T(8,128)} %copy-done.14) | copy-start | bytes 3145732
  96.8 3.7 %copy-start.11 = (bf16[8,64,1536]{2,1,0:T(8,128)(2,1)S(1)}, bf16[8,64,1536]{2,1,0:T(8,128)(2,1)}, u32[]{:S(2)}) copy-start(bf16[8,64,1536]{2,1,0:T(8,128)(2,1)} %copy-done.10) | copy-start | bytes 4718596
  96.8 1.6 %collective-permute-start.13 = (bf16[4,64,512]{2,1,0:T(8,128)(2,1)S(1)}, bf16[4,64,512]{2,1,0:T(8,128)(2,1)S(1)}, u32[]{:S(2)}, u32[]{:S(2)}) collective-permute-start(bf16[4,64,512]{2,1,0:T(8,128)(2,1)S(1)} %get-tuple-element.58), channel_id=1, source_target_pairs={{0,1},{1,0},{2,3},{3,2},{4,5},{5,4},{6,7},{7,6},{8,9},{9,8},{10,11... | collective-permute-start | bytes 786440 | tf_op jit(solution)/shard_map/ppermute | solution.py:41
  96.9 1.9 %collective-permute-start.14 = (bf16[4,64,512]{2,1,0:T(8,128)(2,1)S(1)}, bf16[4,64,512]{2,1,0:T(8,128)(2,1)S(1)}, u32[]{:S(2)}, u32[]{:S(2)}) collective-permute-start(bf16[4,64,512]{2,1,0:T(8,128)(2,1)S(1)} %get-tuple-element.59), channel_id=1, source_target_pairs={{0,1},{1,0},{2,3},{3,2},{4,5},{5,4},{6,7},{7,6},{8,9},{9,8},{10,11... | collective-permute-start | bytes 786440 | tf_op jit(solution)/shard_map/ppermute | solution.py:41
  98.9 14.0 %collective-permute-start.19 = (bf16[8,64,512]{2,1,0:T(8,128)(2,1)S(1)}, bf16[8,64,512]{2,1,0:T(8,128)(2,1)S(1)}, u32[]{:S(2)}, u32[]{:S(2)}) collective-permute-start(bf16[8,64,512]{2,1,0:T(8,128)(2,1)S(1)} %add.8), channel_id=1, source_target_pairs={{0,2},{1,3},{2,0},{3,1},{4,6},{5,7},{6,4},{7,5},{8,10},{9,11},{10,... | collective-permute-start | bytes 1572872 | tf_op jit(solution)/shard_map/ppermute | solution.py:41
  106.4 1.6 %collective-permute-start.17 = (bf16[4,64,512]{2,1,0:T(8,128)(2,1)S(1)}, bf16[4,64,512]{2,1,0:T(8,128)(2,1)S(1)}, u32[]{:S(2)}, u32[]{:S(2)}) collective-permute-start(bf16[4,64,512]{2,1,0:T(8,128)(2,1)S(1)} %get-tuple-element.65), channel_id=1, source_target_pairs={{0,1},{1,0},{2,3},{3,2},{4,5},{5,4},{6,7},{7,6},{8,9},{9,8},{10,11... | collective-permute-start | bytes 786440 | tf_op jit(solution)/shard_map/ppermute | solution.py:41
  106.5 1.9 %collective-permute-start.18 = (bf16[4,64,512]{2,1,0:T(8,128)(2,1)S(1)}, bf16[4,64,512]{2,1,0:T(8,128)(2,1)S(1)}, u32[]{:S(2)}, u32[]{:S(2)}) collective-permute-start(bf16[4,64,512]{2,1,0:T(8,128)(2,1)S(1)} %get-tuple-element.66), channel_id=1, source_target_pairs={{0,1},{1,0},{2,3},{3,2},{4,5},{5,4},{6,7},{7,6},{8,9},{9,8},{10,11... | collective-permute-start | bytes 786440 | tf_op jit(solution)/shard_map/ppermute | solution.py:41
  113.0 13.2 %collective-permute-start.20 = (bf16[8,64,512]{2,1,0:T(8,128)(2,1)S(1)}, bf16[8,64,512]{2,1,0:T(8,128)(2,1)S(1)}, u32[]{:S(2)}, u32[]{:S(2)}) collective-permute-start(bf16[8,64,512]{2,1,0:T(8,128)(2,1)S(1)} %add.9), channel_id=1, source_target_pairs={{0,2},{1,3},{2,0},{3,1},{4,6},{5,7},{6,4},{7,5},{8,10},{9,11},{10,... | collective-permute-start | bytes 1572872 | tf_op jit(solution)/shard_map/ppermute | solution.py:41
  114.4 1.5 collective-permute-start.21
  114.4 1.9 %collective-permute-start.22 = (bf16[4,64,512]{2,1,0:T(8,128)(2,1)S(1)}, bf16[4,64,512]{2,1,0:T(8,128)(2,1)S(1)}, u32[]{:S(2)}, u32[]{:S(2)}) collective-permute-start(bf16[4,64,512]{2,1,0:T(8,128)(2,1)S(1)} %get-tuple-element.70), channel_id=1, source_target_pairs={{0,1},{1,0},{2,3},{3,2},{4,5},{5,4},{6,7},{7,6},{8,9},{9,8},{10,11... | collective-permute-start | bytes 786440 | tf_op jit(solution)/shard_map/ppermute | solution.py:41
  115.0 2.4 %collective-permute-start.15 = (bf16[4,64,512]{2,1,0:T(8,128)(2,1)S(1)}, bf16[4,64,512]{2,1,0:T(8,128)(2,1)S(1)}, u32[]{:S(2)}, u32[]{:S(2)}) collective-permute-start(bf16[4,64,512]{2,1,0:T(8,128)(2,1)S(1)} %get-tuple-element.62), channel_id=1, source_target_pairs={{0,1},{1,0},{2,3},{3,2},{4,5},{5,4},{6,7},{7,6},{8,9},{9,8},{10,11... | collective-permute-start | bytes 786440 | tf_op jit(solution)/shard_map/ppermute | solution.py:41
  115.0 2.4 %collective-permute-start.16 = (bf16[4,64,512]{2,1,0:T(8,128)(2,1)S(1)}, bf16[4,64,512]{2,1,0:T(8,128)(2,1)S(1)}, u32[]{:S(2)}, u32[]{:S(2)}) collective-permute-start(bf16[4,64,512]{2,1,0:T(8,128)(2,1)S(1)} %get-tuple-element.63), channel_id=1, source_target_pairs={{0,1},{1,0},{2,3},{3,2},{4,5},{5,4},{6,7},{7,6},{8,9},{9,8},{10,11... | collective-permute-start | bytes 786440 | tf_op jit(solution)/shard_map/ppermute | solution.py:41
  126.2 6.9 %copy-start.9 = (bf16[512,2048]{1,0:T(8,128)(2,1)S(1)}, bf16[512,2048]{1,0:T(8,128)(2,1)}, u32[]{:S(2)}) copy-start(bf16[512,2048]{1,0:T(8,128)(2,1)} %w_out.3) | copy-start | bytes 6291460
  127.2 30.4 %all-to-all-start.3 = ((bf16[8,128,512]{2,1,0:T(8,128)(2,1)}), bf16[8,128,512]{2,1,0:T(8,128)(2,1)S(1)}, u32[]{:S(2)}, u32[]{:S(2)}) async-start(bf16[8,128,512]{2,1,0:T(8,128)(2,1)} %add.11), calls=%async_computation.3 | async-start | bytes 2097152 | tf_op jit(solution)/shard_map/all_to_all | solution.py:45
  136.2 1.6 %collective-permute-start.10 = (bf16[256,512]{1,0:T(8,128)(2,1)S(1)}, bf16[256,512]{1,0:T(8,128)(2,1)S(1)}, u32[]{:S(2)}, u32[]{:S(2)}) collective-permute-start(bf16[256,512]{1,0:T(8,128)(2,1)S(1)} %get-tuple-element.50), channel_id=1, source_target_pairs={{0,1},{1,0},{2,3},{3,2},{4,5},{5,4},{6,7},{7,6},{8,9},{9,8},{10,11... | collective-permute-start | bytes 786440 | tf_op jit(solution)/shard_map/ppermute | solution.py:41
  136.2 1.9 %collective-permute-start.11 = (bf16[256,512]{1,0:T(8,128)(2,1)S(1)}, bf16[256,512]{1,0:T(8,128)(2,1)S(1)}, u32[]{:S(2)}, u32[]{:S(2)}) collective-permute-start(bf16[256,512]{1,0:T(8,128)(2,1)S(1)} %get-tuple-element.51), channel_id=1, source_target_pairs={{0,1},{1,0},{2,3},{3,2},{4,5},{5,4},{6,7},{7,6},{8,9},{9,8},{10,11... | collective-permute-start | bytes 786440 | tf_op jit(solution)/shard_map/ppermute | solution.py:41
  138.3 14.0 %collective-permute-start.12 = (bf16[512,512]{1,0:T(8,128)(2,1)S(1)}, bf16[512,512]{1,0:T(8,128)(2,1)S(1)}, u32[]{:S(2)}, u32[]{:S(2)}) collective-permute-start(bf16[512,512]{1,0:T(8,128)(2,1)S(1)} %add.6), channel_id=1, source_target_pairs={{0,2},{1,3},{2,0},{3,1},{4,6},{5,7},{6,4},{7,5},{8,10},{9,11},{10,... | collective-permute-start | bytes 1572872 | tf_op jit(solution)/shard_map/ppermute | solution.py:41
  139.8 1.5 collective-permute-start.8
  139.8 1.9 %collective-permute-start.9 = (bf16[256,512]{1,0:T(8,128)(2,1)S(1)}, bf16[256,512]{1,0:T(8,128)(2,1)S(1)}, u32[]{:S(2)}, u32[]{:S(2)}) collective-permute-start(bf16[256,512]{1,0:T(8,128)(2,1)S(1)} %get-tuple-element.48), channel_id=1, source_target_pairs={{0,1},{1,0},{2,3},{3,2},{4,5},{5,4},{6,7},{7,6},{8,9},{9,8},{10,11... | collective-permute-start | bytes 786440 | tf_op jit(solution)/shard_map/ppermute | solution.py:41

commit v5 on v4

--- a/solution.py
+++ b/solution.py
@@ -49,8 +49,15 @@
     return lax.optimization_barrier((x,) + others)[0]
 
 
-def place_kernel(ids_col, x_ref, slot_col, slot_row, out):
-    tokens = x_ref.shape[0]
+def slots_of(out, tokens, chunk, chunks):
+    owners, rows, _ = out.shape
+    shape = (owners, rows, tokens)
+    slot = iota(shape, 0) * (rows * chunks) + iota(shape, 1) + chunk * rows
+    return slot.reshape(owners * rows, tokens)
+
+
+def place_kernel(ids_col, x_ref, slot_col, slot_row, *outs):
+    tokens, width = x_ref.shape
     here, there = (iota((tokens, tokens), 0), iota((tokens, tokens), 1))
     col = ids_col[...]
     row = jnp.sum(jnp.where(here == there, col, 0), axis=0, keepdims=True)
@@ -59,23 +66,26 @@
     later = jnp.where(same & (here < there), 1.0, 0.0)
     slot_col[...] = col * MOST + jnp.sum(earlier, axis=1, keepdims=True).astype(jnp.int32)
     slot_row[...] = row * MOST + jnp.sum(later, axis=0, keepdims=True).astype(jnp.int32)
-    slots, width = out.shape
-    chosen = jnp.where(iota((slots, tokens), 0) == slot_row[...], 1.0, 0.0)
-    taken = jnp.sum(chosen, axis=1, keepdims=True)
-    value = dot(chosen.astype(jnp.bfloat16), x_ref[...])
-    first = iota((slots, width), 1) == 0
-    out[...] = (value + jnp.where(first & (taken == 0.0), EMPTY, 0.0)).astype(jnp.bfloat16)
-
-
-def place(cluster, x):
+    for c, out in enumerate(outs):
+        held = slots_of(out, tokens, c, len(outs)) == slot_row[...]
+        chosen = jnp.where(held, 1.0, 0.0)
+        taken = jnp.sum(chosen, axis=1, keepdims=True)
+        value = dot(chosen.astype(jnp.bfloat16), x_ref[...])
+        first = iota(value.shape, 1) == 0
+        value = value + jnp.where(first & (taken == 0.0), EMPTY, 0.0)
+        out[...] = value.astype(jnp.bfloat16).reshape(out.shape)
+
+
+def place(cluster, x, owners, rows, chunks):
     tokens = x.shape[0]
+    piece = jax.ShapeDtypeStruct((owners, rows, x.shape[1]), jnp.bfloat16)
     return pl.pallas_call(
         place_kernel,
         out_shape=(
             jax.ShapeDtypeStruct((tokens, 1), jnp.int32),
             jax.ShapeDtypeStruct((1, tokens), jnp.int32),
-            jax.ShapeDtypeStruct((CLUSTERS * MOST, x.shape[1]), jnp.bfloat16),
-        ),
+        )
+        + (piece,) * chunks,
         compiler_params=pltpu.CompilerParams(vmem_limit_bytes=GRANT),
         cost_estimate=cost(1),
         name="place",
@@ -253,9 +263,8 @@
     step = step_of(sources, rows)
     steps, groups, members = (rows // step, step // GROUP, sources * GROUP)
     block = pl.BlockSpec((sources, step, width), lambda p: (0, p, 0))
-    whole = pl.BlockSpec((sources, step, width), lambda p: (0, p + chunk * steps, 0))
     weight = VMEM
-    in_specs = [SMEM] + [whole] * 2 + [block] * 2 + [weight] * 3
+    in_specs = [SMEM] + [block] * 4 + [weight] * 3
     operands = [blk, *parts, wq, wk, wv]
     if mixed is not None:
         in_specs.append(pl.BlockSpec(memory_space=pl.ANY))
@@ -275,7 +284,7 @@
             pl.BlockSpec((1, groups, heads, members, members), lambda p: (p, 0, 0, 0, 0)),
         ),
         input_output_aliases={} if mixed is None else {len(operands) - 1: 0},
-        compiler_params=pltpu.CompilerParams(vmem_limit_bytes=GRANT),
+        compiler_params=pltpu.CompilerParams(vmem_limit_bytes=40 * MB),
         cost_estimate=cost(1),
         name="forward",
     )(*operands)
@@ -308,7 +317,7 @@
         ],
         out_specs=(block,) * 2 + (half,) * 4,
         scratch_shapes=[pltpu.VMEM((sources, step, heads_width), jnp.bfloat16)] * 3,
-        compiler_params=pltpu.CompilerParams(vmem_limit_bytes=GRANT),
+        compiler_params=pltpu.CompilerParams(vmem_limit_bytes=50 * MB),
         cost_estimate=cost(1),
         name="backward",
     )(blk, saved, probs, grads, wq, wk, wv)
@@ -394,14 +403,21 @@
     return ((outs[0], outs[2]), (outs[1][:half], outs[1][half:], outs[3][:half], outs[3][half:]))
 
 
-def pick(slot_col, slots):
-    held = iota((1, slots.shape[0]), 1) == slot_col[...]
-    return dot(jnp.where(held, 1.0, 0.0).astype(jnp.bfloat16), slots[...])
+def pick(slot_col, parts):
+    total = None
+    for c, part in enumerate(parts):
+        owners, rows, width = part.shape
+        i = iota((1, owners * rows), 1)
+        slots = i // rows * (rows * len(parts)) + i % rows + c * rows
+        chosen = jnp.where(slots == slot_col[...], 1.0, 0.0).astype(jnp.bfloat16)
+        term = dot(chosen, part[...].reshape(owners * rows, width))
+        total = term if total is None else total + term
+    return total
 
 
 def out_kernel(blk, slot_col, w_out, mixed, *outs):
     keep, give = (outs[:2], outs[2:])
-    heads = pick(slot_col, mixed).astype(jnp.bfloat16)
+    heads = pick(slot_col, (mixed,)).astype(jnp.bfloat16)
     tokens, width = keep[0].shape
     span = spans(blk, width)
     for j in (1, 3, 0, 2):
@@ -429,18 +445,18 @@
     return (outs[:2], outs[2:])
 
 
-def final_kernel(slot_col, slots, out):
-    out[...] = pick(slot_col, slots)
-
-
-def to_tokens(slot_col, slots):
+def final_kernel(slot_col, *refs):
+    refs[-1][...] = pick(slot_col, refs[:-1])
+
+
+def to_tokens(slot_col, parts):
     return pl.pallas_call(
         final_kernel,
-        out_shape=jax.ShapeDtypeStruct((slot_col.shape[0], slots.shape[1]), jnp.float32),
+        out_shape=jax.ShapeDtypeStruct((slot_col.shape[0], parts[0].shape[2]), jnp.float32),
         compiler_params=pltpu.CompilerParams(vmem_limit_bytes=GRANT),
         cost_estimate=cost(1),
         name="to_tokens",
-    )(slot_col, slots)
+    )(slot_col, *parts)
 
 
 def wide(x):
@@ -504,21 +520,20 @@
 
     g_across = swap(grad_out, 2)
     g_parts = (grad_out, swap(grad_out, 1), g_across, swap(g_across, 1))
-    slot_col, slot_row, x_slots = place(cluster, normed)
-    x = exchange(x_slots.reshape(seq_count, per, -1))
+    slot_col, slot_row, *pieces = place(cluster, normed, seq_count, rows, chunks)
+    xs, x_across = ([], [])
+    for piece in pieces:
+        xs.append(exchange(after(piece, *xs[-1:])))
+    for x in xs:
+        x_across.append(swap(x, 2))
     g_slots = head_grads(blk, g_parts, w_out, slot_row).reshape(seq_count, per, -1)
-    x = after(x, g_slots)
-    g = exchange(after(g_slots, x))
-
-    x_core, x_across = (swap(x, 1), [])
-    for c in range(chunks):
-        piece = x[:, c * rows : (c + 1) * rows]
-        x_across.append(swap(piece, 2))
+    g = exchange(after(g_slots, xs[-1], x_across[0]))
+
     mixed, saved = (None, [])
     for c in range(chunks):
         if c > 0:
             x_across[c] = after(x_across[c], mixed)
-        parts = (x, x_core, x_across[c], swap(x_across[c], 1))
+        parts = (xs[c], swap(xs[c], 1), x_across[c], swap(x_across[c], 1))
         if small:
             mixed, *kept = forward(blk, parts, *weights, c, chunks, mixed)
         else:
@@ -534,17 +549,19 @@
             keep, give = backward_many(blk, *saved[c], g, *weights)
         keep, got, partial = reduce_pairs(keep, give)
         g = after(g, partial)
+        before_last = partial
         if c > 0:
             partial = after(partial, saved[c - 1][3])
         saved[c] = (keep, *got, swap(partial, 2))
-    summed = None
+    back, last = ([], mixed_back)
     for c in range(chunks):
-        summed = add(*saved[c], into=summed, chunk=c, chunks=chunks)
-    back = exchange(after(summed, mixed_back))
-    keep, give = project_out(blk, slot_col, w_out, mixed_back.reshape(CLUSTERS * MOST, -1))
-    keep, got, partial = reduce_pairs(keep, give)
-    attended = add(keep, *got, swap(partial, 2))
-    return (attended, to_tokens(slot_col, back.reshape(CLUSTERS * MOST, -1)))
+        last = exchange(after(add(*saved[c]), last, before_last))
+        back.append(last)
+        if c == 0:
+            keep, give = project_out(blk, slot_col, w_out, mixed_back)
+            keep, got, before_last = reduce_pairs(keep, give)
+            attended = add(keep, *got, swap(before_last, 2))
+    return (attended, to_tokens(slot_col, back))
 
 
 def solution(mesh):

time: 160 us -> 151 us (0.944)
  waiting for transfers between devices: 70.2 us -> 43.6 us
  starting transfers between devices: 35.8 us -> 47.4 us
  Pallas kernels: 36.1 us -> 44.2 us
  local copies, waits for them, and re-layouts: 16.4 us -> 14.1 us
    ppermute x23 -> x24, waiting for transfers between devices: 61.4 us -> 29.6 us  [swap(): return lax.ppermute(x, 'tp', [(i, i ^ bit) for i in range(count)])]
    all_to_all x4 -> x6, starting transfers between devices: 23.4 us -> 34 us  [exchange(): return lax.all_to_all(x, 'seq', split_axis=0, concat_axis=0, tiled=True)]
    all_to_all x4 -> x6, waiting for transfers between devices: 8.85 us -> 14 us  [exchange(): return lax.all_to_all(x, 'seq', split_axis=0, concat_axis=0, tiled=True)]
    pallas_call x2, Pallas kernels: 11.9 us -> 16.4 us  [backward(): pl.pallas_call(backward_kernel, grid=(steps,), out_shape=(shape,) * 2 + (...]
    unnamed x43 -> x53, local copies, waits for them, and re-layouts: 16.3 us -> 14.1 us
    pallas_call x2, Pallas kernels: 11.6 us -> 13.3 us  [forward(): pl.pallas_call(forward_kernel, grid=(steps,), out_shape=(jax.ShapeDtypeSt...]
    ppermute x23 -> x24, starting transfers between devices: 12.4 us -> 13.5 us  [swap(): return lax.ppermute(x, 'tp', [(i, i ^ bit) for i in range(count)])]
  transfers between devices with their start and end apart: 27 -> 30, of which waited for: 21 -> 18; matrix products, arithmetic and copies ran while one was open for 0% -> 0% of each run, Pallas kernels for 21% -> 26%
where the time goes in v5:
time: 151 us; the launch traced here: 150 us
  starting transfers between devices  47.4 us (31%)
  Pallas kernels  44.2 us (29%)
  waiting for transfers between devices  43.6 us (29%)
  local copies, waits for them, and re-layouts  14.1 us (9%)
    all_to_all x6, starting transfers between devices, exchange(): return lax.all_to_all(x, 'seq', split_axis=0, concat_axis=0, tiled=True)  34 us
    ppermute x24, waiting for transfers between devices, swap(): return lax.ppermute(x, 'tp', [(i, i ^ bit) for i in range(count)])  29.6 us
    pallas_call x2, Pallas kernels, backward(): pl.pallas_call(backward_kernel, grid=(steps,), out_shape=(shape,) * 2 + (...  16.4 us
    unnamed x53, local copies, waits for them, and re-layouts  14.1 us
    all_to_all x6, waiting for transfers between devices, exchange(): return lax.all_to_all(x, 'seq', split_axis=0, concat_axis=0, tiled=True)  14 us
    ppermute x24, starting transfers between devices, swap(): return lax.ppermute(x, 'tp', [(i, i ^ bit) for i in range(count)])  13.5 us
    pallas_call x2, Pallas kernels, forward(): pl.pallas_call(forward_kernel, grid=(steps,), out_shape=(jax.ShapeDtypeSt...  13.3 us
    pallas_call x1, Pallas kernels, head_grads(): pl.pallas_call(head_grads_kernel, out_shape=jax.ShapeDtypeStruct((CLUSTER...  4.43 us
  transfers between devices with their start and end apart: 30, of which 18 were waited for; matrix products, arithmetic and copies ran while one was open for 0% of the time, Pallas kernels for 26%

profile of v5, /device:TPU:0, one launch (start us, length us, event | category | flops | bytes accessed | tf_op | source)
XLA Modules:
  0.0 150.2 jit_solution(10412389864921298858)
XLA Ops:
  0.6 0.8 copy.10.ids_col
  1.5 1.0 copy-done.17
  2.5 1.7 %place.1 = (s32[512,1]{1,0:T(8,128)S(1)}, s32[1,512]{1,0:T(1,128)S(1)}, bf16[8,64,512]{2,1,0:T(8,128)(2,1)}, bf16[8,64,512]{2,1,0:T(8,128)(2,1)S(1)}) custom-call(s32[512,1]{1,0:T(8,128)S(1)} %copy.10.ids_col, bf16[512,512]{1,0:T(8,128)(2,1)S(1)} %copy-done.17), custom_call_target="tpu_custom_call" | custom-call | flops 1000000000 | bytes 1048576 | tf_op jit(solution)/shard_map/place/pallas_call | solution.py:82
  4.2 0.8 copy-done.12
  5.0 0.7 copy-done.23
  5.7 7.3 %all-to-all-start = ((bf16[8,64,512]{2,1,0:T(8,128)(2,1)}), bf16[8,64,512]{2,1,0:T(8,128)(2,1)S(1)}, u32[]{:S(2)}, u32[]{:S(2)}) async-start(bf16[8,64,512]{2,1,0:T(8,128)(2,1)} %get-tuple-element.41), calls=%async_computation | async-start | bytes 1048576 | tf_op jit(solution)/shard_map/all_to_all | solution.py:45
  13.0 1.5 collective-permute-start.7
  14.5 13.0 %all-to-all-done.x0 = bf16[8,64,512]{2,1,0:T(8,128)(2,1)S(1)} async-done(((bf16[8,64,512]{2,1,0:T(8,128)(2,1)}), bf16[8,64,512]{2,1,0:T(8,128)(2,1)S(1)}, u32[]{:S(2)}, u32[]{:S(2)}) %all-to-all-start) | async-done | bytes 524320 | tf_op jit(solution)/shard_map/all_to_all | solution.py:45
  27.5 3.6 %all-to-all-start.1 = ((bf16[8,64,512]{2,1,0:T(8,128)(2,1)}), bf16[8,64,512]{2,1,0:T(8,128)(2,1)S(1)}, u32[]{:S(2)}, u32[]{:S(2)}) async-start(bf16[8,64,512]{2,1,0:T(8,128)(2,1)} %copy-done.12), calls=%async_computation.1 | async-start | bytes 1048576 | tf_op jit(solution)/shard_map/all_to_all | solution.py:45
  31.1 0.5 collective-permute-start.8
  31.6 1.5 collective-permute-start.3
  33.1 0.2 collective-permute-done.6.a1
  33.4 0.7 collective-permute-done.8.a3
  34.1 4.4 %head_grads.1 = bf16[1024,512]{1,0:T(8,128)(2,1)} custom-call(s32[4]{0:T(128)S(1)} %iota_xor_fusion.blk, bf16[512,512]{1,0:T(8,128)(2,1)} %a0.1, bf16[512,512]{1,0:T(8,128)(2,1)} %collective-permute-done.6.a1, bf16[512,512]{1,0:T(8,128)(2,1)} %collective-permute-done.7.a2, bf16[512,512]{1,0:T(8,128)(2,1)} %collective-permute-done.8.a3, ...), custom_call_target="tpu_custom_call" | custom-call | flops 1000000000 | bytes 1048576 | tf_op jit(solution)/shard_map/head_grads/pallas_call | solution.py:108
  38.6 7.1 %collective-permute-done.3.x2 = bf16[8,64,512]{2,1,0:T(8,128)(2,1)} collective-permute-done((bf16[8,64,512]{2,1,0:T(8,128)(2,1)S(1)}, bf16[8,64,512]{2,1,0:T(8,128)(2,1)}, u32[]{:S(2)}, u32[]{:S(2)}) %collective-permute-start.3) | collective-permute-done | bytes 524320 | tf_op jit(solution)/shard_map/ppermute | solution.py:41
  45.6 0.1 all-to-all-done.1.x0
  45.8 5.9 %all-to-all-start.2 = ((bf16[8,128,512]{2,1,0:T(8,128)(2,1)}), bf16[8,128,512]{2,1,0:T(8,128)(2,1)}, u32[]{:S(2)}, u32[]{:S(2)}) async-start(bf16[8,128,512]{2,1,0:T(8,128)(2,1)} %bitcast), calls=%async_computation.2 | async-start | bytes 2097152 | tf_op jit(solution)/shard_map/all_to_all | solution.py:45
  51.6 0.5 collective-permute-start.4
  52.1 1.5 collective-permute-start.1
  53.6 0.9 collective-permute-done.4.x3
  54.5 1.6 %copy-done.1 = bf16[2048,512]{1,0:T(8,128)(2,1)S(1)} copy-done((bf16[2048,512]{1,0:T(8,128)(2,1)S(1)}, bf16[2048,512]{1,0:T(8,128)(2,1)}, u32[]{:S(2)}) %copy-start.1) | copy-done | bytes 2097176
  56.1 1.6 %copy-done.2 = bf16[2048,512]{1,0:T(8,128)(2,1)S(1)} copy-done((bf16[2048,512]{1,0:T(8,128)(2,1)S(1)}, bf16[2048,512]{1,0:T(8,128)(2,1)}, u32[]{:S(2)}) %copy-start.2) | copy-done | bytes 2097176
  57.7 6.8 %forward.2 = (bf16[8,128,512]{2,1,0:T(8,128)(2,1)}, bf16[8,64,1536]{2,1,0:T(8,128)(2,1)S(1)}, f32[2,2,4,128,128]{4,3,2,1,0:T(8,128)S(1)}) custom-call(s32[4]{0:T(128)S(1)} %iota_xor_fusion.blk, bf16[8,64,512]{2,1,0:T(8,128)(2,1)S(1)} %all-to-all-done.x0, bf16[8,64,512]{2,1,0:T(8,128)(2,1)S(1)} %collective-permute-done.2.x1, ...), custom_call_target="tpu_custom_call" | custom-call | flops 1000000000 | bytes 1048576 | tf_op jit(solution)/shard_map/forward/pallas_call | solution.py:272
  64.5 1.1 copy-done.6
  65.7 1.0 copy-done.9
  66.7 0.1 collective-permute-start.5
  66.8 1.8 %collective-permute-done.5.x3 = bf16[8,64,512]{2,1,0:T(8,128)(2,1)S(1)} collective-permute-done((bf16[8,64,512]{2,1,0:T(8,128)(2,1)S(1)}, bf16[8,64,512]{2,1,0:T(8,128)(2,1)S(1)}, u32[]{:S(2)}, u32[]{:S(2)}) %collective-permute-start.5) | collective-permute-done | bytes 524320 | tf_op jit(solution)/shard_map/ppermute | solution.py:41
  68.6 6.5 %forward.3 = (bf16[8,128,512]{2,1,0:T(8,128)(2,1)}, bf16[8,64,1536]{2,1,0:T(8,128)(2,1)S(1)}, f32[2,2,4,128,128]{4,3,2,1,0:T(8,128)S(1)}) custom-call(s32[4]{0:T(128)S(1)} %iota_xor_fusion.blk, bf16[8,64,512]{2,1,0:T(8,128)(2,1)S(1)} %all-to-all-done.1.x0, bf16[8,64,512]{2,1,0:T(8,128)(2,1)S(1)} %collective-permute-done.x1, ...), custom_call_target="tpu_custom_call", output_to_operand_aliasing={{0}: (8, {})} | custom-call | flops 1000000000 | bytes 1048576 | tf_op jit(solution)/shard_map/forward/pallas_call | solution.py:272
  75.0 1.2 copy-done.5
  76.2 1.0 copy-done.7
  77.2 6.1 %all-to-all-start.3 = ((bf16[8,128,512]{2,1,0:T(8,128)(2,1)}), bf16[8,128,512]{2,1,0:T(8,128)(2,1)S(1)}, u32[]{:S(2)}, u32[]{:S(2)}) async-start(bf16[8,128,512]{2,1,0:T(8,128)(2,1)} %get-tuple-element.48), calls=%async_computation.3 | async-start | bytes 2097152 | tf_op jit(solution)/shard_map/all_to_all | solution.py:45
  83.3 8.2 %backward.2 = (bf16[8,64,512]{2,1,0:T(8,128)(2,1)S(1)}, bf16[8,64,512]{2,1,0:T(8,128)(2,1)S(1)}, bf16[4,64,512]{2,1,0:T(8,128)(2,1)S(1)}, bf16[4,64,512]{2,1,0:T...) custom-call(s32[4]{0:T(128)S(1)} %iota_xor_fusion.blk, ...), custom_call_target="tpu_custom_call" | custom-call | flops 1000000000 | bytes 1048576 | tf_op jit(solution)/shard_map/backward/pallas_call | solution.py:305
  91.6 0.5 collective-permute-start.17
  92.1 1.0 collective-permute-done.16.refs_1_
  93.2 0.4 collective-permute-done.17.refs_2_
  93.7 1.6 %collective-permute-start.18 = (bf16[8,64,512]{2,1,0:T(8,128)(2,1)S(1)}, bf16[8,64,512]{2,1,0:T(8,128)(2,1)S(1)}, u32[]{:S(2)}, u32[]{:S(2)}) collective-permute-start(bf16[8,64,512]{2,1,0:T(8,128)(2,1)S(1)} %add.8), channel_id=1, source_target_pairs={{0,2},{1,3},{2,0},{3,1},{4,6},{5,7},{6,4},{7,5},{8,10},{9,11},{10,... | collective-permute-start | bytes 1572872 | tf_op jit(solution)/shard_map/ppermute | solution.py:41
  95.3 8.2 %backward.3 = (bf16[8,64,512]{2,1,0:T(8,128)(2,1)S(1)}, bf16[8,64,512]{2,1,0:T(8,128)(2,1)S(1)}, bf16[4,64,512]{2,1,0:T(8,128)(2,1)S(1)}, bf16[4,64,512]{2,1,0:T...) custom-call(s32[4]{0:T(128)S(1)} %iota_xor_fusion.blk, ...), custom_call_target="tpu_custom_call" | custom-call | flops 1000000000 | bytes 1048576 | tf_op jit(solution)/shard_map/backward/pallas_call | solution.py:305
  103.5 0.5 collective-permute-start.20
  104.1 0.4 collective-permute-start.15
  104.5 0.5 collective-permute-done.19.refs_1_
  105.1 0.4 collective-permute-done.20.refs_2_
  105.6 0.8 copy-done.11
  106.4 1.3 collective-permute-done.18.refs_3_
  107.7 1.0 add.9
  108.7 0.7 all-to-all-done.3.mixed
  109.4 5.3 %all-to-all-start.4 = ((bf16[8,64,512]{2,1,0:T(8,128)(2,1)}), bf16[8,64,512]{2,1,0:T(8,128)(2,1)}, u32[]{:S(2)}, u32[]{:S(2)}) async-start(bf16[8,64,512]{2,1,0:T(8,128)(2,1)} %add.9), calls=%async_computation.4 | async-start | bytes 1048576 | tf_op jit(solution)/shard_map/all_to_all | solution.py:45
  114.7 1.6 %collective-permute-start.23 = (bf16[8,64,512]{2,1,0:T(8,128)(2,1)}, bf16[8,64,512]{2,1,0:T(8,128)(2,1)S(1)}, u32[]{:S(2)}, u32[]{:S(2)}) collective-permute-start(bf16[8,64,512]{2,1,0:T(8,128)(2,1)} %copy-done.11), channel_id=1, source_target_pairs={{0,2},{1,3},{2,0},{3,1},{4,6},{5,7},{6,4},{7,5},{8,10},{9,11},{10,... | collective-permute-start | bytes 1572872 | tf_op jit(solution)/shard_map/ppermute | solution.py:41
  116.3 0.5 collective-permute-start.22
  116.8 0.9 copy-done.24
  117.7 2.4 %project_out.1 = (bf16[512,512]{1,0:T(8,128)(2,1)S(1)}, bf16[512,512]{1,0:T(8,128)(2,1)S(1)}, bf16[256,512]{1,0:T(8,128)(2,1)S(1)}, bf16[256,512]{1,0:T(8,128)(2...) custom-call(s32[4]{0:T(128)S(1)} %iota_xor_fusion.blk, s32[512,1]{1,0:T(8,128)S(1)} %copy-done.24, ...), custom_call_target="tpu_custom_call" | custom-call | flops 1000000000 | bytes 1048576 | tf_op jit(solution)/shard_map/project_out/pallas_call | solution.py:436
  120.1 0.7 copy-done.19
  120.8 0.7 copy-done.21
  121.5 0.5 collective-permute-start.12
  122.0 5.8 %collective-permute-done.23.refs_3_ = bf16[8,64,512]{2,1,0:T(8,128)(2,1)S(1)} collective-permute-done((bf16[8,64,512]{2,1,0:T(8,128)(2,1)}, bf16[8,64,512]{2,1,0:T(8,128)(2,1)S(1)}, u32[]{:S(2)}, u32[]{:S(2)}) %collective-permute-start.23) | collective-permute-done | bytes 524320 | tf_op jit(solution)/shard_map/ppermute | solution.py:41
  127.8 1.0 add.11
  129.0 5.8 %all-to-all-start.5 = ((bf16[8,64,512]{2,1,0:T(8,128)(2,1)}), bf16[8,64,512]{2,1,0:T(8,128)(2,1)S(1)}, u32[]{:S(2)}, u32[]{:S(2)}) async-start(bf16[8,64,512]{2,1,0:T(8,128)(2,1)} %add.11), calls=%async_computation.5 | async-start | bytes 1048576 | tf_op jit(solution)/shard_map/all_to_all | solution.py:45
  134.8 1.5 %collective-permute-start.13 = (bf16[512,512]{1,0:T(8,128)(2,1)S(1)}, bf16[512,512]{1,0:T(8,128)(2,1)S(1)}, u32[]{:S(2)}, u32[]{:S(2)}) collective-permute-start(bf16[512,512]{1,0:T(8,128)(2,1)S(1)} %add.6), channel_id=1, source_target_pairs={{0,2},{1,3},{2,0},{3,1},{4,6},{5,7},{6,4},{7,5},{8,10},{9,11},{10,... | collective-permute-start | bytes 1572872 | tf_op jit(solution)/shard_map/ppermute | solution.py:41
  136.3 0.5 collective-permute-start.9
  136.8 1.0 collective-permute-done.10.refs_2_
  137.8 0.4 collective-permute-done.9.refs_1_
  138.2 8.1 %collective-permute-done.13.refs_3_ = bf16[512,512]{1,0:T(8,128)(2,1)S(1)} collective-permute-done((bf16[512,512]{1,0:T(8,128)(2,1)S(1)}, bf16[512,512]{1,0:T(8,128)(2,1)S(1)}, u32[]{:S(2)}, u32[]{:S(2)}) %collective-permute-start.13) | collective-permute-done | bytes 524320 | tf_op jit(solution)/shard_map/ppermute | solution.py:41
  146.3 1.0 add.7
  147.2 0.2 all-to-all-done.5.refs_1_
  147.4 2.8 %to_tokens.1 = f32[512,512]{1,0:T(8,128)} custom-call(s32[512,1]{1,0:T(8,128)S(1)} %copy-done.25, bf16[8,64,512]{2,1,0:T(8,128)(2,1)} %all-to-all-done.4.refs_0_, bf16[8,64,512]{2,1,0:T(8,128)(2,1)S(1)} %all-to-all-done.5.refs_1_), custom_call_target="tpu_custom_call" | custom-call | flops 1000000000 | bytes 1048576 | tf_op jit(solution)/shard_map/to_tokens/pallas_call | solution.py:453
  (64 shorter events, 0.7 us)
Async XLA Ops:
  1.5 1.0 copy-start.17
  2.5 31.6 %copy-start.3 = (bf16[512,2048]{1,0:T(8,128)(2,1)S(1)}, bf16[512,2048]{1,0:T(8,128)(2,1)}, u32[]{:S(2)}) copy-start(bf16[512,2048]{1,0:T(8,128)(2,1)} %w_out.3) | copy-start | bytes 6291460
  4.2 0.8 copy-start.12
  5.0 0.7 copy-start.23
  5.7 21.8 %all-to-all-start = ((bf16[8,64,512]{2,1,0:T(8,128)(2,1)}), bf16[8,64,512]{2,1,0:T(8,128)(2,1)S(1)}, u32[]{:S(2)}, u32[]{:S(2)}) async-start(bf16[8,64,512]{2,1,0:T(8,128)(2,1)} %get-tuple-element.41), calls=%async_computation | async-start | bytes 1048576 | tf_op jit(solution)/shard_map/all_to_all | solution.py:45
  13.0 18.1 %collective-permute-start.7 = (bf16[512,512]{1,0:T(8,128)(2,1)}, bf16[512,512]{1,0:T(8,128)(2,1)}, u32[]{:S(2)}, u32[]{:S(2)}) collective-permute-start(bf16[512,512]{1,0:T(8,128)(2,1)} %a0.1), channel_id=1, source_target_pairs={{0,2},{1,3},{2,0},{3,1},{4,6},{5,7},{6,4},{7,5},{8,10},{9,11},{10,... | collective-permute-start | bytes 1572872 | tf_op jit(solution)/shard_map/ppermute | solution.py:41
  27.5 18.3 %all-to-all-start.1 = ((bf16[8,64,512]{2,1,0:T(8,128)(2,1)}), bf16[8,64,512]{2,1,0:T(8,128)(2,1)S(1)}, u32[]{:S(2)}, u32[]{:S(2)}) async-start(bf16[8,64,512]{2,1,0:T(8,128)(2,1)} %copy-done.12), calls=%async_computation.1 | async-start | bytes 1048576 | tf_op jit(solution)/shard_map/all_to_all | solution.py:45
  31.1 2.3 %collective-permute-start.6 = (bf16[512,512]{1,0:T(8,128)(2,1)}, bf16[512,512]{1,0:T(8,128)(2,1)}, u32[]{:S(2)}, u32[]{:S(2)}) collective-permute-start(bf16[512,512]{1,0:T(8,128)(2,1)} %a0.1), channel_id=1, source_target_pairs={{0,1},{1,0},{2,3},{3,2},{4,5},{5,4},{6,7},{7,6},{8,9},{9,8},{10,11... | collective-permute-start | bytes 1572872 | tf_op jit(solution)/shard_map/ppermute | solution.py:41
  31.1 3.0 %collective-permute-start.8 = (bf16[512,512]{1,0:T(8,128)(2,1)}, bf16[512,512]{1,0:T(8,128)(2,1)}, u32[]{:S(2)}, u32[]{:S(2)}) collective-permute-start(bf16[512,512]{1,0:T(8,128)(2,1)} %collective-permute-done.7.a2), channel_id=1, source_target_pairs={{0,1},{1,0},{2,3},{3,2},{4,5},{5,4},{6,7},{7,6},{8,9},{9,8},{10,11... | collective-permute-start | bytes 1572872 | tf_op jit(solution)/shard_map/ppermute | solution.py:41
  31.6 14.0 %collective-permute-start.3 = (bf16[8,64,512]{2,1,0:T(8,128)(2,1)S(1)}, bf16[8,64,512]{2,1,0:T(8,128)(2,1)}, u32[]{:S(2)}, u32[]{:S(2)}) collective-permute-start(bf16[8,64,512]{2,1,0:T(8,128)(2,1)S(1)} %all-to-all-done.x0), channel_id=1, source_target_pairs={{0,2},{1,3},{2,0},{3,1},{4,6},{5,7},{6,4},{7,5},{8,10},{9,11},{10,... | collective-permute-start | bytes 1572872 | tf_op jit(solution)/shard_map/ppermute | solution.py:41
  38.5 16.0 %copy-start = (bf16[2048,512]{1,0:T(8,128)(2,1)S(1)}, bf16[2048,512]{1,0:T(8,128)(2,1)}, u32[]{:S(2)}) copy-start(bf16[2048,512]{1,0:T(8,128)(2,1)} %wq.7) | copy-start | bytes 6291460
  45.8 31.4 %all-to-all-start.2 = ((bf16[8,128,512]{2,1,0:T(8,128)(2,1)}), bf16[8,128,512]{2,1,0:T(8,128)(2,1)}, u32[]{:S(2)}, u32[]{:S(2)}) async-start(bf16[8,128,512]{2,1,0:T(8,128)(2,1)} %bitcast), calls=%async_computation.2 | async-start | bytes 2097152 | tf_op jit(solution)/shard_map/all_to_all | solution.py:45
  51.6 2.0 %collective-permute-start.2 = (bf16[8,64,512]{2,1,0:T(8,128)(2,1)S(1)}, bf16[8,64,512]{2,1,0:T(8,128)(2,1)S(1)}, u32[]{:S(2)}, u32[]{:S(2)}) collective-permute-start(bf16[8,64,512]{2,1,0:T(8,128)(2,1)S(1)} %all-to-all-done.x0), channel_id=1, source_target_pairs={{0,1},{1,0},{2,3},{3,2},{4,5},{5,4},{6,7},{7,6},{8,9},{9,8},{10,11... | collective-permute-start | bytes 1572872 | tf_op jit(solution)/shard_map/ppermute | solution.py:41
  51.6 2.9 %collective-permute-start.4 = (bf16[8,64,512]{2,1,0:T(8,128)(2,1)}, bf16[8,64,512]{2,1,0:T(8,128)(2,1)S(1)}, u32[]{:S(2)}, u32[]{:S(2)}) collective-permute-start(bf16[8,64,512]{2,1,0:T(8,128)(2,1)} %collective-permute-done.3.x2), channel_id=1, source_target_pairs={{0,1},{1,0},{2,3},{3,2},{4,5},{5,4},{6,7},{7,6},{8,9},{9,8},{10,11... | collective-permute-start | bytes 1572872 | tf_op jit(solution)/shard_map/ppermute | solution.py:41
  52.1 14.5 %collective-permute-start.1 = (bf16[8,64,512]{2,1,0:T(8,128)(2,1)S(1)}, bf16[8,64,512]{2,1,0:T(8,128)(2,1)S(1)}, u32[]{:S(2)}, u32[]{:S(2)}) collective-permute-start(bf16[8,64,512]{2,1,0:T(8,128)(2,1)S(1)} %all-to-all-done.1.x0), channel_id=1, source_target_pairs={{0,2},{1,3},{2,0},{3,1},{4,6},{5,7},{6,4},{7,5},{8,10},{9,11},{10,... | collective-permute-start | bytes 1572872 | tf_op jit(solution)/shard_map/ppermute | solution.py:41
  53.6 13.2 %collective-permute-start = (bf16[8,64,512]{2,1,0:T(8,128)(2,1)S(1)}, bf16[8,64,512]{2,1,0:T(8,128)(2,1)S(1)}, u32[]{:S(2)}, u32[]{:S(2)}) collective-permute-start(bf16[8,64,512]{2,1,0:T(8,128)(2,1)S(1)} %all-to-all-done.1.x0), channel_id=1, source_target_pairs={{0,1},{1,0},{2,3},{3,2},{4,5},{5,4},{6,7},{7,6},{8,9},{9,8},{10,11... | collective-permute-start | bytes 1572872 | tf_op jit(solution)/shard_map/ppermute | solution.py:41
  54.5 1.6 %copy-start.1 = (bf16[2048,512]{1,0:T(8,128)(2,1)S(1)}, bf16[2048,512]{1,0:T(8,128)(2,1)}, u32[]{:S(2)}) copy-start(bf16[2048,512]{1,0:T(8,128)(2,1)} %wk.7) | copy-start | bytes 6291460
  56.1 1.6 %copy-start.2 = (bf16[2048,512]{1,0:T(8,128)(2,1)S(1)}, bf16[2048,512]{1,0:T(8,128)(2,1)}, u32[]{:S(2)}) copy-start(bf16[2048,512]{1,0:T(8,128)(2,1)} %wv.7) | copy-start | bytes 6291460
  64.5 1.1 copy-start.6
  65.7 1.0 copy-start.9
  66.7 1.9 %collective-permute-start.5 = (bf16[8,64,512]{2,1,0:T(8,128)(2,1)S(1)}, bf16[8,64,512]{2,1,0:T(8,128)(2,1)S(1)}, u32[]{:S(2)}, u32[]{:S(2)}) collective-permute-start(bf16[8,64,512]{2,1,0:T(8,128)(2,1)S(1)} %collective-permute-done.1.x2), channel_id=1, source_target_pairs={{0,1},{1,0},{2,3},{3,2},{4,5},{5,4},{6,7},{7,6},{8,9},{9,8},{10,11... | collective-permute-start | bytes 1572872 | tf_op jit(solution)/shard_map/ppermute | solution.py:41
  75.0 1.2 copy-start.5
  76.2 1.0 copy-start.7
  77.2 6.1 %copy-start.10 = (f32[2,2,4,128,128]{4,3,2,1,0:T(8,128)S(1)}, f32[2,2,4,128,128]{4,3,2,1,0:T(8,128)}, u32[]{:S(2)}) copy-start(f32[2,2,4,128,128]{4,3,2,1,0:T(8,128)} %copy-done.9) | copy-start | bytes 3145732
  77.2 32.2 %all-to-all-start.3 = ((bf16[8,128,512]{2,1,0:T(8,128)(2,1)}), bf16[8,128,512]{2,1,0:T(8,128)(2,1)S(1)}, u32[]{:S(2)}, u32[]{:S(2)}) async-start(bf16[8,128,512]{2,1,0:T(8,128)(2,1)} %get-tuple-element.48), calls=%async_computation.3 | async-start | bytes 2097152 | tf_op jit(solution)/shard_map/all_to_all | solution.py:45
  91.5 3.7 %copy-start.8 = (f32[2,2,4,128,128]{4,3,2,1,0:T(8,128)S(1)}, f32[2,2,4,128,128]{4,3,2,1,0:T(8,128)}, u32[]{:S(2)}) copy-start(f32[2,2,4,128,128]{4,3,2,1,0:T(8,128)} %copy-done.7) | copy-start | bytes 3145732
  91.6 1.6 %collective-permute-start.16 = (bf16[4,64,512]{2,1,0:T(8,128)(2,1)S(1)}, bf16[4,64,512]{2,1,0:T(8,128)(2,1)S(1)}, u32[]{:S(2)}, u32[]{:S(2)}) collective-permute-start(bf16[4,64,512]{2,1,0:T(8,128)(2,1)S(1)} %get-tuple-element.62), channel_id=1, source_target_pairs={{0,1},{1,0},{2,3},{3,2},{4,5},{5,4},{6,7},{7,6},{8,9},{9,8},{10,11... | collective-permute-start | bytes 786440 | tf_op jit(solution)/shard_map/ppermute | solution.py:41
  91.6 1.9 %collective-permute-start.17 = (bf16[4,64,512]{2,1,0:T(8,128)(2,1)S(1)}, bf16[4,64,512]{2,1,0:T(8,128)(2,1)S(1)}, u32[]{:S(2)}, u32[]{:S(2)}) collective-permute-start(bf16[4,64,512]{2,1,0:T(8,128)(2,1)S(1)} %get-tuple-element.63), channel_id=1, source_target_pairs={{0,1},{1,0},{2,3},{3,2},{4,5},{5,4},{6,7},{7,6},{8,9},{9,8},{10,11... | collective-permute-start | bytes 786440 | tf_op jit(solution)/shard_map/ppermute | solution.py:41
  93.7 14.0 %collective-permute-start.18 = (bf16[8,64,512]{2,1,0:T(8,128)(2,1)S(1)}, bf16[8,64,512]{2,1,0:T(8,128)(2,1)S(1)}, u32[]{:S(2)}, u32[]{:S(2)}) collective-permute-start(bf16[8,64,512]{2,1,0:T(8,128)(2,1)S(1)} %add.8), channel_id=1, source_target_pairs={{0,2},{1,3},{2,0},{3,1},{4,6},{5,7},{6,4},{7,5},{8,10},{9,11},{10,... | collective-permute-start | bytes 1572872 | tf_op jit(solution)/shard_map/ppermute | solution.py:41
  103.4 4.3 %copy-start.13 = (bf16[8,64,512]{2,1,0:T(8,128)(2,1)}, bf16[8,64,512]{2,1,0:T(8,128)(2,1)S(1)}, u32[]{:S(2)}) copy-start(bf16[8,64,512]{2,1,0:T(8,128)(2,1)S(1)} %get-tuple-element.71.refs_0_) | copy-start | bytes 1572868
  103.4 4.3 %copy-start.18 = (bf16[4,64,512]{2,1,0:T(8,128)(2,1)}, bf16[4,64,512]{2,1,0:T(8,128)(2,1)S(1)}, u32[]{:S(2)}) copy-start(bf16[4,64,512]{2,1,0:T(8,128)(2,1)S(1)} %get-tuple-element.72) | copy-start | bytes 786436
  103.5 1.6 %collective-permute-start.19 = (bf16[4,64,512]{2,1,0:T(8,128)(2,1)S(1)}, bf16[4,64,512]{2,1,0:T(8,128)(2,1)S(1)}, u32[]{:S(2)}, u32[]{:S(2)}) collective-permute-start(bf16[4,64,512]{2,1,0:T(8,128)(2,1)S(1)} %get-tuple-element.68), channel_id=1, source_target_pairs={{0,1},{1,0},{2,3},{3,2},{4,5},{5,4},{6,7},{7,6},{8,9},{9,8},{10,11... | collective-permute-start | bytes 786440 | tf_op jit(solution)/shard_map/ppermute | solution.py:41
  103.5 1.9 %collective-permute-start.20 = (bf16[4,64,512]{2,1,0:T(8,128)(2,1)S(1)}, bf16[4,64,512]{2,1,0:T(8,128)(2,1)S(1)}, u32[]{:S(2)}, u32[]{:S(2)}) collective-permute-start(bf16[4,64,512]{2,1,0:T(8,128)(2,1)S(1)} %get-tuple-element.69), channel_id=1, source_target_pairs={{0,1},{1,0},{2,3},{3,2},{4,5},{5,4},{6,7},{7,6},{8,9},{9,8},{10,11... | collective-permute-start | bytes 786440 | tf_op jit(solution)/shard_map/ppermute | solution.py:41
  104.0 2.3 %collective-permute-start.14 = (bf16[4,64,512]{2,1,0:T(8,128)(2,1)S(1)}, bf16[4,64,512]{2,1,0:T(8,128)(2,1)S(1)}, u32[]{:S(2)}, u32[]{:S(2)}) collective-permute-start(bf16[4,64,512]{2,1,0:T(8,128)(2,1)S(1)} %get-tuple-element.59), channel_id=1, source_target_pairs={{0,1},{1,0},{2,3},{3,2},{4,5},{5,4},{6,7},{7,6},{8,9},{9,8},{10,11... | collective-permute-start | bytes 786440 | tf_op jit(solution)/shard_map/ppermute | solution.py:41
  104.1 2.3 %collective-permute-start.15 = (bf16[4,64,512]{2,1,0:T(8,128)(2,1)S(1)}, bf16[4,64,512]{2,1,0:T(8,128)(2,1)S(1)}, u32[]{:S(2)}, u32[]{:S(2)}) collective-permute-start(bf16[4,64,512]{2,1,0:T(8,128)(2,1)S(1)} %get-tuple-element.60), channel_id=1, source_target_pairs={{0,1},{1,0},{2,3},{3,2},{4,5},{5,4},{6,7},{7,6},{8,9},{9,8},{10,11... | collective-permute-start | bytes 786440 | tf_op jit(solution)/shard_map/ppermute | solution.py:41
  105.4 11.3 %copy-start.4 = (bf16[512,2048]{1,0:T(8,128)(2,1)S(1)}, bf16[512,2048]{1,0:T(8,128)(2,1)}, u32[]{:S(2)}) copy-start(bf16[512,2048]{1,0:T(8,128)(2,1)} %w_out.3) | copy-start | bytes 6291460
  105.6 0.8 copy-start.11
  109.4 19.6 %all-to-all-start.4 = ((bf16[8,64,512]{2,1,0:T(8,128)(2,1)}), bf16[8,64,512]{2,1,0:T(8,128)(2,1)}, u32[]{:S(2)}, u32[]{:S(2)}) async-start(bf16[8,64,512]{2,1,0:T(8,128)(2,1)} %add.9), calls=%async_computation.4 | async-start | bytes 1048576 | tf_op jit(solution)/shard_map/all_to_all | solution.py:45
  114.7 13.1 %copy-start.14 = (bf16[8,64,512]{2,1,0:T(8,128)(2,1)S(1)}, bf16[8,64,512]{2,1,0:T(8,128)(2,1)}, u32[]{:S(2)}) copy-start(bf16[8,64,512]{2,1,0:T(8,128)(2,1)} %copy-done.13) | copy-start | bytes 1572868
  114.7 13.1 %collective-permute-start.23 = (bf16[8,64,512]{2,1,0:T(8,128)(2,1)}, bf16[8,64,512]{2,1,0:T(8,128)(2,1)S(1)}, u32[]{:S(2)}, u32[]{:S(2)}) collective-permute-start(bf16[8,64,512]{2,1,0:T(8,128)(2,1)} %copy-done.11), channel_id=1, source_target_pairs={{0,2},{1,3},{2,0},{3,1},{4,6},{5,7},{6,4},{7,5},{8,10},{9,11},{10,... | collective-permute-start | bytes 1572872 | tf_op jit(solution)/shard_map/ppermute | solution.py:41
  116.3 5.7 %collective-permute-start.21 = (bf16[4,64,512]{2,1,0:T(8,128)(2,1)}, bf16[4,64,512]{2,1,0:T(8,128)(2,1)S(1)}, u32[]{:S(2)}, u32[]{:S(2)}) collective-permute-start(bf16[4,64,512]{2,1,0:T(8,128)(2,1)} %copy-done.18), channel_id=1, source_target_pairs={{0,1},{1,0},{2,3},{3,2},{4,5},{5,4},{6,7},{7,6},{8,9},{9,8},{10,11... | collective-permute-start | bytes 786440 | tf_op jit(solution)/shard_map/ppermute | solution.py:41
  116.3 5.7 %collective-permute-start.22 = (bf16[4,64,512]{2,1,0:T(8,128)(2,1)S(1)}, bf16[4,64,512]{2,1,0:T(8,128)(2,1)S(1)}, u32[]{:S(2)}, u32[]{:S(2)}) collective-permute-start(bf16[4,64,512]{2,1,0:T(8,128)(2,1)S(1)} %get-tuple-element.73), channel_id=1, source_target_pairs={{0,1},{1,0},{2,3},{3,2},{4,5},{5,4},{6,7},{7,6},{8,9},{9,8},{10,11... | collective-permute-start | bytes 786440 | tf_op jit(solution)/shard_map/ppermute | solution.py:41
  116.8 1.0 copy-start.24
  120.1 0.7 copy-start.19
  120.8 0.7 copy-start.21
  121.5 7.3 %copy-start.15 = (bf16[512,512]{1,0:T(8,128)(2,1)}, bf16[512,512]{1,0:T(8,128)(2,1)S(1)}, u32[]{:S(2)}) copy-start(bf16[512,512]{1,0:T(8,128)(2,1)S(1)} %get-tuple-element.49.refs_0_) | copy-start | bytes 1572868
  121.5 7.3 %collective-permute-start.11 = (bf16[256,512]{1,0:T(8,128)(2,1)S(1)}, bf16[256,512]{1,0:T(8,128)(2,1)S(1)}, u32[]{:S(2)}, u32[]{:S(2)}) collective-permute-start(bf16[256,512]{1,0:T(8,128)(2,1)S(1)} %get-tuple-element.53), channel_id=1, source_target_pairs={{0,1},{1,0},{2,3},{3,2},{4,5},{5,4},{6,7},{7,6},{8,9},{9,8},{10,11... | collective-permute-start | bytes 786440 | tf_op jit(solution)/shard_map/ppermute | solution.py:41
  121.5 7.3 %collective-permute-start.12 = (bf16[256,512]{1,0:T(8,128)(2,1)S(1)}, bf16[256,512]{1,0:T(8,128)(2,1)S(1)}, u32[]{:S(2)}, u32[]{:S(2)}) collective-permute-start(bf16[256,512]{1,0:T(8,128)(2,1)S(1)} %get-tuple-element.54), channel_id=1, source_target_pairs={{0,1},{1,0},{2,3},{3,2},{4,5},{5,4},{6,7},{7,6},{8,9},{9,8},{10,11... | collective-permute-start | bytes 786440 | tf_op jit(solution)/shard_map/ppermute | solution.py:41
  127.8 8.5 %copy-start.22 = (bf16[256,512]{1,0:T(8,128)(2,1)S(1)}, bf16[256,512]{1,0:T(8,128)(2,1)}, u32[]{:S(2)}) copy-start(bf16[256,512]{1,0:T(8,128)(2,1)} %copy-done.21) | copy-start | bytes 786436
  127.8 8.5 %copy-start.20 = (bf16[256,512]{1,0:T(8,128)(2,1)S(1)}, bf16[256,512]{1,0:T(8,128)(2,1)}, u32[]{:S(2)}) copy-start(bf16[256,512]{1,0:T(8,128)(2,1)} %copy-done.19) | copy-start | bytes 786436
  128.8 17.4 %copy-start.16 = (bf16[512,512]{1,0:T(8,128)(2,1)S(1)}, bf16[512,512]{1,0:T(8,128)(2,1)}, u32[]{:S(2)}) copy-start(bf16[512,512]{1,0:T(8,128)(2,1)} %copy-done.15) | copy-start | bytes 1572868
  128.8 18.6 %copy-start.25 = (s32[512,1]{1,0:T(8,128)S(1)}, s32[512,1]{1,0:T(8,128)}, u32[]{:S(2)}) copy-start(s32[512,1]{1,0:T(8,128)} %copy-done.23) | copy-start | bytes 6148
  129.0 18.4 %all-to-all-start.5 = ((bf16[8,64,512]{2,1,0:T(8,128)(2,1)}), bf16[8,64,512]{2,1,0:T(8,128)(2,1)S(1)}, u32[]{:S(2)}, u32[]{:S(2)}) async-start(bf16[8,64,512]{2,1,0:T(8,128)(2,1)} %add.11), calls=%async_computation.5 | async-start | bytes 1048576 | tf_op jit(solution)/shard_map/all_to_all | solution.py:45
  134.8 11.5 %collective-permute-start.13 = (bf16[512,512]{1,0:T(8,128)(2,1)S(1)}, bf16[512,512]{1,0:T(8,128)(2,1)S(1)}, u32[]{:S(2)}, u32[]{:S(2)}) collective-permute-start(bf16[512,512]{1,0:T(8,128)(2,1)S(1)} %add.6), channel_id=1, source_target_pairs={{0,2},{1,3},{2,0},{3,1},{4,6},{5,7},{6,4},{7,5},{8,10},{9,11},{10,... | collective-permute-start | bytes 1572872 | tf_op jit(solution)/shard_map/ppermute | solution.py:41
  136.3 1.5 %collective-permute-start.10 = (bf16[256,512]{1,0:T(8,128)(2,1)S(1)}, bf16[256,512]{1,0:T(8,128)(2,1)S(1)}, u32[]{:S(2)}, u32[]{:S(2)}) collective-permute-start(bf16[256,512]{1,0:T(8,128)(2,1)S(1)} %copy-done.22), channel_id=1, source_target_pairs={{0,1},{1,0},{2,3},{3,2},{4,5},{5,4},{6,7},{7,6},{8,9},{9,8},{10,11... | collective-permute-start | bytes 786440 | tf_op jit(solution)/shard_map/ppermute | solution.py:41
  136.3 1.9 %collective-permute-start.9 = (bf16[256,512]{1,0:T(8,128)(2,1)S(1)}, bf16[256,512]{1,0:T(8,128)(2,1)S(1)}, u32[]{:S(2)}, u32[]{:S(2)}) collective-permute-start(bf16[256,512]{1,0:T(8,128)(2,1)S(1)} %copy-done.20), channel_id=1, source_target_pairs={{0,1},{1,0},{2,3},{3,2},{4,5},{5,4},{6,7},{7,6},{8,9},{9,8},{10,11... | collective-permute-start | bytes 786440 | tf_op jit(solution)/shard_map/ppermute | solution.py:41

commit v6 on v5

--- a/solution.py
+++ b/solution.py
@@ -17,7 +17,7 @@
 TN = (((0,), (0,)), ((), ()))
 MB = 1024 * 1024
 CHUNKS = 2
-GRANT = 24 * MB
+GRANT = 50 * MB
 
 
 def cost(giga):
@@ -56,40 +56,57 @@
     return slot.reshape(owners * rows, tokens)
 
 
-def place_kernel(ids_col, x_ref, slot_col, slot_row, *outs):
-    tokens, width = x_ref.shape
+def put_rows(slot_row, x_ref, out, chunk, chunks):
+    tokens = x_ref.shape[0]
+    held = slots_of(out, tokens, chunk, chunks) == slot_row
+    chosen = jnp.where(held, 1.0, 0.0)
+    taken = jnp.sum(chosen, axis=1, keepdims=True)
+    value = dot(chosen.astype(jnp.bfloat16), x_ref[...])
+    first = iota(value.shape, 1) == 0
+    value = value + jnp.where(first & (taken == 0.0), EMPTY, 0.0)
+    out[...] = value.astype(jnp.bfloat16).reshape(out.shape)
+
+
+def place_kernel(chunks, ids_row, x_ref, slot_col, slot_row, out):
+    tokens = x_ref.shape[0]
     here, there = (iota((tokens, tokens), 0), iota((tokens, tokens), 1))
-    col = ids_col[...]
-    row = jnp.sum(jnp.where(here == there, col, 0), axis=0, keepdims=True)
+    row = ids_row[...]
+    col = jnp.sum(jnp.where(here == there, row, 0), axis=1, keepdims=True)
     same = col == row
     earlier = jnp.where(same & (there < here), 1.0, 0.0)
     later = jnp.where(same & (here < there), 1.0, 0.0)
     slot_col[...] = col * MOST + jnp.sum(earlier, axis=1, keepdims=True).astype(jnp.int32)
-    slot_row[...] = row * MOST + jnp.sum(later, axis=0, keepdims=True).astype(jnp.int32)
-    for c, out in enumerate(outs):
-        held = slots_of(out, tokens, c, len(outs)) == slot_row[...]
-        chosen = jnp.where(held, 1.0, 0.0)
-        taken = jnp.sum(chosen, axis=1, keepdims=True)
-        value = dot(chosen.astype(jnp.bfloat16), x_ref[...])
-        first = iota(value.shape, 1) == 0
-        value = value + jnp.where(first & (taken == 0.0), EMPTY, 0.0)
-        out[...] = value.astype(jnp.bfloat16).reshape(out.shape)
-
-
-def place(cluster, x, owners, rows, chunks):
+    rows = row * MOST + jnp.sum(later, axis=0, keepdims=True).astype(jnp.int32)
+    slot_row[...] = rows
+    put_rows(rows, x_ref, out, 0, chunks)
+
+
+def place_more_kernel(chunk, chunks, slot_row, x_ref, out):
+    put_rows(slot_row[...], x_ref, out, chunk, chunks)
+
+
+def place(ids_row, x, owners, rows, chunks):
     tokens = x.shape[0]
     piece = jax.ShapeDtypeStruct((owners, rows, x.shape[1]), jnp.bfloat16)
-    return pl.pallas_call(
-        place_kernel,
+    options = dict(
+        compiler_params=pltpu.CompilerParams(vmem_limit_bytes=60 * MB), cost_estimate=cost(1)
+    )
+    slot_col, slot_row, first = pl.pallas_call(
+        functools.partial(place_kernel, chunks),
         out_shape=(
             jax.ShapeDtypeStruct((tokens, 1), jnp.int32),
             jax.ShapeDtypeStruct((1, tokens), jnp.int32),
-        )
-        + (piece,) * chunks,
-        compiler_params=pltpu.CompilerParams(vmem_limit_bytes=GRANT),
-        cost_estimate=cost(1),
+            piece,
+        ),
         name="place",
-    )(cluster, x)
+        **options,
+    )(ids_row, x)
+    pieces = [first]
+    for c in range(1, chunks):
+        kernel = functools.partial(place_more_kernel, c, chunks)
+        more = pl.pallas_call(kernel, out_shape=piece, name="place_more", **options)
+        pieces.append(more(slot_row, x))
+    return (slot_col, slot_row, *pieces)
 
 
 def head_grads_kernel(blk, a0, a1, a2, a3, w_out, slot_row, out_ref):
@@ -111,7 +128,7 @@
         in_specs=[SMEM] + [VMEM] * 6,
         out_specs=VMEM,
         compiler_params=pltpu.CompilerParams(vmem_limit_bytes=GRANT),
-        cost_estimate=cost(1),
+        cost_estimate=cost(2),
         name="head_grads",
     )(blk, *parts, w_out, slot_row)
 
@@ -285,7 +302,7 @@
         ),
         input_output_aliases={} if mixed is None else {len(operands) - 1: 0},
         compiler_params=pltpu.CompilerParams(vmem_limit_bytes=40 * MB),
-        cost_estimate=cost(1),
+        cost_estimate=cost(2),
         name="forward",
     )(*operands)
 
@@ -317,8 +334,8 @@
         ],
         out_specs=(block,) * 2 + (half,) * 4,
         scratch_shapes=[pltpu.VMEM((sources, step, heads_width), jnp.bfloat16)] * 3,
-        compiler_params=pltpu.CompilerParams(vmem_limit_bytes=50 * MB),
-        cost_estimate=cost(1),
+        compiler_params=pltpu.CompilerParams(vmem_limit_bytes=GRANT),
+        cost_estimate=cost(2),
         name="backward",
     )(blk, saved, probs, grads, wq, wk, wv)
     return (outs[:2], outs[2:])
@@ -439,7 +456,7 @@
         in_specs=[SMEM] + [VMEM] * 3,
         out_specs=(VMEM,) * 6,
         compiler_params=pltpu.CompilerParams(vmem_limit_bytes=GRANT),
-        cost_estimate=cost(1),
+        cost_estimate=cost(2),
         name="project_out",
     )(blk, slot_col, w_out, mixed)
     return (outs[:2], outs[2:])
@@ -450,9 +467,16 @@
 
 
 def to_tokens(slot_col, parts):
+    tokens = slot_col.shape[0]
+    width = parts[0].shape[2]
+    block = tokens
     return pl.pallas_call(
         final_kernel,
-        out_shape=jax.ShapeDtypeStruct((slot_col.shape[0], parts[0].shape[2]), jnp.float32),
+        grid=(tokens // block,),
+        out_shape=jax.ShapeDtypeStruct((tokens, width), jnp.float32),
+        in_specs=[pl.BlockSpec((block, 1), lambda p: (p, 0))]
+        + [pl.BlockSpec(parts[0].shape, lambda p: (0, 0, 0))] * len(parts),
+        out_specs=pl.BlockSpec((block, width), lambda p: (p, 0)),
         compiler_params=pltpu.CompilerParams(vmem_limit_bytes=GRANT),
         cost_estimate=cost(1),
         name="to_tokens",
@@ -520,7 +544,7 @@
 
     g_across = swap(grad_out, 2)
     g_parts = (grad_out, swap(grad_out, 1), g_across, swap(g_across, 1))
-    slot_col, slot_row, *pieces = place(cluster, normed, seq_count, rows, chunks)
+    slot_col, slot_row, *pieces = place(cluster.reshape(1, -1), normed, seq_count, rows, chunks)
     xs, x_across = ([], [])
     for piece in pieces:
         xs.append(exchange(after(piece, *xs[-1:])))

time: 151 us -> 147 us (0.974)
  waiting for transfers between devices: 43.6 us -> 40.1 us
  local copies, waits for them, and re-layouts: 14.1 us -> 10.8 us
  Pallas kernels: 44.2 us -> 47.2 us
    unnamed x53 -> x36, local copies, waits for them, and re-layouts: 14.1 us -> 10.8 us
    all_to_all x6, waiting for transfers between devices: 14 us -> 11.6 us  [exchange(): return lax.all_to_all(x, 'seq', split_axis=0, concat_axis=0, tiled=True)]
    pallas_call x2 -> x3, Pallas kernels: 4.44 us -> 6.75 us  [the longest x1 2.68 us: place(): pl.pallas_call(functools.partial(place_kernel, chunks), out_shape=(jax.Sh...]
  transfers between devices with their start and end apart: 30 -> 30, of which waited for: 18 -> 19; matrix products, arithmetic and copies ran while one was open for 0% -> 0% of each run, Pallas kernels for 26% -> 29%
where the time goes in v6:
time: 147 us; the launch traced here: 146 us
  starting transfers between devices  47.3 us (32%)
  Pallas kernels  47.2 us (32%)
  waiting for transfers between devices  40.1 us (27%)
  local copies, waits for them, and re-layouts  10.8 us (7%)
    all_to_all x6, starting transfers between devices, exchange(): return lax.all_to_all(x, 'seq', split_axis=0, concat_axis=0, tiled=True)  33.9 us
    ppermute x24, waiting for transfers between devices, swap(): return lax.ppermute(x, 'tp', [(i, i ^ bit) for i in range(count)])  28.5 us
    pallas_call x2, Pallas kernels, backward(): pl.pallas_call(backward_kernel, grid=(steps,), out_shape=(shape,) * 2 + (...  16.9 us
    ppermute x24, starting transfers between devices, swap(): return lax.ppermute(x, 'tp', [(i, i ^ bit) for i in range(count)])  13.4 us
    pallas_call x2, Pallas kernels, forward(): pl.pallas_call(forward_kernel, grid=(steps,), out_shape=(jax.ShapeDtypeSt...  13.3 us
    all_to_all x6, waiting for transfers between devices, exchange(): return lax.all_to_all(x, 'seq', split_axis=0, concat_axis=0, tiled=True)  11.6 us
    unnamed x36, local copies, waits for them, and re-layouts  10.8 us
    pallas_call x1, Pallas kernels, head_grads(): pl.pallas_call(head_grads_kernel, out_shape=jax.ShapeDtypeStruct((CLUSTER...  3.5 us
  transfers between devices with their start and end apart: 30, of which 19 were waited for; matrix products, arithmetic and copies ran while one was open for 0% of the time, Pallas kernels for 29%

profile of v6, /device:TPU:0, one launch (start us, length us, event | category | flops | bytes accessed | tf_op | source)
XLA Modules:
  0.0 146.2 jit_solution(12718207777595211474)
XLA Ops:
  0.6 2.7 %place.1 = (s32[512,1]{1,0:T(8,128)}, s32[1,512]{1,0:T(1,128)}, bf16[8,64,512]{2,1,0:T(8,128)(2,1)}) custom-call(s32[1,512]{1,0:T(1,128)} %bitcast.3, bf16[512,512]{1,0:T(8,128)(2,1)} %x_ref.3), custom_call_target="tpu_custom_call" | custom-call | flops 1000000000 | bytes 1048576 | tf_op jit(solution)/shard_map/place/pallas_call | solution.py:94
  3.3 7.3 %all-to-all-start = ((bf16[8,64,512]{2,1,0:T(8,128)(2,1)}), bf16[8,64,512]{2,1,0:T(8,128)(2,1)S(1)}, u32[]{:S(2)}, u32[]{:S(2)}) async-start(bf16[8,64,512]{2,1,0:T(8,128)(2,1)} %get-tuple-element.40), calls=%async_computation | async-start | bytes 1048576 | tf_op jit(solution)/shard_map/all_to_all | solution.py:45
  10.6 1.6 %collective-permute-start.7 = (bf16[512,512]{1,0:T(8,128)(2,1)S(1)}, bf16[512,512]{1,0:T(8,128)(2,1)S(1)}, u32[]{:S(2)}, u32[]{:S(2)}) collective-permute-start(bf16[512,512]{1,0:T(8,128)(2,1)S(1)} %copy-done.10), channel_id=1, source_target_pairs={{0,2},{1,3},{2,0},{3,1},{4,6},{5,7},{6,4},{7,5},{8,10},{9,11},{10,... | collective-permute-start | bytes 1572872 | tf_op jit(solution)/shard_map/ppermute | solution.py:41
  12.2 2.3 %place_more.1 = bf16[8,64,512]{2,1,0:T(8,128)(2,1)} custom-call(s32[1,512]{1,0:T(1,128)} %get-tuple-element.39.slot_row, bf16[512,512]{1,0:T(8,128)(2,1)} %x_ref.3), custom_call_target="tpu_custom_call" | custom-call | flops 1000000000 | bytes 1048576 | tf_op jit(solution)/shard_map/place_more/pallas_call | solution.py:108
  14.5 10.6 %all-to-all-done.x0 = bf16[8,64,512]{2,1,0:T(8,128)(2,1)S(1)} async-done(((bf16[8,64,512]{2,1,0:T(8,128)(2,1)}), bf16[8,64,512]{2,1,0:T(8,128)(2,1)S(1)}, u32[]{:S(2)}, u32[]{:S(2)}) %all-to-all-start) | async-done | bytes 524320 | tf_op jit(solution)/shard_map/all_to_all | solution.py:45
  25.1 3.6 %all-to-all-start.1 = ((bf16[8,64,512]{2,1,0:T(8,128)(2,1)}), bf16[8,64,512]{2,1,0:T(8,128)(2,1)S(1)}, u32[]{:S(2)}, u32[]{:S(2)}) async-start(bf16[8,64,512]{2,1,0:T(8,128)(2,1)} %place_more.1), calls=%async_computation.1 | async-start | bytes 1048576 | tf_op jit(solution)/shard_map/all_to_all | solution.py:45
  28.8 0.5 collective-permute-start.8
  29.2 1.5 %collective-permute-start.3 = (bf16[8,64,512]{2,1,0:T(8,128)(2,1)S(1)}, bf16[8,64,512]{2,1,0:T(8,128)(2,1)}, u32[]{:S(2)}, u32[]{:S(2)}) collective-permute-start(bf16[8,64,512]{2,1,0:T(8,128)(2,1)S(1)} %all-to-all-done.x0), channel_id=1, source_target_pairs={{0,2},{1,3},{2,0},{3,1},{4,6},{5,7},{6,4},{7,5},{8,10},{9,11},{10,... | collective-permute-start | bytes 1572872 | tf_op jit(solution)/shard_map/ppermute | solution.py:41
  30.7 0.6 collective-permute-done.8.a3
  31.4 3.5 %head_grads.1 = bf16[1024,512]{1,0:T(8,128)(2,1)S(1)} custom-call(s32[4]{0:T(128)S(1)} %iota_xor_fusion.blk, bf16[512,512]{1,0:T(8,128)(2,1)S(1)} %copy-done.10, bf16[512,512]{1,0:T(8,128)(2,1)S(1)} %collective-permute-done.6.a1, bf16[512,512]{1,0:T(8,128)(2,1)S(1)} %collective-permute-done.7.a2, bf16[512,512]{1,0:T(8,128)(2,1)S(1)} %collective-permute-done.8.a3, ...), custom_call_target="tpu_custom_call" | custom-call | flops 2000000000 | bytes 1048576 | tf_op jit(solution)/shard_map/head_grads/pallas_call | solution.py:125
  34.9 1.0 copy-done.9
  35.9 7.4 %collective-permute-done.3.x2 = bf16[8,64,512]{2,1,0:T(8,128)(2,1)} collective-permute-done((bf16[8,64,512]{2,1,0:T(8,128)(2,1)S(1)}, bf16[8,64,512]{2,1,0:T(8,128)(2,1)}, u32[]{:S(2)}, u32[]{:S(2)}) %collective-permute-start.3) | collective-permute-done | bytes 524320 | tf_op jit(solution)/shard_map/ppermute | solution.py:41
  43.3 0.1 all-to-all-done.1.x0
  43.4 5.9 %all-to-all-start.2 = ((bf16[8,128,512]{2,1,0:T(8,128)(2,1)}), bf16[8,128,512]{2,1,0:T(8,128)(2,1)}, u32[]{:S(2)}, u32[]{:S(2)}) async-start(bf16[8,128,512]{2,1,0:T(8,128)(2,1)} %bitcast.2), calls=%async_computation.2 | async-start | bytes 2097152 | tf_op jit(solution)/shard_map/all_to_all | solution.py:45
  49.3 0.5 collective-permute-start.4
  49.8 1.5 %collective-permute-start.1 = (bf16[8,64,512]{2,1,0:T(8,128)(2,1)S(1)}, bf16[8,64,512]{2,1,0:T(8,128)(2,1)S(1)}, u32[]{:S(2)}, u32[]{:S(2)}) collective-permute-start(bf16[8,64,512]{2,1,0:T(8,128)(2,1)S(1)} %all-to-all-done.1.x0), channel_id=1, source_target_pairs={{0,2},{1,3},{2,0},{3,1},{4,6},{5,7},{6,4},{7,5},{8,10},{9,11},{10,... | collective-permute-start | bytes 1572872 | tf_op jit(solution)/shard_map/ppermute | solution.py:41
  51.3 0.9 collective-permute-done.4.x3
  52.1 1.6 %copy-done.1 = bf16[2048,512]{1,0:T(8,128)(2,1)S(1)} copy-done((bf16[2048,512]{1,0:T(8,128)(2,1)S(1)}, bf16[2048,512]{1,0:T(8,128)(2,1)}, u32[]{:S(2)}) %copy-start.1) | copy-done | bytes 2097176
  53.7 1.6 %copy-done.2 = bf16[2048,512]{1,0:T(8,128)(2,1)S(1)} copy-done((bf16[2048,512]{1,0:T(8,128)(2,1)S(1)}, bf16[2048,512]{1,0:T(8,128)(2,1)}, u32[]{:S(2)}) %copy-start.2) | copy-done | bytes 2097176
  55.3 6.8 %forward.2 = (bf16[8,128,512]{2,1,0:T(8,128)(2,1)}, bf16[8,64,1536]{2,1,0:T(8,128)(2,1)S(1)}, f32[2,2,4,128,128]{4,3,2,1,0:T(8,128)S(1)}) custom-call(s32[4]{0:T(128)S(1)} %iota_xor_fusion.blk, bf16[8,64,512]{2,1,0:T(8,128)(2,1)S(1)} %all-to-all-done.x0, bf16[8,64,512]{2,1,0:T(8,128)(2,1)S(1)} %collective-permute-done.2.x1, ...), custom_call_target="tpu_custom_call" | custom-call | flops 2000000000 | bytes 1048576 | tf_op jit(solution)/shard_map/forward/pallas_call | solution.py:289
  62.1 1.1 copy-done.4
  63.3 1.0 copy-done.7
  64.3 0.1 collective-permute-start.5
  64.4 1.8 %collective-permute-done.5.x3 = bf16[8,64,512]{2,1,0:T(8,128)(2,1)S(1)} collective-permute-done((bf16[8,64,512]{2,1,0:T(8,128)(2,1)S(1)}, bf16[8,64,512]{2,1,0:T(8,128)(2,1)S(1)}, u32[]{:S(2)}, u32[]{:S(2)}) %collective-permute-start.5) | collective-permute-done | bytes 524320 | tf_op jit(solution)/shard_map/ppermute | solution.py:41
  66.2 6.5 %forward.3 = (bf16[8,128,512]{2,1,0:T(8,128)(2,1)}, bf16[8,64,1536]{2,1,0:T(8,128)(2,1)S(1)}, f32[2,2,4,128,128]{4,3,2,1,0:T(8,128)S(1)}) custom-call(s32[4]{0:T(128)S(1)} %iota_xor_fusion.blk, bf16[8,64,512]{2,1,0:T(8,128)(2,1)S(1)} %all-to-all-done.1.x0, bf16[8,64,512]{2,1,0:T(8,128)(2,1)S(1)} %collective-permute-done.x1, ...), custom_call_target="tpu_custom_call", output_to_operand_aliasing={{0}: (8, {})} | custom-call | flops 2000000000 | bytes 1048576 | tf_op jit(solution)/shard_map/forward/pallas_call | solution.py:289
  72.6 1.2 copy-done.3
  73.8 1.0 copy-done.5
  74.8 6.1 %all-to-all-start.3 = ((bf16[8,128,512]{2,1,0:T(8,128)(2,1)}), bf16[8,128,512]{2,1,0:T(8,128)(2,1)S(1)}, u32[]{:S(2)}, u32[]{:S(2)}) async-start(bf16[8,128,512]{2,1,0:T(8,128)(2,1)} %get-tuple-element.46), calls=%async_computation.3 | async-start | bytes 2097152 | tf_op jit(solution)/shard_map/all_to_all | solution.py:45
  80.9 8.2 %backward.2 = (bf16[8,64,512]{2,1,0:T(8,128)(2,1)S(1)}, bf16[8,64,512]{2,1,0:T(8,128)(2,1)S(1)}, bf16[4,64,512]{2,1,0:T(8,128)(2,1)S(1)}, bf16[4,64,512]{2,1,0:T...) custom-call(s32[4]{0:T(128)S(1)} %iota_xor_fusion.blk, ...), custom_call_target="tpu_custom_call" | custom-call | flops 2000000000 | bytes 1048576 | tf_op jit(solution)/shard_map/backward/pallas_call | solution.py:322
  89.2 0.5 collective-permute-start.17
  89.7 1.0 collective-permute-done.16.refs_1_
  90.7 0.4 collective-permute-done.17.refs_2_
  91.1 0.1 add.8
  91.2 1.6 %collective-permute-start.18 = (bf16[8,64,512]{2,1,0:T(8,128)(2,1)S(1)}, bf16[8,64,512]{2,1,0:T(8,128)(2,1)S(1)}, u32[]{:S(2)}, u32[]{:S(2)}) collective-permute-start(bf16[8,64,512]{2,1,0:T(8,128)(2,1)S(1)} %add.8), channel_id=1, source_target_pairs={{0,2},{1,3},{2,0},{3,1},{4,6},{5,7},{6,4},{7,5},{8,10},{9,11},{10,... | collective-permute-start | bytes 1572872 | tf_op jit(solution)/shard_map/ppermute | solution.py:41
  92.8 8.8 %backward.3 = (bf16[8,64,512]{2,1,0:T(8,128)(2,1)S(1)}, bf16[8,64,512]{2,1,0:T(8,128)(2,1)S(1)}, bf16[4,64,512]{2,1,0:T(8,128)(2,1)}, bf16[4,64,512]{2,1,0:T(8,1...) custom-call(s32[4]{0:T(128)S(1)} %iota_xor_fusion.blk, bf16[8,64,1536]{2,1,0:T(8,128)(2,1)} %copy-done.3, ...), custom_call_target="tpu_custom_call" | custom-call | flops 2000000000 | bytes 1048576 | tf_op jit(solution)/shard_map/backward/pallas_call | solution.py:322
  101.6 0.5 collective-permute-start.20
  102.1 0.5 collective-permute-start.15
  102.6 0.5 collective-permute-done.19.refs_1_
  103.1 0.4 collective-permute-done.20.refs_2_
  103.6 0.3 collective-permute-done.14.refs_1_
  103.8 0.4 collective-permute-done.15.refs_2_
  104.2 1.0 collective-permute-done.18.refs_3_
  105.2 1.0 add.9
  106.2 0.7 all-to-all-done.3.mixed
  107.0 5.2 %all-to-all-start.4 = ((bf16[8,64,512]{2,1,0:T(8,128)(2,1)}), bf16[8,64,512]{2,1,0:T(8,128)(2,1)S(1)}, u32[]{:S(2)}, u32[]{:S(2)}) async-start(bf16[8,64,512]{2,1,0:T(8,128)(2,1)} %add.9), calls=%async_computation.4 | async-start | bytes 1048576 | tf_op jit(solution)/shard_map/all_to_all | solution.py:45
  112.2 1.5 %collective-permute-start.23 = (bf16[8,64,512]{2,1,0:T(8,128)(2,1)S(1)}, bf16[8,64,512]{2,1,0:T(8,128)(2,1)S(1)}, u32[]{:S(2)}, u32[]{:S(2)}) collective-permute-start(bf16[8,64,512]{2,1,0:T(8,128)(2,1)S(1)} %add.10), channel_id=1, source_target_pairs={{0,2},{1,3},{2,0},{3,1},{4,6},{5,7},{6,4},{7,5},{8,10},{9,11},{10,... | collective-permute-start | bytes 1572872 | tf_op jit(solution)/shard_map/ppermute | solution.py:41
  113.7 0.5 collective-permute-start.22
  114.2 0.9 copy-done.15
  115.2 3.4 %project_out.1 = (bf16[512,512]{1,0:T(8,128)(2,1)S(1)}, bf16[512,512]{1,0:T(8,128)(2,1)S(1)}, bf16[256,512]{1,0:T(8,128)(2,1)S(1)}, bf16[256,512]{1,0:T(8,128)(2...) custom-call(s32[4]{0:T(128)S(1)} %iota_xor_fusion.blk, s32[512,1]{1,0:T(8,128)S(1)} %copy-done.15, ...), custom_call_target="tpu_custom_call" | custom-call | flops 2000000000 | bytes 1048576 | tf_op jit(solution)/shard_map/project_out/pallas_call | solution.py:453
  118.6 0.7 copy-done.11
  119.3 0.7 copy-done.13
  120.0 0.5 collective-permute-start.12
  120.6 4.5 %collective-permute-done.23.refs_3_ = bf16[8,64,512]{2,1,0:T(8,128)(2,1)S(1)} collective-permute-done((bf16[8,64,512]{2,1,0:T(8,128)(2,1)S(1)}, bf16[8,64,512]{2,1,0:T(8,128)(2,1)S(1)}, u32[]{:S(2)}, u32[]{:S(2)}) %collective-permute-start.23) | collective-permute-done | bytes 524320 | tf_op jit(solution)/shard_map/ppermute | solution.py:41
  125.1 1.0 add.11
  126.1 0.1 add.6
  126.2 5.7 %all-to-all-start.5 = ((bf16[8,64,512]{2,1,0:T(8,128)(2,1)}), bf16[8,64,512]{2,1,0:T(8,128)(2,1)S(1)}, u32[]{:S(2)}, u32[]{:S(2)}) async-start(bf16[8,64,512]{2,1,0:T(8,128)(2,1)} %add.11), calls=%async_computation.5 | async-start | bytes 1048576 | tf_op jit(solution)/shard_map/all_to_all | solution.py:45
  131.9 1.5 %collective-permute-start.13 = (bf16[512,512]{1,0:T(8,128)(2,1)S(1)}, bf16[512,512]{1,0:T(8,128)(2,1)S(1)}, u32[]{:S(2)}, u32[]{:S(2)}) collective-permute-start(bf16[512,512]{1,0:T(8,128)(2,1)S(1)} %add.6), channel_id=1, source_target_pairs={{0,2},{1,3},{2,0},{3,1},{4,6},{5,7},{6,4},{7,5},{8,10},{9,11},{10,... | collective-permute-start | bytes 1572872 | tf_op jit(solution)/shard_map/ppermute | solution.py:41
  133.5 0.5 collective-permute-start.9
  134.0 1.0 collective-permute-done.10.refs_2_
  135.0 0.4 collective-permute-done.9.refs_1_
  135.4 7.9 %collective-permute-done.13.refs_3_ = bf16[512,512]{1,0:T(8,128)(2,1)S(1)} collective-permute-done((bf16[512,512]{1,0:T(8,128)(2,1)S(1)}, bf16[512,512]{1,0:T(8,128)(2,1)S(1)}, u32[]{:S(2)}, u32[]{:S(2)}) %collective-permute-start.13) | collective-permute-done | bytes 524320 | tf_op jit(solution)/shard_map/ppermute | solution.py:41
  143.3 1.0 add.7
  144.3 0.1 all-to-all-done.5.refs_1_
  144.4 1.7 %to_tokens.1 = f32[512,512]{1,0:T(8,128)} custom-call(s32[512,1]{1,0:T(8,128)S(1)} %copy-done.16, bf16[8,64,512]{2,1,0:T(8,128)(2,1)S(1)} %all-to-all-done.4.refs_0_, bf16[8,64,512]{2,1,0:T(8,128)(2,1)S(1)} %all-to-all-done.5.refs_1_), custom_call_target="tpu_custom_call" | custom-call | flops 1000000000 | bytes 1048576 | tf_op jit(solution)/shard_map/to_tokens/pallas_call | solution.py:473
  (48 shorter events, 0.3 us)
Async XLA Ops:
  0.6 10.0 %copy-start.10 = (bf16[512,512]{1,0:T(8,128)(2,1)S(1)}, bf16[512,512]{1,0:T(8,128)(2,1)}, u32[]{:S(2)}) copy-start(bf16[512,512]{1,0:T(8,128)(2,1)} %a0.1) | copy-start | bytes 1572868
  3.3 21.8 %all-to-all-start = ((bf16[8,64,512]{2,1,0:T(8,128)(2,1)}), bf16[8,64,512]{2,1,0:T(8,128)(2,1)S(1)}, u32[]{:S(2)}, u32[]{:S(2)}) async-start(bf16[8,64,512]{2,1,0:T(8,128)(2,1)} %get-tuple-element.40), calls=%async_computation | async-start | bytes 1048576 | tf_op jit(solution)/shard_map/all_to_all | solution.py:45
  10.6 18.1 %collective-permute-start.7 = (bf16[512,512]{1,0:T(8,128)(2,1)S(1)}, bf16[512,512]{1,0:T(8,128)(2,1)S(1)}, u32[]{:S(2)}, u32[]{:S(2)}) collective-permute-start(bf16[512,512]{1,0:T(8,128)(2,1)S(1)} %copy-done.10), channel_id=1, source_target_pairs={{0,2},{1,3},{2,0},{3,1},{4,6},{5,7},{6,4},{7,5},{8,10},{9,11},{10,... | collective-permute-start | bytes 1572872 | tf_op jit(solution)/shard_map/ppermute | solution.py:41
  12.2 19.2 %copy-start.17 = (s32[1,512]{1,0:T(1,128)S(1)}, s32[1,512]{1,0:T(1,128)}, u32[]{:S(2)}) copy-start(s32[1,512]{1,0:T(1,128)} %get-tuple-element.39.slot_row) | copy-start | bytes 6148
  25.1 18.3 %all-to-all-start.1 = ((bf16[8,64,512]{2,1,0:T(8,128)(2,1)}), bf16[8,64,512]{2,1,0:T(8,128)(2,1)S(1)}, u32[]{:S(2)}, u32[]{:S(2)}) async-start(bf16[8,64,512]{2,1,0:T(8,128)(2,1)} %place_more.1), calls=%async_computation.1 | async-start | bytes 1048576 | tf_op jit(solution)/shard_map/all_to_all | solution.py:45
  28.7 2.0 %collective-permute-start.6 = (bf16[512,512]{1,0:T(8,128)(2,1)S(1)}, bf16[512,512]{1,0:T(8,128)(2,1)S(1)}, u32[]{:S(2)}, u32[]{:S(2)}) collective-permute-start(bf16[512,512]{1,0:T(8,128)(2,1)S(1)} %copy-done.10), channel_id=1, source_target_pairs={{0,1},{1,0},{2,3},{3,2},{4,5},{5,4},{6,7},{7,6},{8,9},{9,8},{10,11... | collective-permute-start | bytes 1572872 | tf_op jit(solution)/shard_map/ppermute | solution.py:41
  28.8 2.6 %collective-permute-start.8 = (bf16[512,512]{1,0:T(8,128)(2,1)S(1)}, bf16[512,512]{1,0:T(8,128)(2,1)S(1)}, u32[]{:S(2)}, u32[]{:S(2)}) collective-permute-start(bf16[512,512]{1,0:T(8,128)(2,1)S(1)} %collective-permute-done.7.a2), channel_id=1, source_target_pairs={{0,1},{1,0},{2,3},{3,2},{4,5},{5,4},{6,7},{7,6},{8,9},{9,8},{10,11... | collective-permute-start | bytes 1572872 | tf_op jit(solution)/shard_map/ppermute | solution.py:41
  29.2 14.0 %collective-permute-start.3 = (bf16[8,64,512]{2,1,0:T(8,128)(2,1)S(1)}, bf16[8,64,512]{2,1,0:T(8,128)(2,1)}, u32[]{:S(2)}, u32[]{:S(2)}) collective-permute-start(bf16[8,64,512]{2,1,0:T(8,128)(2,1)S(1)} %all-to-all-done.x0), channel_id=1, source_target_pairs={{0,2},{1,3},{2,0},{3,1},{4,6},{5,7},{6,4},{7,5},{8,10},{9,11},{10,... | collective-permute-start | bytes 1572872 | tf_op jit(solution)/shard_map/ppermute | solution.py:41
  34.9 1.0 copy-start.9
  35.9 16.2 %copy-start = (bf16[2048,512]{1,0:T(8,128)(2,1)S(1)}, bf16[2048,512]{1,0:T(8,128)(2,1)}, u32[]{:S(2)}) copy-start(bf16[2048,512]{1,0:T(8,128)(2,1)} %wq.7) | copy-start | bytes 6291460
  43.4 31.4 %all-to-all-start.2 = ((bf16[8,128,512]{2,1,0:T(8,128)(2,1)}), bf16[8,128,512]{2,1,0:T(8,128)(2,1)}, u32[]{:S(2)}, u32[]{:S(2)}) async-start(bf16[8,128,512]{2,1,0:T(8,128)(2,1)} %bitcast.2), calls=%async_computation.2 | async-start | bytes 2097152 | tf_op jit(solution)/shard_map/all_to_all | solution.py:45
  49.3 2.0 %collective-permute-start.2 = (bf16[8,64,512]{2,1,0:T(8,128)(2,1)S(1)}, bf16[8,64,512]{2,1,0:T(8,128)(2,1)S(1)}, u32[]{:S(2)}, u32[]{:S(2)}) collective-permute-start(bf16[8,64,512]{2,1,0:T(8,128)(2,1)S(1)} %all-to-all-done.x0), channel_id=1, source_target_pairs={{0,1},{1,0},{2,3},{3,2},{4,5},{5,4},{6,7},{7,6},{8,9},{9,8},{10,11... | collective-permute-start | bytes 1572872 | tf_op jit(solution)/shard_map/ppermute | solution.py:41
  49.3 2.9 %collective-permute-start.4 = (bf16[8,64,512]{2,1,0:T(8,128)(2,1)}, bf16[8,64,512]{2,1,0:T(8,128)(2,1)S(1)}, u32[]{:S(2)}, u32[]{:S(2)}) collective-permute-start(bf16[8,64,512]{2,1,0:T(8,128)(2,1)} %collective-permute-done.3.x2), channel_id=1, source_target_pairs={{0,1},{1,0},{2,3},{3,2},{4,5},{5,4},{6,7},{7,6},{8,9},{9,8},{10,11... | collective-permute-start | bytes 1572872 | tf_op jit(solution)/shard_map/ppermute | solution.py:41
  49.8 14.5 %collective-permute-start.1 = (bf16[8,64,512]{2,1,0:T(8,128)(2,1)S(1)}, bf16[8,64,512]{2,1,0:T(8,128)(2,1)S(1)}, u32[]{:S(2)}, u32[]{:S(2)}) collective-permute-start(bf16[8,64,512]{2,1,0:T(8,128)(2,1)S(1)} %all-to-all-done.1.x0), channel_id=1, source_target_pairs={{0,2},{1,3},{2,0},{3,1},{4,6},{5,7},{6,4},{7,5},{8,10},{9,11},{10,... | collective-permute-start | bytes 1572872 | tf_op jit(solution)/shard_map/ppermute | solution.py:41
  51.3 13.1 %collective-permute-start = (bf16[8,64,512]{2,1,0:T(8,128)(2,1)S(1)}, bf16[8,64,512]{2,1,0:T(8,128)(2,1)S(1)}, u32[]{:S(2)}, u32[]{:S(2)}) collective-permute-start(bf16[8,64,512]{2,1,0:T(8,128)(2,1)S(1)} %all-to-all-done.1.x0), channel_id=1, source_target_pairs={{0,1},{1,0},{2,3},{3,2},{4,5},{5,4},{6,7},{7,6},{8,9},{9,8},{10,11... | collective-permute-start | bytes 1572872 | tf_op jit(solution)/shard_map/ppermute | solution.py:41
  52.1 1.6 %copy-start.1 = (bf16[2048,512]{1,0:T(8,128)(2,1)S(1)}, bf16[2048,512]{1,0:T(8,128)(2,1)}, u32[]{:S(2)}) copy-start(bf16[2048,512]{1,0:T(8,128)(2,1)} %wk.7) | copy-start | bytes 6291460
  53.7 1.6 %copy-start.2 = (bf16[2048,512]{1,0:T(8,128)(2,1)S(1)}, bf16[2048,512]{1,0:T(8,128)(2,1)}, u32[]{:S(2)}) copy-start(bf16[2048,512]{1,0:T(8,128)(2,1)} %wv.7) | copy-start | bytes 6291460
  62.1 1.1 copy-start.4
  63.3 1.0 copy-start.7
  64.3 1.9 %collective-permute-start.5 = (bf16[8,64,512]{2,1,0:T(8,128)(2,1)S(1)}, bf16[8,64,512]{2,1,0:T(8,128)(2,1)S(1)}, u32[]{:S(2)}, u32[]{:S(2)}) collective-permute-start(bf16[8,64,512]{2,1,0:T(8,128)(2,1)S(1)} %collective-permute-done.1.x2), channel_id=1, source_target_pairs={{0,1},{1,0},{2,3},{3,2},{4,5},{5,4},{6,7},{7,6},{8,9},{9,8},{10,11... | collective-permute-start | bytes 1572872 | tf_op jit(solution)/shard_map/ppermute | solution.py:41
  72.6 1.2 copy-start.3
  73.8 1.0 copy-start.5
  74.8 6.1 %copy-start.8 = (f32[2,2,4,128,128]{4,3,2,1,0:T(8,128)S(1)}, f32[2,2,4,128,128]{4,3,2,1,0:T(8,128)}, u32[]{:S(2)}) copy-start(f32[2,2,4,128,128]{4,3,2,1,0:T(8,128)} %copy-done.7) | copy-start | bytes 3145732
  74.8 32.2 %all-to-all-start.3 = ((bf16[8,128,512]{2,1,0:T(8,128)(2,1)}), bf16[8,128,512]{2,1,0:T(8,128)(2,1)S(1)}, u32[]{:S(2)}, u32[]{:S(2)}) async-start(bf16[8,128,512]{2,1,0:T(8,128)(2,1)} %get-tuple-element.46), calls=%async_computation.3 | async-start | bytes 2097152 | tf_op jit(solution)/shard_map/all_to_all | solution.py:45
  89.1 3.7 %copy-start.6 = (f32[2,2,4,128,128]{4,3,2,1,0:T(8,128)S(1)}, f32[2,2,4,128,128]{4,3,2,1,0:T(8,128)}, u32[]{:S(2)}) copy-start(f32[2,2,4,128,128]{4,3,2,1,0:T(8,128)} %copy-done.5) | copy-start | bytes 3145732
  89.1 1.6 %collective-permute-start.16 = (bf16[4,64,512]{2,1,0:T(8,128)(2,1)S(1)}, bf16[4,64,512]{2,1,0:T(8,128)(2,1)S(1)}, u32[]{:S(2)}, u32[]{:S(2)}) collective-permute-start(bf16[4,64,512]{2,1,0:T(8,128)(2,1)S(1)} %get-tuple-element.60), channel_id=1, source_target_pairs={{0,1},{1,0},{2,3},{3,2},{4,5},{5,4},{6,7},{7,6},{8,9},{9,8},{10,11... | collective-permute-start | bytes 786440 | tf_op jit(solution)/shard_map/ppermute | solution.py:41
  89.2 1.9 %collective-permute-start.17 = (bf16[4,64,512]{2,1,0:T(8,128)(2,1)S(1)}, bf16[4,64,512]{2,1,0:T(8,128)(2,1)S(1)}, u32[]{:S(2)}, u32[]{:S(2)}) collective-permute-start(bf16[4,64,512]{2,1,0:T(8,128)(2,1)S(1)} %get-tuple-element.61), channel_id=1, source_target_pairs={{0,1},{1,0},{2,3},{3,2},{4,5},{5,4},{6,7},{7,6},{8,9},{9,8},{10,11... | collective-permute-start | bytes 786440 | tf_op jit(solution)/shard_map/ppermute | solution.py:41
  91.2 14.0 %collective-permute-start.18 = (bf16[8,64,512]{2,1,0:T(8,128)(2,1)S(1)}, bf16[8,64,512]{2,1,0:T(8,128)(2,1)S(1)}, u32[]{:S(2)}, u32[]{:S(2)}) collective-permute-start(bf16[8,64,512]{2,1,0:T(8,128)(2,1)S(1)} %add.8), channel_id=1, source_target_pairs={{0,2},{1,3},{2,0},{3,1},{4,6},{5,7},{6,4},{7,5},{8,10},{9,11},{10,... | collective-permute-start | bytes 1572872 | tf_op jit(solution)/shard_map/ppermute | solution.py:41
  101.6 1.5 %collective-permute-start.19 = (bf16[4,64,512]{2,1,0:T(8,128)(2,1)S(1)}, bf16[4,64,512]{2,1,0:T(8,128)(2,1)S(1)}, u32[]{:S(2)}, u32[]{:S(2)}) collective-permute-start(bf16[4,64,512]{2,1,0:T(8,128)(2,1)S(1)} %get-tuple-element.66), channel_id=1, source_target_pairs={{0,1},{1,0},{2,3},{3,2},{4,5},{5,4},{6,7},{7,6},{8,9},{9,8},{10,11... | collective-permute-start | bytes 786440 | tf_op jit(solution)/shard_map/ppermute | solution.py:41
  101.6 1.9 %collective-permute-start.20 = (bf16[4,64,512]{2,1,0:T(8,128)(2,1)S(1)}, bf16[4,64,512]{2,1,0:T(8,128)(2,1)S(1)}, u32[]{:S(2)}, u32[]{:S(2)}) collective-permute-start(bf16[4,64,512]{2,1,0:T(8,128)(2,1)S(1)} %get-tuple-element.67), channel_id=1, source_target_pairs={{0,1},{1,0},{2,3},{3,2},{4,5},{5,4},{6,7},{7,6},{8,9},{9,8},{10,11... | collective-permute-start | bytes 786440 | tf_op jit(solution)/shard_map/ppermute | solution.py:41
  102.1 1.8 %collective-permute-start.14 = (bf16[4,64,512]{2,1,0:T(8,128)(2,1)S(1)}, bf16[4,64,512]{2,1,0:T(8,128)(2,1)S(1)}, u32[]{:S(2)}, u32[]{:S(2)}) collective-permute-start(bf16[4,64,512]{2,1,0:T(8,128)(2,1)S(1)} %get-tuple-element.57), channel_id=1, source_target_pairs={{0,1},{1,0},{2,3},{3,2},{4,5},{5,4},{6,7},{7,6},{8,9},{9,8},{10,11... | collective-permute-start | bytes 786440 | tf_op jit(solution)/shard_map/ppermute | solution.py:41
  102.1 2.1 %collective-permute-start.15 = (bf16[4,64,512]{2,1,0:T(8,128)(2,1)S(1)}, bf16[4,64,512]{2,1,0:T(8,128)(2,1)S(1)}, u32[]{:S(2)}, u32[]{:S(2)}) collective-permute-start(bf16[4,64,512]{2,1,0:T(8,128)(2,1)S(1)} %get-tuple-element.58), channel_id=1, source_target_pairs={{0,1},{1,0},{2,3},{3,2},{4,5},{5,4},{6,7},{7,6},{8,9},{9,8},{10,11... | collective-permute-start | bytes 786440 | tf_op jit(solution)/shard_map/ppermute | solution.py:41
  107.0 19.3 %all-to-all-start.4 = ((bf16[8,64,512]{2,1,0:T(8,128)(2,1)}), bf16[8,64,512]{2,1,0:T(8,128)(2,1)S(1)}, u32[]{:S(2)}, u32[]{:S(2)}) async-start(bf16[8,64,512]{2,1,0:T(8,128)(2,1)} %add.9), calls=%async_computation.4 | async-start | bytes 1048576 | tf_op jit(solution)/shard_map/all_to_all | solution.py:45
  112.2 12.9 %collective-permute-start.23 = (bf16[8,64,512]{2,1,0:T(8,128)(2,1)S(1)}, bf16[8,64,512]{2,1,0:T(8,128)(2,1)S(1)}, u32[]{:S(2)}, u32[]{:S(2)}) collective-permute-start(bf16[8,64,512]{2,1,0:T(8,128)(2,1)S(1)} %add.10), channel_id=1, source_target_pairs={{0,2},{1,3},{2,0},{3,1},{4,6},{5,7},{6,4},{7,5},{8,10},{9,11},{10,... | collective-permute-start | bytes 1572872 | tf_op jit(solution)/shard_map/ppermute | solution.py:41
  113.7 6.8 %collective-permute-start.21 = (bf16[4,64,512]{2,1,0:T(8,128)(2,1)}, bf16[4,64,512]{2,1,0:T(8,128)(2,1)S(1)}, u32[]{:S(2)}, u32[]{:S(2)}) collective-permute-start(bf16[4,64,512]{2,1,0:T(8,128)(2,1)} %get-tuple-element.70), channel_id=1, source_target_pairs={{0,1},{1,0},{2,3},{3,2},{4,5},{5,4},{6,7},{7,6},{8,9},{9,8},{10,11... | collective-permute-start | bytes 786440 | tf_op jit(solution)/shard_map/ppermute | solution.py:41
  113.7 6.8 %collective-permute-start.22 = (bf16[4,64,512]{2,1,0:T(8,128)(2,1)S(1)}, bf16[4,64,512]{2,1,0:T(8,128)(2,1)S(1)}, u32[]{:S(2)}, u32[]{:S(2)}) collective-permute-start(bf16[4,64,512]{2,1,0:T(8,128)(2,1)S(1)} %get-tuple-element.71), channel_id=1, source_target_pairs={{0,1},{1,0},{2,3},{3,2},{4,5},{5,4},{6,7},{7,6},{8,9},{9,8},{10,11... | collective-permute-start | bytes 786440 | tf_op jit(solution)/shard_map/ppermute | solution.py:41
  114.2 0.9 copy-start.15
  118.6 0.7 copy-start.11
  119.3 0.7 copy-start.13
  120.0 6.0 %collective-permute-start.11 = (bf16[256,512]{1,0:T(8,128)(2,1)S(1)}, bf16[256,512]{1,0:T(8,128)(2,1)S(1)}, u32[]{:S(2)}, u32[]{:S(2)}) collective-permute-start(bf16[256,512]{1,0:T(8,128)(2,1)S(1)} %get-tuple-element.51), channel_id=1, source_target_pairs={{0,1},{1,0},{2,3},{3,2},{4,5},{5,4},{6,7},{7,6},{8,9},{9,8},{10,11... | collective-permute-start | bytes 786440 | tf_op jit(solution)/shard_map/ppermute | solution.py:41
  120.0 6.0 %collective-permute-start.12 = (bf16[256,512]{1,0:T(8,128)(2,1)S(1)}, bf16[256,512]{1,0:T(8,128)(2,1)S(1)}, u32[]{:S(2)}, u32[]{:S(2)}) collective-permute-start(bf16[256,512]{1,0:T(8,128)(2,1)S(1)} %get-tuple-element.52), channel_id=1, source_target_pairs={{0,1},{1,0},{2,3},{3,2},{4,5},{5,4},{6,7},{7,6},{8,9},{9,8},{10,11... | collective-permute-start | bytes 786440 | tf_op jit(solution)/shard_map/ppermute | solution.py:41
  125.1 8.4 %copy-start.14 = (bf16[256,512]{1,0:T(8,128)(2,1)S(1)}, bf16[256,512]{1,0:T(8,128)(2,1)}, u32[]{:S(2)}) copy-start(bf16[256,512]{1,0:T(8,128)(2,1)} %copy-done.13) | copy-start | bytes 786436
  125.1 8.4 %copy-start.12 = (bf16[256,512]{1,0:T(8,128)(2,1)S(1)}, bf16[256,512]{1,0:T(8,128)(2,1)}, u32[]{:S(2)}) copy-start(bf16[256,512]{1,0:T(8,128)(2,1)} %copy-done.11) | copy-start | bytes 786436
  126.1 18.4 %copy-start.16 = (s32[512,1]{1,0:T(8,128)S(1)}, s32[512,1]{1,0:T(8,128)}, u32[]{:S(2)}) copy-start(s32[512,1]{1,0:T(8,128)} %get-tuple-element.38.slot_col) | copy-start | bytes 6148
  126.2 18.2 %all-to-all-start.5 = ((bf16[8,64,512]{2,1,0:T(8,128)(2,1)}), bf16[8,64,512]{2,1,0:T(8,128)(2,1)S(1)}, u32[]{:S(2)}, u32[]{:S(2)}) async-start(bf16[8,64,512]{2,1,0:T(8,128)(2,1)} %add.11), calls=%async_computation.5 | async-start | bytes 1048576 | tf_op jit(solution)/shard_map/all_to_all | solution.py:45
  131.9 11.4 %collective-permute-start.13 = (bf16[512,512]{1,0:T(8,128)(2,1)S(1)}, bf16[512,512]{1,0:T(8,128)(2,1)S(1)}, u32[]{:S(2)}, u32[]{:S(2)}) collective-permute-start(bf16[512,512]{1,0:T(8,128)(2,1)S(1)} %add.6), channel_id=1, source_target_pairs={{0,2},{1,3},{2,0},{3,1},{4,6},{5,7},{6,4},{7,5},{8,10},{9,11},{10,... | collective-permute-start | bytes 1572872 | tf_op jit(solution)/shard_map/ppermute | solution.py:41
  133.5 1.5 %collective-permute-start.10 = (bf16[256,512]{1,0:T(8,128)(2,1)S(1)}, bf16[256,512]{1,0:T(8,128)(2,1)S(1)}, u32[]{:S(2)}, u32[]{:S(2)}) collective-permute-start(bf16[256,512]{1,0:T(8,128)(2,1)S(1)} %copy-done.14), channel_id=1, source_target_pairs={{0,1},{1,0},{2,3},{3,2},{4,5},{5,4},{6,7},{7,6},{8,9},{9,8},{10,11... | collective-permute-start | bytes 786440 | tf_op jit(solution)/shard_map/ppermute | solution.py:41
  133.5 1.9 %collective-permute-start.9 = (bf16[256,512]{1,0:T(8,128)(2,1)S(1)}, bf16[256,512]{1,0:T(8,128)(2,1)S(1)}, u32[]{:S(2)}, u32[]{:S(2)}) collective-permute-start(bf16[256,512]{1,0:T(8,128)(2,1)S(1)} %copy-done.12), channel_id=1, source_target_pairs={{0,1},{1,0},{2,3},{3,2},{4,5},{5,4},{6,7},{7,6},{8,9},{9,8},{10,11... | collective-permute-start | bytes 786440 | tf_op jit(solution)/shard_map/ppermute | solution.py:41

commit v7 on v6

--- a/solution.py
+++ b/solution.py
@@ -268,7 +268,7 @@
 
 def step_of(sources, rows):
     step = GROUP
-    while step * 2 * sources <= 256 and rows % (step * 2) == 0:
+    while step * 2 * sources <= 512 and rows % (step * 2) == 0:
         step *= 2
     return step
 

time: 147 us -> 146 us (level)
  transfers between devices with their start and end apart: 30 -> 30, of which waited for: 19 -> 20; matrix products, arithmetic and copies ran while one was open for 0% -> 0% of each run, Pallas kernels for 29% -> 28%
where the time goes in v7:
time: 146 us
  starting transfers between devices  46.8 us (32%)
  Pallas kernels  45.8 us (31%)
  waiting for transfers between devices  41.4 us (28%)
  local copies, waits for them, and re-layouts  10.8 us (7%)
    all_to_all x6, starting transfers between devices, exchange(): return lax.all_to_all(x, 'seq', split_axis=0, concat_axis=0, tiled=True)  33.4 us
    ppermute x24, waiting for transfers between devices, swap(): return lax.ppermute(x, 'tp', [(i, i ^ bit) for i in range(count)])  29.2 us
    pallas_call x2, Pallas kernels, backward(): pl.pallas_call(backward_kernel, grid=(steps,), out_shape=(shape,) * 2 + (...  15.8 us
    ppermute x24, starting transfers between devices, swap(): return lax.ppermute(x, 'tp', [(i, i ^ bit) for i in range(count)])  13.5 us
    pallas_call x2, Pallas kernels, forward(): pl.pallas_call(forward_kernel, grid=(steps,), out_shape=(jax.ShapeDtypeSt...  13 us
    all_to_all x6, waiting for transfers between devices, exchange(): return lax.all_to_all(x, 'seq', split_axis=0, concat_axis=0, tiled=True)  12.1 us
    unnamed x36, local copies, waits for them, and re-layouts  10.8 us
    pallas_call x1, Pallas kernels, head_grads(): pl.pallas_call(head_grads_kernel, out_shape=jax.ShapeDtypeStruct((CLUSTER...  3.5 us
  transfers between devices with their start and end apart: 30, of which 20 were waited for; matrix products, arithmetic and copies ran while one was open for 0% of the time, Pallas kernels for 28%

profile of v7, /device:TPU:0, one launch (start us, length us, event | category | flops | bytes accessed | tf_op | source)
XLA Modules:
  0.0 145.6 jit_solution(7424282865700931624)
XLA Ops:
  0.6 2.7 %place.1 = (s32[512,1]{1,0:T(8,128)}, s32[1,512]{1,0:T(1,128)}, bf16[8,64,512]{2,1,0:T(8,128)(2,1)}) custom-call(s32[1,512]{1,0:T(1,128)} %bitcast.3, bf16[512,512]{1,0:T(8,128)(2,1)} %x_ref.3), custom_call_target="tpu_custom_call" | custom-call | flops 1000000000 | bytes 1048576 | tf_op jit(solution)/shard_map/place/pallas_call | solution.py:94
  3.3 7.3 %all-to-all-start = ((bf16[8,64,512]{2,1,0:T(8,128)(2,1)}), bf16[8,64,512]{2,1,0:T(8,128)(2,1)S(1)}, u32[]{:S(2)}, u32[]{:S(2)}) async-start(bf16[8,64,512]{2,1,0:T(8,128)(2,1)} %get-tuple-element.40), calls=%async_computation | async-start | bytes 1048576 | tf_op jit(solution)/shard_map/all_to_all | solution.py:45
  10.6 1.6 %collective-permute-start.7 = (bf16[512,512]{1,0:T(8,128)(2,1)S(1)}, bf16[512,512]{1,0:T(8,128)(2,1)S(1)}, u32[]{:S(2)}, u32[]{:S(2)}) collective-permute-start(bf16[512,512]{1,0:T(8,128)(2,1)S(1)} %copy-done.10), channel_id=1, source_target_pairs={{0,2},{1,3},{2,0},{3,1},{4,6},{5,7},{6,4},{7,5},{8,10},{9,11},{10,... | collective-permute-start | bytes 1572872 | tf_op jit(solution)/shard_map/ppermute | solution.py:41
  12.2 2.3 %place_more.1 = bf16[8,64,512]{2,1,0:T(8,128)(2,1)} custom-call(s32[1,512]{1,0:T(1,128)} %get-tuple-element.39.slot_row, bf16[512,512]{1,0:T(8,128)(2,1)} %x_ref.3), custom_call_target="tpu_custom_call" | custom-call | flops 1000000000 | bytes 1048576 | tf_op jit(solution)/shard_map/place_more/pallas_call | solution.py:108
  14.5 10.6 %all-to-all-done.x0 = bf16[8,64,512]{2,1,0:T(8,128)(2,1)S(1)} async-done(((bf16[8,64,512]{2,1,0:T(8,128)(2,1)}), bf16[8,64,512]{2,1,0:T(8,128)(2,1)S(1)}, u32[]{:S(2)}, u32[]{:S(2)}) %all-to-all-start) | async-done | bytes 524320 | tf_op jit(solution)/shard_map/all_to_all | solution.py:45
  25.1 3.6 %all-to-all-start.1 = ((bf16[8,64,512]{2,1,0:T(8,128)(2,1)}), bf16[8,64,512]{2,1,0:T(8,128)(2,1)S(1)}, u32[]{:S(2)}, u32[]{:S(2)}) async-start(bf16[8,64,512]{2,1,0:T(8,128)(2,1)} %place_more.1), calls=%async_computation.1 | async-start | bytes 1048576 | tf_op jit(solution)/shard_map/all_to_all | solution.py:45
  28.8 0.5 collective-permute-start.8
  29.2 1.5 %collective-permute-start.3 = (bf16[8,64,512]{2,1,0:T(8,128)(2,1)S(1)}, bf16[8,64,512]{2,1,0:T(8,128)(2,1)}, u32[]{:S(2)}, u32[]{:S(2)}) collective-permute-start(bf16[8,64,512]{2,1,0:T(8,128)(2,1)S(1)} %all-to-all-done.x0), channel_id=1, source_target_pairs={{0,2},{1,3},{2,0},{3,1},{4,6},{5,7},{6,4},{7,5},{8,10},{9,11},{10,... | collective-permute-start | bytes 1572872 | tf_op jit(solution)/shard_map/ppermute | solution.py:41
  30.7 0.6 collective-permute-done.8.a3
  31.4 3.5 %head_grads.1 = bf16[1024,512]{1,0:T(8,128)(2,1)S(1)} custom-call(s32[4]{0:T(128)S(1)} %iota_xor_fusion.blk, bf16[512,512]{1,0:T(8,128)(2,1)S(1)} %copy-done.10, bf16[512,512]{1,0:T(8,128)(2,1)S(1)} %collective-permute-done.6.a1, bf16[512,512]{1,0:T(8,128)(2,1)S(1)} %collective-permute-done.7.a2, bf16[512,512]{1,0:T(8,128)(2,1)S(1)} %collective-permute-done.8.a3, ...), custom_call_target="tpu_custom_call" | custom-call | flops 2000000000 | bytes 1048576 | tf_op jit(solution)/shard_map/head_grads/pallas_call | solution.py:125
  34.9 1.0 copy-done.9
  35.9 7.4 %collective-permute-done.3.x2 = bf16[8,64,512]{2,1,0:T(8,128)(2,1)} collective-permute-done((bf16[8,64,512]{2,1,0:T(8,128)(2,1)S(1)}, bf16[8,64,512]{2,1,0:T(8,128)(2,1)}, u32[]{:S(2)}, u32[]{:S(2)}) %collective-permute-start.3) | collective-permute-done | bytes 524320 | tf_op jit(solution)/shard_map/ppermute | solution.py:41
  43.3 0.1 all-to-all-done.1.x0
  43.4 5.9 %all-to-all-start.2 = ((bf16[8,128,512]{2,1,0:T(8,128)(2,1)}), bf16[8,128,512]{2,1,0:T(8,128)(2,1)}, u32[]{:S(2)}, u32[]{:S(2)}) async-start(bf16[8,128,512]{2,1,0:T(8,128)(2,1)} %bitcast.2), calls=%async_computation.2 | async-start | bytes 2097152 | tf_op jit(solution)/shard_map/all_to_all | solution.py:45
  49.3 0.5 collective-permute-start.4
  49.8 1.5 %collective-permute-start.1 = (bf16[8,64,512]{2,1,0:T(8,128)(2,1)S(1)}, bf16[8,64,512]{2,1,0:T(8,128)(2,1)S(1)}, u32[]{:S(2)}, u32[]{:S(2)}) collective-permute-start(bf16[8,64,512]{2,1,0:T(8,128)(2,1)S(1)} %all-to-all-done.1.x0), channel_id=1, source_target_pairs={{0,2},{1,3},{2,0},{3,1},{4,6},{5,7},{6,4},{7,5},{8,10},{9,11},{10,... | collective-permute-start | bytes 1572872 | tf_op jit(solution)/shard_map/ppermute | solution.py:41
  51.3 0.9 collective-permute-done.4.x3
  52.1 1.6 %copy-done.1 = bf16[2048,512]{1,0:T(8,128)(2,1)S(1)} copy-done((bf16[2048,512]{1,0:T(8,128)(2,1)S(1)}, bf16[2048,512]{1,0:T(8,128)(2,1)}, u32[]{:S(2)}) %copy-start.1) | copy-done | bytes 2097176
  53.7 1.6 %copy-done.2 = bf16[2048,512]{1,0:T(8,128)(2,1)S(1)} copy-done((bf16[2048,512]{1,0:T(8,128)(2,1)S(1)}, bf16[2048,512]{1,0:T(8,128)(2,1)}, u32[]{:S(2)}) %copy-start.2) | copy-done | bytes 2097176
  55.3 6.8 %forward.2 = (bf16[8,128,512]{2,1,0:T(8,128)(2,1)}, bf16[8,64,1536]{2,1,0:T(8,128)(2,1)S(1)}, f32[1,4,4,128,128]{4,3,2,1,0:T(8,128)S(1)}) custom-call(s32[4]{0:T(128)S(1)} %iota_xor_fusion.blk, bf16[8,64,512]{2,1,0:T(8,128)(2,1)S(1)} %all-to-all-done.x0, bf16[8,64,512]{2,1,0:T(8,128)(2,1)S(1)} %collective-permute-done.2.x1, ...), custom_call_target="tpu_custom_call" | custom-call | flops 2000000000 | bytes 1048576 | tf_op jit(solution)/shard_map/forward/pallas_call | solution.py:289
  62.1 1.1 copy-done.4
  63.2 1.0 copy-done.7
  64.2 0.1 collective-permute-start.5
  64.3 1.8 %collective-permute-done.5.x3 = bf16[8,64,512]{2,1,0:T(8,128)(2,1)S(1)} collective-permute-done((bf16[8,64,512]{2,1,0:T(8,128)(2,1)S(1)}, bf16[8,64,512]{2,1,0:T(8,128)(2,1)S(1)}, u32[]{:S(2)}, u32[]{:S(2)}) %collective-permute-start.5) | collective-permute-done | bytes 524320 | tf_op jit(solution)/shard_map/ppermute | solution.py:41
  66.1 6.3 %forward.3 = (bf16[8,128,512]{2,1,0:T(8,128)(2,1)}, bf16[8,64,1536]{2,1,0:T(8,128)(2,1)S(1)}, f32[1,4,4,128,128]{4,3,2,1,0:T(8,128)S(1)}) custom-call(s32[4]{0:T(128)S(1)} %iota_xor_fusion.blk, bf16[8,64,512]{2,1,0:T(8,128)(2,1)S(1)} %all-to-all-done.1.x0, bf16[8,64,512]{2,1,0:T(8,128)(2,1)S(1)} %collective-permute-done.x1, ...), custom_call_target="tpu_custom_call", output_to_operand_aliasing={{0}: (8, {})} | custom-call | flops 2000000000 | bytes 1048576 | tf_op jit(solution)/shard_map/forward/pallas_call | solution.py:289
  72.4 1.2 copy-done.3
  73.6 1.0 copy-done.5
  74.5 0.2 all-to-all-done.2.g_ref
  74.7 5.9 %all-to-all-start.3 = ((bf16[8,128,512]{2,1,0:T(8,128)(2,1)}), bf16[8,128,512]{2,1,0:T(8,128)(2,1)S(1)}, u32[]{:S(2)}, u32[]{:S(2)}) async-start(bf16[8,128,512]{2,1,0:T(8,128)(2,1)} %get-tuple-element.46), calls=%async_computation.3 | async-start | bytes 2097152 | tf_op jit(solution)/shard_map/all_to_all | solution.py:45
  80.7 7.9 %backward.2 = (bf16[8,64,512]{2,1,0:T(8,128)(2,1)S(1)}, bf16[8,64,512]{2,1,0:T(8,128)(2,1)S(1)}, bf16[4,64,512]{2,1,0:T(8,128)(2,1)S(1)}, bf16[4,64,512]{2,1,0:T...) custom-call(s32[4]{0:T(128)S(1)} %iota_xor_fusion.blk, ...), custom_call_target="tpu_custom_call" | custom-call | flops 2000000000 | bytes 1048576 | tf_op jit(solution)/shard_map/backward/pallas_call | solution.py:322
  88.6 0.5 collective-permute-start.17
  89.1 1.0 collective-permute-done.16.refs_1_
  90.2 0.4 collective-permute-done.17.refs_2_
  90.7 1.6 %collective-permute-start.18 = (bf16[8,64,512]{2,1,0:T(8,128)(2,1)S(1)}, bf16[8,64,512]{2,1,0:T(8,128)(2,1)S(1)}, u32[]{:S(2)}, u32[]{:S(2)}) collective-permute-start(bf16[8,64,512]{2,1,0:T(8,128)(2,1)S(1)} %add.8), channel_id=1, source_target_pairs={{0,2},{1,3},{2,0},{3,1},{4,6},{5,7},{6,4},{7,5},{8,10},{9,11},{10,... | collective-permute-start | bytes 1572872 | tf_op jit(solution)/shard_map/ppermute | solution.py:41
  92.2 7.9 %backward.3 = (bf16[8,64,512]{2,1,0:T(8,128)(2,1)S(1)}, bf16[8,64,512]{2,1,0:T(8,128)(2,1)S(1)}, bf16[4,64,512]{2,1,0:T(8,128)(2,1)}, bf16[4,64,512]{2,1,0:T(8,1...) custom-call(s32[4]{0:T(128)S(1)} %iota_xor_fusion.blk, bf16[8,64,1536]{2,1,0:T(8,128)(2,1)} %copy-done.3, ...), custom_call_target="tpu_custom_call" | custom-call | flops 2000000000 | bytes 1048576 | tf_op jit(solution)/shard_map/backward/pallas_call | solution.py:322
  100.2 0.5 collective-permute-start.20
  100.8 0.4 collective-permute-start.15
  101.2 0.5 collective-permute-done.19.refs_1_
  101.7 0.4 collective-permute-done.20.refs_2_
  102.2 0.3 collective-permute-done.14.refs_1_
  102.5 0.4 collective-permute-done.15.refs_2_
  102.9 1.8 %collective-permute-done.18.refs_3_ = bf16[8,64,512]{2,1,0:T(8,128)(2,1)S(1)} collective-permute-done((bf16[8,64,512]{2,1,0:T(8,128)(2,1)S(1)}, bf16[8,64,512]{2,1,0:T(8,128)(2,1)S(1)}, u32[]{:S(2)}, u32[]{:S(2)}) %collective-permute-start.18) | collective-permute-done | bytes 524320 | tf_op jit(solution)/shard_map/ppermute | solution.py:41
  104.7 1.0 add.9
  105.7 1.0 all-to-all-done.3.mixed
  106.7 4.9 %all-to-all-start.4 = ((bf16[8,64,512]{2,1,0:T(8,128)(2,1)}), bf16[8,64,512]{2,1,0:T(8,128)(2,1)S(1)}, u32[]{:S(2)}, u32[]{:S(2)}) async-start(bf16[8,64,512]{2,1,0:T(8,128)(2,1)} %add.9), calls=%async_computation.4 | async-start | bytes 1048576 | tf_op jit(solution)/shard_map/all_to_all | solution.py:45
  111.7 1.5 %collective-permute-start.23 = (bf16[8,64,512]{2,1,0:T(8,128)(2,1)S(1)}, bf16[8,64,512]{2,1,0:T(8,128)(2,1)S(1)}, u32[]{:S(2)}, u32[]{:S(2)}) collective-permute-start(bf16[8,64,512]{2,1,0:T(8,128)(2,1)S(1)} %add.10), channel_id=1, source_target_pairs={{0,2},{1,3},{2,0},{3,1},{4,6},{5,7},{6,4},{7,5},{8,10},{9,11},{10,... | collective-permute-start | bytes 1572872 | tf_op jit(solution)/shard_map/ppermute | solution.py:41
  113.2 0.5 collective-permute-start.22
  113.7 0.9 copy-done.15
  114.7 3.4 %project_out.1 = (bf16[512,512]{1,0:T(8,128)(2,1)S(1)}, bf16[512,512]{1,0:T(8,128)(2,1)S(1)}, bf16[256,512]{1,0:T(8,128)(2,1)S(1)}, bf16[256,512]{1,0:T(8,128)(2...) custom-call(s32[4]{0:T(128)S(1)} %iota_xor_fusion.blk, s32[512,1]{1,0:T(8,128)S(1)} %copy-done.15, ...), custom_call_target="tpu_custom_call" | custom-call | flops 2000000000 | bytes 1048576 | tf_op jit(solution)/shard_map/project_out/pallas_call | solution.py:453
  118.1 0.7 copy-done.11
  118.8 0.7 copy-done.13
  119.5 0.5 collective-permute-start.12
  120.0 4.5 %collective-permute-done.23.refs_3_ = bf16[8,64,512]{2,1,0:T(8,128)(2,1)S(1)} collective-permute-done((bf16[8,64,512]{2,1,0:T(8,128)(2,1)S(1)}, bf16[8,64,512]{2,1,0:T(8,128)(2,1)S(1)}, u32[]{:S(2)}, u32[]{:S(2)}) %collective-permute-start.23) | collective-permute-done | bytes 524320 | tf_op jit(solution)/shard_map/ppermute | solution.py:41
  124.5 1.0 add.11
  125.5 0.1 add.6
  125.7 5.7 %all-to-all-start.5 = ((bf16[8,64,512]{2,1,0:T(8,128)(2,1)}), bf16[8,64,512]{2,1,0:T(8,128)(2,1)S(1)}, u32[]{:S(2)}, u32[]{:S(2)}) async-start(bf16[8,64,512]{2,1,0:T(8,128)(2,1)} %add.11), calls=%async_computation.5 | async-start | bytes 1048576 | tf_op jit(solution)/shard_map/all_to_all | solution.py:45
  131.4 1.5 %collective-permute-start.13 = (bf16[512,512]{1,0:T(8,128)(2,1)S(1)}, bf16[512,512]{1,0:T(8,128)(2,1)S(1)}, u32[]{:S(2)}, u32[]{:S(2)}) collective-permute-start(bf16[512,512]{1,0:T(8,128)(2,1)S(1)} %add.6), channel_id=1, source_target_pairs={{0,2},{1,3},{2,0},{3,1},{4,6},{5,7},{6,4},{7,5},{8,10},{9,11},{10,... | collective-permute-start | bytes 1572872 | tf_op jit(solution)/shard_map/ppermute | solution.py:41
  132.9 0.5 collective-permute-start.9
  133.4 1.0 collective-permute-done.10.refs_2_
  134.5 0.4 collective-permute-done.9.refs_1_
  134.8 7.9 %collective-permute-done.13.refs_3_ = bf16[512,512]{1,0:T(8,128)(2,1)S(1)} collective-permute-done((bf16[512,512]{1,0:T(8,128)(2,1)S(1)}, bf16[512,512]{1,0:T(8,128)(2,1)S(1)}, u32[]{:S(2)}, u32[]{:S(2)}) %collective-permute-start.13) | collective-permute-done | bytes 524320 | tf_op jit(solution)/shard_map/ppermute | solution.py:41
  142.8 1.0 add.7
  143.8 0.1 all-to-all-done.5.refs_1_
  143.9 1.7 %to_tokens.1 = f32[512,512]{1,0:T(8,128)} custom-call(s32[512,1]{1,0:T(8,128)S(1)} %copy-done.16, bf16[8,64,512]{2,1,0:T(8,128)(2,1)S(1)} %all-to-all-done.4.refs_0_, bf16[8,64,512]{2,1,0:T(8,128)(2,1)S(1)} %all-to-all-done.5.refs_1_), custom_call_target="tpu_custom_call" | custom-call | flops 1000000000 | bytes 1048576 | tf_op jit(solution)/shard_map/to_tokens/pallas_call | solution.py:473
  (48 shorter events, 0.6 us)
Async XLA Ops:
  0.6 10.0 %copy-start.10 = (bf16[512,512]{1,0:T(8,128)(2,1)S(1)}, bf16[512,512]{1,0:T(8,128)(2,1)}, u32[]{:S(2)}) copy-start(bf16[512,512]{1,0:T(8,128)(2,1)} %a0.1) | copy-start | bytes 1572868
  3.3 21.8 %all-to-all-start = ((bf16[8,64,512]{2,1,0:T(8,128)(2,1)}), bf16[8,64,512]{2,1,0:T(8,128)(2,1)S(1)}, u32[]{:S(2)}, u32[]{:S(2)}) async-start(bf16[8,64,512]{2,1,0:T(8,128)(2,1)} %get-tuple-element.40), calls=%async_computation | async-start | bytes 1048576 | tf_op jit(solution)/shard_map/all_to_all | solution.py:45
  10.6 18.1 %collective-permute-start.7 = (bf16[512,512]{1,0:T(8,128)(2,1)S(1)}, bf16[512,512]{1,0:T(8,128)(2,1)S(1)}, u32[]{:S(2)}, u32[]{:S(2)}) collective-permute-start(bf16[512,512]{1,0:T(8,128)(2,1)S(1)} %copy-done.10), channel_id=1, source_target_pairs={{0,2},{1,3},{2,0},{3,1},{4,6},{5,7},{6,4},{7,5},{8,10},{9,11},{10,... | collective-permute-start | bytes 1572872 | tf_op jit(solution)/shard_map/ppermute | solution.py:41
  12.2 19.2 %copy-start.17 = (s32[1,512]{1,0:T(1,128)S(1)}, s32[1,512]{1,0:T(1,128)}, u32[]{:S(2)}) copy-start(s32[1,512]{1,0:T(1,128)} %get-tuple-element.39.slot_row) | copy-start | bytes 6148
  25.1 18.3 %all-to-all-start.1 = ((bf16[8,64,512]{2,1,0:T(8,128)(2,1)}), bf16[8,64,512]{2,1,0:T(8,128)(2,1)S(1)}, u32[]{:S(2)}, u32[]{:S(2)}) async-start(bf16[8,64,512]{2,1,0:T(8,128)(2,1)} %place_more.1), calls=%async_computation.1 | async-start | bytes 1048576 | tf_op jit(solution)/shard_map/all_to_all | solution.py:45
  28.7 2.0 %collective-permute-start.6 = (bf16[512,512]{1,0:T(8,128)(2,1)S(1)}, bf16[512,512]{1,0:T(8,128)(2,1)S(1)}, u32[]{:S(2)}, u32[]{:S(2)}) collective-permute-start(bf16[512,512]{1,0:T(8,128)(2,1)S(1)} %copy-done.10), channel_id=1, source_target_pairs={{0,1},{1,0},{2,3},{3,2},{4,5},{5,4},{6,7},{7,6},{8,9},{9,8},{10,11... | collective-permute-start | bytes 1572872 | tf_op jit(solution)/shard_map/ppermute | solution.py:41
  28.8 2.6 %collective-permute-start.8 = (bf16[512,512]{1,0:T(8,128)(2,1)S(1)}, bf16[512,512]{1,0:T(8,128)(2,1)S(1)}, u32[]{:S(2)}, u32[]{:S(2)}) collective-permute-start(bf16[512,512]{1,0:T(8,128)(2,1)S(1)} %collective-permute-done.7.a2), channel_id=1, source_target_pairs={{0,1},{1,0},{2,3},{3,2},{4,5},{5,4},{6,7},{7,6},{8,9},{9,8},{10,11... | collective-permute-start | bytes 1572872 | tf_op jit(solution)/shard_map/ppermute | solution.py:41
  29.2 14.0 %collective-permute-start.3 = (bf16[8,64,512]{2,1,0:T(8,128)(2,1)S(1)}, bf16[8,64,512]{2,1,0:T(8,128)(2,1)}, u32[]{:S(2)}, u32[]{:S(2)}) collective-permute-start(bf16[8,64,512]{2,1,0:T(8,128)(2,1)S(1)} %all-to-all-done.x0), channel_id=1, source_target_pairs={{0,2},{1,3},{2,0},{3,1},{4,6},{5,7},{6,4},{7,5},{8,10},{9,11},{10,... | collective-permute-start | bytes 1572872 | tf_op jit(solution)/shard_map/ppermute | solution.py:41
  34.9 1.0 copy-start.9
  35.9 16.2 %copy-start = (bf16[2048,512]{1,0:T(8,128)(2,1)S(1)}, bf16[2048,512]{1,0:T(8,128)(2,1)}, u32[]{:S(2)}) copy-start(bf16[2048,512]{1,0:T(8,128)(2,1)} %wq.7) | copy-start | bytes 6291460
  43.4 31.3 %all-to-all-start.2 = ((bf16[8,128,512]{2,1,0:T(8,128)(2,1)}), bf16[8,128,512]{2,1,0:T(8,128)(2,1)}, u32[]{:S(2)}, u32[]{:S(2)}) async-start(bf16[8,128,512]{2,1,0:T(8,128)(2,1)} %bitcast.2), calls=%async_computation.2 | async-start | bytes 2097152 | tf_op jit(solution)/shard_map/all_to_all | solution.py:45
  49.3 2.0 %collective-permute-start.2 = (bf16[8,64,512]{2,1,0:T(8,128)(2,1)S(1)}, bf16[8,64,512]{2,1,0:T(8,128)(2,1)S(1)}, u32[]{:S(2)}, u32[]{:S(2)}) collective-permute-start(bf16[8,64,512]{2,1,0:T(8,128)(2,1)S(1)} %all-to-all-done.x0), channel_id=1, source_target_pairs={{0,1},{1,0},{2,3},{3,2},{4,5},{5,4},{6,7},{7,6},{8,9},{9,8},{10,11... | collective-permute-start | bytes 1572872 | tf_op jit(solution)/shard_map/ppermute | solution.py:41
  49.3 2.9 %collective-permute-start.4 = (bf16[8,64,512]{2,1,0:T(8,128)(2,1)}, bf16[8,64,512]{2,1,0:T(8,128)(2,1)S(1)}, u32[]{:S(2)}, u32[]{:S(2)}) collective-permute-start(bf16[8,64,512]{2,1,0:T(8,128)(2,1)} %collective-permute-done.3.x2), channel_id=1, source_target_pairs={{0,1},{1,0},{2,3},{3,2},{4,5},{5,4},{6,7},{7,6},{8,9},{9,8},{10,11... | collective-permute-start | bytes 1572872 | tf_op jit(solution)/shard_map/ppermute | solution.py:41
  49.8 14.4 %collective-permute-start.1 = (bf16[8,64,512]{2,1,0:T(8,128)(2,1)S(1)}, bf16[8,64,512]{2,1,0:T(8,128)(2,1)S(1)}, u32[]{:S(2)}, u32[]{:S(2)}) collective-permute-start(bf16[8,64,512]{2,1,0:T(8,128)(2,1)S(1)} %all-to-all-done.1.x0), channel_id=1, source_target_pairs={{0,2},{1,3},{2,0},{3,1},{4,6},{5,7},{6,4},{7,5},{8,10},{9,11},{10,... | collective-permute-start | bytes 1572872 | tf_op jit(solution)/shard_map/ppermute | solution.py:41
  51.3 13.1 %collective-permute-start = (bf16[8,64,512]{2,1,0:T(8,128)(2,1)S(1)}, bf16[8,64,512]{2,1,0:T(8,128)(2,1)S(1)}, u32[]{:S(2)}, u32[]{:S(2)}) collective-permute-start(bf16[8,64,512]{2,1,0:T(8,128)(2,1)S(1)} %all-to-all-done.1.x0), channel_id=1, source_target_pairs={{0,1},{1,0},{2,3},{3,2},{4,5},{5,4},{6,7},{7,6},{8,9},{9,8},{10,11... | collective-permute-start | bytes 1572872 | tf_op jit(solution)/shard_map/ppermute | solution.py:41
  52.1 1.6 %copy-start.1 = (bf16[2048,512]{1,0:T(8,128)(2,1)S(1)}, bf16[2048,512]{1,0:T(8,128)(2,1)}, u32[]{:S(2)}) copy-start(bf16[2048,512]{1,0:T(8,128)(2,1)} %wk.7) | copy-start | bytes 6291460
  53.7 1.6 %copy-start.2 = (bf16[2048,512]{1,0:T(8,128)(2,1)S(1)}, bf16[2048,512]{1,0:T(8,128)(2,1)}, u32[]{:S(2)}) copy-start(bf16[2048,512]{1,0:T(8,128)(2,1)} %wv.7) | copy-start | bytes 6291460
  62.1 1.1 copy-start.4
  63.2 1.0 copy-start.7
  64.2 1.9 %collective-permute-start.5 = (bf16[8,64,512]{2,1,0:T(8,128)(2,1)S(1)}, bf16[8,64,512]{2,1,0:T(8,128)(2,1)S(1)}, u32[]{:S(2)}, u32[]{:S(2)}) collective-permute-start(bf16[8,64,512]{2,1,0:T(8,128)(2,1)S(1)} %collective-permute-done.1.x2), channel_id=1, source_target_pairs={{0,1},{1,0},{2,3},{3,2},{4,5},{5,4},{6,7},{7,6},{8,9},{9,8},{10,11... | collective-permute-start | bytes 1572872 | tf_op jit(solution)/shard_map/ppermute | solution.py:41
  72.4 1.2 copy-start.3
  73.6 1.0 copy-start.5
  74.5 6.1 %copy-start.8 = (f32[1,4,4,128,128]{4,3,2,1,0:T(8,128)S(1)}, f32[1,4,4,128,128]{4,3,2,1,0:T(8,128)}, u32[]{:S(2)}) copy-start(f32[1,4,4,128,128]{4,3,2,1,0:T(8,128)} %copy-done.7) | copy-start | bytes 3145732
  74.7 32.0 %all-to-all-start.3 = ((bf16[8,128,512]{2,1,0:T(8,128)(2,1)}), bf16[8,128,512]{2,1,0:T(8,128)(2,1)S(1)}, u32[]{:S(2)}, u32[]{:S(2)}) async-start(bf16[8,128,512]{2,1,0:T(8,128)(2,1)} %get-tuple-element.46), calls=%async_computation.3 | async-start | bytes 2097152 | tf_op jit(solution)/shard_map/all_to_all | solution.py:45
  88.6 3.7 %copy-start.6 = (f32[1,4,4,128,128]{4,3,2,1,0:T(8,128)S(1)}, f32[1,4,4,128,128]{4,3,2,1,0:T(8,128)}, u32[]{:S(2)}) copy-start(f32[1,4,4,128,128]{4,3,2,1,0:T(8,128)} %copy-done.5) | copy-start | bytes 3145732
  88.6 1.6 %collective-permute-start.16 = (bf16[4,64,512]{2,1,0:T(8,128)(2,1)S(1)}, bf16[4,64,512]{2,1,0:T(8,128)(2,1)S(1)}, u32[]{:S(2)}, u32[]{:S(2)}) collective-permute-start(bf16[4,64,512]{2,1,0:T(8,128)(2,1)S(1)} %get-tuple-element.60), channel_id=1, source_target_pairs={{0,1},{1,0},{2,3},{3,2},{4,5},{5,4},{6,7},{7,6},{8,9},{9,8},{10,11... | collective-permute-start | bytes 786440 | tf_op jit(solution)/shard_map/ppermute | solution.py:41
  88.6 1.9 %collective-permute-start.17 = (bf16[4,64,512]{2,1,0:T(8,128)(2,1)S(1)}, bf16[4,64,512]{2,1,0:T(8,128)(2,1)S(1)}, u32[]{:S(2)}, u32[]{:S(2)}) collective-permute-start(bf16[4,64,512]{2,1,0:T(8,128)(2,1)S(1)} %get-tuple-element.61), channel_id=1, source_target_pairs={{0,1},{1,0},{2,3},{3,2},{4,5},{5,4},{6,7},{7,6},{8,9},{9,8},{10,11... | collective-permute-start | bytes 786440 | tf_op jit(solution)/shard_map/ppermute | solution.py:41
  90.7 14.0 %collective-permute-start.18 = (bf16[8,64,512]{2,1,0:T(8,128)(2,1)S(1)}, bf16[8,64,512]{2,1,0:T(8,128)(2,1)S(1)}, u32[]{:S(2)}, u32[]{:S(2)}) collective-permute-start(bf16[8,64,512]{2,1,0:T(8,128)(2,1)S(1)} %add.8), channel_id=1, source_target_pairs={{0,2},{1,3},{2,0},{3,1},{4,6},{5,7},{6,4},{7,5},{8,10},{9,11},{10,... | collective-permute-start | bytes 1572872 | tf_op jit(solution)/shard_map/ppermute | solution.py:41
  100.1 1.6 %collective-permute-start.19 = (bf16[4,64,512]{2,1,0:T(8,128)(2,1)S(1)}, bf16[4,64,512]{2,1,0:T(8,128)(2,1)S(1)}, u32[]{:S(2)}, u32[]{:S(2)}) collective-permute-start(bf16[4,64,512]{2,1,0:T(8,128)(2,1)S(1)} %get-tuple-element.66), channel_id=1, source_target_pairs={{0,1},{1,0},{2,3},{3,2},{4,5},{5,4},{6,7},{7,6},{8,9},{9,8},{10,11... | collective-permute-start | bytes 786440 | tf_op jit(solution)/shard_map/ppermute | solution.py:41
  100.2 1.9 %collective-permute-start.20 = (bf16[4,64,512]{2,1,0:T(8,128)(2,1)S(1)}, bf16[4,64,512]{2,1,0:T(8,128)(2,1)S(1)}, u32[]{:S(2)}, u32[]{:S(2)}) collective-permute-start(bf16[4,64,512]{2,1,0:T(8,128)(2,1)S(1)} %get-tuple-element.67), channel_id=1, source_target_pairs={{0,1},{1,0},{2,3},{3,2},{4,5},{5,4},{6,7},{7,6},{8,9},{9,8},{10,11... | collective-permute-start | bytes 786440 | tf_op jit(solution)/shard_map/ppermute | solution.py:41
  100.7 1.8 %collective-permute-start.14 = (bf16[4,64,512]{2,1,0:T(8,128)(2,1)S(1)}, bf16[4,64,512]{2,1,0:T(8,128)(2,1)S(1)}, u32[]{:S(2)}, u32[]{:S(2)}) collective-permute-start(bf16[4,64,512]{2,1,0:T(8,128)(2,1)S(1)} %get-tuple-element.57), channel_id=1, source_target_pairs={{0,1},{1,0},{2,3},{3,2},{4,5},{5,4},{6,7},{7,6},{8,9},{9,8},{10,11... | collective-permute-start | bytes 786440 | tf_op jit(solution)/shard_map/ppermute | solution.py:41
  100.8 2.1 %collective-permute-start.15 = (bf16[4,64,512]{2,1,0:T(8,128)(2,1)S(1)}, bf16[4,64,512]{2,1,0:T(8,128)(2,1)S(1)}, u32[]{:S(2)}, u32[]{:S(2)}) collective-permute-start(bf16[4,64,512]{2,1,0:T(8,128)(2,1)S(1)} %get-tuple-element.58), channel_id=1, source_target_pairs={{0,1},{1,0},{2,3},{3,2},{4,5},{5,4},{6,7},{7,6},{8,9},{9,8},{10,11... | collective-permute-start | bytes 786440 | tf_op jit(solution)/shard_map/ppermute | solution.py:41
  106.7 19.0 %all-to-all-start.4 = ((bf16[8,64,512]{2,1,0:T(8,128)(2,1)}), bf16[8,64,512]{2,1,0:T(8,128)(2,1)S(1)}, u32[]{:S(2)}, u32[]{:S(2)}) async-start(bf16[8,64,512]{2,1,0:T(8,128)(2,1)} %add.9), calls=%async_computation.4 | async-start | bytes 1048576 | tf_op jit(solution)/shard_map/all_to_all | solution.py:45
  111.7 12.9 %collective-permute-start.23 = (bf16[8,64,512]{2,1,0:T(8,128)(2,1)S(1)}, bf16[8,64,512]{2,1,0:T(8,128)(2,1)S(1)}, u32[]{:S(2)}, u32[]{:S(2)}) collective-permute-start(bf16[8,64,512]{2,1,0:T(8,128)(2,1)S(1)} %add.10), channel_id=1, source_target_pairs={{0,2},{1,3},{2,0},{3,1},{4,6},{5,7},{6,4},{7,5},{8,10},{9,11},{10,... | collective-permute-start | bytes 1572872 | tf_op jit(solution)/shard_map/ppermute | solution.py:41
  113.2 6.8 %collective-permute-start.21 = (bf16[4,64,512]{2,1,0:T(8,128)(2,1)}, bf16[4,64,512]{2,1,0:T(8,128)(2,1)S(1)}, u32[]{:S(2)}, u32[]{:S(2)}) collective-permute-start(bf16[4,64,512]{2,1,0:T(8,128)(2,1)} %get-tuple-element.70), channel_id=1, source_target_pairs={{0,1},{1,0},{2,3},{3,2},{4,5},{5,4},{6,7},{7,6},{8,9},{9,8},{10,11... | collective-permute-start | bytes 786440 | tf_op jit(solution)/shard_map/ppermute | solution.py:41
  113.2 6.8 %collective-permute-start.22 = (bf16[4,64,512]{2,1,0:T(8,128)(2,1)S(1)}, bf16[4,64,512]{2,1,0:T(8,128)(2,1)S(1)}, u32[]{:S(2)}, u32[]{:S(2)}) collective-permute-start(bf16[4,64,512]{2,1,0:T(8,128)(2,1)S(1)} %get-tuple-element.71), channel_id=1, source_target_pairs={{0,1},{1,0},{2,3},{3,2},{4,5},{5,4},{6,7},{7,6},{8,9},{9,8},{10,11... | collective-permute-start | bytes 786440 | tf_op jit(solution)/shard_map/ppermute | solution.py:41
  113.7 0.9 copy-start.15
  118.1 0.7 copy-start.11
  118.8 0.7 copy-start.13
  119.5 6.0 %collective-permute-start.11 = (bf16[256,512]{1,0:T(8,128)(2,1)S(1)}, bf16[256,512]{1,0:T(8,128)(2,1)S(1)}, u32[]{:S(2)}, u32[]{:S(2)}) collective-permute-start(bf16[256,512]{1,0:T(8,128)(2,1)S(1)} %get-tuple-element.51), channel_id=1, source_target_pairs={{0,1},{1,0},{2,3},{3,2},{4,5},{5,4},{6,7},{7,6},{8,9},{9,8},{10,11... | collective-permute-start | bytes 786440 | tf_op jit(solution)/shard_map/ppermute | solution.py:41
  119.5 6.0 %collective-permute-start.12 = (bf16[256,512]{1,0:T(8,128)(2,1)S(1)}, bf16[256,512]{1,0:T(8,128)(2,1)S(1)}, u32[]{:S(2)}, u32[]{:S(2)}) collective-permute-start(bf16[256,512]{1,0:T(8,128)(2,1)S(1)} %get-tuple-element.52), channel_id=1, source_target_pairs={{0,1},{1,0},{2,3},{3,2},{4,5},{5,4},{6,7},{7,6},{8,9},{9,8},{10,11... | collective-permute-start | bytes 786440 | tf_op jit(solution)/shard_map/ppermute | solution.py:41
  124.5 8.4 %copy-start.14 = (bf16[256,512]{1,0:T(8,128)(2,1)S(1)}, bf16[256,512]{1,0:T(8,128)(2,1)}, u32[]{:S(2)}) copy-start(bf16[256,512]{1,0:T(8,128)(2,1)} %copy-done.13) | copy-start | bytes 786436
  124.5 8.4 %copy-start.12 = (bf16[256,512]{1,0:T(8,128)(2,1)S(1)}, bf16[256,512]{1,0:T(8,128)(2,1)}, u32[]{:S(2)}) copy-start(bf16[256,512]{1,0:T(8,128)(2,1)} %copy-done.11) | copy-start | bytes 786436
  125.5 18.4 %copy-start.16 = (s32[512,1]{1,0:T(8,128)S(1)}, s32[512,1]{1,0:T(8,128)}, u32[]{:S(2)}) copy-start(s32[512,1]{1,0:T(8,128)} %get-tuple-element.38.slot_col) | copy-start | bytes 6148
  125.7 18.2 %all-to-all-start.5 = ((bf16[8,64,512]{2,1,0:T(8,128)(2,1)}), bf16[8,64,512]{2,1,0:T(8,128)(2,1)S(1)}, u32[]{:S(2)}, u32[]{:S(2)}) async-start(bf16[8,64,512]{2,1,0:T(8,128)(2,1)} %add.11), calls=%async_computation.5 | async-start | bytes 1048576 | tf_op jit(solution)/shard_map/all_to_all | solution.py:45
  131.4 11.4 %collective-permute-start.13 = (bf16[512,512]{1,0:T(8,128)(2,1)S(1)}, bf16[512,512]{1,0:T(8,128)(2,1)S(1)}, u32[]{:S(2)}, u32[]{:S(2)}) collective-permute-start(bf16[512,512]{1,0:T(8,128)(2,1)S(1)} %add.6), channel_id=1, source_target_pairs={{0,2},{1,3},{2,0},{3,1},{4,6},{5,7},{6,4},{7,5},{8,10},{9,11},{10,... | collective-permute-start | bytes 1572872 | tf_op jit(solution)/shard_map/ppermute | solution.py:41
  132.9 1.5 %collective-permute-start.10 = (bf16[256,512]{1,0:T(8,128)(2,1)S(1)}, bf16[256,512]{1,0:T(8,128)(2,1)S(1)}, u32[]{:S(2)}, u32[]{:S(2)}) collective-permute-start(bf16[256,512]{1,0:T(8,128)(2,1)S(1)} %copy-done.14), channel_id=1, source_target_pairs={{0,1},{1,0},{2,3},{3,2},{4,5},{5,4},{6,7},{7,6},{8,9},{9,8},{10,11... | collective-permute-start | bytes 786440 | tf_op jit(solution)/shard_map/ppermute | solution.py:41
  132.9 1.9 %collective-permute-start.9 = (bf16[256,512]{1,0:T(8,128)(2,1)S(1)}, bf16[256,512]{1,0:T(8,128)(2,1)S(1)}, u32[]{:S(2)}, u32[]{:S(2)}) collective-permute-start(bf16[256,512]{1,0:T(8,128)(2,1)S(1)} %copy-done.12), channel_id=1, source_target_pairs={{0,1},{1,0},{2,3},{3,2},{4,5},{5,4},{6,7},{7,6},{8,9},{9,8},{10,11... | collective-permute-start | bytes 786440 | tf_op jit(solution)/shard_map/ppermute | solution.py:41

commit v8 on v7

--- a/solution.py
+++ b/solution.py
@@ -551,7 +551,7 @@
     for x in xs:
         x_across.append(swap(x, 2))
     g_slots = head_grads(blk, g_parts, w_out, slot_row).reshape(seq_count, per, -1)
-    g = exchange(after(g_slots, xs[-1], x_across[0]))
+    g = exchange(after(g_slots, xs[-1]))
 
     mixed, saved = (None, [])
     for c in range(chunks):

time: 146 us -> 145 us (level)
  starting transfers between devices: 46.8 us -> 45 us
    all_to_all x6, waiting for transfers between devices: 12.1 us -> 19.6 us  [exchange(): return lax.all_to_all(x, 'seq', split_axis=0, concat_axis=0, tiled=True)]
    ppermute x24, waiting for transfers between devices: 29.2 us -> 22 us  [swap(): return lax.ppermute(x, 'tp', [(i, i ^ bit) for i in range(count)])]
    all_to_all x6, starting transfers between devices: 33.4 us -> 31.5 us  [exchange(): return lax.all_to_all(x, 'seq', split_axis=0, concat_axis=0, tiled=True)]
  transfers between devices with their start and end apart: 30 -> 30, of which waited for: 20 -> 19; matrix products, arithmetic and copies ran while one was open for 0% -> 0% of each run, Pallas kernels for 28% -> 29%
where the time goes in v8:
time: 145 us; the launch traced here: 144 us
  Pallas kernels  45.8 us (32%)
  starting transfers between devices  45 us (31%)
  waiting for transfers between devices  41.6 us (29%)
  local copies, waits for them, and re-layouts  10.8 us (7%)
    all_to_all x6, starting transfers between devices, exchange(): return lax.all_to_all(x, 'seq', split_axis=0, concat_axis=0, tiled=True)  31.5 us
    ppermute x24, waiting for transfers between devices, swap(): return lax.ppermute(x, 'tp', [(i, i ^ bit) for i in range(count)])  22 us
    all_to_all x6, waiting for transfers between devices, exchange(): return lax.all_to_all(x, 'seq', split_axis=0, concat_axis=0, tiled=True)  19.6 us
    pallas_call x2, Pallas kernels, backward(): pl.pallas_call(backward_kernel, grid=(steps,), out_shape=(shape,) * 2 + (...  15.8 us
    ppermute x24, starting transfers between devices, swap(): return lax.ppermute(x, 'tp', [(i, i ^ bit) for i in range(count)])  13.4 us
    pallas_call x2, Pallas kernels, forward(): pl.pallas_call(forward_kernel, grid=(steps,), out_shape=(jax.ShapeDtypeSt...  13 us
    unnamed x36, local copies, waits for them, and re-layouts  10.8 us
    pallas_call x1, Pallas kernels, head_grads(): pl.pallas_call(head_grads_kernel, out_shape=jax.ShapeDtypeStruct((CLUSTER...  3.5 us
  transfers between devices with their start and end apart: 30, of which 19 were waited for; matrix products, arithmetic and copies ran while one was open for 0% of the time, Pallas kernels for 29%

profile of v8, /device:TPU:0, one launch (start us, length us, event | category | flops | bytes accessed | tf_op | source)
XLA Modules:
  0.0 143.9 jit_solution(7116280677869787003)
XLA Ops:
  0.6 2.7 %place.1 = (s32[512,1]{1,0:T(8,128)}, s32[1,512]{1,0:T(1,128)}, bf16[8,64,512]{2,1,0:T(8,128)(2,1)}) custom-call(s32[1,512]{1,0:T(1,128)} %bitcast.3, bf16[512,512]{1,0:T(8,128)(2,1)} %x_ref.3), custom_call_target="tpu_custom_call" | custom-call | flops 1000000000 | bytes 1048576 | tf_op jit(solution)/shard_map/place/pallas_call | solution.py:94
  3.3 7.3 %all-to-all-start = ((bf16[8,64,512]{2,1,0:T(8,128)(2,1)}), bf16[8,64,512]{2,1,0:T(8,128)(2,1)S(1)}, u32[]{:S(2)}, u32[]{:S(2)}) async-start(bf16[8,64,512]{2,1,0:T(8,128)(2,1)} %get-tuple-element.40), calls=%async_computation | async-start | bytes 1048576 | tf_op jit(solution)/shard_map/all_to_all | solution.py:45
  10.6 1.6 %collective-permute-start.7 = (bf16[512,512]{1,0:T(8,128)(2,1)S(1)}, bf16[512,512]{1,0:T(8,128)(2,1)S(1)}, u32[]{:S(2)}, u32[]{:S(2)}) collective-permute-start(bf16[512,512]{1,0:T(8,128)(2,1)S(1)} %copy-done.10), channel_id=1, source_target_pairs={{0,2},{1,3},{2,0},{3,1},{4,6},{5,7},{6,4},{7,5},{8,10},{9,11},{10,... | collective-permute-start | bytes 1572872 | tf_op jit(solution)/shard_map/ppermute | solution.py:41
  12.2 2.3 %place_more.1 = bf16[8,64,512]{2,1,0:T(8,128)(2,1)} custom-call(s32[1,512]{1,0:T(1,128)} %get-tuple-element.39.slot_row, bf16[512,512]{1,0:T(8,128)(2,1)} %x_ref.3), custom_call_target="tpu_custom_call" | custom-call | flops 1000000000 | bytes 1048576 | tf_op jit(solution)/shard_map/place_more/pallas_call | solution.py:108
  14.5 10.6 %all-to-all-done.x0 = bf16[8,64,512]{2,1,0:T(8,128)(2,1)S(1)} async-done(((bf16[8,64,512]{2,1,0:T(8,128)(2,1)}), bf16[8,64,512]{2,1,0:T(8,128)(2,1)S(1)}, u32[]{:S(2)}, u32[]{:S(2)}) %all-to-all-start) | async-done | bytes 524320 | tf_op jit(solution)/shard_map/all_to_all | solution.py:45
  25.1 3.6 %all-to-all-start.1 = ((bf16[8,64,512]{2,1,0:T(8,128)(2,1)}), bf16[8,64,512]{2,1,0:T(8,128)(2,1)S(1)}, u32[]{:S(2)}, u32[]{:S(2)}) async-start(bf16[8,64,512]{2,1,0:T(8,128)(2,1)} %place_more.1), calls=%async_computation.1 | async-start | bytes 1048576 | tf_op jit(solution)/shard_map/all_to_all | solution.py:45
  28.8 0.5 collective-permute-start.8
  29.3 1.5 %collective-permute-start.3 = (bf16[8,64,512]{2,1,0:T(8,128)(2,1)S(1)}, bf16[8,64,512]{2,1,0:T(8,128)(2,1)}, u32[]{:S(2)}, u32[]{:S(2)}) collective-permute-start(bf16[8,64,512]{2,1,0:T(8,128)(2,1)S(1)} %all-to-all-done.x0), channel_id=1, source_target_pairs={{0,2},{1,3},{2,0},{3,1},{4,6},{5,7},{6,4},{7,5},{8,10},{9,11},{10,... | collective-permute-start | bytes 1572872 | tf_op jit(solution)/shard_map/ppermute | solution.py:41
  30.7 0.6 collective-permute-done.8.a3
  31.4 3.5 %head_grads.1 = bf16[1024,512]{1,0:T(8,128)(2,1)S(1)} custom-call(s32[4]{0:T(128)S(1)} %iota_xor_fusion.blk, bf16[512,512]{1,0:T(8,128)(2,1)S(1)} %copy-done.10, bf16[512,512]{1,0:T(8,128)(2,1)S(1)} %collective-permute-done.6.a1, bf16[512,512]{1,0:T(8,128)(2,1)S(1)} %collective-permute-done.7.a2, bf16[512,512]{1,0:T(8,128)(2,1)S(1)} %collective-permute-done.8.a3, ...), custom_call_target="tpu_custom_call" | custom-call | flops 2000000000 | bytes 1048576 | tf_op jit(solution)/shard_map/head_grads/pallas_call | solution.py:125
  34.9 1.0 copy-done.9
  35.9 7.5 %all-to-all-done.1.x0 = bf16[8,64,512]{2,1,0:T(8,128)(2,1)S(1)} async-done(((bf16[8,64,512]{2,1,0:T(8,128)(2,1)}), bf16[8,64,512]{2,1,0:T(8,128)(2,1)S(1)}, u32[]{:S(2)}, u32[]{:S(2)}) %all-to-all-start.1) | async-done | bytes 524320 | tf_op jit(solution)/shard_map/all_to_all | solution.py:45
  43.4 4.2 %all-to-all-start.2 = ((bf16[8,128,512]{2,1,0:T(8,128)(2,1)}), bf16[8,128,512]{2,1,0:T(8,128)(2,1)}, u32[]{:S(2)}, u32[]{:S(2)}) async-start(bf16[8,128,512]{2,1,0:T(8,128)(2,1)} %bitcast.2), calls=%async_computation.2 | async-start | bytes 2097152 | tf_op jit(solution)/shard_map/all_to_all | solution.py:45
  47.7 0.5 collective-permute-start.4
  48.2 1.5 %collective-permute-start.1 = (bf16[8,64,512]{2,1,0:T(8,128)(2,1)S(1)}, bf16[8,64,512]{2,1,0:T(8,128)(2,1)S(1)}, u32[]{:S(2)}, u32[]{:S(2)}) collective-permute-start(bf16[8,64,512]{2,1,0:T(8,128)(2,1)S(1)} %all-to-all-done.1.x0), channel_id=1, source_target_pairs={{0,2},{1,3},{2,0},{3,1},{4,6},{5,7},{6,4},{7,5},{8,10},{9,11},{10,... | collective-permute-start | bytes 1572872 | tf_op jit(solution)/shard_map/ppermute | solution.py:41
  49.7 0.9 collective-permute-done.4.x3
  50.6 1.6 %copy-done.1 = bf16[2048,512]{1,0:T(8,128)(2,1)S(1)} copy-done((bf16[2048,512]{1,0:T(8,128)(2,1)S(1)}, bf16[2048,512]{1,0:T(8,128)(2,1)}, u32[]{:S(2)}) %copy-start.1) | copy-done | bytes 2097176
  52.2 1.6 %copy-done.2 = bf16[2048,512]{1,0:T(8,128)(2,1)S(1)} copy-done((bf16[2048,512]{1,0:T(8,128)(2,1)S(1)}, bf16[2048,512]{1,0:T(8,128)(2,1)}, u32[]{:S(2)}) %copy-start.2) | copy-done | bytes 2097176
  53.8 6.8 %forward.2 = (bf16[8,128,512]{2,1,0:T(8,128)(2,1)}, bf16[8,64,1536]{2,1,0:T(8,128)(2,1)S(1)}, f32[1,4,4,128,128]{4,3,2,1,0:T(8,128)S(1)}) custom-call(s32[4]{0:T(128)S(1)} %iota_xor_fusion.blk, bf16[8,64,512]{2,1,0:T(8,128)(2,1)S(1)} %all-to-all-done.x0, bf16[8,64,512]{2,1,0:T(8,128)(2,1)S(1)} %collective-permute-done.2.x1, ...), custom_call_target="tpu_custom_call" | custom-call | flops 2000000000 | bytes 1048576 | tf_op jit(solution)/shard_map/forward/pallas_call | solution.py:289
  60.6 1.1 copy-done.4
  61.7 1.0 copy-done.7
  62.7 0.1 collective-permute-start.5
  62.8 1.8 %collective-permute-done.5.x3 = bf16[8,64,512]{2,1,0:T(8,128)(2,1)S(1)} collective-permute-done((bf16[8,64,512]{2,1,0:T(8,128)(2,1)S(1)}, bf16[8,64,512]{2,1,0:T(8,128)(2,1)S(1)}, u32[]{:S(2)}, u32[]{:S(2)}) %collective-permute-start.5) | collective-permute-done | bytes 524320 | tf_op jit(solution)/shard_map/ppermute | solution.py:41
  64.6 6.3 %forward.3 = (bf16[8,128,512]{2,1,0:T(8,128)(2,1)}, bf16[8,64,1536]{2,1,0:T(8,128)(2,1)S(1)}, f32[1,4,4,128,128]{4,3,2,1,0:T(8,128)S(1)}) custom-call(s32[4]{0:T(128)S(1)} %iota_xor_fusion.blk, bf16[8,64,512]{2,1,0:T(8,128)(2,1)S(1)} %all-to-all-done.1.x0, bf16[8,64,512]{2,1,0:T(8,128)(2,1)S(1)} %collective-permute-done.x1, ...), custom_call_target="tpu_custom_call", output_to_operand_aliasing={{0}: (8, {})} | custom-call | flops 2000000000 | bytes 1048576 | tf_op jit(solution)/shard_map/forward/pallas_call | solution.py:289
  70.8 1.2 copy-done.3
  72.0 1.0 copy-done.5
  73.0 0.3 all-to-all-done.2.g_ref
  73.3 5.7 %all-to-all-start.3 = ((bf16[8,128,512]{2,1,0:T(8,128)(2,1)}), bf16[8,128,512]{2,1,0:T(8,128)(2,1)S(1)}, u32[]{:S(2)}, u32[]{:S(2)}) async-start(bf16[8,128,512]{2,1,0:T(8,128)(2,1)} %get-tuple-element.46), calls=%async_computation.3 | async-start | bytes 2097152 | tf_op jit(solution)/shard_map/all_to_all | solution.py:45
  79.0 7.9 %backward.2 = (bf16[8,64,512]{2,1,0:T(8,128)(2,1)S(1)}, bf16[8,64,512]{2,1,0:T(8,128)(2,1)S(1)}, bf16[4,64,512]{2,1,0:T(8,128)(2,1)S(1)}, bf16[4,64,512]{2,1,0:T...) custom-call(s32[4]{0:T(128)S(1)} %iota_xor_fusion.blk, ...), custom_call_target="tpu_custom_call" | custom-call | flops 2000000000 | bytes 1048576 | tf_op jit(solution)/shard_map/backward/pallas_call | solution.py:322
  87.0 0.5 collective-permute-start.17
  87.5 1.0 collective-permute-done.16.refs_1_
  88.5 0.4 collective-permute-done.17.refs_2_
  88.9 0.1 add.8
  89.0 1.6 %collective-permute-start.18 = (bf16[8,64,512]{2,1,0:T(8,128)(2,1)S(1)}, bf16[8,64,512]{2,1,0:T(8,128)(2,1)S(1)}, u32[]{:S(2)}, u32[]{:S(2)}) collective-permute-start(bf16[8,64,512]{2,1,0:T(8,128)(2,1)S(1)} %add.8), channel_id=1, source_target_pairs={{0,2},{1,3},{2,0},{3,1},{4,6},{5,7},{6,4},{7,5},{8,10},{9,11},{10,... | collective-permute-start | bytes 1572872 | tf_op jit(solution)/shard_map/ppermute | solution.py:41
  90.5 7.9 %backward.3 = (bf16[8,64,512]{2,1,0:T(8,128)(2,1)S(1)}, bf16[8,64,512]{2,1,0:T(8,128)(2,1)S(1)}, bf16[4,64,512]{2,1,0:T(8,128)(2,1)}, bf16[4,64,512]{2,1,0:T(8,1...) custom-call(s32[4]{0:T(128)S(1)} %iota_xor_fusion.blk, bf16[8,64,1536]{2,1,0:T(8,128)(2,1)} %copy-done.3, ...), custom_call_target="tpu_custom_call" | custom-call | flops 2000000000 | bytes 1048576 | tf_op jit(solution)/shard_map/backward/pallas_call | solution.py:322
  98.5 0.5 collective-permute-start.20
  99.1 0.4 collective-permute-start.15
  99.5 0.5 collective-permute-done.19.refs_1_
  100.0 0.4 collective-permute-done.20.refs_2_
  100.5 0.3 collective-permute-done.14.refs_1_
  100.8 0.4 collective-permute-done.15.refs_2_
  101.1 1.9 %collective-permute-done.18.refs_3_ = bf16[8,64,512]{2,1,0:T(8,128)(2,1)S(1)} collective-permute-done((bf16[8,64,512]{2,1,0:T(8,128)(2,1)S(1)}, bf16[8,64,512]{2,1,0:T(8,128)(2,1)S(1)}, u32[]{:S(2)}, u32[]{:S(2)}) %collective-permute-start.18) | collective-permute-done | bytes 524320 | tf_op jit(solution)/shard_map/ppermute | solution.py:41
  103.0 1.0 add.9
  104.0 1.0 all-to-all-done.3.mixed
  105.0 4.9 %all-to-all-start.4 = ((bf16[8,64,512]{2,1,0:T(8,128)(2,1)}), bf16[8,64,512]{2,1,0:T(8,128)(2,1)S(1)}, u32[]{:S(2)}, u32[]{:S(2)}) async-start(bf16[8,64,512]{2,1,0:T(8,128)(2,1)} %add.9), calls=%async_computation.4 | async-start | bytes 1048576 | tf_op jit(solution)/shard_map/all_to_all | solution.py:45
  110.0 1.5 %collective-permute-start.23 = (bf16[8,64,512]{2,1,0:T(8,128)(2,1)S(1)}, bf16[8,64,512]{2,1,0:T(8,128)(2,1)S(1)}, u32[]{:S(2)}, u32[]{:S(2)}) collective-permute-start(bf16[8,64,512]{2,1,0:T(8,128)(2,1)S(1)} %add.10), channel_id=1, source_target_pairs={{0,2},{1,3},{2,0},{3,1},{4,6},{5,7},{6,4},{7,5},{8,10},{9,11},{10,... | collective-permute-start | bytes 1572872 | tf_op jit(solution)/shard_map/ppermute | solution.py:41
  111.5 0.5 collective-permute-start.22
  112.0 0.9 copy-done.15
  112.9 3.4 %project_out.1 = (bf16[512,512]{1,0:T(8,128)(2,1)S(1)}, bf16[512,512]{1,0:T(8,128)(2,1)S(1)}, bf16[256,512]{1,0:T(8,128)(2,1)S(1)}, bf16[256,512]{1,0:T(8,128)(2...) custom-call(s32[4]{0:T(128)S(1)} %iota_xor_fusion.blk, s32[512,1]{1,0:T(8,128)S(1)} %copy-done.15, ...), custom_call_target="tpu_custom_call" | custom-call | flops 2000000000 | bytes 1048576 | tf_op jit(solution)/shard_map/project_out/pallas_call | solution.py:453
  116.4 0.7 copy-done.11
  117.1 0.7 copy-done.13
  117.8 0.5 collective-permute-start.12
  118.3 4.5 %collective-permute-done.23.refs_3_ = bf16[8,64,512]{2,1,0:T(8,128)(2,1)S(1)} collective-permute-done((bf16[8,64,512]{2,1,0:T(8,128)(2,1)S(1)}, bf16[8,64,512]{2,1,0:T(8,128)(2,1)S(1)}, u32[]{:S(2)}, u32[]{:S(2)}) %collective-permute-start.23) | collective-permute-done | bytes 524320 | tf_op jit(solution)/shard_map/ppermute | solution.py:41
  122.8 1.0 add.11
  123.8 0.1 add.6
  124.0 5.7 %all-to-all-start.5 = ((bf16[8,64,512]{2,1,0:T(8,128)(2,1)}), bf16[8,64,512]{2,1,0:T(8,128)(2,1)S(1)}, u32[]{:S(2)}, u32[]{:S(2)}) async-start(bf16[8,64,512]{2,1,0:T(8,128)(2,1)} %add.11), calls=%async_computation.5 | async-start | bytes 1048576 | tf_op jit(solution)/shard_map/all_to_all | solution.py:45
  129.7 1.5 %collective-permute-start.13 = (bf16[512,512]{1,0:T(8,128)(2,1)S(1)}, bf16[512,512]{1,0:T(8,128)(2,1)S(1)}, u32[]{:S(2)}, u32[]{:S(2)}) collective-permute-start(bf16[512,512]{1,0:T(8,128)(2,1)S(1)} %add.6), channel_id=1, source_target_pairs={{0,2},{1,3},{2,0},{3,1},{4,6},{5,7},{6,4},{7,5},{8,10},{9,11},{10,... | collective-permute-start | bytes 1572872 | tf_op jit(solution)/shard_map/ppermute | solution.py:41
  131.2 0.5 collective-permute-start.9
  131.7 1.0 collective-permute-done.10.refs_2_
  132.7 0.4 collective-permute-done.9.refs_1_
  133.1 8.0 %collective-permute-done.13.refs_3_ = bf16[512,512]{1,0:T(8,128)(2,1)S(1)} collective-permute-done((bf16[512,512]{1,0:T(8,128)(2,1)S(1)}, bf16[512,512]{1,0:T(8,128)(2,1)S(1)}, u32[]{:S(2)}, u32[]{:S(2)}) %collective-permute-start.13) | collective-permute-done | bytes 524320 | tf_op jit(solution)/shard_map/ppermute | solution.py:41
  141.1 1.0 add.7
  142.1 0.1 all-to-all-done.5.refs_1_
  142.2 1.7 %to_tokens.1 = f32[512,512]{1,0:T(8,128)} custom-call(s32[512,1]{1,0:T(8,128)S(1)} %copy-done.16, bf16[8,64,512]{2,1,0:T(8,128)(2,1)S(1)} %all-to-all-done.4.refs_0_, bf16[8,64,512]{2,1,0:T(8,128)(2,1)S(1)} %all-to-all-done.5.refs_1_), custom_call_target="tpu_custom_call" | custom-call | flops 1000000000 | bytes 1048576 | tf_op jit(solution)/shard_map/to_tokens/pallas_call | solution.py:473
  (48 shorter events, 0.5 us)
Async XLA Ops:
  0.6 10.0 %copy-start.10 = (bf16[512,512]{1,0:T(8,128)(2,1)S(1)}, bf16[512,512]{1,0:T(8,128)(2,1)}, u32[]{:S(2)}) copy-start(bf16[512,512]{1,0:T(8,128)(2,1)} %a0.1) | copy-start | bytes 1572868
  3.3 21.8 %all-to-all-start = ((bf16[8,64,512]{2,1,0:T(8,128)(2,1)}), bf16[8,64,512]{2,1,0:T(8,128)(2,1)S(1)}, u32[]{:S(2)}, u32[]{:S(2)}) async-start(bf16[8,64,512]{2,1,0:T(8,128)(2,1)} %get-tuple-element.40), calls=%async_computation | async-start | bytes 1048576 | tf_op jit(solution)/shard_map/all_to_all | solution.py:45
  10.6 18.1 %collective-permute-start.7 = (bf16[512,512]{1,0:T(8,128)(2,1)S(1)}, bf16[512,512]{1,0:T(8,128)(2,1)S(1)}, u32[]{:S(2)}, u32[]{:S(2)}) collective-permute-start(bf16[512,512]{1,0:T(8,128)(2,1)S(1)} %copy-done.10), channel_id=1, source_target_pairs={{0,2},{1,3},{2,0},{3,1},{4,6},{5,7},{6,4},{7,5},{8,10},{9,11},{10,... | collective-permute-start | bytes 1572872 | tf_op jit(solution)/shard_map/ppermute | solution.py:41
  12.2 19.2 %copy-start.17 = (s32[1,512]{1,0:T(1,128)S(1)}, s32[1,512]{1,0:T(1,128)}, u32[]{:S(2)}) copy-start(s32[1,512]{1,0:T(1,128)} %get-tuple-element.39.slot_row) | copy-start | bytes 6148
  25.1 18.3 %all-to-all-start.1 = ((bf16[8,64,512]{2,1,0:T(8,128)(2,1)}), bf16[8,64,512]{2,1,0:T(8,128)(2,1)S(1)}, u32[]{:S(2)}, u32[]{:S(2)}) async-start(bf16[8,64,512]{2,1,0:T(8,128)(2,1)} %place_more.1), calls=%async_computation.1 | async-start | bytes 1048576 | tf_op jit(solution)/shard_map/all_to_all | solution.py:45
  28.7 2.0 %collective-permute-start.6 = (bf16[512,512]{1,0:T(8,128)(2,1)S(1)}, bf16[512,512]{1,0:T(8,128)(2,1)S(1)}, u32[]{:S(2)}, u32[]{:S(2)}) collective-permute-start(bf16[512,512]{1,0:T(8,128)(2,1)S(1)} %copy-done.10), channel_id=1, source_target_pairs={{0,1},{1,0},{2,3},{3,2},{4,5},{5,4},{6,7},{7,6},{8,9},{9,8},{10,11... | collective-permute-start | bytes 1572872 | tf_op jit(solution)/shard_map/ppermute | solution.py:41
  28.8 2.6 %collective-permute-start.8 = (bf16[512,512]{1,0:T(8,128)(2,1)S(1)}, bf16[512,512]{1,0:T(8,128)(2,1)S(1)}, u32[]{:S(2)}, u32[]{:S(2)}) collective-permute-start(bf16[512,512]{1,0:T(8,128)(2,1)S(1)} %collective-permute-done.7.a2), channel_id=1, source_target_pairs={{0,1},{1,0},{2,3},{3,2},{4,5},{5,4},{6,7},{7,6},{8,9},{9,8},{10,11... | collective-permute-start | bytes 1572872 | tf_op jit(solution)/shard_map/ppermute | solution.py:41
  29.3 18.5 %collective-permute-start.3 = (bf16[8,64,512]{2,1,0:T(8,128)(2,1)S(1)}, bf16[8,64,512]{2,1,0:T(8,128)(2,1)}, u32[]{:S(2)}, u32[]{:S(2)}) collective-permute-start(bf16[8,64,512]{2,1,0:T(8,128)(2,1)S(1)} %all-to-all-done.x0), channel_id=1, source_target_pairs={{0,2},{1,3},{2,0},{3,1},{4,6},{5,7},{6,4},{7,5},{8,10},{9,11},{10,... | collective-permute-start | bytes 1572872 | tf_op jit(solution)/shard_map/ppermute | solution.py:41
  34.9 1.0 copy-start.9
  35.9 14.7 %copy-start = (bf16[2048,512]{1,0:T(8,128)(2,1)S(1)}, bf16[2048,512]{1,0:T(8,128)(2,1)}, u32[]{:S(2)}) copy-start(bf16[2048,512]{1,0:T(8,128)(2,1)} %wq.7) | copy-start | bytes 6291460
  43.4 29.9 %all-to-all-start.2 = ((bf16[8,128,512]{2,1,0:T(8,128)(2,1)}), bf16[8,128,512]{2,1,0:T(8,128)(2,1)}, u32[]{:S(2)}, u32[]{:S(2)}) async-start(bf16[8,128,512]{2,1,0:T(8,128)(2,1)} %bitcast.2), calls=%async_computation.2 | async-start | bytes 2097152 | tf_op jit(solution)/shard_map/all_to_all | solution.py:45
  47.7 2.1 %collective-permute-start.2 = (bf16[8,64,512]{2,1,0:T(8,128)(2,1)S(1)}, bf16[8,64,512]{2,1,0:T(8,128)(2,1)S(1)}, u32[]{:S(2)}, u32[]{:S(2)}) collective-permute-start(bf16[8,64,512]{2,1,0:T(8,128)(2,1)S(1)} %all-to-all-done.x0), channel_id=1, source_target_pairs={{0,1},{1,0},{2,3},{3,2},{4,5},{5,4},{6,7},{7,6},{8,9},{9,8},{10,11... | collective-permute-start | bytes 1572872 | tf_op jit(solution)/shard_map/ppermute | solution.py:41
  47.7 2.8 %collective-permute-start.4 = (bf16[8,64,512]{2,1,0:T(8,128)(2,1)}, bf16[8,64,512]{2,1,0:T(8,128)(2,1)S(1)}, u32[]{:S(2)}, u32[]{:S(2)}) collective-permute-start(bf16[8,64,512]{2,1,0:T(8,128)(2,1)} %collective-permute-done.3.x2), channel_id=1, source_target_pairs={{0,1},{1,0},{2,3},{3,2},{4,5},{5,4},{6,7},{7,6},{8,9},{9,8},{10,11... | collective-permute-start | bytes 1572872 | tf_op jit(solution)/shard_map/ppermute | solution.py:41
  48.2 14.4 %collective-permute-start.1 = (bf16[8,64,512]{2,1,0:T(8,128)(2,1)S(1)}, bf16[8,64,512]{2,1,0:T(8,128)(2,1)S(1)}, u32[]{:S(2)}, u32[]{:S(2)}) collective-permute-start(bf16[8,64,512]{2,1,0:T(8,128)(2,1)S(1)} %all-to-all-done.1.x0), channel_id=1, source_target_pairs={{0,2},{1,3},{2,0},{3,1},{4,6},{5,7},{6,4},{7,5},{8,10},{9,11},{10,... | collective-permute-start | bytes 1572872 | tf_op jit(solution)/shard_map/ppermute | solution.py:41
  49.7 13.1 %collective-permute-start = (bf16[8,64,512]{2,1,0:T(8,128)(2,1)S(1)}, bf16[8,64,512]{2,1,0:T(8,128)(2,1)S(1)}, u32[]{:S(2)}, u32[]{:S(2)}) collective-permute-start(bf16[8,64,512]{2,1,0:T(8,128)(2,1)S(1)} %all-to-all-done.1.x0), channel_id=1, source_target_pairs={{0,1},{1,0},{2,3},{3,2},{4,5},{5,4},{6,7},{7,6},{8,9},{9,8},{10,11... | collective-permute-start | bytes 1572872 | tf_op jit(solution)/shard_map/ppermute | solution.py:41
  50.6 1.6 %copy-start.1 = (bf16[2048,512]{1,0:T(8,128)(2,1)S(1)}, bf16[2048,512]{1,0:T(8,128)(2,1)}, u32[]{:S(2)}) copy-start(bf16[2048,512]{1,0:T(8,128)(2,1)} %wk.7) | copy-start | bytes 6291460
  52.2 1.6 %copy-start.2 = (bf16[2048,512]{1,0:T(8,128)(2,1)S(1)}, bf16[2048,512]{1,0:T(8,128)(2,1)}, u32[]{:S(2)}) copy-start(bf16[2048,512]{1,0:T(8,128)(2,1)} %wv.7) | copy-start | bytes 6291460
  60.6 1.1 copy-start.4
  61.7 1.0 copy-start.7
  62.7 1.9 %collective-permute-start.5 = (bf16[8,64,512]{2,1,0:T(8,128)(2,1)S(1)}, bf16[8,64,512]{2,1,0:T(8,128)(2,1)S(1)}, u32[]{:S(2)}, u32[]{:S(2)}) collective-permute-start(bf16[8,64,512]{2,1,0:T(8,128)(2,1)S(1)} %collective-permute-done.1.x2), channel_id=1, source_target_pairs={{0,1},{1,0},{2,3},{3,2},{4,5},{5,4},{6,7},{7,6},{8,9},{9,8},{10,11... | collective-permute-start | bytes 1572872 | tf_op jit(solution)/shard_map/ppermute | solution.py:41
  70.8 1.2 copy-start.3
  72.0 1.0 copy-start.5
  73.0 6.0 %copy-start.8 = (f32[1,4,4,128,128]{4,3,2,1,0:T(8,128)S(1)}, f32[1,4,4,128,128]{4,3,2,1,0:T(8,128)}, u32[]{:S(2)}) copy-start(f32[1,4,4,128,128]{4,3,2,1,0:T(8,128)} %copy-done.7) | copy-start | bytes 3145732
  73.3 31.8 %all-to-all-start.3 = ((bf16[8,128,512]{2,1,0:T(8,128)(2,1)}), bf16[8,128,512]{2,1,0:T(8,128)(2,1)S(1)}, u32[]{:S(2)}, u32[]{:S(2)}) async-start(bf16[8,128,512]{2,1,0:T(8,128)(2,1)} %get-tuple-element.46), calls=%async_computation.3 | async-start | bytes 2097152 | tf_op jit(solution)/shard_map/all_to_all | solution.py:45
  86.9 3.7 %copy-start.6 = (f32[1,4,4,128,128]{4,3,2,1,0:T(8,128)S(1)}, f32[1,4,4,128,128]{4,3,2,1,0:T(8,128)}, u32[]{:S(2)}) copy-start(f32[1,4,4,128,128]{4,3,2,1,0:T(8,128)} %copy-done.5) | copy-start | bytes 3145732
  86.9 1.6 %collective-permute-start.16 = (bf16[4,64,512]{2,1,0:T(8,128)(2,1)S(1)}, bf16[4,64,512]{2,1,0:T(8,128)(2,1)S(1)}, u32[]{:S(2)}, u32[]{:S(2)}) collective-permute-start(bf16[4,64,512]{2,1,0:T(8,128)(2,1)S(1)} %get-tuple-element.60), channel_id=1, source_target_pairs={{0,1},{1,0},{2,3},{3,2},{4,5},{5,4},{6,7},{7,6},{8,9},{9,8},{10,11... | collective-permute-start | bytes 786440 | tf_op jit(solution)/shard_map/ppermute | solution.py:41
  87.0 1.9 %collective-permute-start.17 = (bf16[4,64,512]{2,1,0:T(8,128)(2,1)S(1)}, bf16[4,64,512]{2,1,0:T(8,128)(2,1)S(1)}, u32[]{:S(2)}, u32[]{:S(2)}) collective-permute-start(bf16[4,64,512]{2,1,0:T(8,128)(2,1)S(1)} %get-tuple-element.61), channel_id=1, source_target_pairs={{0,1},{1,0},{2,3},{3,2},{4,5},{5,4},{6,7},{7,6},{8,9},{9,8},{10,11... | collective-permute-start | bytes 786440 | tf_op jit(solution)/shard_map/ppermute | solution.py:41
  89.0 14.0 %collective-permute-start.18 = (bf16[8,64,512]{2,1,0:T(8,128)(2,1)S(1)}, bf16[8,64,512]{2,1,0:T(8,128)(2,1)S(1)}, u32[]{:S(2)}, u32[]{:S(2)}) collective-permute-start(bf16[8,64,512]{2,1,0:T(8,128)(2,1)S(1)} %add.8), channel_id=1, source_target_pairs={{0,2},{1,3},{2,0},{3,1},{4,6},{5,7},{6,4},{7,5},{8,10},{9,11},{10,... | collective-permute-start | bytes 1572872 | tf_op jit(solution)/shard_map/ppermute | solution.py:41
  98.4 1.6 %collective-permute-start.19 = (bf16[4,64,512]{2,1,0:T(8,128)(2,1)S(1)}, bf16[4,64,512]{2,1,0:T(8,128)(2,1)S(1)}, u32[]{:S(2)}, u32[]{:S(2)}) collective-permute-start(bf16[4,64,512]{2,1,0:T(8,128)(2,1)S(1)} %get-tuple-element.66), channel_id=1, source_target_pairs={{0,1},{1,0},{2,3},{3,2},{4,5},{5,4},{6,7},{7,6},{8,9},{9,8},{10,11... | collective-permute-start | bytes 786440 | tf_op jit(solution)/shard_map/ppermute | solution.py:41
  98.5 1.9 %collective-permute-start.20 = (bf16[4,64,512]{2,1,0:T(8,128)(2,1)S(1)}, bf16[4,64,512]{2,1,0:T(8,128)(2,1)S(1)}, u32[]{:S(2)}, u32[]{:S(2)}) collective-permute-start(bf16[4,64,512]{2,1,0:T(8,128)(2,1)S(1)} %get-tuple-element.67), channel_id=1, source_target_pairs={{0,1},{1,0},{2,3},{3,2},{4,5},{5,4},{6,7},{7,6},{8,9},{9,8},{10,11... | collective-permute-start | bytes 786440 | tf_op jit(solution)/shard_map/ppermute | solution.py:41
  99.0 1.8 %collective-permute-start.14 = (bf16[4,64,512]{2,1,0:T(8,128)(2,1)S(1)}, bf16[4,64,512]{2,1,0:T(8,128)(2,1)S(1)}, u32[]{:S(2)}, u32[]{:S(2)}) collective-permute-start(bf16[4,64,512]{2,1,0:T(8,128)(2,1)S(1)} %get-tuple-element.57), channel_id=1, source_target_pairs={{0,1},{1,0},{2,3},{3,2},{4,5},{5,4},{6,7},{7,6},{8,9},{9,8},{10,11... | collective-permute-start | bytes 786440 | tf_op jit(solution)/shard_map/ppermute | solution.py:41
  99.1 2.1 %collective-permute-start.15 = (bf16[4,64,512]{2,1,0:T(8,128)(2,1)S(1)}, bf16[4,64,512]{2,1,0:T(8,128)(2,1)S(1)}, u32[]{:S(2)}, u32[]{:S(2)}) collective-permute-start(bf16[4,64,512]{2,1,0:T(8,128)(2,1)S(1)} %get-tuple-element.58), channel_id=1, source_target_pairs={{0,1},{1,0},{2,3},{3,2},{4,5},{5,4},{6,7},{7,6},{8,9},{9,8},{10,11... | collective-permute-start | bytes 786440 | tf_op jit(solution)/shard_map/ppermute | solution.py:41
  105.0 19.0 %all-to-all-start.4 = ((bf16[8,64,512]{2,1,0:T(8,128)(2,1)}), bf16[8,64,512]{2,1,0:T(8,128)(2,1)S(1)}, u32[]{:S(2)}, u32[]{:S(2)}) async-start(bf16[8,64,512]{2,1,0:T(8,128)(2,1)} %add.9), calls=%async_computation.4 | async-start | bytes 1048576 | tf_op jit(solution)/shard_map/all_to_all | solution.py:45
  110.0 12.9 %collective-permute-start.23 = (bf16[8,64,512]{2,1,0:T(8,128)(2,1)S(1)}, bf16[8,64,512]{2,1,0:T(8,128)(2,1)S(1)}, u32[]{:S(2)}, u32[]{:S(2)}) collective-permute-start(bf16[8,64,512]{2,1,0:T(8,128)(2,1)S(1)} %add.10), channel_id=1, source_target_pairs={{0,2},{1,3},{2,0},{3,1},{4,6},{5,7},{6,4},{7,5},{8,10},{9,11},{10,... | collective-permute-start | bytes 1572872 | tf_op jit(solution)/shard_map/ppermute | solution.py:41
  111.5 6.8 %collective-permute-start.21 = (bf16[4,64,512]{2,1,0:T(8,128)(2,1)}, bf16[4,64,512]{2,1,0:T(8,128)(2,1)S(1)}, u32[]{:S(2)}, u32[]{:S(2)}) collective-permute-start(bf16[4,64,512]{2,1,0:T(8,128)(2,1)} %get-tuple-element.70), channel_id=1, source_target_pairs={{0,1},{1,0},{2,3},{3,2},{4,5},{5,4},{6,7},{7,6},{8,9},{9,8},{10,11... | collective-permute-start | bytes 786440 | tf_op jit(solution)/shard_map/ppermute | solution.py:41
  111.5 6.8 %collective-permute-start.22 = (bf16[4,64,512]{2,1,0:T(8,128)(2,1)S(1)}, bf16[4,64,512]{2,1,0:T(8,128)(2,1)S(1)}, u32[]{:S(2)}, u32[]{:S(2)}) collective-permute-start(bf16[4,64,512]{2,1,0:T(8,128)(2,1)S(1)} %get-tuple-element.71), channel_id=1, source_target_pairs={{0,1},{1,0},{2,3},{3,2},{4,5},{5,4},{6,7},{7,6},{8,9},{9,8},{10,11... | collective-permute-start | bytes 786440 | tf_op jit(solution)/shard_map/ppermute | solution.py:41
  112.0 0.9 copy-start.15
  116.4 0.7 copy-start.11
  117.1 0.7 copy-start.13
  117.8 6.0 %collective-permute-start.11 = (bf16[256,512]{1,0:T(8,128)(2,1)S(1)}, bf16[256,512]{1,0:T(8,128)(2,1)S(1)}, u32[]{:S(2)}, u32[]{:S(2)}) collective-permute-start(bf16[256,512]{1,0:T(8,128)(2,1)S(1)} %get-tuple-element.51), channel_id=1, source_target_pairs={{0,1},{1,0},{2,3},{3,2},{4,5},{5,4},{6,7},{7,6},{8,9},{9,8},{10,11... | collective-permute-start | bytes 786440 | tf_op jit(solution)/shard_map/ppermute | solution.py:41
  117.8 6.0 %collective-permute-start.12 = (bf16[256,512]{1,0:T(8,128)(2,1)S(1)}, bf16[256,512]{1,0:T(8,128)(2,1)S(1)}, u32[]{:S(2)}, u32[]{:S(2)}) collective-permute-start(bf16[256,512]{1,0:T(8,128)(2,1)S(1)} %get-tuple-element.52), channel_id=1, source_target_pairs={{0,1},{1,0},{2,3},{3,2},{4,5},{5,4},{6,7},{7,6},{8,9},{9,8},{10,11... | collective-permute-start | bytes 786440 | tf_op jit(solution)/shard_map/ppermute | solution.py:41
  122.8 8.4 %copy-start.14 = (bf16[256,512]{1,0:T(8,128)(2,1)S(1)}, bf16[256,512]{1,0:T(8,128)(2,1)}, u32[]{:S(2)}) copy-start(bf16[256,512]{1,0:T(8,128)(2,1)} %copy-done.13) | copy-start | bytes 786436
  122.8 8.4 %copy-start.12 = (bf16[256,512]{1,0:T(8,128)(2,1)S(1)}, bf16[256,512]{1,0:T(8,128)(2,1)}, u32[]{:S(2)}) copy-start(bf16[256,512]{1,0:T(8,128)(2,1)} %copy-done.11) | copy-start | bytes 786436
  123.8 18.4 %copy-start.16 = (s32[512,1]{1,0:T(8,128)S(1)}, s32[512,1]{1,0:T(8,128)}, u32[]{:S(2)}) copy-start(s32[512,1]{1,0:T(8,128)} %get-tuple-element.38.slot_col) | copy-start | bytes 6148
  124.0 18.2 %all-to-all-start.5 = ((bf16[8,64,512]{2,1,0:T(8,128)(2,1)}), bf16[8,64,512]{2,1,0:T(8,128)(2,1)S(1)}, u32[]{:S(2)}, u32[]{:S(2)}) async-start(bf16[8,64,512]{2,1,0:T(8,128)(2,1)} %add.11), calls=%async_computation.5 | async-start | bytes 1048576 | tf_op jit(solution)/shard_map/all_to_all | solution.py:45
  129.7 11.4 %collective-permute-start.13 = (bf16[512,512]{1,0:T(8,128)(2,1)S(1)}, bf16[512,512]{1,0:T(8,128)(2,1)S(1)}, u32[]{:S(2)}, u32[]{:S(2)}) collective-permute-start(bf16[512,512]{1,0:T(8,128)(2,1)S(1)} %add.6), channel_id=1, source_target_pairs={{0,2},{1,3},{2,0},{3,1},{4,6},{5,7},{6,4},{7,5},{8,10},{9,11},{10,... | collective-permute-start | bytes 1572872 | tf_op jit(solution)/shard_map/ppermute | solution.py:41
  131.2 1.5 %collective-permute-start.10 = (bf16[256,512]{1,0:T(8,128)(2,1)S(1)}, bf16[256,512]{1,0:T(8,128)(2,1)S(1)}, u32[]{:S(2)}, u32[]{:S(2)}) collective-permute-start(bf16[256,512]{1,0:T(8,128)(2,1)S(1)} %copy-done.14), channel_id=1, source_target_pairs={{0,1},{1,0},{2,3},{3,2},{4,5},{5,4},{6,7},{7,6},{8,9},{9,8},{10,11... | collective-permute-start | bytes 786440 | tf_op jit(solution)/shard_map/ppermute | solution.py:41
  131.2 1.9 %collective-permute-start.9 = (bf16[256,512]{1,0:T(8,128)(2,1)S(1)}, bf16[256,512]{1,0:T(8,128)(2,1)S(1)}, u32[]{:S(2)}, u32[]{:S(2)}) collective-permute-start(bf16[256,512]{1,0:T(8,128)(2,1)S(1)} %copy-done.12), channel_id=1, source_target_pairs={{0,1},{1,0},{2,3},{3,2},{4,5},{5,4},{6,7},{7,6},{8,9},{9,8},{10,11... | collective-permute-start | bytes 786440 | tf_op jit(solution)/shard_map/ppermute | solution.py:41
